TPU v7x, 128 devices: a whole 4x4x4 slice. The times are simulated.
128 devices in a mesh: depth: 16 (over x_lo, z, core), mod: 8 (over x_hi, y).
Axes of the slice: x: 4 (x_hi: 2, x_lo: 2; x = x_hi * 2 + x_lo), y: 4, z: 4, core: 2. Of those that a mesh axis runs over, the one named last changes fastest.
Arguments:
- tokens: bfloat16 [64, 1024, 768], P('depth', 'mod'), may hold values from -40 to 40
- cotangent: bfloat16 [64, 1024, 768], P('depth', 'mod'), may hold values from -6 to 6
- lesion: int32 [64, 1024], P('depth', 'mod'), may hold values 0 or 1
- w_qkv: bfloat16 [768, 2304], replicated, may hold values from -5 to 5
- w_out: bfloat16 [768, 768], replicated, may hold values from -0.21875 to 0.21875
- norm_gain: float32 [768], replicated, may hold values from 0.5 to 1.5
Outputs:
- mixed: bfloat16 [64, 1024, 768], P('depth', 'mod')
- grad_tokens: bfloat16 [64, 1024, 768], P('depth', 'mod')
- grad_qkv_weight: float32 [768, 2304], P(('depth', 'mod'))
- grad_out_weight: float32 [768, 768], P(('depth', 'mod'))
- grad_gain: float32 [768], P(('depth', 'mod'))
All inputs are finite; a program needn't handle non-finite values. No bound on the sum of `lesion` on one device may be relied on, other than what follows from the above.
Results may differ from a plain program's by a relative error of at most 0.007.
The roundings to bfloat16 on the way count: a program that leaves them out, or rounds other values in their place, can miss the bound.
Values may be sent and summed in bfloat16 or wider, within the bound.
No kernel may reach another device: no remote copies, remote signals or barrier semaphores. Data moves between devices by JAX's collectives and lax.ppermute only.
A program may use at most 128 MiB of HBM per device.

v0:
```python
import jax
import jax.numpy as jnp
from jax import lax
from jax.sharding import PartitionSpec as P

HEADS = 12
HEAD_DIM = 64


EPS = 1e-06
LESION_GAIN = 3.0


def partner(array, axis, distance):
    return lax.ppermute(array, axis, [(i, i ^ 1 << distance) for i in range(lax.axis_size(axis))])


def attend_forward(query, keys, values):
    depth_len, positions, width = query.shape
    scale = float(HEAD_DIM) ** (-0.5)
    q_heads = query.reshape(depth_len, positions, HEADS, HEAD_DIM)
    k_heads = keys.reshape(2 * depth_len, positions, HEADS, HEAD_DIM)
    v_heads = values.reshape(2 * depth_len, positions, HEADS, HEAD_DIM)
    scores = (
        jnp.einsum("qphd,kphd->phqk", q_heads, k_heads, preferred_element_type=jnp.float32) * scale
    )
    top = jnp.max(scores, axis=-1, keepdims=True)
    expd = jnp.exp(scores - top)
    probs = expd / jnp.sum(expd, axis=-1, keepdims=True)
    probs_bf = probs.astype(jnp.bfloat16)
    attn = jnp.einsum("phqk,kphd->qphd", probs_bf, v_heads, preferred_element_type=jnp.float32)
    return (attn.astype(jnp.bfloat16).reshape(depth_len, positions, width), probs, probs_bf)


def attend_backward(query, keys, values, probs, probs_bf, grad_attn):
    depth_len, positions, width = query.shape
    scale = float(HEAD_DIM) ** (-0.5)
    q_heads = query.reshape(depth_len, positions, HEADS, HEAD_DIM)
    k_heads = keys.reshape(2 * depth_len, positions, HEADS, HEAD_DIM)
    v_heads = values.reshape(2 * depth_len, positions, HEADS, HEAD_DIM)
    g_heads = grad_attn.reshape(depth_len, positions, HEADS, HEAD_DIM)
    dprob = jnp.einsum("qphd,kphd->phqk", g_heads, v_heads, preferred_element_type=jnp.float32)
    delta = jnp.sum(probs * dprob, axis=-1, keepdims=True)
    dscore = (probs * (dprob - delta) * scale).astype(jnp.bfloat16)
    grad_query = jnp.einsum("phqk,kphd->qphd", dscore, k_heads, preferred_element_type=jnp.float32)
    kterm = jnp.einsum("phqk,qphd->kphd", dscore, q_heads, preferred_element_type=jnp.float32)
    vterm = jnp.einsum("phqk,qphd->kphd", probs_bf, g_heads, preferred_element_type=jnp.float32)
    grad_query = grad_query.astype(jnp.bfloat16).reshape(depth_len, positions, width)
    return (
        grad_query,
        kterm.reshape(2 * depth_len, positions, width),
        vterm.reshape(2 * depth_len, positions, width),
    )


def per_device(tokens, cotangent, lesion, w_qkv, w_out, norm_gain):
    width = tokens.shape[-1]
    n_mod = lax.axis_size("mod")
    partner_bit = n_mod.bit_length() - 2
    xf = tokens.astype(jnp.float32)
    inv_rms = lax.rsqrt(jnp.mean(xf * xf, axis=-1, keepdims=True) + EPS)
    unit = xf * inv_rms
    normed = (unit * norm_gain).astype(jnp.bfloat16)
    qkv = jnp.einsum("srd,de->sre", normed, w_qkv, preferred_element_type=jnp.float32).astype(
        jnp.bfloat16
    )
    qkv_col = lax.all_to_all(qkv, "depth", split_axis=1, concat_axis=0, tiled=True)
    own_kv = qkv_col[..., width:]
    other_kv = partner(own_kv, "mod", partner_bit)
    depth_len = qkv_col.shape[0]
    query = qkv_col[..., :width]
    keys = jnp.concatenate([own_kv[..., :width], other_kv[..., :width]], axis=0)
    values = jnp.concatenate([own_kv[..., width:], other_kv[..., width:]], axis=0)
    attn_col, probs, probs_bf = attend_forward(query, keys, values)
    weight = 1.0 + LESION_GAIN * lesion.astype(jnp.float32)
    grad_y = (cotangent.astype(jnp.float32) * weight[..., None]).astype(jnp.bfloat16)
    attn = lax.all_to_all(attn_col, "depth", split_axis=0, concat_axis=1, tiled=True)
    proj = jnp.einsum("srd,de->sre", attn, w_out, preferred_element_type=jnp.float32).astype(
        jnp.bfloat16
    )
    out_term = jnp.einsum("srd,sre->de", attn, grad_y, preferred_element_type=jnp.float32)
    grad_attn_rows = jnp.einsum(
        "sre,de->srd", grad_y, w_out, preferred_element_type=jnp.float32
    ).astype(jnp.bfloat16)
    grad_attn = lax.all_to_all(grad_attn_rows, "depth", split_axis=1, concat_axis=0, tiled=True)
    mixed = (xf + proj.astype(jnp.float32)).astype(jnp.bfloat16)
    grad_query, kterm, vterm = attend_backward(query, keys, values, probs, probs_bf, grad_attn)
    cross_terms = jnp.concatenate([kterm[depth_len:], vterm[depth_len:]], axis=-1).astype(
        jnp.bfloat16
    )
    returned = partner(cross_terms, "mod", partner_bit)
    grad_key = (kterm[:depth_len] + returned[..., :width].astype(jnp.float32)).astype(jnp.bfloat16)
    grad_value = (vterm[:depth_len] + returned[..., width:].astype(jnp.float32)).astype(
        jnp.bfloat16
    )
    grad_qkv_col = jnp.concatenate([grad_query, grad_key, grad_value], axis=-1)
    grad_qkv = lax.all_to_all(grad_qkv_col, "depth", split_axis=0, concat_axis=1, tiled=True)
    qkv_term = jnp.einsum("srd,sre->de", normed, grad_qkv, preferred_element_type=jnp.float32)
    grad_normed = jnp.einsum(
        "sre,de->srd", grad_qkv, w_qkv, preferred_element_type=jnp.float32
    ).astype(jnp.bfloat16)
    gradient_n = grad_normed.astype(jnp.float32)
    gain_term = jnp.sum(gradient_n * unit, axis=(0, 1))
    dunit = gradient_n * norm_gain
    norm_back = inv_rms * (dunit - unit * jnp.mean(dunit * unit, axis=-1, keepdims=True))
    grad_tokens = (grad_y.astype(jnp.float32) + norm_back).astype(jnp.bfloat16)
    qkv_share, out_share, gain_share = (
        lax.psum_scatter(qkv_term, ("depth", "mod"), scatter_dimension=0, tiled=True),
        lax.psum_scatter(out_term, ("depth", "mod"), scatter_dimension=0, tiled=True),
        lax.psum_scatter(gain_term, ("depth", "mod"), scatter_dimension=0, tiled=True),
    )
    return (mixed, grad_tokens, qkv_share, out_share, gain_share)


def solution(mesh):
    in_specs = (P("depth", "mod", None), P("depth", "mod", None), P("depth", "mod"), P(), P(), P())
    out_specs = (
        P("depth", "mod", None),
        P("depth", "mod", None),
        P(("depth", "mod"), None),
        P(("depth", "mod"), None),
        P(("depth", "mod")),
    )
    return jax.shard_map(
        per_device, mesh=mesh, in_specs=in_specs, out_specs=out_specs, check_vma=False
    )
```

profile of v0, /device:TPU:0, one launch (start us, length us, event | category | flops | bytes accessed | tf_op | source)
XLA Modules:
  0.0 1035.6 jit_solution(8474201058728375290)
XLA Ops:
  2.9 3.2 convolution_convert_fusion
  7.9 36.8 %all_to_all.69 = bf16[4,128,2304]{2,0,1:T(4,128)(2,1)S(1)} all-to-all(bf16[4,128,2304]{2,0,1:T(4,128)(2,1)S(1)} %copy.54), channel_id=1, replica_groups=mesh['depth'=16,'mod'=8] {'depth'}, dimensions={1} | all-to-all | bytes 4718592 | tf_op jit(solution)/shard_map/all_to_all | solution.py:67
  51.4 42.1 %all_to_all.70 = bf16[4,128,768]{2,0,1:T(4,128)(2,1)S(1)} all-to-all(bf16[4,128,768]{2,0,1:T(4,128)(2,1)S(1)} %copy.62), channel_id=1, replica_groups=mesh['depth'=16,'mod'=8] {'depth'}, dimensions={1} | all-to-all | bytes 1572864 | tf_op jit(solution)/shard_map/all_to_all | solution.py:85
  94.5 3.8 reshape.61
  98.2 4.1 copy.66
  102.4 3.1 fusion.68
  117.6 4.3 fusion.71
  121.9 5.7 fusion.70
  127.6 5.0 convolution_bitcast_fusion.1
  132.6 39.6 %fusion.27 = f32[128,8,12,64]{0,3,2,1:T(8,128)} fusion(bf16[64,8,12,64]{0,3,2,1:T(8,128)(2,1)} %bitcast.89, f32[8,12,64,128]{3,2,1,0:T(8,128)} %fusion.71, f32[8,12,64,128]{3,2,1,0:T(8,128)} %get-tuple-element.19, f32[8,12,64]{2,1,0:T(8,128)} %get-tuple-element.18), kind=kOutput, calls=%fused_computation.31 | convolution fusion | flops 106174592 | bytes 10248192 | tf_op jit(solution)/shard_map/phqk,qphd->kphd/dot_general | solution.py:46
  172.2 3.6 slice.86
  178.4 3.6 slice.87
  189.3 39.3 %fusion.31 = bf16[8,12,64,64]{3,2,1,0:T(8,128)(2,1)} fusion(bf16[128,8,12,64]{0,3,2,1:T(8,128)(2,1)} %bitcast.91, f32[8,12,64,128]{3,2,1,0:T(8,128)} %fusion.71, f32[8,12,64,128]{3,2,1,0:T(8,128)} %get-tuple-element.19, f32[8,12,64]{2,1,0:T(8,128)} %get-tuple-element.18), kind=kOutput, calls=%fused_computation.35 | convolution fusion | flops 106567808 | bytes 8675328 | tf_op jit(solution)/shard_map/phqk,kphd->qphd/dot_general | solution.py:45
  231.2 4.6 convolution_convert_fusion.1
  238.3 4.3 all-to-all-start.1
  242.6 3.4 copy.70
  246.0 3.3 copy.69
  256.4 4.4 all-to-all-start.3
  260.9 3.8 convolution_bitcast_fusion.2
  264.6 27.9 %all-to-all-done.3 = bf16[64,8,2304]{2,1,0:T(8,128)(2,1)} async-done(((bf16[64,8,2304]{2,1,0:T(8,128)(2,1)}), bf16[64,8,2304]{2,1,0:T(8,128)(2,1)}, u32[]{:S(2)}, u32[]{:S(2)}) %all-to-all-start.3) | async-done | bytes 2359328 | tf_op jit(solution)/shard_map/all_to_all | solution.py:97
  292.5 6.9 convolution_bitcast_fusion
  299.4 379.0 %fusion.67 = (f32[8,2304]{1,0:T(8,128)}, f32[8,768]{1,0:T(8,128)}) fusion(f32[768,2304]{1,0:T(8,128)} %convolution_bitcast_fusion, f32[768,768]{1,0:T(8,128)} %convolution_bitcast_fusion.2), kind=kCustom, calls=%all-reduce-scatter.2 | all-reduce-scatter fusion | flops 3145729 | bytes 9535488
  690.9 14.2 %collective-permute-start.56 = (f32[8,768]{1,0:T(8,128)}, f32[8,768]{1,0:T(8,128)S(1)}, u32[]{:S(2)}, u32[]{:S(2)}) collective-permute-start(f32[8,768]{1,0:T(8,128)} %get-tuple-element.10), channel_id=1, source_target_pairs={{0,23},{1,24},{2,25},{3,26},{4,27},{5,28},{6,29},{7,30},{8,31},{9,... | collective-permute-start | bytes 73736
  705.1 5.4 collective-permute-start.55
  710.5 3.4 collective-permute-start.54
  722.3 7.3 collective-permute-start.48
  730.9 2.9 collective-permute-start.46
  733.9 3.3 collective-permute-start.45
  738.6 3.9 collective-permute-start.43
  745.6 6.9 collective-permute-start.40
  758.8 3.8 collective-permute-start.38
  765.2 3.1 collective-permute-start.36
  768.3 4.9 collective-permute-start.35
  774.6 4.5 collective-permute-start.31
  790.3 6.0 collective-permute-start.24
  800.2 3.4 fusion.41
  807.2 3.3 collective-permute-start.19
  814.9 3.9 fusion.39
  818.8 6.5 collective-permute-start.16
  829.2 3.7 collective-permute-start.13
  841.2 5.0 collective-permute-start.8
  849.9 62.6 %all-reduce.2 = f32[768]{0:T(1024)S(1)} all-reduce(f32[768]{0:T(1024)S(1)} %get-tuple-element.5), channel_id=4, replica_groups=mesh['depth'=16,'mod'=8] {'depth','mod'}, use_global_device_ids=true, to_apply=%region_8.0.clone | all-reduce | flops 768 | bytes 6144
  913.0 47.3 %concatenate.18 = f32[262,768]{1,0:T(8,128)} concatenate(f32[6,768]{1,0:T(8,128)} %copy-done.21, f32[8,768]{1,0:T(8,128)} %copy-done.20, f32[8,768]{1,0:T(8,128)} %copy-done.22, f32[8,768]{1,0:T(8,128)} %copy-done.23, f32[8,768]{1,0:T(8,128)} %copy-done.24, f32[8,768]{1,0:T(8,128)} %copy-done.25, f32[8,768]{1,0:T(8,128)} %copy-done.26, f32[8,768]{1,0:T(8,128)} %copy-done.27, ...), dimensions={0} | concatenate | bytes 1609728
  960.3 3.5 collective-permute-start.6
  963.9 4.0 collective-permute-start.5
  967.9 3.4 collective-permute-start.4
  971.3 4.1 collective-permute-start.3
  979.8 54.1 %concatenate.17 = f32[262,2304]{1,0:T(8,128)} concatenate(f32[6,2304]{1,0:T(8,128)} %copy-done.9, f32[8,2304]{1,0:T(8,128)} %collective-permute-done.32, f32[8,2304]{1,0:T(8,128)} %collective-permute-done.31, f32[8,2304]{1,0:T(8,128)} %collective-permute-done.30, f32[8,2304]{1,0:T(8,128)} %collective-permute-done.29, f32[8,2304]{1,0:T(8,128)} %collective-permute-done.28, ...), dimensions={0} | concatenate | bytes 4829184
  (249 shorter events, 127.5 us)
Async XLA Ops:
  47.2 60.9 %collective-permute-start = (bf16[64,8,1536]{2,1,0:T(8,128)(2,1)}, bf16[64,8,1536]{2,1,0:T(8,128)(2,1)}, u32[]{:S(2)}, u32[]{:S(2)}) collective-permute-start(bf16[64,8,1536]{2,1,0:T(8,128)(2,1)} %slice.69), channel_id=1, source_target_pairs={{0,4},{1,5},{2,6},{3,7},{4,0},{5,1},{6,2},{7,3},{8,12},{9,13},{10,... | collective-permute-start | bytes 4718600 | tf_op jit(solution)/shard_map/ppermute | solution.py:15
  187.1 62.2 %collective-permute-start.1 = (bf16[64,8,1536]{2,1,0:T(8,128)(2,1)}, bf16[64,8,1536]{2,1,0:T(8,128)(2,1)}, u32[]{:S(2)}, u32[]{:S(2)}) collective-permute-start(bf16[64,8,1536]{2,1,0:T(8,128)(2,1)} %pad_maximum_fusion.3), channel_id=1, source_target_pairs={{0,4},{1,5},{2,6},{3,7},{4,0},{5,1},{6,2},{7,3},{8,12},{9,13},{10,... | collective-permute-start | bytes 4718600 | tf_op jit(solution)/shard_map/ppermute | solution.py:15
  238.3 18.1 %all-to-all-start.1 = ((bf16[64,8,768]{2,1,0:T(8,128)(2,1)}), bf16[64,8,768]{2,1,0:T(8,128)(2,1)}, u32[]{:S(2)}, u32[]{:S(2)}) async-start(bf16[64,8,768]{2,1,0:T(8,128)(2,1)} %copy.60), calls=%async_computation.1 | async-start | bytes 1572864 | tf_op jit(solution)/shard_map/all_to_all | solution.py:77
  256.4 36.1 %all-to-all-start.3 = ((bf16[64,8,2304]{2,1,0:T(8,128)(2,1)}), bf16[64,8,2304]{2,1,0:T(8,128)(2,1)}, u32[]{:S(2)}, u32[]{:S(2)}) async-start(bf16[64,8,2304]{2,1,0:T(8,128)(2,1)} %pad_maximum_fusion), calls=%async_computation.3 | async-start | bytes 4718592 | tf_op jit(solution)/shard_map/all_to_all | solution.py:97
  685.6 19.5 %collective-permute-start.60 = (f32[8,768]{1,0:T(8,128)}, f32[8,768]{1,0:T(8,128)S(1)}, u32[]{:S(2)}, u32[]{:S(2)}) collective-permute-start(f32[8,768]{1,0:T(8,128)} %get-tuple-element.10), channel_id=1, source_target_pairs={{0,27},{1,28},{2,29},{3,30},{4,31},{5,32},{6,33},{7,34},{8,35},{9,... | collective-permute-start | bytes 73736
  686.9 23.5 %collective-permute-start.59 = (f32[8,768]{1,0:T(8,128)}, f32[8,768]{1,0:T(8,128)S(1)}, u32[]{:S(2)}, u32[]{:S(2)}) collective-permute-start(f32[8,768]{1,0:T(8,128)} %get-tuple-element.10), channel_id=1, source_target_pairs={{0,26},{1,27},{2,28},{3,29},{4,30},{5,31},{6,32},{7,33},{8,34},{9,... | collective-permute-start | bytes 73736
  688.2 25.7 %collective-permute-start.58 = (f32[8,768]{1,0:T(8,128)}, f32[8,768]{1,0:T(8,128)S(1)}, u32[]{:S(2)}, u32[]{:S(2)}) collective-permute-start(f32[8,768]{1,0:T(8,128)} %get-tuple-element.10), channel_id=1, source_target_pairs={{0,25},{1,26},{2,27},{3,28},{4,29},{5,30},{6,31},{7,32},{8,33},{9,... | collective-permute-start | bytes 73736
  689.6 25.7 %collective-permute-start.57 = (f32[8,768]{1,0:T(8,128)}, f32[8,768]{1,0:T(8,128)S(1)}, u32[]{:S(2)}, u32[]{:S(2)}) collective-permute-start(f32[8,768]{1,0:T(8,128)} %get-tuple-element.10), channel_id=1, source_target_pairs={{0,24},{1,25},{2,26},{3,27},{4,28},{5,29},{6,30},{7,31},{8,32},{9,... | collective-permute-start | bytes 73736
  690.9 25.7 %collective-permute-start.56 = (f32[8,768]{1,0:T(8,128)}, f32[8,768]{1,0:T(8,128)S(1)}, u32[]{:S(2)}, u32[]{:S(2)}) collective-permute-start(f32[8,768]{1,0:T(8,128)} %get-tuple-element.10), channel_id=1, source_target_pairs={{0,23},{1,24},{2,25},{3,26},{4,27},{5,28},{6,29},{7,30},{8,31},{9,... | collective-permute-start | bytes 73736
  705.1 13.9 %collective-permute-start.55 = (f32[8,768]{1,0:T(8,128)}, f32[8,768]{1,0:T(8,128)S(1)}, u32[]{:S(2)}, u32[]{:S(2)}) collective-permute-start(f32[8,768]{1,0:T(8,128)} %get-tuple-element.10), channel_id=1, source_target_pairs={{0,22},{1,23},{2,24},{3,25},{4,26},{5,27},{6,28},{7,29},{8,30},{9,... | collective-permute-start | bytes 73736
  715.3 14.3 %collective-permute-start.52 = (f32[8,768]{1,0:T(8,128)}, f32[8,768]{1,0:T(8,128)S(1)}, u32[]{:S(2)}, u32[]{:S(2)}) collective-permute-start(f32[8,768]{1,0:T(8,128)} %get-tuple-element.10), channel_id=1, source_target_pairs={{0,19},{1,20},{2,21},{3,22},{4,23},{5,24},{6,25},{7,26},{8,27},{9,... | collective-permute-start | bytes 73736
  716.6 14.3 %collective-permute-start.51 = (f32[8,768]{1,0:T(8,128)}, f32[8,768]{1,0:T(8,128)S(1)}, u32[]{:S(2)}, u32[]{:S(2)}) collective-permute-start(f32[8,768]{1,0:T(8,128)} %get-tuple-element.10), channel_id=1, source_target_pairs={{0,18},{1,19},{2,20},{3,21},{4,22},{5,23},{6,24},{7,25},{8,26},{9,... | collective-permute-start | bytes 73736
  719.0 14.9 %collective-permute-start.50 = (f32[8,768]{1,0:T(8,128)}, f32[8,768]{1,0:T(8,128)S(1)}, u32[]{:S(2)}, u32[]{:S(2)}) collective-permute-start(f32[8,768]{1,0:T(8,128)} %get-tuple-element.10), channel_id=1, source_target_pairs={{0,17},{1,18},{2,19},{3,20},{4,21},{5,22},{6,23},{7,24},{8,25},{9,... | collective-permute-start | bytes 73736
  721.0 16.2 %collective-permute-start.49 = (f32[8,768]{1,0:T(8,128)}, f32[8,768]{1,0:T(8,128)S(1)}, u32[]{:S(2)}, u32[]{:S(2)}) collective-permute-start(f32[8,768]{1,0:T(8,128)} %get-tuple-element.10), channel_id=1, source_target_pairs={{0,16},{1,17},{2,18},{3,19},{4,20},{5,21},{6,22},{7,23},{8,24},{9,... | collective-permute-start | bytes 73736
  722.3 16.3 %collective-permute-start.48 = (f32[8,768]{1,0:T(8,128)}, f32[8,768]{1,0:T(8,128)S(1)}, u32[]{:S(2)}, u32[]{:S(2)}) collective-permute-start(f32[8,768]{1,0:T(8,128)} %get-tuple-element.10), channel_id=1, source_target_pairs={{0,15},{1,16},{2,17},{3,18},{4,19},{5,20},{6,21},{7,22},{8,23},{9,... | collective-permute-start | bytes 73736
  729.6 12.9 %collective-permute-start.47 = (f32[8,768]{1,0:T(8,128)}, f32[8,768]{1,0:T(8,128)S(1)}, u32[]{:S(2)}, u32[]{:S(2)}) collective-permute-start(f32[8,768]{1,0:T(8,128)} %get-tuple-element.10), channel_id=1, source_target_pairs={{0,14},{1,15},{2,16},{3,17},{4,18},{5,19},{6,20},{7,21},{8,22},{9,... | collective-permute-start | bytes 73736
  730.9 13.0 %collective-permute-start.46 = (f32[8,768]{1,0:T(8,128)}, f32[8,768]{1,0:T(8,128)S(1)}, u32[]{:S(2)}, u32[]{:S(2)}) collective-permute-start(f32[8,768]{1,0:T(8,128)} %get-tuple-element.10), channel_id=1, source_target_pairs={{0,13},{1,14},{2,15},{3,16},{4,17},{5,18},{6,19},{7,20},{8,21},{9,... | collective-permute-start | bytes 73736
  737.2 15.3 %collective-permute-start.44 = (f32[8,768]{1,0:T(8,128)}, f32[8,768]{1,0:T(8,128)S(1)}, u32[]{:S(2)}, u32[]{:S(2)}) collective-permute-start(f32[8,768]{1,0:T(8,128)} %get-tuple-element.10), channel_id=1, source_target_pairs={{0,11},{1,12},{2,13},{3,14},{4,15},{5,16},{6,17},{7,18},{8,19},{9,... | collective-permute-start | bytes 73736
  738.6 17.3 %collective-permute-start.43 = (f32[8,768]{1,0:T(8,128)}, f32[8,768]{1,0:T(8,128)S(1)}, u32[]{:S(2)}, u32[]{:S(2)}) collective-permute-start(f32[8,768]{1,0:T(8,128)} %get-tuple-element.10), channel_id=1, source_target_pairs={{0,10},{1,11},{2,12},{3,13},{4,14},{5,15},{6,16},{7,17},{8,18},{9,... | collective-permute-start | bytes 73736
  742.6 14.7 %collective-permute-start.42 = (f32[8,768]{1,0:T(8,128)}, f32[8,768]{1,0:T(8,128)S(1)}, u32[]{:S(2)}, u32[]{:S(2)}) collective-permute-start(f32[8,768]{1,0:T(8,128)} %get-tuple-element.10), channel_id=1, source_target_pairs={{0,9},{1,10},{2,11},{3,12},{4,13},{5,14},{6,15},{7,16},{8,17},{9,1... | collective-permute-start | bytes 73736
  743.9 14.9 %collective-permute-start.41 = (f32[8,768]{1,0:T(8,128)}, f32[8,768]{1,0:T(8,128)S(1)}, u32[]{:S(2)}, u32[]{:S(2)}) collective-permute-start(f32[8,768]{1,0:T(8,128)} %get-tuple-element.10), channel_id=1, source_target_pairs={{0,8},{1,9},{2,10},{3,11},{4,12},{5,13},{6,14},{7,15},{8,16},{9,17... | collective-permute-start | bytes 73736
  745.6 17.0 %collective-permute-start.40 = (f32[8,768]{1,0:T(8,128)}, f32[8,768]{1,0:T(8,128)S(1)}, u32[]{:S(2)}, u32[]{:S(2)}) collective-permute-start(f32[8,768]{1,0:T(8,128)} %get-tuple-element.10), channel_id=1, source_target_pairs={{0,7},{1,8},{2,9},{3,10},{4,11},{5,12},{6,13},{7,14},{8,15},{9,16}... | collective-permute-start | bytes 73736
  753.1 32.4 %collective-permute-start.32 = (f32[8,2304]{1,0:T(8,128)}, f32[8,2304]{1,0:T(8,128)}, u32[]{:S(2)}, u32[]{:S(2)}) collective-permute-start(f32[8,2304]{1,0:T(8,128)} %get-tuple-element.9), channel_id=1, source_target_pairs={{0,31},{1,32},{2,33},{3,34},{4,35},{5,36},{6,37},{7,38},{8,39},{9,... | collective-permute-start | bytes 221192
  755.9 27.0 %collective-permute-start.33 = (f32[6,2304]{1,0:T(8,128)S(1)}, f32[6,2304]{1,0:T(8,128)S(1)}, u32[]{:S(2)}, u32[]{:S(2)}) collective-permute-start(f32[6,2304]{1,0:T(8,128)S(1)} %slice.80), channel_id=1, source_target_pairs={{0,32},{1,33},{2,34},{3,35},{4,36},{5,37},{6,38},{7,39},{8,40},{9,... | collective-permute-start | bytes 165896
  774.6 13.0 %collective-permute-start.31 = (f32[8,2304]{1,0:T(8,128)}, f32[8,2304]{1,0:T(8,128)}, u32[]{:S(2)}, u32[]{:S(2)}) collective-permute-start(f32[8,2304]{1,0:T(8,128)} %get-tuple-element.9), channel_id=1, source_target_pairs={{0,30},{1,31},{2,32},{3,33},{4,34},{5,35},{6,36},{7,37},{8,38},{9,... | collective-permute-start | bytes 221192
  783.6 12.7 %collective-permute-start.28 = (f32[8,2304]{1,0:T(8,128)}, f32[8,2304]{1,0:T(8,128)}, u32[]{:S(2)}, u32[]{:S(2)}) collective-permute-start(f32[8,2304]{1,0:T(8,128)} %get-tuple-element.9), channel_id=1, source_target_pairs={{0,27},{1,28},{2,29},{3,30},{4,31},{5,32},{6,33},{7,34},{8,35},{9,... | collective-permute-start | bytes 221192
  785.5 12.3 %collective-permute-start.27 = (f32[8,2304]{1,0:T(8,128)}, f32[8,2304]{1,0:T(8,128)}, u32[]{:S(2)}, u32[]{:S(2)}) collective-permute-start(f32[8,2304]{1,0:T(8,128)} %get-tuple-element.9), channel_id=1, source_target_pairs={{0,26},{1,27},{2,28},{3,29},{4,30},{5,31},{6,32},{7,33},{8,34},{9,... | collective-permute-start | bytes 221192
  787.5 16.1 %collective-permute-start.26 = (f32[8,2304]{1,0:T(8,128)}, f32[8,2304]{1,0:T(8,128)S(1)}, u32[]{:S(2)}, u32[]{:S(2)}) collective-permute-start(f32[8,2304]{1,0:T(8,128)} %get-tuple-element.9), channel_id=1, source_target_pairs={{0,25},{1,26},{2,27},{3,28},{4,29},{5,30},{6,31},{7,32},{8,33},{9,... | collective-permute-start | bytes 221192
  789.0 16.1 %collective-permute-start.25 = (f32[8,2304]{1,0:T(8,128)}, f32[8,2304]{1,0:T(8,128)S(1)}, u32[]{:S(2)}, u32[]{:S(2)}) collective-permute-start(f32[8,2304]{1,0:T(8,128)} %get-tuple-element.9), channel_id=1, source_target_pairs={{0,24},{1,25},{2,26},{3,27},{4,28},{5,29},{6,30},{7,31},{8,32},{9,... | collective-permute-start | bytes 221192
  790.3 16.8 %collective-permute-start.24 = (f32[8,2304]{1,0:T(8,128)}, f32[8,2304]{1,0:T(8,128)S(1)}, u32[]{:S(2)}, u32[]{:S(2)}) collective-permute-start(f32[8,2304]{1,0:T(8,128)} %get-tuple-element.9), channel_id=1, source_target_pairs={{0,23},{1,24},{2,25},{3,26},{4,27},{5,28},{6,29},{7,30},{8,31},{9,... | collective-permute-start | bytes 221192
  796.3 14.2 %collective-permute-start.23 = (f32[8,2304]{1,0:T(8,128)}, f32[8,2304]{1,0:T(8,128)S(1)}, u32[]{:S(2)}, u32[]{:S(2)}) collective-permute-start(f32[8,2304]{1,0:T(8,128)} %get-tuple-element.9), channel_id=1, source_target_pairs={{0,22},{1,23},{2,24},{3,25},{4,26},{5,27},{6,28},{7,29},{8,30},{9,... | collective-permute-start | bytes 221192
  797.8 14.4 %collective-permute-start.22 = (f32[8,2304]{1,0:T(8,128)}, f32[8,2304]{1,0:T(8,128)S(1)}, u32[]{:S(2)}, u32[]{:S(2)}) collective-permute-start(f32[8,2304]{1,0:T(8,128)} %get-tuple-element.9), channel_id=1, source_target_pairs={{0,21},{1,22},{2,23},{3,24},{4,25},{5,26},{6,27},{7,28},{8,29},{9,... | collective-permute-start | bytes 221192
  803.6 15.1 %collective-permute-start.21 = (f32[8,2304]{1,0:T(8,128)}, f32[8,2304]{1,0:T(8,128)S(1)}, u32[]{:S(2)}, u32[]{:S(2)}) collective-permute-start(f32[8,2304]{1,0:T(8,128)} %get-tuple-element.9), channel_id=1, source_target_pairs={{0,20},{1,21},{2,22},{3,23},{4,24},{5,25},{6,26},{7,27},{8,28},{9,... | collective-permute-start | bytes 221192
  805.1 20.2 %collective-permute-start.20 = (f32[8,2304]{1,0:T(8,128)}, f32[8,2304]{1,0:T(8,128)S(1)}, u32[]{:S(2)}, u32[]{:S(2)}) collective-permute-start(f32[8,2304]{1,0:T(8,128)} %get-tuple-element.9), channel_id=1, source_target_pairs={{0,19},{1,20},{2,21},{3,22},{4,23},{5,24},{6,25},{7,26},{8,27},{9,... | collective-permute-start | bytes 221192
  807.2 20.1 %collective-permute-start.19 = (f32[8,2304]{1,0:T(8,128)}, f32[8,2304]{1,0:T(8,128)S(1)}, u32[]{:S(2)}, u32[]{:S(2)}) collective-permute-start(f32[8,2304]{1,0:T(8,128)} %get-tuple-element.9), channel_id=1, source_target_pairs={{0,18},{1,19},{2,20},{3,21},{4,22},{5,23},{6,24},{7,25},{8,26},{9,... | collective-permute-start | bytes 221192
  810.5 18.7 %collective-permute-start.18 = (f32[8,2304]{1,0:T(8,128)}, f32[8,2304]{1,0:T(8,128)S(1)}, u32[]{:S(2)}, u32[]{:S(2)}) collective-permute-start(f32[8,2304]{1,0:T(8,128)} %get-tuple-element.9), channel_id=1, source_target_pairs={{0,17},{1,18},{2,19},{3,20},{4,21},{5,22},{6,23},{7,24},{8,25},{9,... | collective-permute-start | bytes 221192
  813.0 20.0 %collective-permute-start.17 = (f32[8,2304]{1,0:T(8,128)}, f32[8,2304]{1,0:T(8,128)S(1)}, u32[]{:S(2)}, u32[]{:S(2)}) collective-permute-start(f32[8,2304]{1,0:T(8,128)} %get-tuple-element.9), channel_id=1, source_target_pairs={{0,16},{1,17},{2,18},{3,19},{4,20},{5,21},{6,22},{7,23},{8,24},{9,... | collective-permute-start | bytes 221192
  818.8 16.1 %collective-permute-start.16 = (f32[8,2304]{1,0:T(8,128)}, f32[8,2304]{1,0:T(8,128)}, u32[]{:S(2)}, u32[]{:S(2)}) collective-permute-start(f32[8,2304]{1,0:T(8,128)} %get-tuple-element.9), channel_id=1, source_target_pairs={{0,15},{1,16},{2,17},{3,18},{4,19},{5,20},{6,21},{7,22},{8,23},{9,... | collective-permute-start | bytes 221192
  825.3 12.1 %collective-permute-start.15 = (f32[8,2304]{1,0:T(8,128)}, f32[8,2304]{1,0:T(8,128)}, u32[]{:S(2)}, u32[]{:S(2)}) collective-permute-start(f32[8,2304]{1,0:T(8,128)} %get-tuple-element.9), channel_id=1, source_target_pairs={{0,14},{1,15},{2,16},{3,17},{4,18},{5,19},{6,20},{7,21},{8,22},{9,... | collective-permute-start | bytes 221192
  827.2 12.0 %collective-permute-start.14 = (f32[8,2304]{1,0:T(8,128)}, f32[8,2304]{1,0:T(8,128)}, u32[]{:S(2)}, u32[]{:S(2)}) collective-permute-start(f32[8,2304]{1,0:T(8,128)} %get-tuple-element.9), channel_id=1, source_target_pairs={{0,13},{1,14},{2,15},{3,16},{4,17},{5,18},{6,19},{7,20},{8,21},{9,... | collective-permute-start | bytes 221192
  832.9 13.3 %collective-permute-start.12 = (f32[8,2304]{1,0:T(8,128)}, f32[8,2304]{1,0:T(8,128)}, u32[]{:S(2)}, u32[]{:S(2)}) collective-permute-start(f32[8,2304]{1,0:T(8,128)} %get-tuple-element.9), channel_id=1, source_target_pairs={{0,11},{1,12},{2,13},{3,14},{4,15},{5,16},{6,17},{7,18},{8,19},{9,... | collective-permute-start | bytes 221192
  834.8 125.5 %collective-permute-start.11 = (f32[8,2304]{1,0:T(8,128)}, f32[8,2304]{1,0:T(8,128)}, u32[]{:S(2)}, u32[]{:S(2)}) collective-permute-start(f32[8,2304]{1,0:T(8,128)} %get-tuple-element.9), channel_id=1, source_target_pairs={{0,10},{1,11},{2,12},{3,13},{4,14},{5,15},{6,16},{7,17},{8,18},{9,... | collective-permute-start | bytes 221192
  837.4 126.5 %collective-permute-start.10 = (f32[8,2304]{1,0:T(8,128)}, f32[8,2304]{1,0:T(8,128)}, u32[]{:S(2)}, u32[]{:S(2)}) collective-permute-start(f32[8,2304]{1,0:T(8,128)} %get-tuple-element.9), channel_id=1, source_target_pairs={{0,9},{1,10},{2,11},{3,12},{4,13},{5,14},{6,15},{7,16},{8,17},{9,1... | collective-permute-start | bytes 221192
  839.3 128.6 %collective-permute-start.9 = (f32[8,2304]{1,0:T(8,128)}, f32[8,2304]{1,0:T(8,128)}, u32[]{:S(2)}, u32[]{:S(2)}) collective-permute-start(f32[8,2304]{1,0:T(8,128)} %get-tuple-element.9), channel_id=1, source_target_pairs={{0,8},{1,9},{2,10},{3,11},{4,12},{5,13},{6,14},{7,15},{8,16},{9,17... | collective-permute-start | bytes 221192
  841.2 130.0 %collective-permute-start.8 = (f32[8,2304]{1,0:T(8,128)}, f32[8,2304]{1,0:T(8,128)}, u32[]{:S(2)}, u32[]{:S(2)}) collective-permute-start(f32[8,2304]{1,0:T(8,128)} %get-tuple-element.9), channel_id=1, source_target_pairs={{0,7},{1,8},{2,9},{3,10},{4,11},{5,12},{6,13},{7,14},{8,15},{9,16}... | collective-permute-start | bytes 221192
  846.2 129.1 %collective-permute-start.7 = (f32[8,2304]{1,0:T(8,128)}, f32[8,2304]{1,0:T(8,128)}, u32[]{:S(2)}, u32[]{:S(2)}) collective-permute-start(f32[8,2304]{1,0:T(8,128)} %get-tuple-element.9), channel_id=1, source_target_pairs={{0,6},{1,7},{2,8},{3,9},{4,10},{5,11},{6,12},{7,13},{8,14},{9,15},... | collective-permute-start | bytes 221192
  960.3 18.7 %collective-permute-start.6 = (f32[8,2304]{1,0:T(8,128)}, f32[8,2304]{1,0:T(8,128)}, u32[]{:S(2)}, u32[]{:S(2)}) collective-permute-start(f32[8,2304]{1,0:T(8,128)} %get-tuple-element.9), channel_id=1, source_target_pairs={{0,5},{1,6},{2,7},{3,8},{4,9},{5,10},{6,11},{7,12},{8,13},{9,14},{... | collective-permute-start | bytes 221192
  963.9 15.2 %collective-permute-start.5 = (f32[8,2304]{1,0:T(8,128)}, f32[8,2304]{1,0:T(8,128)}, u32[]{:S(2)}, u32[]{:S(2)}) collective-permute-start(f32[8,2304]{1,0:T(8,128)} %get-tuple-element.9), channel_id=1, source_target_pairs={{0,4},{1,5},{2,6},{3,7},{4,8},{5,9},{6,10},{7,11},{8,12},{9,13},{1... | collective-permute-start | bytes 221192
  (74 other events, 1376.4 us)
where the time goes:
time: 1050 us; the launch traced here: 1040 us
  blocking collectives  520 us (50%)
  starting transfers between devices  189 us (18%)
  local copies, waits for them, and re-layouts  160 us (15%)
  matrix products  121 us (12%)
  waiting for transfers between devices  31.5 us (3%)
  other arithmetic  11.9 us (1%)
    unnamed x2, blocking collectives  442 us
    unnamed x64, starting transfers between devices  175 us
    unnamed x115, local copies, waits for them, and re-layouts  110 us
    all_to_all x1, blocking collectives, per_device(): lax.all_to_all(grad_attn_rows, 'depth', split_axis=1, concat_axis=0, tile...  42.1 us
    dot_general x1, matrix products, attend_backward(): jnp.einsum('phqk,qphd->kphd', dscore, q_heads, preferred_element_type=jnp...  39.6 us
    dot_general x1, matrix products, attend_backward(): jnp.einsum('phqk,kphd->qphd', dscore, k_heads, preferred_element_type=jnp...  39.3 us
    all_to_all x1, blocking collectives, per_device(): lax.all_to_all(qkv, 'depth', split_axis=1, concat_axis=0, tiled=True)  36.8 us
    all_to_all x1, waiting for transfers between devices, per_device(): lax.all_to_all(grad_qkv_col, 'depth', split_axis=0, concat_axis=1, tiled=...  27.9 us
  transfers between devices with their start and end apart: 68, of which 3 were waited for; matrix products, arithmetic and copies ran while one was open for 13% of the time, Pallas kernels for 0%

commit v1 on v0

v1 whole, which is shorter than its diff:
```python
import jax
import jax.numpy as jnp
import numpy as np
from jax import lax
from jax.experimental import pallas as pl
from jax.experimental.pallas import tpu as pltpu
from jax.sharding import PartitionSpec as P

HEADS = 12
HEAD_DIM = 64
EPS = 1e-06
LESION_GAIN = 3.0
D = 768
TOK = 512
AXES = ("depth", "mod")
BF = jnp.bfloat16
F32 = jnp.float32
MB = 1024 * 1024


def place(xlo, z, c, xhi, y):
    return (xlo * 8 + z * 2 + c) * 8 + xhi * 4 + y


def parts_of(i):
    d, m = divmod(i, 8)
    return d // 8, (d // 2) % 4, d % 2, m // 4, m % 4


PLANE = [
    [place(a, z, c, b, y) for a in range(2) for z in range(4) for c in range(2) for b in range(2)]
    for y in range(4)
]
CHIPS = [
    [place(a, z, c, b, y) for a in range(2) for z in range(4) for b in range(2)]
    for c in range(2)
    for y in range(4)
]
CORE_SWAP = [(i, i ^ 8) for i in range(128)]


def y_shift(s):
    out = []
    for i in range(128):
        a, z, c, b, y = parts_of(i)
        out.append((i, place(a, z, c, b, (y + s) % 4)))
    return out


def feature_table():
    table = np.zeros((8, D), np.int32)
    for c in range(2):
        for y in range(4):
            n = 0
            for rc in range(2):
                for ry in range(4):
                    for a in range(2):
                        for z in range(4):
                            for b in range(2):
                                i = place(a, z, c ^ rc, b, (y + ry) % 4)
                                for r in range(6):
                                    table[c * 4 + y, n] = 6 * i + r
                                    n += 1
    return table


FEATURES = feature_table()


def dot(a, b, ca, cb):
    return lax.dot_general(a, b, (((ca,), (cb,)), ((), ())), preferred_element_type=F32)


def send_order():
    i = lax.broadcasted_iota(jnp.int32, (TOK, TOK), 0)
    s = lax.broadcasted_iota(jnp.int32, (TOK, TOK), 1)
    src = ((i >> 2) & 3) * 128 + (i >> 4) * 4 + (i & 3)
    return s == src


def position_order():
    i = lax.broadcasted_iota(jnp.int32, (TOK, TOK), 0)
    s = lax.broadcasted_iota(jnp.int32, (TOK, TOK), 1)
    return s == (i & 127) * 4 + (i >> 7)


def onehot(mask):
    return jnp.where(mask, 1.0, 0.0).astype(BF)


def pack_kernel(tok_ref, cot_ref, les_ref, out_ref):
    mask = send_order()
    les = les_ref[...]
    weight = 1.0 + LESION_GAIN * les.astype(F32)
    row = jnp.concatenate([weight[d : d + 1, :] for d in range(4)], axis=1)
    plain = onehot(mask)
    scaled = jnp.where(mask, row, 0.0).astype(BF)
    t = dot(plain, tok_ref[...].reshape(TOK, D), 1, 0).astype(BF)
    out_ref[:, 0] = t.reshape(32, 16, D)
    g = dot(scaled, cot_ref[...].reshape(TOK, D), 1, 0).astype(BF)
    out_ref[:, 1] = g.reshape(32, 16, D)


def unpack_kernel(in_ref, mixed_ref, grad_ref):
    sel = onehot(send_order())
    a = dot(sel, in_ref[:, 0].reshape(TOK, D), 0, 0).astype(BF)
    mixed_ref[...] = a.reshape(4, 128, D)
    b = dot(sel, in_ref[:, 1].reshape(TOK, D), 0, 0).astype(BF)
    grad_ref[...] = b.reshape(4, 128, D)


def normalise(x):
    xf = x.astype(F32)
    inv_rms = lax.rsqrt(jnp.mean(xf * xf, axis=-1, keepdims=True) + EPS)
    return xf, inv_rms, xf * inv_rms


def main_kernel(
    recv_ref, gain_ref, feat_ref, wqkv_ref, wout_ref,
    keep_ref, send_ref, attn_ref, dqkv_ref,
    qkv_ref, ga_ref, norm_ref, gy_ref, lhs_ref,
):
    scale = float(HEAD_DIM) ** (-0.5)
    _, _, unit = normalise(recv_ref[:, 0].reshape(TOK, D))
    normed = (unit * gain_ref[...]).astype(BF)
    order = onehot(position_order())
    norm_ref[...] = dot(order, normed, 1, 0).astype(BF)
    gy_ref[...] = dot(order, recv_ref[:, 1].reshape(TOK, D), 1, 0).astype(BF)

    def project(n, _):
        cols = pl.ds(pl.multiple_of(n * 768, 768), 768)
        qkv_ref[:, cols] = dot(norm_ref[...], wqkv_ref[:, cols], 1, 0).astype(BF)
        return 0

    lax.fori_loop(0, 3, project, 0)
    ga_ref[...] = dot(gy_ref[...], wout_ref[...], 1, 1).astype(BF)
    first = lax.broadcasted_iota(jnp.int32, (128, 128), 1) < 64

    def split(x):
        zero = jnp.zeros_like(x)
        return jnp.concatenate([jnp.where(first, x, zero), jnp.where(first, zero, x)], axis=0)

    def heads(hp, _):
        base = pl.multiple_of(hp * 128, 128)
        for p in range(4):
            rows = slice(p * 128, (p + 1) * 128)
            q = qkv_ref[rows, pl.ds(base, 128)]
            kb = split(qkv_ref[rows, pl.ds(base + D, 128)])
            vb = split(qkv_ref[rows, pl.ds(base + 2 * D, 128)])
            ga = ga_ref[rows, pl.ds(base, 128)]
            s = (dot(kb, q, 1, 1) * scale).reshape(2, 128, 128)
            e = jnp.exp(s - jnp.max(s, axis=1, keepdims=True))
            probs = e * (1.0 / jnp.sum(e, axis=1, keepdims=True))
            dp = dot(vb, ga, 1, 1).reshape(2, 128, 128)
            delta = jnp.sum(probs * dp, axis=1, keepdims=True)
            ds = (probs * (dp - delta) * scale).astype(BF).reshape(256, 128)
            pb = probs.astype(BF).reshape(256, 128)
            attn_ref[rows, pl.ds(base, 128)] = dot(pb, vb, 0, 0).astype(BF)
            dqkv_ref[rows, pl.ds(base, 128)] = dot(ds, kb, 0, 0).astype(BF)
            dk = dot(ds, q, 1, 0)
            dv = dot(pb, ga, 1, 0)
            dqkv_ref[rows, pl.ds(base + D, 128)] = jnp.where(first, dk[:128], dk[128:]).astype(BF)
            dqkv_ref[rows, pl.ds(base + 2 * D, 128)] = jnp.where(first, dv[:128], dv[128:]).astype(BF)
        return 0

    lax.fori_loop(0, HEADS // 2, heads, 0)
    pick = onehot(lax.broadcasted_iota(jnp.int32, (D, D), 0) == feat_ref[...])
    lhs_ref[...] = dot(pick, norm_ref[...], 0, 1).astype(BF)

    def weight_grad(n, _):
        cols = pl.ds(pl.multiple_of(n * 768, 768), 768)
        g = dot(lhs_ref[...], dqkv_ref[:, cols], 1, 0).astype(BF)
        keep_ref[:, cols] = g[:384]
        send_ref[:, cols] = g[384:]
        return 0

    lax.fori_loop(0, 3, weight_grad, 0)
    lhs_ref[...] = dot(pick, attn_ref[...], 0, 1).astype(BF)
    g = dot(lhs_ref[...], gy_ref[...], 1, 0).astype(BF)
    keep_ref[:, 3 * D :] = g[:384]
    send_ref[:, 3 * D :] = g[384:]


def token_kernel(recv_ref, gain_ref, attn_ref, dqkv_ref, wqkv_ref, wout_ref, ret_ref, gain_out_ref):
    order = onehot(position_order())
    gn = dot(dqkv_ref[...], wqkv_ref[...], 1, 1).astype(BF)
    gn = dot(order, gn, 0, 0)
    xf, inv_rms, unit = normalise(recv_ref[:, 0].reshape(TOK, D))
    gain_out_ref[...] = jnp.sum(gn * unit, axis=0, keepdims=True)
    dunit = gn * gain_ref[...]
    back = inv_rms * (dunit - unit * jnp.mean(dunit * unit, axis=-1, keepdims=True))
    gy = recv_ref[:, 1].reshape(TOK, D).astype(F32)
    ret_ref[:, 1] = (gy + back).astype(BF).reshape(32, 16, D)
    attn = dot(order, attn_ref[...], 0, 0).astype(BF)
    proj = dot(attn, wout_ref[...], 1, 0).astype(BF)
    ret_ref[:, 0] = (xf + proj.astype(F32)).astype(BF).reshape(32, 16, D)


def pair_sum_kernel(a_ref, b_ref, o0, o1, o2, o3):
    s = (a_ref[...].astype(F32) + b_ref[...].astype(F32)).astype(BF)
    for n, o in enumerate((o0, o1, o2, o3)):
        o[...] = s[n * 96 : (n + 1) * 96]


def ring_sum_kernel(a, b, c, d, o):
    s = (a[...].astype(F32) + b[...].astype(F32)) + (c[...].astype(F32) + d[...].astype(F32))
    o[...] = s.astype(BF)


def params(mb):
    return pltpu.CompilerParams(vmem_limit_bytes=mb * MB)


def cost(flops, nbytes):
    return pl.CostEstimate(flops=int(flops), bytes_accessed=int(nbytes), transcendentals=0)


def shape(*dims, dtype=BF):
    return jax.ShapeDtypeStruct(dims, dtype)


def per_device(tokens, cotangent, lesion, w_qkv, w_out, norm_gain):
    gain = norm_gain.reshape(1, D)
    core = lax.axis_index("depth") & 1
    y = lax.axis_index("mod") & 3
    feat = lax.dynamic_slice(jnp.asarray(FEATURES), (core * 4 + y, 0), (1, D))
    packed = pl.pallas_call(
        pack_kernel, out_shape=shape(32, 2, 16, D), compiler_params=params(24),
        cost_estimate=cost(1e9, 4e6), name="pack",
    )(tokens, cotangent, lesion)
    recv = lax.all_to_all(packed, AXES, 0, 0, tiled=True, axis_index_groups=PLANE)
    keep, send, attn, dqkv = pl.pallas_call(
        main_kernel,
        out_shape=(shape(384, 4 * D), shape(384, 4 * D), shape(TOK, D), shape(TOK, 3 * D)),
        scratch_shapes=[
            pltpu.VMEM((TOK, 3 * D), BF), pltpu.VMEM((TOK, D), BF), pltpu.VMEM((TOK, D), BF),
            pltpu.VMEM((TOK, D), BF), pltpu.VMEM((D, TOK), BF),
        ],
        compiler_params=params(48), cost_estimate=cost(1e10, 1.5e7), name="main",
    )(recv, gain, feat, w_qkv, w_out)
    got = lax.ppermute(send, AXES, CORE_SWAP)
    ret, gain_part = pl.pallas_call(
        token_kernel, out_shape=(shape(32, 2, 16, D), shape(1, D, dtype=F32)),
        compiler_params=params(40), cost_estimate=cost(3.5e9, 1.2e7), name="token_grads",
    )(recv, gain, attn, dqkv, w_qkv, w_out)
    quarters = pl.pallas_call(
        pair_sum_kernel, out_shape=tuple(shape(96, 4 * D) for _ in range(4)),
        compiler_params=params(24), cost_estimate=cost(1e6, 7e6), name="pair_sum",
    )(keep, got)
    moved = [lax.ppermute(quarters[s], AXES, y_shift(s)) for s in range(1, 4)]
    back = lax.all_to_all(ret, AXES, 0, 0, tiled=True, axis_index_groups=PLANE)
    mine = pl.pallas_call(
        ring_sum_kernel, out_shape=shape(96, 4 * D), compiler_params=params(24),
        cost_estimate=cost(1e6, 3e6), name="ring_sum",
    )(quarters[0], *moved)
    mixed, grad_tokens = pl.pallas_call(
        unpack_kernel, out_shape=(shape(4, 128, D), shape(4, 128, D)),
        compiler_params=params(24), cost_estimate=cost(1e9, 4e6), name="unpack",
    )(back)
    last = lax.all_to_all(
        mine.reshape(16, 144, 128), AXES, 0, 0, tiled=True, axis_index_groups=CHIPS
    )
    share = jnp.sum(last.astype(F32), axis=0).reshape(6, 4 * D)
    gain_share = lax.psum_scatter(gain_part.reshape(D), AXES, scatter_dimension=0, tiled=True)
    return mixed, grad_tokens, share[:, : 3 * D], share[:, 3 * D :], gain_share


def solution(mesh):
    in_specs = (P("depth", "mod", None), P("depth", "mod", None), P("depth", "mod"), P(), P(), P())
    out_specs = (
        P("depth", "mod", None),
        P("depth", "mod", None),
        P(("depth", "mod"), None),
        P(("depth", "mod"), None),
        P(("depth", "mod")),
    )
    return jax.shard_map(
        per_device, mesh=mesh, in_specs=in_specs, out_specs=out_specs, check_vma=False
    )
```

time: 1050 us -> 190 us (0.18); the launches traced: 1040 us -> 189 us
  blocking collectives: 520 us -> 66.4 us
  starting transfers between devices: 189 us -> 25.8 us
  local copies, waits for them, and re-layouts: 160 us -> 13.5 us
  matrix products: 121 us -> 0 us
  Pallas kernels: 0 us -> 35 us
  waiting for transfers between devices: 31.5 us -> 47.2 us
  other arithmetic: 11.9 us -> 0.1 us
    unnamed x2 -> x1, blocking collectives: 442 us -> 66.4 us
    unnamed x64 -> x0, starting transfers between devices: 175 us -> none
    dot_general x11 -> x0, matrix products: 115 us -> none  [the longest x1 39.6 us: attend_backward(): jnp.einsum('phqk,qphd->kphd', dscore, q_heads, preferred_element_type=jnp...]
    unnamed x115 -> x23, local copies, waits for them, and re-layouts: 110 us -> 10.4 us
    all_to_all x2 -> x0, blocking collectives: 78.9 us -> none  [the longest x1 42.1 us: per_device(): lax.all_to_all(grad_attn_rows, 'depth', split_axis=1, concat_axis=0, tile...]
    pallas_call x0 -> x6, Pallas kernels: none -> 35 us  [the longest x1 22.3 us: per_device(): pl.pallas_call(main_kernel, out_shape=(shape(384, 4 * D), shape(384, 4 *...]
    ppermute x2 -> x4, waiting for transfers between devices: 0.01 us -> 24.8 us  [the longest x3 24.8 us: per_device(): moved = [lax.ppermute(quarters[s], AXES, y_shift(s)) for s in range(1, 4)]]
    slice x9 -> x2, local copies, waits for them, and re-layouts: 25 us -> 1.25 us  [per_device(): return (mixed, grad_tokens, share[:, :3 * D], share[:, 3 * D:], gain_share)]
  transfers between devices with their start and end apart: 68 -> 7, of which waited for: 3 -> 3; matrix products, arithmetic and copies ran while one was open for 13% -> 1% of each run, Pallas kernels for 0% -> 6%
where the time goes in v1:
time: 190 us; the launch traced here: 189 us
  blocking collectives  66.4 us (35%)
  waiting for transfers between devices  47.2 us (25%)
  Pallas kernels  35 us (18%)
  starting transfers between devices  25.8 us (14%)
  local copies, waits for them, and re-layouts  13.5 us (7%)
    unnamed x1, blocking collectives  66.4 us
    ppermute x3, waiting for transfers between devices, per_device(): moved = [lax.ppermute(quarters[s], AXES, y_shift(s)) for s in range(1, 4)]  24.8 us
    all_to_all x1, waiting for transfers between devices, per_device(): lax.all_to_all(packed, AXES, 0, 0, tiled=True, axis_index_groups=PLANE)  22.4 us
    pallas_call x1, Pallas kernels, per_device(): pl.pallas_call(main_kernel, out_shape=(shape(384, 4 * D), shape(384, 4 *...  22.3 us
    unnamed x23, local copies, waits for them, and re-layouts  10.4 us
    all_to_all x1, starting transfers between devices, per_device(): lax.all_to_all(packed, AXES, 0, 0, tiled=True, axis_index_groups=PLANE)  8.38 us
    all_to_all x1, starting transfers between devices, per_device(): lax.all_to_all(mine.reshape(16, 144, 128), AXES, 0, 0, tiled=True, axis_i...  6.64 us
    ppermute x3, starting transfers between devices, per_device(): moved = [lax.ppermute(quarters[s], AXES, y_shift(s)) for s in range(1, 4)]  5.9 us
  transfers between devices with their start and end apart: 7, of which 3 were waited for; matrix products, arithmetic and copies ran while one was open for 1% of the time, Pallas kernels for 6%

profile of v1, /device:TPU:0, one launch (start us, length us, event | category | flops | bytes accessed | tf_op | source)
XLA Modules:
  0.0 188.7 jit_solution(3816503817547277918)
XLA Ops:
  0.6 0.0 copy-start.6
  0.6 1.1 copy-done.6
  1.8 0.0 copy-start.7
  1.8 1.1 copy-done.7
  2.9 0.0 copy-start.8
  2.9 0.7 copy-done.8
  3.6 2.2 %pack.1 = bf16[32,2,16,768]{3,2,1,0:T(8,128)(2,1)} custom-call(bf16[4,128,768]{2,1,0:T(8,128)(2,1)S(1)} %copy-done.6, bf16[4,128,768]{2,1,0:T(8,128)(2,1)S(1)} %copy-done.7, s32[4,128]{1,0:T(4,128)S(1)} %copy-done.8), custom_call_target="tpu_custom_call" | custom-call | flops 1000000000 | bytes 4000000 | tf_op jit(solution)/shard_map/pack/pallas_call | solution.py:227
  5.8 0.0 copy-start.10
  5.8 0.0 copy-start.5
  5.8 8.4 %all-to-all-start = ((bf16[32,2,16,768]{3,2,1,0:T(8,128)(2,1)}), bf16[32,2,16,768]{3,2,1,0:T(8,128)(2,1)S(1)}, u32[]{:S(2)}, u32[]{:S(2)}) async-start(bf16[32,2,16,768]{3,2,1,0:T(8,128)(2,1)} %pack.1), calls=%async_computation | async-start | bytes 3145728 | tf_op jit(solution)/shard_map/all_to_all | solution.py:231
  14.1 0.0 copy-done.10
  14.2 0.8 constant_dynamic-slice_fusion.feat_ref
  14.9 22.4 %all-to-all-done.recv_ref = bf16[32,2,16,768]{3,2,1,0:T(8,128)(2,1)S(1)} async-done(((bf16[32,2,16,768]{3,2,1,0:T(8,128)(2,1)}), bf16[32,2,16,768]{3,2,1,0:T(8,128)(2,1)S(1)}, u32[]{:S(2)}, u32[]{:S(2)}) %all-to-all-start) | async-done | bytes 1572896 | tf_op jit(solution)/shard_map/all_to_all | solution.py:231
  37.3 0.0 copy-start
  37.3 1.2 copy-done
  38.5 0.0 copy-done.5
  38.5 0.0 copy-start.1
  38.5 1.4 copy-done.1
  39.9 0.0 copy-start.4
  39.9 22.3 %main.1 = (bf16[384,3072]{1,0:T(8,128)(2,1)S(1)}, bf16[384,3072]{1,0:T(8,128)(2,1)}, bf16[512,768]{1,0:T(8,128)(2,1)S(1)}, bf16[512,2304]{1,0:T(8,128)(2,1)}) custom-call(bf16[32,2,16,768]{3,2,1,0:T(8,128)(2,1)S(1)} %copy-done.1, f32[1,768]{1,0:T(1,128)S(1)} %reshape.22.gain_ref, s32[1,768]{1,0:T(1,128)S(1)} %constant_dynamic-slice_fusion.feat_ref, ...), custom_call_target="tpu_custom_call" | custom-call | flops 10000000000 | bytes 15000000 | tf_op jit(solution)/shard_map/main/pallas_call | solution.py:232
  62.2 0.0 collective-permute-start
  62.2 0.0 copy-done.4
  62.2 0.0 copy-start.2
  62.3 1.4 copy-done.2
  63.7 1.7 copy-done.9
  65.3 4.7 %token_grads.1 = (bf16[32,2,16,768]{3,2,1,0:T(8,128)(2,1)S(1)}, f32[1,768]{1,0:T(1,128)S(1)}) custom-call(bf16[32,2,16,768]{3,2,1,0:T(8,128)(2,1)S(1)} %copy-done.2, f32[1,768]{1,0:T(1,128)S(1)} %reshape.22.gain_ref, bf16[512,768]{1,0:T(8,128)(2,1)S(1)} %get-tuple-element.17.attn_ref, bf16[512,2304]{1,0:T(8,128)(2,1)S(1)} %copy-done.9, ...), custom_call_target="tpu_custom_call" | custom-call | flops 3500000000 | bytes 12000000 | tf_op jit(solution)/shard_map/token_grads/pallas_call | solution.py:242
  70.0 0.0 copy-start.3
  70.0 1.1 copy-done.3
  71.1 4.9 %all-to-all-start.1 = ((bf16[32,2,16,768]{3,2,1,0:T(8,128)(2,1)}), bf16[32,2,16,768]{3,2,1,0:T(8,128)(2,1)}, u32[]{:S(2)}, u32[]{:S(2)}) async-start(bf16[32,2,16,768]{3,2,1,0:T(8,128)(2,1)} %copy-done.3), calls=%async_computation.1 | async-start | bytes 3145728 | tf_op jit(solution)/shard_map/all_to_all | solution.py:251
  76.0 0.0 collective-permute-done.b_ref
  76.0 2.2 %pair_sum.1 = (bf16[96,3072]{1,0:T(8,128)(2,1)S(1)}, bf16[96,3072]{1,0:T(8,128)(2,1)S(1)}, bf16[96,3072]{1,0:T(8,128)(2,1)S(1)}, bf16[96,3072]{1,0:T(8,128)(2,1)S(1)}) custom-call(bf16[384,3072]{1,0:T(8,128)(2,1)S(1)} %get-tuple-element.22.a_ref, bf16[384,3072]{1,0:T(8,128)(2,1)} %collective-permute-done.b_ref), custom_call_target="tpu_custom_call" | custom-call | flops 1000000 | bytes 7000000 | tf_op jit(solution)/shard_map/pair_sum/pallas_call | solution.py:246
  78.3 1.6 collective-permute-start.1
  79.9 2.9 %collective-permute-start.2 = (bf16[96,3072]{1,0:T(8,128)(2,1)S(1)}, bf16[96,3072]{1,0:T(8,128)(2,1)S(1)}, u32[]{:S(2)}, u32[]{:S(2)}) collective-permute-start(bf16[96,3072]{1,0:T(8,128)(2,1)S(1)} %get-tuple-element.26), channel_id=1, source_target_pairs={{0,2},{1,3},{2,0},{3,1},{4,6},{5,7},{6,4},{7,5},{8,10},{9,11},{10,... | collective-permute-start | bytes 1769480 | tf_op jit(solution)/shard_map/ppermute | solution.py:250
  82.8 1.3 collective-permute-start.3
  84.1 11.0 %collective-permute-done.1.b = bf16[96,3072]{1,0:T(8,128)(2,1)S(1)} collective-permute-done((bf16[96,3072]{1,0:T(8,128)(2,1)S(1)}, bf16[96,3072]{1,0:T(8,128)(2,1)S(1)}, u32[]{:S(2)}, u32[]{:S(2)}) %collective-permute-start.1) | collective-permute-done | bytes 589856 | tf_op jit(solution)/shard_map/ppermute | solution.py:250
  95.1 13.8 %collective-permute-done.2.c = bf16[96,3072]{1,0:T(8,128)(2,1)S(1)} collective-permute-done((bf16[96,3072]{1,0:T(8,128)(2,1)S(1)}, bf16[96,3072]{1,0:T(8,128)(2,1)S(1)}, u32[]{:S(2)}, u32[]{:S(2)}) %collective-permute-start.2) | collective-permute-done | bytes 589856 | tf_op jit(solution)/shard_map/ppermute | solution.py:250
  108.9 0.0 collective-permute-done.3.d
  108.9 0.3 ring_sum.1
  109.2 1.1 reshape.23
  110.3 0.0 all-to-all-done.1.in_ref
  110.3 6.6 %all-to-all-start.2 = ((bf16[16,144,128]{2,1,0:T(8,128)(2,1)}), bf16[16,144,128]{2,1,0:T(8,128)(2,1)S(1)}, u32[]{:S(2)}, u32[]{:S(2)}) async-start(bf16[16,144,128]{2,1,0:T(8,128)(2,1)} %reshape.23), calls=%async_computation.2 | async-start | bytes 1179648 | tf_op jit(solution)/shard_map/all_to_all | solution.py:260
  117.0 66.4 %all-reduce = f32[768]{0:T(1024)S(1)} all-reduce(f32[768]{0:T(1024)S(1)} %reduce), channel_id=2, replica_groups=mesh['depth'=16,'mod'=8] {'depth','mod'}, use_global_device_ids=true, to_apply=%region_1.0.clone | all-reduce | flops 768 | bytes 6144
  183.4 0.6 dynamic-slice
  184.0 3.3 %unpack.1 = (bf16[4,128,768]{2,1,0:T(8,128)(2,1)}, bf16[4,128,768]{2,1,0:T(8,128)(2,1)}) custom-call(bf16[32,2,16,768]{3,2,1,0:T(8,128)(2,1)} %all-to-all-done.1.in_ref), custom_call_target="tpu_custom_call" | custom-call | flops 1000000000 | bytes 4000000 | tf_op jit(solution)/shard_map/unpack/pallas_call | solution.py:256
  187.3 0.0 all-to-all-done.2
  187.3 0.1 convert_reduce_fusion
  187.4 0.6 slice.8
  188.1 0.6 slice.9
  (4 shorter events, 0.0 us)
Async XLA Ops:
  0.6 1.1 copy-start.6
  1.8 1.1 copy-start.7
  2.9 0.7 copy-start.8
  5.8 8.4 %copy-start.10 = (f32[768]{0:T(1024)S(1)}, f32[768]{0:T(1024)}, u32[]{:S(2)}) copy-start(f32[768]{0:T(1024)} %param.12) | copy-start | bytes 9220
  5.8 32.8 %copy-start.5 = (bf16[768,768]{1,0:T(8,128)(2,1)S(1)}, bf16[768,768]{1,0:T(8,128)(2,1)}, u32[]{:S(2)}) copy-start(bf16[768,768]{1,0:T(8,128)(2,1)} %wout_ref.3) | copy-start | bytes 3538948
  5.8 31.5 %all-to-all-start = ((bf16[32,2,16,768]{3,2,1,0:T(8,128)(2,1)}), bf16[32,2,16,768]{3,2,1,0:T(8,128)(2,1)S(1)}, u32[]{:S(2)}, u32[]{:S(2)}) async-start(bf16[32,2,16,768]{3,2,1,0:T(8,128)(2,1)} %pack.1), calls=%async_computation | async-start | bytes 3145728 | tf_op jit(solution)/shard_map/all_to_all | solution.py:231
  37.3 1.2 copy-start
  38.5 1.4 copy-start.1
  39.9 22.3 %copy-start.4 = (bf16[768,2304]{1,0:T(8,128)(2,1)S(1)}, bf16[768,2304]{1,0:T(8,128)(2,1)}, u32[]{:S(2)}) copy-start(bf16[768,2304]{1,0:T(8,128)(2,1)} %wqkv_ref.3) | copy-start | bytes 10616836
  62.2 13.8 %collective-permute-start = (bf16[384,3072]{1,0:T(8,128)(2,1)}, bf16[384,3072]{1,0:T(8,128)(2,1)}, u32[]{:S(2)}, u32[]{:S(2)}) collective-permute-start(bf16[384,3072]{1,0:T(8,128)(2,1)} %get-tuple-element.23), channel_id=1, source_target_pairs={{0,8},{1,9},{2,10},{3,11},{4,12},{5,13},{6,14},{7,15},{8,0},{9,1},... | collective-permute-start | bytes 7077896 | tf_op jit(solution)/shard_map/ppermute | solution.py:241
  62.2 1.4 copy-start.2
  63.7 1.7 copy-start.9
  70.0 1.1 copy-start.3
  71.1 39.2 %all-to-all-start.1 = ((bf16[32,2,16,768]{3,2,1,0:T(8,128)(2,1)}), bf16[32,2,16,768]{3,2,1,0:T(8,128)(2,1)}, u32[]{:S(2)}, u32[]{:S(2)}) async-start(bf16[32,2,16,768]{3,2,1,0:T(8,128)(2,1)} %copy-done.3), calls=%async_computation.1 | async-start | bytes 3145728 | tf_op jit(solution)/shard_map/all_to_all | solution.py:251
  78.3 16.9 %collective-permute-start.1 = (bf16[96,3072]{1,0:T(8,128)(2,1)S(1)}, bf16[96,3072]{1,0:T(8,128)(2,1)S(1)}, u32[]{:S(2)}, u32[]{:S(2)}) collective-permute-start(bf16[96,3072]{1,0:T(8,128)(2,1)S(1)} %get-tuple-element.25), channel_id=1, source_target_pairs={{0,1},{1,2},{2,3},{3,0},{4,5},{5,6},{6,7},{7,4},{8,9},{9,10},{10,1... | collective-permute-start | bytes 1769480 | tf_op jit(solution)/shard_map/ppermute | solution.py:250
  79.9 29.1 %collective-permute-start.2 = (bf16[96,3072]{1,0:T(8,128)(2,1)S(1)}, bf16[96,3072]{1,0:T(8,128)(2,1)S(1)}, u32[]{:S(2)}, u32[]{:S(2)}) collective-permute-start(bf16[96,3072]{1,0:T(8,128)(2,1)S(1)} %get-tuple-element.26), channel_id=1, source_target_pairs={{0,2},{1,3},{2,0},{3,1},{4,6},{5,7},{6,4},{7,5},{8,10},{9,11},{10,... | collective-permute-start | bytes 1769480 | tf_op jit(solution)/shard_map/ppermute | solution.py:250
  82.8 26.1 %collective-permute-start.3 = (bf16[96,3072]{1,0:T(8,128)(2,1)S(1)}, bf16[96,3072]{1,0:T(8,128)(2,1)S(1)}, u32[]{:S(2)}, u32[]{:S(2)}) collective-permute-start(bf16[96,3072]{1,0:T(8,128)(2,1)S(1)} %get-tuple-element.27), channel_id=1, source_target_pairs={{0,3},{1,0},{2,1},{3,2},{4,7},{5,4},{6,5},{7,6},{8,11},{9,8},{10,9... | collective-permute-start | bytes 1769480 | tf_op jit(solution)/shard_map/ppermute | solution.py:250
  110.3 77.0 %all-to-all-start.2 = ((bf16[16,144,128]{2,1,0:T(8,128)(2,1)}), bf16[16,144,128]{2,1,0:T(8,128)(2,1)S(1)}, u32[]{:S(2)}, u32[]{:S(2)}) async-start(bf16[16,144,128]{2,1,0:T(8,128)(2,1)} %reshape.23), calls=%async_computation.2 | async-start | bytes 1179648 | tf_op jit(solution)/shard_map/all_to_all | solution.py:260

commit v2 on v1

--- a/solution.py
+++ b/solution.py
@@ -16,6 +16,9 @@
 BF = jnp.bfloat16
 F32 = jnp.float32
 MB = 1024 * 1024
+WIDE = 4 * D + 128
+MAIN_MB = 24
+TOKEN_MB = 20
 
 
 def place(xlo, z, c, xhi, y):
@@ -181,12 +184,29 @@
     send_ref[:, 3 * D :] = g[384:]
 
 
-def token_kernel(recv_ref, gain_ref, attn_ref, dqkv_ref, wqkv_ref, wout_ref, ret_ref, gain_out_ref):
+def split_sum(v):
+    v = jnp.sum(v, axis=1, keepdims=True)
+    lane = lax.broadcasted_iota(jnp.int32, (v.shape[0], 128), 1)
+    high = v.astype(BF).astype(F32)
+    return jnp.where(lane == 0, high, jnp.where(lane == 1, v - high, 0.0)).astype(BF)
+
+
+def token_kernel(
+    recv_ref, gain_ref, feat_ref, attn_ref, dqkv_ref, wqkv_ref, wout_ref,
+    ret_ref, gkeep_ref, gsend_ref,
+):
     order = onehot(position_order())
     gn = dot(dqkv_ref[...], wqkv_ref[...], 1, 1).astype(BF)
     gn = dot(order, gn, 0, 0)
     xf, inv_rms, unit = normalise(recv_ref[:, 0].reshape(TOK, D))
-    gain_out_ref[...] = jnp.sum(gn * unit, axis=0, keepdims=True)
+    g = jnp.sum(gn * unit, axis=0, keepdims=True)
+    high = g.astype(BF).astype(F32)
+    mid = (g - high).astype(BF).astype(F32)
+    terms = jnp.concatenate([high, mid, g - high - mid, jnp.zeros((125, D), F32)], axis=0)
+    pick = onehot(lax.broadcasted_iota(jnp.int32, (D, D), 0) == feat_ref[...])
+    cols = dot(pick, terms.astype(BF), 0, 1)
+    gkeep_ref[...] = cols[:384]
+    gsend_ref[...] = cols[384:]
     dunit = gn * gain_ref[...]
     back = inv_rms * (dunit - unit * jnp.mean(dunit * unit, axis=-1, keepdims=True))
     gy = recv_ref[:, 1].reshape(TOK, D).astype(F32)
@@ -196,15 +216,18 @@
     ret_ref[:, 0] = (xf + proj.astype(F32)).astype(BF).reshape(32, 16, D)
 
 
-def pair_sum_kernel(a_ref, b_ref, o0, o1, o2, o3):
+def pair_sum_kernel(a_ref, b_ref, ga_ref, gb_ref, o0, o1, o2, o3):
     s = (a_ref[...].astype(F32) + b_ref[...].astype(F32)).astype(BF)
+    g = split_sum(ga_ref[...] + gb_ref[...])
     for n, o in enumerate((o0, o1, o2, o3)):
-        o[...] = s[n * 96 : (n + 1) * 96]
+        o[:, : 4 * D] = s[n * 96 : (n + 1) * 96]
+        o[:, 4 * D :] = g[n * 96 : (n + 1) * 96]
 
 
 def ring_sum_kernel(a, b, c, d, o):
     s = (a[...].astype(F32) + b[...].astype(F32)) + (c[...].astype(F32) + d[...].astype(F32))
-    o[...] = s.astype(BF)
+    o[:, : 4 * D] = s[:, : 4 * D].astype(BF)
+    o[:, 4 * D :] = split_sum(s[:, 4 * D :])
 
 
 def params(mb):
@@ -225,7 +248,7 @@
     y = lax.axis_index("mod") & 3
     feat = lax.dynamic_slice(jnp.asarray(FEATURES), (core * 4 + y, 0), (1, D))
     packed = pl.pallas_call(
-        pack_kernel, out_shape=shape(32, 2, 16, D), compiler_params=params(24),
+        pack_kernel, out_shape=shape(32, 2, 16, D), compiler_params=params(16),
         cost_estimate=cost(1e9, 4e6), name="pack",
     )(tokens, cotangent, lesion)
     recv = lax.all_to_all(packed, AXES, 0, 0, tiled=True, axis_index_groups=PLANE)
@@ -236,21 +259,23 @@
             pltpu.VMEM((TOK, 3 * D), BF), pltpu.VMEM((TOK, D), BF), pltpu.VMEM((TOK, D), BF),
             pltpu.VMEM((TOK, D), BF), pltpu.VMEM((D, TOK), BF),
         ],
-        compiler_params=params(48), cost_estimate=cost(1e10, 1.5e7), name="main",
+        compiler_params=params(MAIN_MB), cost_estimate=cost(1e10, 1.5e7), name="main",
     )(recv, gain, feat, w_qkv, w_out)
     got = lax.ppermute(send, AXES, CORE_SWAP)
-    ret, gain_part = pl.pallas_call(
-        token_kernel, out_shape=(shape(32, 2, 16, D), shape(1, D, dtype=F32)),
-        compiler_params=params(40), cost_estimate=cost(3.5e9, 1.2e7), name="token_grads",
-    )(recv, gain, attn, dqkv, w_qkv, w_out)
+    ret, gain_keep, gain_send = pl.pallas_call(
+        token_kernel,
+        out_shape=(shape(32, 2, 16, D), shape(384, 128, dtype=F32), shape(384, 128, dtype=F32)),
+        compiler_params=params(TOKEN_MB), cost_estimate=cost(3.5e9, 1.2e7), name="token_grads",
+    )(recv, gain, feat, attn, dqkv, w_qkv, w_out)
+    gain_got = lax.ppermute(gain_send, AXES, CORE_SWAP)
     quarters = pl.pallas_call(
-        pair_sum_kernel, out_shape=tuple(shape(96, 4 * D) for _ in range(4)),
-        compiler_params=params(24), cost_estimate=cost(1e6, 7e6), name="pair_sum",
-    )(keep, got)
+        pair_sum_kernel, out_shape=tuple(shape(96, WIDE) for _ in range(4)),
+        compiler_params=params(16), cost_estimate=cost(1e6, 7e6), name="pair_sum",
+    )(keep, got, gain_keep, gain_got)
     moved = [lax.ppermute(quarters[s], AXES, y_shift(s)) for s in range(1, 4)]
     back = lax.all_to_all(ret, AXES, 0, 0, tiled=True, axis_index_groups=PLANE)
     mine = pl.pallas_call(
-        ring_sum_kernel, out_shape=shape(96, 4 * D), compiler_params=params(24),
+        ring_sum_kernel, out_shape=shape(96, WIDE), compiler_params=params(16),
         cost_estimate=cost(1e6, 3e6), name="ring_sum",
     )(quarters[0], *moved)
     mixed, grad_tokens = pl.pallas_call(
@@ -258,11 +283,11 @@
         compiler_params=params(24), cost_estimate=cost(1e9, 4e6), name="unpack",
     )(back)
     last = lax.all_to_all(
-        mine.reshape(16, 144, 128), AXES, 0, 0, tiled=True, axis_index_groups=CHIPS
+        mine.reshape(16, 150, 128), AXES, 0, 0, tiled=True, axis_index_groups=CHIPS
     )
-    share = jnp.sum(last.astype(F32), axis=0).reshape(6, 4 * D)
-    gain_share = lax.psum_scatter(gain_part.reshape(D), AXES, scatter_dimension=0, tiled=True)
-    return mixed, grad_tokens, share[:, : 3 * D], share[:, 3 * D :], gain_share
+    share = jnp.sum(last.astype(F32), axis=0).reshape(6, WIDE)
+    gain_share = jnp.sum(share[:, 4 * D :], axis=1)
+    return mixed, grad_tokens, share[:, : 3 * D], share[:, 3 * D : 4 * D], gain_share
 
 
 def solution(mesh):

time: 190 us -> 133 us (0.70)
  blocking collectives: 66.4 us -> 0 us
  waiting for transfers between devices: 47.2 us -> 57.5 us
  Pallas kernels: 35 us -> 32.1 us
    unnamed x1 -> x0, blocking collectives: 66.4 us -> none
    all_to_all x1, waiting for transfers between devices: 0.01 us -> 8.14 us  [per_device(): lax.all_to_all(mine.reshape(16, 150, 128), AXES, 0, 0, tiled=True, axis_i...]
    pallas_call x1, Pallas kernels: 22.3 us -> 19.5 us  [per_device(): pl.pallas_call(main_kernel, out_shape=(shape(384, 4 * D), shape(384, 4 *...]
    unnamed x23 -> x22, local copies, waits for them, and re-layouts: 10.4 us -> 11.1 us
  transfers between devices with their start and end apart: 7 -> 8, of which waited for: 3 -> 5; matrix products, arithmetic and copies ran while one was open for 1% -> 2% of each run, Pallas kernels for 6% -> 9%
where the time goes in v2:
time: 133 us; the launch traced here: 132 us
  waiting for transfers between devices  57.5 us (43%)
  Pallas kernels  32.1 us (24%)
  starting transfers between devices  26.3 us (20%)
  local copies, waits for them, and re-layouts  14.7 us (11%)
    ppermute x3, waiting for transfers between devices, per_device(): moved = [lax.ppermute(quarters[s], AXES, y_shift(s)) for s in range(1, 4)]  25.8 us
    all_to_all x1, waiting for transfers between devices, per_device(): lax.all_to_all(packed, AXES, 0, 0, tiled=True, axis_index_groups=PLANE)  22.4 us
    pallas_call x1, Pallas kernels, per_device(): pl.pallas_call(main_kernel, out_shape=(shape(384, 4 * D), shape(384, 4 *...  19.5 us
    unnamed x22, local copies, waits for them, and re-layouts  11.1 us
    all_to_all x1, starting transfers between devices, per_device(): lax.all_to_all(packed, AXES, 0, 0, tiled=True, axis_index_groups=PLANE)  8.38 us
    all_to_all x1, waiting for transfers between devices, per_device(): lax.all_to_all(mine.reshape(16, 150, 128), AXES, 0, 0, tiled=True, axis_i...  8.14 us
    all_to_all x1, starting transfers between devices, per_device(): lax.all_to_all(mine.reshape(16, 150, 128), AXES, 0, 0, tiled=True, axis_i...  6.82 us
    ppermute x3, starting transfers between devices, per_device(): moved = [lax.ppermute(quarters[s], AXES, y_shift(s)) for s in range(1, 4)]  5.9 us
  transfers between devices with their start and end apart: 8, of which 5 were waited for; matrix products, arithmetic and copies ran while one was open for 2% of the time, Pallas kernels for 9%

profile of v2, /device:TPU:0, one launch (start us, length us, event | category | flops | bytes accessed | tf_op | source)
XLA Modules:
  0.0 132.1 jit_solution(7638042701187778463)
XLA Ops:
  0.6 0.0 copy-start.7
  0.6 1.1 copy-done.7
  1.8 0.0 copy-start.8
  1.8 1.1 copy-done.8
  2.9 0.0 copy-start.9
  2.9 0.7 copy-done.9
  3.6 1.0 pack.1
  4.6 0.0 copy-start.3
  4.6 1.2 copy-done.3
  5.7 0.0 copy-start.10
  5.8 8.4 %all-to-all-start = ((bf16[32,2,16,768]{3,2,1,0:T(8,128)(2,1)}), bf16[32,2,16,768]{3,2,1,0:T(8,128)(2,1)S(1)}, u32[]{:S(2)}, u32[]{:S(2)}) async-start(bf16[32,2,16,768]{3,2,1,0:T(8,128)(2,1)} %copy-done.3), calls=%async_computation | async-start | bytes 3145728 | tf_op jit(solution)/shard_map/all_to_all | solution.py:254
  14.1 0.0 copy-done.10
  14.2 0.8 constant_dynamic-slice_fusion.feat_ref
  14.9 22.4 %all-to-all-done.recv_ref = bf16[32,2,16,768]{3,2,1,0:T(8,128)(2,1)S(1)} async-done(((bf16[32,2,16,768]{3,2,1,0:T(8,128)(2,1)}), bf16[32,2,16,768]{3,2,1,0:T(8,128)(2,1)S(1)}, u32[]{:S(2)}, u32[]{:S(2)}) %all-to-all-start) | async-done | bytes 1572896 | tf_op jit(solution)/shard_map/all_to_all | solution.py:254
  37.3 0.0 copy-start.1
  37.3 1.2 copy-done.1
  38.4 0.0 copy-start.2
  38.4 1.4 %copy-done.2 = bf16[32,2,16,768]{3,2,1,0:T(8,128)(2,1)S(1)} copy-done((bf16[32,2,16,768]{3,2,1,0:T(8,128)(2,1)S(1)}, bf16[32,2,16,768]{3,2,1,0:T(8,128)(2,1)}, u32[]{:S(2)}) %copy-start.2) | copy-done | bytes 1572888
  39.9 0.0 copy-start.4
  39.9 2.0 %copy-done.4 = bf16[768,2304]{1,0:T(8,128)(2,1)S(1)} copy-done((bf16[768,2304]{1,0:T(8,128)(2,1)S(1)}, bf16[768,2304]{1,0:T(8,128)(2,1)}, u32[]{:S(2)}) %copy-start.4) | copy-done | bytes 3538968
  41.9 1.3 copy-done.6
  43.1 19.5 %main.1 = (bf16[384,3072]{1,0:T(8,128)(2,1)S(1)}, bf16[384,3072]{1,0:T(8,128)(2,1)}, bf16[512,768]{1,0:T(8,128)(2,1)S(1)}, bf16[512,2304]{1,0:T(8,128)(2,1)S(1)}) custom-call(bf16[32,2,16,768]{3,2,1,0:T(8,128)(2,1)S(1)} %copy-done.2, f32[1,768]{1,0:T(1,128)S(1)} %reshape.19.gain_ref, s32[1,768]{1,0:T(1,128)S(1)} %constant_dynamic-slice_fusion.feat_ref, ...), custom_call_target="tpu_custom_call" | custom-call | flops 10000000000 | bytes 15000000 | tf_op jit(solution)/shard_map/main/pallas_call | solution.py:255
  62.7 0.0 collective-permute-start
  62.7 0.0 copy-done.5
  62.7 4.7 %token_grads.1 = (bf16[32,2,16,768]{3,2,1,0:T(8,128)(2,1)S(1)}, f32[384,128]{1,0:T(8,128)S(1)}, f32[384,128]{1,0:T(8,128)S(1)}) custom-call(bf16[32,2,16,768]{3,2,1,0:T(8,128)(2,1)S(1)} %copy-done.2, f32[1,768]{1,0:T(1,128)S(1)} %reshape.19.gain_ref, s32[1,768]{1,0:T(1,128)S(1)} %constant_dynamic-slice_fusion.feat_ref, ...), custom_call_target="tpu_custom_call" | custom-call | flops 3500000000 | bytes 12000000 | tf_op jit(solution)/shard_map/token_grads/pallas_call | solution.py:265
  67.4 0.0 copy-start
  67.4 1.1 copy-done
  68.5 4.7 %all-to-all-start.1 = ((bf16[32,2,16,768]{3,2,1,0:T(8,128)(2,1)}), bf16[32,2,16,768]{3,2,1,0:T(8,128)(2,1)}, u32[]{:S(2)}, u32[]{:S(2)}) async-start(bf16[32,2,16,768]{3,2,1,0:T(8,128)(2,1)} %copy-done), calls=%async_computation.1 | async-start | bytes 3145728 | tf_op jit(solution)/shard_map/all_to_all | solution.py:276
  73.2 0.5 collective-permute-start.1
  73.8 1.2 collective-permute-done.1.gb_ref
  74.9 0.0 collective-permute-done.b_ref
  74.9 3.0 %pair_sum.1 = (bf16[96,3200]{1,0:T(8,128)(2,1)S(1)}, bf16[96,3200]{1,0:T(8,128)(2,1)S(1)}, bf16[96,3200]{1,0:T(8,128)(2,1)S(1)}, bf16[96,3200]{1,0:T(8,128)(2,1)S(1)}) custom-call(bf16[384,3072]{1,0:T(8,128)(2,1)S(1)} %get-tuple-element.23.a_ref, bf16[384,3072]{1,0:T(8,128)(2,1)} %collective-permute-done.b_ref, f32[384,128]{1,0:T(8,128)S(1)} %get-tuple-element.25.ga_ref, ...), custom_call_target="tpu_custom_call" | custom-call | flops 1000000 | bytes 7000000 | tf_op jit(solution)/shard_map/pair_sum/pallas_call | solution.py:271
  77.9 1.7 %collective-permute-start.2 = (bf16[96,3200]{1,0:T(8,128)(2,1)S(1)}, bf16[96,3200]{1,0:T(8,128)(2,1)S(1)}, u32[]{:S(2)}, u32[]{:S(2)}) collective-permute-start(bf16[96,3200]{1,0:T(8,128)(2,1)S(1)} %get-tuple-element.28), channel_id=1, source_target_pairs={{0,1},{1,2},{2,3},{3,0},{4,5},{5,6},{6,7},{7,4},{8,9},{9,10},{10,1... | collective-permute-start | bytes 1843208 | tf_op jit(solution)/shard_map/ppermute | solution.py:275
  79.6 2.9 %collective-permute-start.3 = (bf16[96,3200]{1,0:T(8,128)(2,1)S(1)}, bf16[96,3200]{1,0:T(8,128)(2,1)S(1)}, u32[]{:S(2)}, u32[]{:S(2)}) collective-permute-start(bf16[96,3200]{1,0:T(8,128)(2,1)S(1)} %get-tuple-element.29), channel_id=1, source_target_pairs={{0,2},{1,3},{2,0},{3,1},{4,6},{5,7},{6,4},{7,5},{8,10},{9,11},{10,... | collective-permute-start | bytes 1843208 | tf_op jit(solution)/shard_map/ppermute | solution.py:275
  82.4 1.3 %collective-permute-start.4 = (bf16[96,3200]{1,0:T(8,128)(2,1)S(1)}, bf16[96,3200]{1,0:T(8,128)(2,1)S(1)}, u32[]{:S(2)}, u32[]{:S(2)}) collective-permute-start(bf16[96,3200]{1,0:T(8,128)(2,1)S(1)} %get-tuple-element.30), channel_id=1, source_target_pairs={{0,3},{1,0},{2,1},{3,2},{4,7},{5,4},{6,5},{7,6},{8,11},{9,8},{10,9... | collective-permute-start | bytes 1843208 | tf_op jit(solution)/shard_map/ppermute | solution.py:275
  83.8 11.5 %collective-permute-done.2.b = bf16[96,3200]{1,0:T(8,128)(2,1)S(1)} collective-permute-done((bf16[96,3200]{1,0:T(8,128)(2,1)S(1)}, bf16[96,3200]{1,0:T(8,128)(2,1)S(1)}, u32[]{:S(2)}, u32[]{:S(2)}) %collective-permute-start.2) | collective-permute-done | bytes 614432 | tf_op jit(solution)/shard_map/ppermute | solution.py:275
  95.3 14.3 %collective-permute-done.3.c = bf16[96,3200]{1,0:T(8,128)(2,1)S(1)} collective-permute-done((bf16[96,3200]{1,0:T(8,128)(2,1)S(1)}, bf16[96,3200]{1,0:T(8,128)(2,1)S(1)}, u32[]{:S(2)}, u32[]{:S(2)}) %collective-permute-start.3) | collective-permute-done | bytes 614432 | tf_op jit(solution)/shard_map/ppermute | solution.py:275
  109.6 0.0 collective-permute-done.4.d
  109.6 0.6 ring_sum.1
  110.2 1.6 %reshape.20 = bf16[16,150,128]{2,1,0:T(8,128)(2,1)} reshape(bf16[96,3200]{1,0:T(8,128)(2,1)S(1)} %ring_sum.1) | data formatting | bytes 1228800 | tf_op jit(solution)/shard_map/reshape | solution.py:286
  111.8 0.0 all-to-all-done.1.in_ref
  111.8 6.8 %all-to-all-start.2 = ((bf16[16,150,128]{2,1,0:T(8,128)(2,1)}), bf16[16,150,128]{2,1,0:T(8,128)(2,1)S(1)}, u32[]{:S(2)}, u32[]{:S(2)}) async-start(bf16[16,150,128]{2,1,0:T(8,128)(2,1)} %reshape.20), calls=%async_computation.2 | async-start | bytes 1245184 | tf_op jit(solution)/shard_map/all_to_all | solution.py:285
  118.6 3.3 %unpack.1 = (bf16[4,128,768]{2,1,0:T(8,128)(2,1)}, bf16[4,128,768]{2,1,0:T(8,128)(2,1)}) custom-call(bf16[32,2,16,768]{3,2,1,0:T(8,128)(2,1)} %all-to-all-done.1.in_ref), custom_call_target="tpu_custom_call" | custom-call | flops 1000000000 | bytes 4000000 | tf_op jit(solution)/shard_map/unpack/pallas_call | solution.py:281
  122.0 8.1 %all-to-all-done.2 = bf16[16,150,128]{2,1,0:T(8,128)(2,1)S(1)} async-done(((bf16[16,150,128]{2,1,0:T(8,128)(2,1)}), bf16[16,150,128]{2,1,0:T(8,128)(2,1)S(1)}, u32[]{:S(2)}, u32[]{:S(2)}) %all-to-all-start.2) | async-done | bytes 614432 | tf_op jit(solution)/shard_map/all_to_all | solution.py:285
  130.1 0.1 convert_reduce_fusion
  130.2 0.6 slice_reduce_fusion
  130.8 0.6 slice.13
  131.5 0.6 slice.12
  (4 shorter events, 0.0 us)
Async XLA Ops:
  0.6 1.1 copy-start.7
  1.8 1.1 copy-start.8
  2.9 0.7 copy-start.9
  4.6 1.2 copy-start.3
  5.7 8.4 %copy-start.10 = (f32[768]{0:T(1024)S(1)}, f32[768]{0:T(1024)}, u32[]{:S(2)}) copy-start(f32[768]{0:T(1024)} %param.12) | copy-start | bytes 9220
  5.8 31.5 %all-to-all-start = ((bf16[32,2,16,768]{3,2,1,0:T(8,128)(2,1)}), bf16[32,2,16,768]{3,2,1,0:T(8,128)(2,1)S(1)}, u32[]{:S(2)}, u32[]{:S(2)}) async-start(bf16[32,2,16,768]{3,2,1,0:T(8,128)(2,1)} %copy-done.3), calls=%async_computation | async-start | bytes 3145728 | tf_op jit(solution)/shard_map/all_to_all | solution.py:254
  37.3 1.2 copy-start.1
  38.4 1.4 %copy-start.2 = (bf16[32,2,16,768]{3,2,1,0:T(8,128)(2,1)S(1)}, bf16[32,2,16,768]{3,2,1,0:T(8,128)(2,1)}, u32[]{:S(2)}) copy-start(bf16[32,2,16,768]{3,2,1,0:T(8,128)(2,1)} %copy-done.1) | copy-start | bytes 4718596
  39.9 2.0 %copy-start.4 = (bf16[768,2304]{1,0:T(8,128)(2,1)S(1)}, bf16[768,2304]{1,0:T(8,128)(2,1)}, u32[]{:S(2)}) copy-start(bf16[768,2304]{1,0:T(8,128)(2,1)} %wqkv_ref.3) | copy-start | bytes 10616836
  41.9 1.3 copy-start.6
  43.1 19.5 %copy-start.5 = (bf16[768,2304]{1,0:T(8,128)(2,1)S(1)}, bf16[768,2304]{1,0:T(8,128)(2,1)}, u32[]{:S(2)}) copy-start(bf16[768,2304]{1,0:T(8,128)(2,1)} %wqkv_ref.3) | copy-start | bytes 10616836
  62.7 12.3 %collective-permute-start = (bf16[384,3072]{1,0:T(8,128)(2,1)}, bf16[384,3072]{1,0:T(8,128)(2,1)}, u32[]{:S(2)}, u32[]{:S(2)}) collective-permute-start(bf16[384,3072]{1,0:T(8,128)(2,1)} %get-tuple-element.24), channel_id=1, source_target_pairs={{0,8},{1,9},{2,10},{3,11},{4,12},{5,13},{6,14},{7,15},{8,0},{9,1},... | collective-permute-start | bytes 7077896 | tf_op jit(solution)/shard_map/ppermute | solution.py:264
  67.4 1.1 copy-start
  68.5 43.3 %all-to-all-start.1 = ((bf16[32,2,16,768]{3,2,1,0:T(8,128)(2,1)}), bf16[32,2,16,768]{3,2,1,0:T(8,128)(2,1)}, u32[]{:S(2)}, u32[]{:S(2)}) async-start(bf16[32,2,16,768]{3,2,1,0:T(8,128)(2,1)} %copy-done), calls=%async_computation.1 | async-start | bytes 3145728 | tf_op jit(solution)/shard_map/all_to_all | solution.py:276
  73.2 1.7 %collective-permute-start.1 = (f32[384,128]{1,0:T(8,128)S(1)}, f32[384,128]{1,0:T(8,128)S(1)}, u32[]{:S(2)}, u32[]{:S(2)}) collective-permute-start(f32[384,128]{1,0:T(8,128)S(1)} %get-tuple-element.26), channel_id=1, source_target_pairs={{0,8},{1,9},{2,10},{3,11},{4,12},{5,13},{6,14},{7,15},{8,0},{9,1},... | collective-permute-start | bytes 589832 | tf_op jit(solution)/shard_map/ppermute | solution.py:270
  77.9 17.4 %collective-permute-start.2 = (bf16[96,3200]{1,0:T(8,128)(2,1)S(1)}, bf16[96,3200]{1,0:T(8,128)(2,1)S(1)}, u32[]{:S(2)}, u32[]{:S(2)}) collective-permute-start(bf16[96,3200]{1,0:T(8,128)(2,1)S(1)} %get-tuple-element.28), channel_id=1, source_target_pairs={{0,1},{1,2},{2,3},{3,0},{4,5},{5,6},{6,7},{7,4},{8,9},{9,10},{10,1... | collective-permute-start | bytes 1843208 | tf_op jit(solution)/shard_map/ppermute | solution.py:275
  79.6 30.1 %collective-permute-start.3 = (bf16[96,3200]{1,0:T(8,128)(2,1)S(1)}, bf16[96,3200]{1,0:T(8,128)(2,1)S(1)}, u32[]{:S(2)}, u32[]{:S(2)}) collective-permute-start(bf16[96,3200]{1,0:T(8,128)(2,1)S(1)} %get-tuple-element.29), channel_id=1, source_target_pairs={{0,2},{1,3},{2,0},{3,1},{4,6},{5,7},{6,4},{7,5},{8,10},{9,11},{10,... | collective-permute-start | bytes 1843208 | tf_op jit(solution)/shard_map/ppermute | solution.py:275
  82.4 27.2 %collective-permute-start.4 = (bf16[96,3200]{1,0:T(8,128)(2,1)S(1)}, bf16[96,3200]{1,0:T(8,128)(2,1)S(1)}, u32[]{:S(2)}, u32[]{:S(2)}) collective-permute-start(bf16[96,3200]{1,0:T(8,128)(2,1)S(1)} %get-tuple-element.30), channel_id=1, source_target_pairs={{0,3},{1,0},{2,1},{3,2},{4,7},{5,4},{6,5},{7,6},{8,11},{9,8},{10,9... | collective-permute-start | bytes 1843208 | tf_op jit(solution)/shard_map/ppermute | solution.py:275
  111.8 18.3 %all-to-all-start.2 = ((bf16[16,150,128]{2,1,0:T(8,128)(2,1)}), bf16[16,150,128]{2,1,0:T(8,128)(2,1)S(1)}, u32[]{:S(2)}, u32[]{:S(2)}) async-start(bf16[16,150,128]{2,1,0:T(8,128)(2,1)} %reshape.20), calls=%async_computation.2 | async-start | bytes 1245184 | tf_op jit(solution)/shard_map/all_to_all | solution.py:285

commit v3 on v1

v3 whole, which is shorter than its diff:
```python
import jax
import jax.numpy as jnp
import numpy as np
from jax import lax
from jax.experimental import pallas as pl
from jax.experimental.pallas import tpu as pltpu
from jax.sharding import PartitionSpec as P

HEADS = 12
HEAD_DIM = 64
EPS = 1e-06
LESION_GAIN = 3.0
D = 768
TOK = 512
AXES = ("depth", "mod")
BF = jnp.bfloat16
F32 = jnp.float32
MB = 1024 * 1024
MAIN_MB = 46
TOKEN_MB = 20


def place(xlo, z, c, xhi, y):
    return (xlo * 8 + z * 2 + c) * 8 + xhi * 4 + y


def parts_of(i):
    d, m = divmod(i, 8)
    return d // 8, (d // 2) % 4, d % 2, m // 4, m % 4


PLANE = [
    [place(a, z, c, b, y) for a in range(2) for z in range(4) for c in range(2) for b in range(2)]
    for y in range(4)
]
CHIPS = [
    [place(a, z, c, b, y) for a in range(2) for z in range(4) for b in range(2)]
    for c in range(2)
    for y in range(4)
]
CORE_SWAP = [(i, i ^ 8) for i in range(128)]


def y_shift(s):
    out = []
    for i in range(128):
        a, z, c, b, y = parts_of(i)
        out.append((i, place(a, z, c, b, (y + s) % 4)))
    return out


def feature_table():
    table = np.zeros((8, D), np.int32)
    for c in range(2):
        for y in range(4):
            n = 0
            for rc in range(2):
                for ry in range(4):
                    for a in range(2):
                        for z in range(4):
                            for b in range(2):
                                i = place(a, z, c ^ rc, b, (y + ry) % 4)
                                for r in range(6):
                                    table[c * 4 + y, n] = 6 * i + r
                                    n += 1
    return table


FEATURES = feature_table()


def dot(a, b, ca, cb):
    return lax.dot_general(a, b, (((ca,), (cb,)), ((), ())), preferred_element_type=F32)


def send_order():
    i = lax.broadcasted_iota(jnp.int32, (TOK, TOK), 0)
    s = lax.broadcasted_iota(jnp.int32, (TOK, TOK), 1)
    src = ((i >> 2) & 3) * 128 + (i >> 4) * 4 + (i & 3)
    return s == src


def position_order():
    i = lax.broadcasted_iota(jnp.int32, (TOK, TOK), 0)
    s = lax.broadcasted_iota(jnp.int32, (TOK, TOK), 1)
    return s == (i & 127) * 4 + (i >> 7)


def onehot(mask):
    return jnp.where(mask, 1.0, 0.0).astype(BF)


def pack_kernel(tok_hbm, cot_hbm, les_hbm, out_hbm, tok_ref, cot_ref, les_ref, out_ref, sems):
    loads = [
        pltpu.make_async_copy(src, dst, sems.at[n])
        for n, (src, dst) in enumerate(
            ((les_hbm, les_ref), (tok_hbm, tok_ref), (cot_hbm, cot_ref))
        )
    ]
    for c in loads:
        c.start()
    mask = send_order()
    plain = onehot(mask)
    loads[0].wait()
    weight = 1.0 + LESION_GAIN * les_ref[...].astype(F32)
    row = jnp.concatenate([weight[d : d + 1, :] for d in range(4)], axis=1)
    scaled = jnp.where(mask, row, 0.0).astype(BF)
    loads[1].wait()
    t = dot(plain, tok_ref[...].reshape(TOK, D), 1, 0).astype(BF)
    out_ref[0] = t.reshape(32, 16, D)
    store_t = pltpu.make_async_copy(out_ref.at[0], out_hbm.at[:, 0], sems.at[3])
    store_t.start()
    loads[2].wait()
    g = dot(scaled, cot_ref[...].reshape(TOK, D), 1, 0).astype(BF)
    out_ref[1] = g.reshape(32, 16, D)
    store_g = pltpu.make_async_copy(out_ref.at[1], out_hbm.at[:, 1], sems.at[4])
    store_g.start()
    store_t.wait()
    store_g.wait()


def unpack_kernel(in_ref, mixed_ref, grad_ref, gain_ref):
    sel = onehot(send_order())
    for n, out in enumerate((mixed_ref, grad_ref)):
        base = n * 96
        x = jnp.concatenate(
            [in_ref[:, base + l * 16 : base + l * 16 + 16].reshape(TOK, 128) for l in range(6)],
            axis=1,
        )
        out[...] = dot(sel, x, 0, 0).astype(BF).reshape(4, 128, D)
    g = jnp.sum(in_ref[:, 192:].astype(F32), axis=0)
    gain_ref[...] = jnp.broadcast_to(jnp.sum(g, axis=0, keepdims=True), (8, 128))


def normalise(x):
    xf = x.astype(F32)
    inv_rms = lax.rsqrt(jnp.mean(xf * xf, axis=-1, keepdims=True) + EPS)
    return xf, inv_rms, xf * inv_rms


def main_kernel(
    recv_hbm, gain_ref, feat_ref, wqkv_hbm, wout_hbm,
    keep_ref, send_ref, attn_ref, dqkv_ref,
    recv_ref, wqkv_ref, wout_ref, qkv_ref, ga_ref, norm_ref, gy_ref, lhs_ref, sems,
):
    scale = float(HEAD_DIM) ** (-0.5)
    loads = [
        pltpu.make_async_copy(src, dst, sems.at[n])
        for n, (src, dst) in enumerate(
            ((recv_hbm, recv_ref), (wqkv_hbm, wqkv_ref), (wout_hbm, wout_ref))
        )
    ]
    for c in loads:
        c.start()
    order = onehot(position_order())
    loads[0].wait()
    _, _, unit = normalise(recv_ref[:, 0].reshape(TOK, D))
    normed = (unit * gain_ref[...]).astype(BF)
    norm_ref[...] = dot(order, normed, 1, 0).astype(BF)
    gy_ref[...] = dot(order, recv_ref[:, 1].reshape(TOK, D), 1, 0).astype(BF)
    loads[1].wait()

    def project(n, _):
        cols = pl.ds(pl.multiple_of(n * 768, 768), 768)
        qkv_ref[:, cols] = dot(norm_ref[...], wqkv_ref[:, cols], 1, 0).astype(BF)
        return 0

    lax.fori_loop(0, 3, project, 0)
    loads[2].wait()
    ga_ref[...] = dot(gy_ref[...], wout_ref[...], 1, 1).astype(BF)
    first = lax.broadcasted_iota(jnp.int32, (128, 128), 1) < 64

    def split(x):
        zero = jnp.zeros_like(x)
        return jnp.concatenate([jnp.where(first, x, zero), jnp.where(first, zero, x)], axis=0)

    def heads(hp, _):
        base = pl.multiple_of(hp * 128, 128)
        rows = [slice(p * 128, (p + 1) * 128) for p in range(4)]
        q = [qkv_ref[r, pl.ds(base, 128)] for r in rows]
        kb = [split(qkv_ref[r, pl.ds(base + D, 128)]) for r in rows]
        vb = [split(qkv_ref[r, pl.ds(base + 2 * D, 128)]) for r in rows]
        ga = [ga_ref[r, pl.ds(base, 128)] for r in rows]
        s = [dot(kb[p], q[p], 1, 1).reshape(2, 128, 128) for p in range(4)]
        dp = [dot(vb[p], ga[p], 1, 1).reshape(2, 128, 128) for p in range(4)]
        pb, ds = [], []
        for p in range(4):
            sp = s[p] * scale
            e = jnp.exp(sp - jnp.max(sp, axis=1, keepdims=True))
            probs = e * (1.0 / jnp.sum(e, axis=1, keepdims=True))
            delta = jnp.sum(probs * dp[p], axis=1, keepdims=True)
            ds.append((probs * (dp[p] - delta) * scale).astype(BF).reshape(256, 128))
            pb.append(probs.astype(BF).reshape(256, 128))
        for p in range(4):
            attn_ref[rows[p], pl.ds(base, 128)] = dot(pb[p], vb[p], 0, 0).astype(BF)
            dqkv_ref[rows[p], pl.ds(base, 128)] = dot(ds[p], kb[p], 0, 0).astype(BF)
            dk = dot(ds[p], q[p], 1, 0)
            dv = dot(pb[p], ga[p], 1, 0)
            dqkv_ref[rows[p], pl.ds(base + D, 128)] = jnp.where(first, dk[:128], dk[128:]).astype(BF)
            dqkv_ref[rows[p], pl.ds(base + 2 * D, 128)] = jnp.where(first, dv[:128], dv[128:]).astype(BF)
        return 0

    lax.fori_loop(0, HEADS // 2, heads, 0)
    pick = onehot(lax.broadcasted_iota(jnp.int32, (D, D), 0) == feat_ref[...])
    lhs_ref[...] = dot(pick, norm_ref[...], 0, 1).astype(BF)

    def weight_grad(n, _):
        cols = pl.ds(pl.multiple_of(n * 768, 768), 768)
        g = dot(lhs_ref[...], dqkv_ref[:, cols], 1, 0).astype(BF)
        keep_ref[:, cols] = g[:384]
        send_ref[:, cols] = g[384:]
        return 0

    lax.fori_loop(0, 3, weight_grad, 0)
    lhs_ref[...] = dot(pick, attn_ref[...], 0, 1).astype(BF)
    g = dot(lhs_ref[...], gy_ref[...], 1, 0).astype(BF)
    keep_ref[:, 3 * D :] = g[:384]
    send_ref[:, 3 * D :] = g[384:]


def token_kernel(recv_ref, gain_ref, dqkv_ref, wqkv_ref, ret_ref):
    order = onehot(position_order())
    gn = dot(dqkv_ref[...], wqkv_ref[...], 1, 1).astype(BF)
    gn = dot(order, gn, 0, 0)
    _, inv_rms, unit = normalise(recv_ref[:, 0].reshape(TOK, D))
    g = jnp.sum(gn * unit, axis=0, keepdims=True)
    dunit = gn * gain_ref[...]
    back = inv_rms * (dunit - unit * jnp.mean(dunit * unit, axis=-1, keepdims=True))
    gy = recv_ref[:, 1].reshape(TOK, D).astype(F32)
    grad = (gy + back).astype(BF)
    for l in range(6):
        ret_ref[:, l * 16 : l * 16 + 16] = grad[:, l * 128 : l * 128 + 128].reshape(32, 16, 128)
    k = lax.broadcasted_iota(jnp.int32, (32, 8, 128), 0) * 24
    lane = lax.broadcasted_iota(jnp.int32, (32, 8, 128), 2)
    own = jnp.zeros((32, 8, 128), F32)
    for l in range(6):
        f = lane + l * 128
        part = g[:, l * 128 : l * 128 + 128].reshape(1, 1, 128)
        own = own + jnp.where(jnp.logical_and(f >= k, f < k + 24), part, 0.0)
    high = own.astype(BF).astype(F32)
    mid = (own - high).astype(BF).astype(F32)
    row = lax.broadcasted_iota(jnp.int32, (32, 8, 128), 1)
    low = own - high - mid
    terms = jnp.where(row == 0, high, jnp.where(row == 1, mid, jnp.where(row == 2, low, 0.0)))
    ret_ref[:, 96:] = terms.astype(BF)


def mixed_kernel(recv_ref, attn_ref, wout_ref, grad_ref, ret_hbm, ret_ref, sems):
    store_g = pltpu.make_async_copy(grad_ref, ret_hbm.at[:, 96:], sems.at[0])
    store_g.start()
    attn = dot(onehot(position_order()), attn_ref[...], 0, 0).astype(BF)
    proj = dot(attn, wout_ref[...], 1, 0).astype(BF)
    mixed = (recv_ref[:, 0].reshape(TOK, D).astype(F32) + proj.astype(F32)).astype(BF)
    for l in range(6):
        ret_ref[:, l * 16 : l * 16 + 16] = mixed[:, l * 128 : l * 128 + 128].reshape(32, 16, 128)
    store_m = pltpu.make_async_copy(ret_ref, ret_hbm.at[:, :96], sems.at[1])
    store_m.start()
    store_g.wait()
    store_m.wait()


def pair_sum_kernel(a_ref, b_ref, o0, o1, o2, o3):
    for n, o in enumerate((o0, o1, o2, o3)):
        rows = slice(n * 96, n * 96 + 96)
        o[...] = (a_ref[rows].astype(F32) + b_ref[rows].astype(F32)).astype(BF)


def ring_sum_kernel(a, b, c, d, o, sum_ref, out_ref):
    sum_ref[...] = (a[...].astype(F32) + b[...].astype(F32)) + (
        c[...].astype(F32) + d[...].astype(F32)
    )
    for k in range(16):
        for l in range(24):
            out_ref[k, l * 6 : l * 6 + 6] = sum_ref[k * 6 : k * 6 + 6, l * 128 : l * 128 + 128]
    o[...] = out_ref[...].astype(BF)


def final_kernel(first_ref, in_ref, g0, g1, g2, g3, qkv_ref, out_ref, gain_ref, sum_ref):
    sum_ref[...] = jnp.sum(in_ref[...].astype(F32), axis=0)
    for l in range(24):
        v = sum_ref[l * 6 : l * 6 + 6]
        if l < 18:
            qkv_ref[:, l * 128 : l * 128 + 128] = v
        else:
            out_ref[:, (l - 18) * 128 : (l - 17) * 128] = v
    g = (g0[...] + g1[...]) + (g2[...] + g3[...])
    r = lax.broadcasted_iota(jnp.int32, (8, 128), 0)
    lane = lax.broadcasted_iota(jnp.int32, (8, 128), 1)
    mine = jnp.sum(
        jnp.where(lane == ((first_ref[0] + r) & 127), g, 0.0), axis=1, keepdims=True
    )
    gain_ref[...] = jnp.sum(jnp.where(lane == r, mine, 0.0), axis=0, keepdims=True)[:, :6]


def params(mb):
    return pltpu.CompilerParams(vmem_limit_bytes=mb * MB)


def cost(flops, nbytes):
    return pl.CostEstimate(flops=int(flops), bytes_accessed=int(nbytes), transcendentals=0)


def shape(*dims, dtype=BF):
    return jax.ShapeDtypeStruct(dims, dtype)


HBM = pl.BlockSpec(memory_space=pltpu.HBM)
VM = pl.BlockSpec(memory_space=pltpu.VMEM)
DMA = pltpu.SemaphoreType.DMA


def per_device(tokens, cotangent, lesion, w_qkv, w_out, norm_gain):
    gain = norm_gain.reshape(1, D)
    depth = lax.axis_index("depth")
    mod = lax.axis_index("mod")
    feat = lax.dynamic_slice(jnp.asarray(FEATURES), ((depth & 1) * 4 + (mod & 3), 0), (1, D))
    first = ((depth * 8 + mod) * 6).astype(jnp.int32).reshape(1)
    packed = pl.pallas_call(
        pack_kernel, out_shape=shape(32, 2, 16, D), in_specs=[HBM] * 3, out_specs=HBM,
        scratch_shapes=[
            pltpu.VMEM((4, 128, D), BF), pltpu.VMEM((4, 128, D), BF), pltpu.VMEM((4, 128), jnp.int32),
            pltpu.VMEM((2, 32, 16, D), BF), DMA((5,)),
        ],
        compiler_params=params(60), cost_estimate=cost(1e9, 4e6), name="pack",
    )(tokens, cotangent, lesion)
    recv = lax.all_to_all(packed, AXES, 0, 0, tiled=True, axis_index_groups=PLANE)
    keep, send, attn, dqkv = pl.pallas_call(
        main_kernel,
        out_shape=(shape(384, 4 * D), shape(384, 4 * D), shape(TOK, D), shape(TOK, 3 * D)),
        in_specs=[HBM, VM, VM, HBM, HBM],
        scratch_shapes=[
            pltpu.VMEM((32, 2, 16, D), BF), pltpu.VMEM((D, 3 * D), BF), pltpu.VMEM((D, D), BF),
            pltpu.VMEM((TOK, 3 * D), BF), pltpu.VMEM((TOK, D), BF), pltpu.VMEM((TOK, D), BF),
            pltpu.VMEM((TOK, D), BF), pltpu.VMEM((D, TOK), BF), DMA((3,)),
        ],
        compiler_params=params(MAIN_MB), cost_estimate=cost(1e10, 1.5e7), name="main",
    )(recv, gain, feat, w_qkv, w_out)
    got = lax.ppermute(send, AXES, CORE_SWAP)
    grads = pl.pallas_call(
        token_kernel, out_shape=shape(32, 104, 128),
        compiler_params=params(TOKEN_MB), cost_estimate=cost(2.8e9, 9e6), name="token_grads",
    )(recv, gain, dqkv, w_qkv)
    quarters = pl.pallas_call(
        pair_sum_kernel, out_shape=tuple(shape(96, 4 * D) for _ in range(4)),
        compiler_params=params(16), cost_estimate=cost(1e6, 7e6), name="pair_sum",
    )(keep, got)
    q0, q1, q2, q3, attn, grads = lax.optimization_barrier((*quarters, attn, grads))
    moved = [lax.ppermute(q, AXES, y_shift(s)) for s, q in ((1, q1), (2, q2), (3, q3))]
    ret = pl.pallas_call(
        mixed_kernel, out_shape=shape(32, 200, 128), out_specs=HBM,
        scratch_shapes=[pltpu.VMEM((32, 96, 128), BF), DMA((2,))],
        compiler_params=params(16), cost_estimate=cost(1e9, 5e6), name="mixed",
    )(recv, attn, w_out, grads)
    back = lax.all_to_all(ret, AXES, 0, 0, tiled=True, axis_index_groups=PLANE)
    mine = pl.pallas_call(
        ring_sum_kernel, out_shape=shape(16, 144, 128),
        scratch_shapes=[pltpu.VMEM((96, 4 * D), F32), pltpu.VMEM((16, 144, 128), F32)],
        compiler_params=params(16), cost_estimate=cost(1e6, 3e6), name="ring_sum",
    )(q0, *moved)
    mixed, grad_tokens, gain_part = pl.pallas_call(
        unpack_kernel,
        out_shape=(shape(4, 128, D), shape(4, 128, D), shape(8, 128, dtype=F32)),
        compiler_params=params(20), cost_estimate=cost(1e9, 4e6), name="unpack",
    )(back)
    last = lax.all_to_all(mine, AXES, 0, 0, tiled=True, axis_index_groups=CHIPS)
    gains = [gain_part] + [lax.ppermute(gain_part, AXES, y_shift(s)) for s in range(1, 4)]
    grad_qkv, grad_out, grad_gain = pl.pallas_call(
        final_kernel,
        out_shape=(shape(6, 3 * D, dtype=F32), shape(6, D, dtype=F32), shape(1, 6, dtype=F32)),
        in_specs=[pl.BlockSpec(memory_space=pltpu.SMEM)] + [VM] * 5,
        scratch_shapes=[pltpu.VMEM((144, 128), F32)],
        compiler_params=params(16), cost_estimate=cost(1e6, 1e6), name="final",
    )(first, last, *gains)
    return mixed, grad_tokens, grad_qkv, grad_out, grad_gain.reshape(6)


def solution(mesh):
    in_specs = (P("depth", "mod", None), P("depth", "mod", None), P("depth", "mod"), P(), P(), P())
    out_specs = (
        P("depth", "mod", None),
        P("depth", "mod", None),
        P(("depth", "mod"), None),
        P(("depth", "mod"), None),
        P(("depth", "mod")),
    )
    return jax.shard_map(
        per_device, mesh=mesh, in_specs=in_specs, out_specs=out_specs, check_vma=False
    )
```

time: 190 us -> 117 us (0.62)
  blocking collectives: 66.4 us -> 0 us
  local copies, waits for them, and re-layouts: 13.5 us -> 4.88 us
  Pallas kernels: 35 us -> 29 us
  waiting for transfers between devices: 47.2 us -> 52.4 us
  starting transfers between devices: 25.8 us -> 29.6 us
    unnamed x1 -> x0, blocking collectives: 66.4 us -> none
    pallas_call x1, Pallas kernels: 22.3 us -> 15.1 us  [per_device(): pl.pallas_call(main_kernel, out_shape=(shape(384, 4 * D), shape(384, 4 *...]
    unnamed x23 -> x16, local copies, waits for them, and re-layouts: 10.4 us -> 4.12 us
    all_to_all x1, waiting for transfers between devices: 0.01 us -> 5.07 us  [per_device(): last = lax.all_to_all(mine, AXES, 0, 0, tiled=True, axis_index_groups=CHIPS)]
    pallas_call x3 -> x5, Pallas kernels: 7.13 us -> 11.3 us  [the longest x1 3.49 us: per_device(): pl.pallas_call(pack_kernel, out_shape=shape(32, 2, 16, D), in_specs=[HBM]...]
    ppermute x3 -> x6, starting transfers between devices: 5.9 us -> 9.89 us  [the longest x3 5.9 us: per_device(): lax.ppermute(q, AXES, y_shift(s))]
    ppermute x3 -> x6, waiting for transfers between devices: 24.8 us -> 25 us  [the longest x3 25 us: per_device(): lax.ppermute(q, AXES, y_shift(s))]
  transfers between devices with their start and end apart: 7 -> 10, of which waited for: 3 -> 4; matrix products, arithmetic and copies ran while one was open for 1% -> 1% of each run, Pallas kernels for 6% -> 6%
where the time goes in v3:
time: 117 us
  waiting for transfers between devices  52.4 us (45%)
  starting transfers between devices  29.6 us (25%)
  Pallas kernels  29 us (25%)
  local copies, waits for them, and re-layouts  4.88 us (4%)
    ppermute x3, waiting for transfers between devices, per_device(): lax.ppermute(q, AXES, y_shift(s))  25 us
    all_to_all x1, waiting for transfers between devices, per_device(): lax.all_to_all(packed, AXES, 0, 0, tiled=True, axis_index_groups=PLANE)  22.4 us
    pallas_call x1, Pallas kernels, per_device(): pl.pallas_call(main_kernel, out_shape=(shape(384, 4 * D), shape(384, 4 *...  15.1 us
    all_to_all x1, starting transfers between devices, per_device(): lax.all_to_all(packed, AXES, 0, 0, tiled=True, axis_index_groups=PLANE)  8.38 us
    all_to_all x1, starting transfers between devices, per_device(): last = lax.all_to_all(mine, AXES, 0, 0, tiled=True, axis_index_groups=CHIPS)  6.93 us
    ppermute x3, starting transfers between devices, per_device(): lax.ppermute(q, AXES, y_shift(s))  5.9 us
    all_to_all x1, waiting for transfers between devices, per_device(): last = lax.all_to_all(mine, AXES, 0, 0, tiled=True, axis_index_groups=CHIPS)  5.07 us
    unnamed x16, local copies, waits for them, and re-layouts  4.12 us
  transfers between devices with their start and end apart: 10, of which 4 were waited for; matrix products, arithmetic and copies ran while one was open for 1% of the time, Pallas kernels for 6%

profile of v3, /device:TPU:0, one launch (start us, length us, event | category | flops | bytes accessed | tf_op | source)
XLA Modules:
  0.0 116.7 jit_solution(11554129482442148799)
XLA Ops:
  0.6 3.5 %pack.1 = bf16[32,2,16,768]{3,2,1,0:T(8,128)(2,1)} custom-call(bf16[4,128,768]{2,1,0:T(8,128)(2,1)} %tok_hbm.1, bf16[4,128,768]{2,1,0:T(8,128)(2,1)} %cot_hbm.1, s32[4,128]{1,0:T(4,128)} %les_hbm.1), custom_call_target="tpu_custom_call" | custom-call | flops 1000000000 | bytes 4000000 | tf_op jit(solution)/shard_map/pack/pallas_call | solution.py:318
  4.1 0.0 copy-start.7
  4.1 0.0 copy-start
  4.2 8.4 %all-to-all-start = ((bf16[32,2,16,768]{3,2,1,0:T(8,128)(2,1)}), bf16[32,2,16,768]{3,2,1,0:T(8,128)(2,1)S(1)}, u32[]{:S(2)}, u32[]{:S(2)}) async-start(bf16[32,2,16,768]{3,2,1,0:T(8,128)(2,1)} %pack.1), calls=%async_computation | async-start | bytes 3145728 | tf_op jit(solution)/shard_map/all_to_all | solution.py:326
  12.6 0.0 copy-done.7
  12.6 0.8 constant_dynamic-slice_fusion.feat_ref
  13.3 22.4 %all-to-all-done.recv_hbm.recv_ref = bf16[32,2,16,768]{3,2,1,0:T(8,128)(2,1)S(1)} async-done(((bf16[32,2,16,768]{3,2,1,0:T(8,128)(2,1)}), bf16[32,2,16,768]{3,2,1,0:T(8,128)(2,1)S(1)}, u32[]{:S(2)}, u32[]{:S(2)}) %all-to-all-start) | async-done | bytes 1572896 | tf_op jit(solution)/shard_map/all_to_all | solution.py:326
  35.7 0.0 copy-done
  35.7 0.0 copy-start.1
  35.7 15.1 %main.1 = (bf16[384,3072]{1,0:T(8,128)(2,1)S(1)}, bf16[384,3072]{1,0:T(8,128)(2,1)S(1)}, bf16[512,768]{1,0:T(8,128)(2,1)S(1)}, bf16[512,2304]{1,0:T(8,128)(2,1)}) custom-call(bf16[32,2,16,768]{3,2,1,0:T(8,128)(2,1)S(1)} %all-to-all-done.recv_hbm.recv_ref, f32[1,768]{1,0:T(1,128)S(1)} %reshape.19.gain_ref, s32[1,768]{1,0:T(1,128)S(1)} %constant_dynamic-slice_fusion.feat_ref, ...), custom_call_target="tpu_custom_call" | custom-call | flops 10000000000 | bytes 15000000 | tf_op jit(solution)/shard_map/main/pallas_call | solution.py:327
  50.8 0.3 collective-permute-start
  51.0 0.0 copy-done.1
  51.1 0.0 copy-start.6
  51.1 1.7 %copy-done.6 = bf16[512,2304]{1,0:T(8,128)(2,1)S(1)} copy-done((bf16[512,2304]{1,0:T(8,128)(2,1)S(1)}, bf16[512,2304]{1,0:T(8,128)(2,1)}, u32[]{:S(2)}) %copy-start.6) | copy-done | bytes 2359320
  52.7 3.1 %token_grads.1.grad_ref = bf16[32,104,128]{2,1,0:T(8,128)(2,1)S(1)} custom-call(bf16[32,2,16,768]{3,2,1,0:T(8,128)(2,1)S(1)} %all-to-all-done.recv_hbm.recv_ref, f32[1,768]{1,0:T(1,128)S(1)} %reshape.19.gain_ref, bf16[512,2304]{1,0:T(8,128)(2,1)S(1)} %copy-done.6, bf16[768,2304]{1,0:T(8,128)(2,1)S(1)} %copy-done.1), custom_call_target="tpu_custom_call" | custom-call | flops 2800000000 | bytes 9000000 | tf_op jit(solution)/shard_map/token_grads/pallas_call | solution.py:339
  55.8 0.0 collective-permute-done.b_ref
  55.9 0.5 pair_sum.1
  56.4 0.0 copy-start.2
  56.4 0.8 copy-done.2
  57.2 0.0 copy-start.4
  57.2 0.8 copy-done.4
  58.0 0.0 copy-start.5
  58.0 0.8 copy-done.5
  58.8 2.3 %mixed.1 = bf16[32,200,128]{2,1,0:T(8,128)(2,1)} custom-call(bf16[32,2,16,768]{3,2,1,0:T(8,128)(2,1)S(1)} %all-to-all-done.recv_hbm.recv_ref, bf16[512,768]{1,0:T(8,128)(2,1)S(1)} %get-tuple-element.33.attn_ref, bf16[768,768]{1,0:T(8,128)(2,1)S(1)} %copy-done, bf16[32,104,128]{2,1,0:T(8,128)(2,1)S(1)} %token_grads.1.grad_ref), custom_call_target="tpu_custom_call" | custom-call | flops 1000000000 | bytes 5000000 | tf_op jit(solution)/shard_map/mixed/pallas_call | solution.py:349
  61.2 0.0 copy-start.3
  61.2 4.1 %all-to-all-start.1 = ((bf16[32,200,128]{2,1,0:T(8,128)(2,1)}), bf16[32,200,128]{2,1,0:T(8,128)(2,1)S(1)}, u32[]{:S(2)}, u32[]{:S(2)}) async-start(bf16[32,200,128]{2,1,0:T(8,128)(2,1)} %mixed.1), calls=%async_computation.1 | async-start | bytes 3276800 | tf_op jit(solution)/shard_map/all_to_all | solution.py:354
  65.3 1.6 %collective-permute-start.1 = (bf16[96,3072]{1,0:T(8,128)(2,1)}, bf16[96,3072]{1,0:T(8,128)(2,1)S(1)}, u32[]{:S(2)}, u32[]{:S(2)}) collective-permute-start(bf16[96,3072]{1,0:T(8,128)(2,1)} %copy-done.5), channel_id=1, source_target_pairs={{0,1},{1,2},{2,3},{3,0},{4,5},{5,6},{6,7},{7,4},{8,9},{9,10},{10,1... | collective-permute-start | bytes 1769480 | tf_op jit(solution)/shard_map/ppermute | solution.py:348
  67.0 2.9 %collective-permute-start.2 = (bf16[96,3072]{1,0:T(8,128)(2,1)}, bf16[96,3072]{1,0:T(8,128)(2,1)S(1)}, u32[]{:S(2)}, u32[]{:S(2)}) collective-permute-start(bf16[96,3072]{1,0:T(8,128)(2,1)} %copy-done.4), channel_id=1, source_target_pairs={{0,2},{1,3},{2,0},{3,1},{4,6},{5,7},{6,4},{7,5},{8,10},{9,11},{10,... | collective-permute-start | bytes 1769480 | tf_op jit(solution)/shard_map/ppermute | solution.py:348
  69.9 0.0 copy-done.3
  69.9 1.3 %collective-permute-start.3 = (bf16[96,3072]{1,0:T(8,128)(2,1)S(1)}, bf16[96,3072]{1,0:T(8,128)(2,1)S(1)}, u32[]{:S(2)}, u32[]{:S(2)}) collective-permute-start(bf16[96,3072]{1,0:T(8,128)(2,1)S(1)} %copy-done.3), channel_id=1, source_target_pairs={{0,3},{1,0},{2,1},{3,2},{4,7},{5,4},{6,5},{7,6},{8,11},{9,8},{10,9... | collective-permute-start | bytes 1769480 | tf_op jit(solution)/shard_map/ppermute | solution.py:348
  71.2 11.2 %collective-permute-done.1.b = bf16[96,3072]{1,0:T(8,128)(2,1)S(1)} collective-permute-done((bf16[96,3072]{1,0:T(8,128)(2,1)}, bf16[96,3072]{1,0:T(8,128)(2,1)S(1)}, u32[]{:S(2)}, u32[]{:S(2)}) %collective-permute-start.1) | collective-permute-done | bytes 589856 | tf_op jit(solution)/shard_map/ppermute | solution.py:348
  82.4 13.8 %collective-permute-done.2.c = bf16[96,3072]{1,0:T(8,128)(2,1)S(1)} collective-permute-done((bf16[96,3072]{1,0:T(8,128)(2,1)}, bf16[96,3072]{1,0:T(8,128)(2,1)S(1)}, u32[]{:S(2)}, u32[]{:S(2)}) %collective-permute-start.2) | collective-permute-done | bytes 589856 | tf_op jit(solution)/shard_map/ppermute | solution.py:348
  96.2 0.0 collective-permute-done.3.d
  96.2 1.6 %ring_sum.1 = bf16[16,144,128]{2,1,0:T(8,128)(2,1)} custom-call(bf16[96,3072]{1,0:T(8,128)(2,1)S(1)} %get-tuple-element.37.a, bf16[96,3072]{1,0:T(8,128)(2,1)S(1)} %collective-permute-done.1.b, bf16[96,3072]{1,0:T(8,128)(2,1)S(1)} %collective-permute-done.2.c, bf16[96,3072]{1,0:T(8,128)(2,1)S(1)} %collective-permute-done.3.d), custom_call_target="tpu_custom_call" | custom-call | flops 1000000 | bytes 3000000 | tf_op jit(solution)/shard_map/ring_sum/pallas_call | solution.py:355
  97.8 0.0 all-to-all-done.1.in_ref
  97.8 6.9 %all-to-all-start.2 = ((bf16[16,144,128]{2,1,0:T(8,128)(2,1)}), bf16[16,144,128]{2,1,0:T(8,128)(2,1)S(1)}, u32[]{:S(2)}, u32[]{:S(2)}) async-start(bf16[16,144,128]{2,1,0:T(8,128)(2,1)} %ring_sum.1), calls=%async_computation.2 | async-start | bytes 1179648 | tf_op jit(solution)/shard_map/all_to_all | solution.py:365
  104.7 2.1 %unpack.1 = (bf16[4,128,768]{2,1,0:T(8,128)(2,1)}, bf16[4,128,768]{2,1,0:T(8,128)(2,1)}, f32[8,128]{1,0:T(8,128)S(1)}) custom-call(bf16[32,200,128]{2,1,0:T(8,128)(2,1)S(1)} %all-to-all-done.1.in_ref), custom_call_target="tpu_custom_call" | custom-call | flops 1000000000 | bytes 4000000 | tf_op jit(solution)/shard_map/unpack/pallas_call | solution.py:360
  106.8 2.2 %collective-permute-start.6 = (f32[8,128]{1,0:T(8,128)S(1)}, f32[8,128]{1,0:T(8,128)S(1)}, u32[]{:S(2)}, u32[]{:S(2)}) collective-permute-start(f32[8,128]{1,0:T(8,128)S(1)} %get-tuple-element.41.g0), channel_id=1, source_target_pairs={{0,3},{1,0},{2,1},{3,2},{4,7},{5,4},{6,5},{7,6},{8,11},{9,8},{10,9... | collective-permute-start | bytes 12296 | tf_op jit(solution)/shard_map/ppermute | solution.py:366
  109.0 0.9 collective-permute-start.5
  109.9 0.9 collective-permute-start.4
  110.8 5.1 %all-to-all-done.2.in_ref = bf16[16,144,128]{2,1,0:T(8,128)(2,1)S(1)} async-done(((bf16[16,144,128]{2,1,0:T(8,128)(2,1)}), bf16[16,144,128]{2,1,0:T(8,128)(2,1)S(1)}, u32[]{:S(2)}, u32[]{:S(2)}) %all-to-all-start.2) | async-done | bytes 589856 | tf_op jit(solution)/shard_map/all_to_all | solution.py:365
  115.9 0.0 collective-permute-done.6.g3
  115.9 0.0 collective-permute-done.5.g2
  115.9 0.0 collective-permute-done.4.g1
  115.9 0.7 final.1
  (1 shorter events, 0.0 us)
Async XLA Ops:
  4.1 8.4 %copy-start.7 = (f32[768]{0:T(1024)S(1)}, f32[768]{0:T(1024)}, u32[]{:S(2)}) copy-start(f32[768]{0:T(1024)} %param.12) | copy-start | bytes 9220
  4.1 31.5 %copy-start = (bf16[768,768]{1,0:T(8,128)(2,1)S(1)}, bf16[768,768]{1,0:T(8,128)(2,1)}, u32[]{:S(2)}) copy-start(bf16[768,768]{1,0:T(8,128)(2,1)} %wout_ref.1) | copy-start | bytes 3538948
  4.2 31.5 %all-to-all-start = ((bf16[32,2,16,768]{3,2,1,0:T(8,128)(2,1)}), bf16[32,2,16,768]{3,2,1,0:T(8,128)(2,1)S(1)}, u32[]{:S(2)}, u32[]{:S(2)}) async-start(bf16[32,2,16,768]{3,2,1,0:T(8,128)(2,1)} %pack.1), calls=%async_computation | async-start | bytes 3145728 | tf_op jit(solution)/shard_map/all_to_all | solution.py:326
  35.7 15.4 %copy-start.1 = (bf16[768,2304]{1,0:T(8,128)(2,1)S(1)}, bf16[768,2304]{1,0:T(8,128)(2,1)}, u32[]{:S(2)}) copy-start(bf16[768,2304]{1,0:T(8,128)(2,1)} %wqkv_ref.1) | copy-start | bytes 10616836
  50.8 5.1 %collective-permute-start = (bf16[384,3072]{1,0:T(8,128)(2,1)S(1)}, bf16[384,3072]{1,0:T(8,128)(2,1)S(1)}, u32[]{:S(2)}, u32[]{:S(2)}) collective-permute-start(bf16[384,3072]{1,0:T(8,128)(2,1)S(1)} %get-tuple-element.26), channel_id=1, source_target_pairs={{0,8},{1,9},{2,10},{3,11},{4,12},{5,13},{6,14},{7,15},{8,0},{9,1},... | collective-permute-start | bytes 7077896 | tf_op jit(solution)/shard_map/ppermute | solution.py:338
  51.1 1.7 %copy-start.6 = (bf16[512,2304]{1,0:T(8,128)(2,1)S(1)}, bf16[512,2304]{1,0:T(8,128)(2,1)}, u32[]{:S(2)}) copy-start(bf16[512,2304]{1,0:T(8,128)(2,1)} %get-tuple-element.32.dqkv_ref) | copy-start | bytes 7077892
  56.4 0.8 copy-start.2
  57.2 0.8 copy-start.4
  58.0 0.8 copy-start.5
  61.2 8.7 %copy-start.3 = (bf16[96,3072]{1,0:T(8,128)(2,1)S(1)}, bf16[96,3072]{1,0:T(8,128)(2,1)}, u32[]{:S(2)}) copy-start(bf16[96,3072]{1,0:T(8,128)(2,1)} %copy-done.2) | copy-start | bytes 1769476
  61.2 36.6 %all-to-all-start.1 = ((bf16[32,200,128]{2,1,0:T(8,128)(2,1)}), bf16[32,200,128]{2,1,0:T(8,128)(2,1)S(1)}, u32[]{:S(2)}, u32[]{:S(2)}) async-start(bf16[32,200,128]{2,1,0:T(8,128)(2,1)} %mixed.1), calls=%async_computation.1 | async-start | bytes 3276800 | tf_op jit(solution)/shard_map/all_to_all | solution.py:354
  65.3 17.1 %collective-permute-start.1 = (bf16[96,3072]{1,0:T(8,128)(2,1)}, bf16[96,3072]{1,0:T(8,128)(2,1)S(1)}, u32[]{:S(2)}, u32[]{:S(2)}) collective-permute-start(bf16[96,3072]{1,0:T(8,128)(2,1)} %copy-done.5), channel_id=1, source_target_pairs={{0,1},{1,2},{2,3},{3,0},{4,5},{5,6},{6,7},{7,4},{8,9},{9,10},{10,1... | collective-permute-start | bytes 1769480 | tf_op jit(solution)/shard_map/ppermute | solution.py:348
  67.0 29.2 %collective-permute-start.2 = (bf16[96,3072]{1,0:T(8,128)(2,1)}, bf16[96,3072]{1,0:T(8,128)(2,1)S(1)}, u32[]{:S(2)}, u32[]{:S(2)}) collective-permute-start(bf16[96,3072]{1,0:T(8,128)(2,1)} %copy-done.4), channel_id=1, source_target_pairs={{0,2},{1,3},{2,0},{3,1},{4,6},{5,7},{6,4},{7,5},{8,10},{9,11},{10,... | collective-permute-start | bytes 1769480 | tf_op jit(solution)/shard_map/ppermute | solution.py:348
  69.9 26.3 %collective-permute-start.3 = (bf16[96,3072]{1,0:T(8,128)(2,1)S(1)}, bf16[96,3072]{1,0:T(8,128)(2,1)S(1)}, u32[]{:S(2)}, u32[]{:S(2)}) collective-permute-start(bf16[96,3072]{1,0:T(8,128)(2,1)S(1)} %copy-done.3), channel_id=1, source_target_pairs={{0,3},{1,0},{2,1},{3,2},{4,7},{5,4},{6,5},{7,6},{8,11},{9,8},{10,9... | collective-permute-start | bytes 1769480 | tf_op jit(solution)/shard_map/ppermute | solution.py:348
  97.8 18.1 %all-to-all-start.2 = ((bf16[16,144,128]{2,1,0:T(8,128)(2,1)}), bf16[16,144,128]{2,1,0:T(8,128)(2,1)S(1)}, u32[]{:S(2)}, u32[]{:S(2)}) async-start(bf16[16,144,128]{2,1,0:T(8,128)(2,1)} %ring_sum.1), calls=%async_computation.2 | async-start | bytes 1179648 | tf_op jit(solution)/shard_map/all_to_all | solution.py:365
  106.8 9.1 %collective-permute-start.6 = (f32[8,128]{1,0:T(8,128)S(1)}, f32[8,128]{1,0:T(8,128)S(1)}, u32[]{:S(2)}, u32[]{:S(2)}) collective-permute-start(f32[8,128]{1,0:T(8,128)S(1)} %get-tuple-element.41.g0), channel_id=1, source_target_pairs={{0,3},{1,0},{2,1},{3,2},{4,7},{5,4},{6,5},{7,6},{8,11},{9,8},{10,9... | collective-permute-start | bytes 12296 | tf_op jit(solution)/shard_map/ppermute | solution.py:366
  109.0 6.9 %collective-permute-start.5 = (f32[8,128]{1,0:T(8,128)S(1)}, f32[8,128]{1,0:T(8,128)S(1)}, u32[]{:S(2)}, u32[]{:S(2)}) collective-permute-start(f32[8,128]{1,0:T(8,128)S(1)} %get-tuple-element.41.g0), channel_id=1, source_target_pairs={{0,2},{1,3},{2,0},{3,1},{4,6},{5,7},{6,4},{7,5},{8,10},{9,11},{10,... | collective-permute-start | bytes 12296 | tf_op jit(solution)/shard_map/ppermute | solution.py:366
  109.9 6.0 %collective-permute-start.4 = (f32[8,128]{1,0:T(8,128)S(1)}, f32[8,128]{1,0:T(8,128)S(1)}, u32[]{:S(2)}, u32[]{:S(2)}) collective-permute-start(f32[8,128]{1,0:T(8,128)S(1)} %get-tuple-element.41.g0), channel_id=1, source_target_pairs={{0,1},{1,2},{2,3},{3,0},{4,5},{5,6},{6,7},{7,4},{8,9},{9,10},{10,1... | collective-permute-start | bytes 12296 | tf_op jit(solution)/shard_map/ppermute | solution.py:366

commit v4 on v3

--- a/solution.py
+++ b/solution.py
@@ -16,7 +16,8 @@
 BF = jnp.bfloat16
 F32 = jnp.float32
 MB = 1024 * 1024
-MAIN_MB = 46
+RING = 2e10
+MAIN_MB = 42
 TOKEN_MB = 20
 
 
@@ -340,22 +341,22 @@
         token_kernel, out_shape=shape(32, 104, 128),
         compiler_params=params(TOKEN_MB), cost_estimate=cost(2.8e9, 9e6), name="token_grads",
     )(recv, gain, dqkv, w_qkv)
-    quarters = pl.pallas_call(
-        pair_sum_kernel, out_shape=tuple(shape(96, 4 * D) for _ in range(4)),
-        compiler_params=params(16), cost_estimate=cost(1e6, 7e6), name="pair_sum",
-    )(keep, got)
-    q0, q1, q2, q3, attn, grads = lax.optimization_barrier((*quarters, attn, grads))
-    moved = [lax.ppermute(q, AXES, y_shift(s)) for s, q in ((1, q1), (2, q2), (3, q3))]
     ret = pl.pallas_call(
         mixed_kernel, out_shape=shape(32, 200, 128), out_specs=HBM,
         scratch_shapes=[pltpu.VMEM((32, 96, 128), BF), DMA((2,))],
         compiler_params=params(16), cost_estimate=cost(1e9, 5e6), name="mixed",
     )(recv, attn, w_out, grads)
+    quarters = pl.pallas_call(
+        pair_sum_kernel, out_shape=tuple(shape(96, 4 * D) for _ in range(4)),
+        compiler_params=params(16), cost_estimate=cost(1e6, 7e6), name="pair_sum",
+    )(keep, got)
+    q0, q1, q2, q3, ret = lax.optimization_barrier((*quarters, ret))
+    moved = [lax.ppermute(q, AXES, y_shift(s)) for s, q in ((1, q1), (2, q2), (3, q3))]
     back = lax.all_to_all(ret, AXES, 0, 0, tiled=True, axis_index_groups=PLANE)
     mine = pl.pallas_call(
         ring_sum_kernel, out_shape=shape(16, 144, 128),
         scratch_shapes=[pltpu.VMEM((96, 4 * D), F32), pltpu.VMEM((16, 144, 128), F32)],
-        compiler_params=params(16), cost_estimate=cost(1e6, 3e6), name="ring_sum",
+        compiler_params=params(16), cost_estimate=cost(RING, 3e6), name="ring_sum",
     )(q0, *moved)
     mixed, grad_tokens, gain_part = pl.pallas_call(
         unpack_kernel,

time: 117 us -> 109 us (0.932)
  local copies, waits for them, and re-layouts: 4.88 us -> 0.77 us
  starting transfers between devices: 29.6 us -> 26 us
  waiting for transfers between devices: 52.4 us -> 49.3 us
  Pallas kernels: 29 us -> 31.1 us
    unnamed x16 -> x6, local copies, waits for them, and re-layouts: 4.12 us -> 0.02 us
    ppermute x3, waiting for transfers between devices: 25 us -> 21.3 us  [per_device(): lax.ppermute(q, AXES, y_shift(s))]
    all_to_all x1, starting transfers between devices: 6.93 us -> 3.58 us  [per_device(): last = lax.all_to_all(mine, AXES, 0, 0, tiled=True, axis_index_groups=CHIPS)]
    pallas_call x1, Pallas kernels: 1.59 us -> 2.84 us  [per_device(): pl.pallas_call(ring_sum_kernel, out_shape=shape(16, 144, 128), scratch_sh...]
  transfers between devices with their start and end apart: 10 -> 10, of which waited for: 4 -> 4; matrix products, arithmetic and copies ran while one was open for 1% -> 1% of each run, Pallas kernels for 6% -> 10%
where the time goes in v4:
time: 109 us; the launch traced here: 108 us
  waiting for transfers between devices  49.3 us (45%)
  Pallas kernels  31.1 us (29%)
  starting transfers between devices  26 us (24%)
    all_to_all x1, waiting for transfers between devices, per_device(): lax.all_to_all(packed, AXES, 0, 0, tiled=True, axis_index_groups=PLANE)  22.4 us
    ppermute x3, waiting for transfers between devices, per_device(): lax.ppermute(q, AXES, y_shift(s))  21.3 us
    pallas_call x1, Pallas kernels, per_device(): pl.pallas_call(main_kernel, out_shape=(shape(384, 4 * D), shape(384, 4 *...  15.1 us
    all_to_all x1, starting transfers between devices, per_device(): lax.all_to_all(packed, AXES, 0, 0, tiled=True, axis_index_groups=PLANE)  8.38 us
    ppermute x3, starting transfers between devices, per_device(): lax.ppermute(q, AXES, y_shift(s))  5.83 us
    all_to_all x1, waiting for transfers between devices, per_device(): last = lax.all_to_all(mine, AXES, 0, 0, tiled=True, axis_index_groups=CHIPS)  5.65 us
    ppermute x3, starting transfers between devices, per_device(): lax.ppermute(gain_part, AXES, y_shift(s))  3.99 us
    all_to_all x1, starting transfers between devices, per_device(): back = lax.all_to_all(ret, AXES, 0, 0, tiled=True, axis_index_groups=PLANE)  3.98 us
  transfers between devices with their start and end apart: 10, of which 4 were waited for; matrix products, arithmetic and copies ran while one was open for 1% of the time, Pallas kernels for 10%

profile of v4, /device:TPU:0, one launch (start us, length us, event | category | flops | bytes accessed | tf_op | source)
XLA Modules:
  0.0 108.0 jit_solution(8776180104697402221)
XLA Ops:
  0.6 3.5 %pack.1 = bf16[32,2,16,768]{3,2,1,0:T(8,128)(2,1)} custom-call(bf16[4,128,768]{2,1,0:T(8,128)(2,1)} %tok_hbm.1, bf16[4,128,768]{2,1,0:T(8,128)(2,1)} %cot_hbm.1, s32[4,128]{1,0:T(4,128)} %les_hbm.1), custom_call_target="tpu_custom_call" | custom-call | flops 1000000000 | bytes 4000000 | tf_op jit(solution)/shard_map/pack/pallas_call | solution.py:319
  4.1 0.0 copy-start.2
  4.2 0.0 copy-start
  4.2 8.4 %all-to-all-start = ((bf16[32,2,16,768]{3,2,1,0:T(8,128)(2,1)}), bf16[32,2,16,768]{3,2,1,0:T(8,128)(2,1)S(1)}, u32[]{:S(2)}, u32[]{:S(2)}) async-start(bf16[32,2,16,768]{3,2,1,0:T(8,128)(2,1)} %pack.1), calls=%async_computation | async-start | bytes 3145728 | tf_op jit(solution)/shard_map/all_to_all | solution.py:327
  12.6 0.0 copy-done.2
  12.6 0.8 constant_dynamic-slice_fusion.feat_ref
  13.3 22.4 %all-to-all-done.recv_hbm.recv_ref = bf16[32,2,16,768]{3,2,1,0:T(8,128)(2,1)S(1)} async-done(((bf16[32,2,16,768]{3,2,1,0:T(8,128)(2,1)}), bf16[32,2,16,768]{3,2,1,0:T(8,128)(2,1)S(1)}, u32[]{:S(2)}, u32[]{:S(2)}) %all-to-all-start) | async-done | bytes 1572896 | tf_op jit(solution)/shard_map/all_to_all | solution.py:327
  35.7 0.0 copy-done
  35.7 0.0 copy-start.1
  35.7 15.1 %main.1 = (bf16[384,3072]{1,0:T(8,128)(2,1)S(1)}, bf16[384,3072]{1,0:T(8,128)(2,1)S(1)}, bf16[512,768]{1,0:T(8,128)(2,1)S(1)}, bf16[512,2304]{1,0:T(8,128)(2,1)S(1)}) custom-call(bf16[32,2,16,768]{3,2,1,0:T(8,128)(2,1)S(1)} %all-to-all-done.recv_hbm.recv_ref, f32[1,768]{1,0:T(1,128)S(1)} %reshape.19.gain_ref, ...), custom_call_target="tpu_custom_call" | custom-call | flops 10000000000 | bytes 15000000 | tf_op jit(solution)/shard_map/main/pallas_call | solution.py:328
  50.8 0.3 collective-permute-start
  51.1 0.0 copy-done.1
  51.1 3.1 %token_grads.1.grad_ref = bf16[32,104,128]{2,1,0:T(8,128)(2,1)S(1)} custom-call(bf16[32,2,16,768]{3,2,1,0:T(8,128)(2,1)S(1)} %all-to-all-done.recv_hbm.recv_ref, f32[1,768]{1,0:T(1,128)S(1)} %reshape.19.gain_ref, bf16[512,2304]{1,0:T(8,128)(2,1)S(1)} %get-tuple-element.31.dqkv_ref, bf16[768,2304]{1,0:T(8,128)(2,1)S(1)} %copy-done.1), custom_call_target="tpu_custom_call" | custom-call | flops 2800000000 | bytes 9000000 | tf_op jit(solution)/shard_map/token_grads/pallas_call | solution.py:340
  54.2 2.3 %mixed.1 = bf16[32,200,128]{2,1,0:T(8,128)(2,1)} custom-call(bf16[32,2,16,768]{3,2,1,0:T(8,128)(2,1)S(1)} %all-to-all-done.recv_hbm.recv_ref, bf16[512,768]{1,0:T(8,128)(2,1)S(1)} %get-tuple-element.30.attn_ref, bf16[768,768]{1,0:T(8,128)(2,1)S(1)} %copy-done, bf16[32,104,128]{2,1,0:T(8,128)(2,1)S(1)} %token_grads.1.grad_ref), custom_call_target="tpu_custom_call" | custom-call | flops 1000000000 | bytes 5000000 | tf_op jit(solution)/shard_map/mixed/pallas_call | solution.py:344
  56.5 0.0 collective-permute-done.b_ref
  56.5 1.5 %pair_sum.1 = (bf16[96,3072]{1,0:T(8,128)(2,1)S(1)}, bf16[96,3072]{1,0:T(8,128)(2,1)}, bf16[96,3072]{1,0:T(8,128)(2,1)}, bf16[96,3072]{1,0:T(8,128)(2,1)S(1)}) custom-call(bf16[384,3072]{1,0:T(8,128)(2,1)S(1)} %get-tuple-element.24.a_ref, bf16[384,3072]{1,0:T(8,128)(2,1)S(1)} %collective-permute-done.b_ref), custom_call_target="tpu_custom_call" | custom-call | flops 1000000 | bytes 7000000 | tf_op jit(solution)/shard_map/pair_sum/pallas_call | solution.py:349
  58.0 1.6 %collective-permute-start.1 = (bf16[96,3072]{1,0:T(8,128)(2,1)}, bf16[96,3072]{1,0:T(8,128)(2,1)S(1)}, u32[]{:S(2)}, u32[]{:S(2)}) collective-permute-start(bf16[96,3072]{1,0:T(8,128)(2,1)} %get-tuple-element.36), channel_id=1, source_target_pairs={{0,1},{1,2},{2,3},{3,0},{4,5},{5,6},{6,7},{7,4},{8,9},{9,10},{10,1... | collective-permute-start | bytes 1769480 | tf_op jit(solution)/shard_map/ppermute | solution.py:354
  59.5 2.9 %collective-permute-start.2 = (bf16[96,3072]{1,0:T(8,128)(2,1)}, bf16[96,3072]{1,0:T(8,128)(2,1)}, u32[]{:S(2)}, u32[]{:S(2)}) collective-permute-start(bf16[96,3072]{1,0:T(8,128)(2,1)} %get-tuple-element.37), channel_id=1, source_target_pairs={{0,2},{1,3},{2,0},{3,1},{4,6},{5,7},{6,4},{7,5},{8,10},{9,11},{10,... | collective-permute-start | bytes 1769480 | tf_op jit(solution)/shard_map/ppermute | solution.py:354
  62.4 1.3 %collective-permute-start.3 = (bf16[96,3072]{1,0:T(8,128)(2,1)S(1)}, bf16[96,3072]{1,0:T(8,128)(2,1)}, u32[]{:S(2)}, u32[]{:S(2)}) collective-permute-start(bf16[96,3072]{1,0:T(8,128)(2,1)S(1)} %get-tuple-element.38), channel_id=1, source_target_pairs={{0,3},{1,0},{2,1},{3,2},{4,7},{5,4},{6,5},{7,6},{8,11},{9,8},{10,9... | collective-permute-start | bytes 1769480 | tf_op jit(solution)/shard_map/ppermute | solution.py:354
  63.8 4.0 %all-to-all-start.1 = ((bf16[32,200,128]{2,1,0:T(8,128)(2,1)}), bf16[32,200,128]{2,1,0:T(8,128)(2,1)S(1)}, u32[]{:S(2)}, u32[]{:S(2)}) async-start(bf16[32,200,128]{2,1,0:T(8,128)(2,1)} %mixed.1), calls=%async_computation.1 | async-start | bytes 3276800 | tf_op jit(solution)/shard_map/all_to_all | solution.py:355
  67.8 7.4 %collective-permute-done.1.b = bf16[96,3072]{1,0:T(8,128)(2,1)S(1)} collective-permute-done((bf16[96,3072]{1,0:T(8,128)(2,1)}, bf16[96,3072]{1,0:T(8,128)(2,1)S(1)}, u32[]{:S(2)}, u32[]{:S(2)}) %collective-permute-start.1) | collective-permute-done | bytes 589856 | tf_op jit(solution)/shard_map/ppermute | solution.py:354
  75.2 13.9 %collective-permute-done.2.c = bf16[96,3072]{1,0:T(8,128)(2,1)} collective-permute-done((bf16[96,3072]{1,0:T(8,128)(2,1)}, bf16[96,3072]{1,0:T(8,128)(2,1)}, u32[]{:S(2)}, u32[]{:S(2)}) %collective-permute-start.2) | collective-permute-done | bytes 589856 | tf_op jit(solution)/shard_map/ppermute | solution.py:354
  89.1 0.0 collective-permute-done.3.d
  89.1 2.8 %ring_sum.1 = bf16[16,144,128]{2,1,0:T(8,128)(2,1)} custom-call(bf16[96,3072]{1,0:T(8,128)(2,1)S(1)} %get-tuple-element.35.a, bf16[96,3072]{1,0:T(8,128)(2,1)S(1)} %collective-permute-done.1.b, bf16[96,3072]{1,0:T(8,128)(2,1)} %collective-permute-done.2.c, bf16[96,3072]{1,0:T(8,128)(2,1)} %collective-permute-done.3.d), custom_call_target="tpu_custom_call" | custom-call | flops 20000000000 | bytes 3000000 | tf_op jit(solution)/shard_map/ring_sum/pallas_call | solution.py:356
  91.9 0.0 all-to-all-done.1.in_ref
  91.9 3.6 %all-to-all-start.2 = ((bf16[16,144,128]{2,1,0:T(8,128)(2,1)}), bf16[16,144,128]{2,1,0:T(8,128)(2,1)S(1)}, u32[]{:S(2)}, u32[]{:S(2)}) async-start(bf16[16,144,128]{2,1,0:T(8,128)(2,1)} %ring_sum.1), calls=%async_computation.2 | async-start | bytes 1179648 | tf_op jit(solution)/shard_map/all_to_all | solution.py:366
  95.5 2.1 %unpack.1 = (bf16[4,128,768]{2,1,0:T(8,128)(2,1)}, bf16[4,128,768]{2,1,0:T(8,128)(2,1)}, f32[8,128]{1,0:T(8,128)S(1)}) custom-call(bf16[32,200,128]{2,1,0:T(8,128)(2,1)S(1)} %all-to-all-done.1.in_ref), custom_call_target="tpu_custom_call" | custom-call | flops 1000000000 | bytes 4000000 | tf_op jit(solution)/shard_map/unpack/pallas_call | solution.py:361
  97.6 2.1 %collective-permute-start.6 = (f32[8,128]{1,0:T(8,128)S(1)}, f32[8,128]{1,0:T(8,128)S(1)}, u32[]{:S(2)}, u32[]{:S(2)}) collective-permute-start(f32[8,128]{1,0:T(8,128)S(1)} %get-tuple-element.39.g0), channel_id=1, source_target_pairs={{0,3},{1,0},{2,1},{3,2},{4,7},{5,4},{6,5},{7,6},{8,11},{9,8},{10,9... | collective-permute-start | bytes 12296 | tf_op jit(solution)/shard_map/ppermute | solution.py:367
  99.7 0.9 collective-permute-start.5
  100.6 1.0 collective-permute-start.4
  101.6 5.6 %all-to-all-done.2.in_ref = bf16[16,144,128]{2,1,0:T(8,128)(2,1)S(1)} async-done(((bf16[16,144,128]{2,1,0:T(8,128)(2,1)}), bf16[16,144,128]{2,1,0:T(8,128)(2,1)S(1)}, u32[]{:S(2)}, u32[]{:S(2)}) %all-to-all-start.2) | async-done | bytes 589856 | tf_op jit(solution)/shard_map/all_to_all | solution.py:366
  107.3 0.0 collective-permute-done.6.g3
  107.3 0.0 collective-permute-done.5.g2
  107.3 0.0 collective-permute-done.4.g1
  107.3 0.7 final.1
  (1 shorter events, 0.0 us)
Async XLA Ops:
  4.1 8.4 %copy-start.2 = (f32[768]{0:T(1024)S(1)}, f32[768]{0:T(1024)}, u32[]{:S(2)}) copy-start(f32[768]{0:T(1024)} %param.12) | copy-start | bytes 9220
  4.2 31.5 %copy-start = (bf16[768,768]{1,0:T(8,128)(2,1)S(1)}, bf16[768,768]{1,0:T(8,128)(2,1)}, u32[]{:S(2)}) copy-start(bf16[768,768]{1,0:T(8,128)(2,1)} %wout_ref.1) | copy-start | bytes 3538948
  4.2 31.5 %all-to-all-start = ((bf16[32,2,16,768]{3,2,1,0:T(8,128)(2,1)}), bf16[32,2,16,768]{3,2,1,0:T(8,128)(2,1)S(1)}, u32[]{:S(2)}, u32[]{:S(2)}) async-start(bf16[32,2,16,768]{3,2,1,0:T(8,128)(2,1)} %pack.1), calls=%async_computation | async-start | bytes 3145728 | tf_op jit(solution)/shard_map/all_to_all | solution.py:327
  35.7 15.4 %copy-start.1 = (bf16[768,2304]{1,0:T(8,128)(2,1)S(1)}, bf16[768,2304]{1,0:T(8,128)(2,1)}, u32[]{:S(2)}) copy-start(bf16[768,2304]{1,0:T(8,128)(2,1)} %wqkv_ref.1) | copy-start | bytes 10616836
  50.8 5.7 %collective-permute-start = (bf16[384,3072]{1,0:T(8,128)(2,1)S(1)}, bf16[384,3072]{1,0:T(8,128)(2,1)S(1)}, u32[]{:S(2)}, u32[]{:S(2)}) collective-permute-start(bf16[384,3072]{1,0:T(8,128)(2,1)S(1)} %get-tuple-element.25), channel_id=1, source_target_pairs={{0,8},{1,9},{2,10},{3,11},{4,12},{5,13},{6,14},{7,15},{8,0},{9,1},... | collective-permute-start | bytes 7077896 | tf_op jit(solution)/shard_map/ppermute | solution.py:339
  58.0 17.2 %collective-permute-start.1 = (bf16[96,3072]{1,0:T(8,128)(2,1)}, bf16[96,3072]{1,0:T(8,128)(2,1)S(1)}, u32[]{:S(2)}, u32[]{:S(2)}) collective-permute-start(bf16[96,3072]{1,0:T(8,128)(2,1)} %get-tuple-element.36), channel_id=1, source_target_pairs={{0,1},{1,2},{2,3},{3,0},{4,5},{5,6},{6,7},{7,4},{8,9},{9,10},{10,1... | collective-permute-start | bytes 1769480 | tf_op jit(solution)/shard_map/ppermute | solution.py:354
  59.5 29.6 %collective-permute-start.2 = (bf16[96,3072]{1,0:T(8,128)(2,1)}, bf16[96,3072]{1,0:T(8,128)(2,1)}, u32[]{:S(2)}, u32[]{:S(2)}) collective-permute-start(bf16[96,3072]{1,0:T(8,128)(2,1)} %get-tuple-element.37), channel_id=1, source_target_pairs={{0,2},{1,3},{2,0},{3,1},{4,6},{5,7},{6,4},{7,5},{8,10},{9,11},{10,... | collective-permute-start | bytes 1769480 | tf_op jit(solution)/shard_map/ppermute | solution.py:354
  62.4 26.7 %collective-permute-start.3 = (bf16[96,3072]{1,0:T(8,128)(2,1)S(1)}, bf16[96,3072]{1,0:T(8,128)(2,1)}, u32[]{:S(2)}, u32[]{:S(2)}) collective-permute-start(bf16[96,3072]{1,0:T(8,128)(2,1)S(1)} %get-tuple-element.38), channel_id=1, source_target_pairs={{0,3},{1,0},{2,1},{3,2},{4,7},{5,4},{6,5},{7,6},{8,11},{9,8},{10,9... | collective-permute-start | bytes 1769480 | tf_op jit(solution)/shard_map/ppermute | solution.py:354
  63.8 28.1 %all-to-all-start.1 = ((bf16[32,200,128]{2,1,0:T(8,128)(2,1)}), bf16[32,200,128]{2,1,0:T(8,128)(2,1)S(1)}, u32[]{:S(2)}, u32[]{:S(2)}) async-start(bf16[32,200,128]{2,1,0:T(8,128)(2,1)} %mixed.1), calls=%async_computation.1 | async-start | bytes 3276800 | tf_op jit(solution)/shard_map/all_to_all | solution.py:355
  91.9 15.3 %all-to-all-start.2 = ((bf16[16,144,128]{2,1,0:T(8,128)(2,1)}), bf16[16,144,128]{2,1,0:T(8,128)(2,1)S(1)}, u32[]{:S(2)}, u32[]{:S(2)}) async-start(bf16[16,144,128]{2,1,0:T(8,128)(2,1)} %ring_sum.1), calls=%async_computation.2 | async-start | bytes 1179648 | tf_op jit(solution)/shard_map/all_to_all | solution.py:366
  97.6 9.6 %collective-permute-start.6 = (f32[8,128]{1,0:T(8,128)S(1)}, f32[8,128]{1,0:T(8,128)S(1)}, u32[]{:S(2)}, u32[]{:S(2)}) collective-permute-start(f32[8,128]{1,0:T(8,128)S(1)} %get-tuple-element.39.g0), channel_id=1, source_target_pairs={{0,3},{1,0},{2,1},{3,2},{4,7},{5,4},{6,5},{7,6},{8,11},{9,8},{10,9... | collective-permute-start | bytes 12296 | tf_op jit(solution)/shard_map/ppermute | solution.py:367
  99.7 7.6 %collective-permute-start.5 = (f32[8,128]{1,0:T(8,128)S(1)}, f32[8,128]{1,0:T(8,128)S(1)}, u32[]{:S(2)}, u32[]{:S(2)}) collective-permute-start(f32[8,128]{1,0:T(8,128)S(1)} %get-tuple-element.39.g0), channel_id=1, source_target_pairs={{0,2},{1,3},{2,0},{3,1},{4,6},{5,7},{6,4},{7,5},{8,10},{9,11},{10,... | collective-permute-start | bytes 12296 | tf_op jit(solution)/shard_map/ppermute | solution.py:367
  100.6 6.7 %collective-permute-start.4 = (f32[8,128]{1,0:T(8,128)S(1)}, f32[8,128]{1,0:T(8,128)S(1)}, u32[]{:S(2)}, u32[]{:S(2)}) collective-permute-start(f32[8,128]{1,0:T(8,128)S(1)} %get-tuple-element.39.g0), channel_id=1, source_target_pairs={{0,1},{1,2},{2,3},{3,0},{4,5},{5,6},{6,7},{7,4},{8,9},{9,10},{10,1... | collective-permute-start | bytes 12296 | tf_op jit(solution)/shard_map/ppermute | solution.py:367

commit v5 on v4

--- a/solution.py
+++ b/solution.py
@@ -74,21 +74,40 @@
     return lax.dot_general(a, b, (((ca,), (cb,)), ((), ())), preferred_element_type=F32)
 
 
-def send_order():
-    i = lax.broadcasted_iota(jnp.int32, (TOK, TOK), 0)
-    s = lax.broadcasted_iota(jnp.int32, (TOK, TOK), 1)
-    src = ((i >> 2) & 3) * 128 + (i >> 4) * 4 + (i & 3)
-    return s == src
-
-
-def position_order():
-    i = lax.broadcasted_iota(jnp.int32, (TOK, TOK), 0)
-    s = lax.broadcasted_iota(jnp.int32, (TOK, TOK), 1)
-    return s == (i & 127) * 4 + (i >> 7)
-
-
 def onehot(mask):
     return jnp.where(mask, 1.0, 0.0).astype(BF)
+
+
+def rows_and_columns():
+    i = lax.broadcasted_iota(jnp.int32, (128, 128), 0)
+    return i, lax.broadcasted_iota(jnp.int32, (128, 128), 1)
+
+
+def send_order():
+    i, s = rows_and_columns()
+    return s == ((i >> 2) & 3) * 32 + (i >> 4) * 4 + (i & 3)
+
+
+def position_order():
+    i, s = rows_and_columns()
+    return onehot(s == ((i >> 2) & 7) * 16 + (i & 3) * 4 + (i >> 5))
+
+
+def by_position(x):
+    order = position_order()
+    parts = [dot(order, x[n * 128 : n * 128 + 128], 1, 0).astype(BF) for n in range(4)]
+    return jnp.concatenate(
+        [parts[n][p * 32 : p * 32 + 32] for p in range(4) for n in range(4)], axis=0
+    )
+
+
+def by_source(x):
+    order = position_order()
+    parts = [
+        jnp.concatenate([x[p * 128 + n * 32 : p * 128 + n * 32 + 32] for p in range(4)], axis=0)
+        for n in range(4)
+    ]
+    return jnp.concatenate([dot(order, part, 0, 0).astype(BF) for part in parts], axis=0)
 
 
 def pack_kernel(tok_hbm, cot_hbm, les_hbm, out_hbm, tok_ref, cot_ref, les_ref, out_ref, sems):
@@ -102,18 +121,24 @@
         c.start()
     mask = send_order()
     plain = onehot(mask)
+
+    def block(ref, n):
+        return jnp.concatenate([ref[d, n * 32 : n * 32 + 32] for d in range(4)], axis=0)
+
+    loads[1].wait()
+    for n in range(4):
+        t = dot(plain, block(tok_ref, n), 1, 0).astype(BF)
+        out_ref[0, n * 8 : n * 8 + 8] = t.reshape(8, 16, D)
+    store_t = pltpu.make_async_copy(out_ref.at[0], out_hbm.at[:, 0], sems.at[3])
+    store_t.start()
     loads[0].wait()
     weight = 1.0 + LESION_GAIN * les_ref[...].astype(F32)
-    row = jnp.concatenate([weight[d : d + 1, :] for d in range(4)], axis=1)
-    scaled = jnp.where(mask, row, 0.0).astype(BF)
-    loads[1].wait()
-    t = dot(plain, tok_ref[...].reshape(TOK, D), 1, 0).astype(BF)
-    out_ref[0] = t.reshape(32, 16, D)
-    store_t = pltpu.make_async_copy(out_ref.at[0], out_hbm.at[:, 0], sems.at[3])
-    store_t.start()
     loads[2].wait()
-    g = dot(scaled, cot_ref[...].reshape(TOK, D), 1, 0).astype(BF)
-    out_ref[1] = g.reshape(32, 16, D)
+    for n in range(4):
+        row = jnp.concatenate([weight[d : d + 1, n * 32 : n * 32 + 32] for d in range(4)], axis=1)
+        scaled = jnp.where(mask, row, 0.0).astype(BF)
+        g = dot(scaled, block(cot_ref, n), 1, 0).astype(BF)
+        out_ref[1, n * 8 : n * 8 + 8] = g.reshape(8, 16, D)
     store_g = pltpu.make_async_copy(out_ref.at[1], out_hbm.at[:, 1], sems.at[4])
     store_g.start()
     store_t.wait()
@@ -128,7 +153,10 @@
             [in_ref[:, base + l * 16 : base + l * 16 + 16].reshape(TOK, 128) for l in range(6)],
             axis=1,
         )
-        out[...] = dot(sel, x, 0, 0).astype(BF).reshape(4, 128, D)
+        for b in range(4):
+            y = dot(sel, x[b * 128 : b * 128 + 128], 0, 0).astype(BF)
+            for d in range(4):
+                out[d, b * 32 : b * 32 + 32] = y[d * 32 : d * 32 + 32]
     g = jnp.sum(in_ref[:, 192:].astype(F32), axis=0)
     gain_ref[...] = jnp.broadcast_to(jnp.sum(g, axis=0, keepdims=True), (8, 128))
 
@@ -148,60 +176,61 @@
     loads = [
         pltpu.make_async_copy(src, dst, sems.at[n])
         for n, (src, dst) in enumerate(
-            ((recv_hbm, recv_ref), (wqkv_hbm, wqkv_ref), (wout_hbm, wout_ref))
+            ((recv_hbm, recv_ref), (wout_hbm, wout_ref), (wqkv_hbm, wqkv_ref))
         )
     ]
     for c in loads:
         c.start()
-    order = onehot(position_order())
     loads[0].wait()
     _, _, unit = normalise(recv_ref[:, 0].reshape(TOK, D))
     normed = (unit * gain_ref[...]).astype(BF)
-    norm_ref[...] = dot(order, normed, 1, 0).astype(BF)
-    gy_ref[...] = dot(order, recv_ref[:, 1].reshape(TOK, D), 1, 0).astype(BF)
+    norm_ref[...] = by_position(normed)
+    gy_ref[...] = by_position(recv_ref[:, 1].reshape(TOK, D))
     loads[1].wait()
+    ga_ref[...] = dot(gy_ref[...], wout_ref[...], 1, 1).astype(BF)
+    loads[2].wait()
 
     def project(n, _):
         cols = pl.ds(pl.multiple_of(n * 768, 768), 768)
         qkv_ref[:, cols] = dot(norm_ref[...], wqkv_ref[:, cols], 1, 0).astype(BF)
         return 0
 
-    lax.fori_loop(0, 3, project, 0)
-    loads[2].wait()
-    ga_ref[...] = dot(gy_ref[...], wout_ref[...], 1, 1).astype(BF)
+    lax.fori_loop(0, 3, project, 0, unroll=True)
     first = lax.broadcasted_iota(jnp.int32, (128, 128), 1) < 64
 
     def split(x):
         zero = jnp.zeros_like(x)
         return jnp.concatenate([jnp.where(first, x, zero), jnp.where(first, zero, x)], axis=0)
+
+    def stack(x):
+        return jnp.concatenate([x[:, :128], x[:, 128:]], axis=0)
 
     def heads(hp, _):
         base = pl.multiple_of(hp * 128, 128)
         rows = [slice(p * 128, (p + 1) * 128) for p in range(4)]
         q = [qkv_ref[r, pl.ds(base, 128)] for r in rows]
-        kb = [split(qkv_ref[r, pl.ds(base + D, 128)]) for r in rows]
-        vb = [split(qkv_ref[r, pl.ds(base + 2 * D, 128)]) for r in rows]
-        ga = [ga_ref[r, pl.ds(base, 128)] for r in rows]
-        s = [dot(kb[p], q[p], 1, 1).reshape(2, 128, 128) for p in range(4)]
-        dp = [dot(vb[p], ga[p], 1, 1).reshape(2, 128, 128) for p in range(4)]
+        k = [qkv_ref[r, pl.ds(base + D, 128)] for r in rows]
+        v = [qkv_ref[r, pl.ds(base + 2 * D, 128)] for r in rows]
+        qb = [split(x) for x in q]
+        gb = [split(ga_ref[r, pl.ds(base, 128)]) for r in rows]
+        s = [dot(k[p], qb[p], 1, 1) for p in range(4)]
+        dp = [dot(v[p], gb[p], 1, 1) for p in range(4)]
         pb, ds = [], []
         for p in range(4):
             sp = s[p] * scale
-            e = jnp.exp(sp - jnp.max(sp, axis=1, keepdims=True))
-            probs = e * (1.0 / jnp.sum(e, axis=1, keepdims=True))
-            delta = jnp.sum(probs * dp[p], axis=1, keepdims=True)
-            ds.append((probs * (dp[p] - delta) * scale).astype(BF).reshape(256, 128))
-            pb.append(probs.astype(BF).reshape(256, 128))
+            e = jnp.exp(sp - jnp.max(sp, axis=0, keepdims=True))
+            probs = e * (1.0 / jnp.sum(e, axis=0, keepdims=True))
+            delta = jnp.sum(probs * dp[p], axis=0, keepdims=True)
+            ds.append((probs * (dp[p] - delta) * scale).astype(BF))
+            pb.append(probs.astype(BF))
         for p in range(4):
-            attn_ref[rows[p], pl.ds(base, 128)] = dot(pb[p], vb[p], 0, 0).astype(BF)
-            dqkv_ref[rows[p], pl.ds(base, 128)] = dot(ds[p], kb[p], 0, 0).astype(BF)
-            dk = dot(ds[p], q[p], 1, 0)
-            dv = dot(pb[p], ga[p], 1, 0)
-            dqkv_ref[rows[p], pl.ds(base + D, 128)] = jnp.where(first, dk[:128], dk[128:]).astype(BF)
-            dqkv_ref[rows[p], pl.ds(base + 2 * D, 128)] = jnp.where(first, dv[:128], dv[128:]).astype(BF)
+            attn_ref[rows[p], pl.ds(base, 128)] = dot(stack(pb[p]), split(v[p]), 0, 0).astype(BF)
+            dqkv_ref[rows[p], pl.ds(base, 128)] = dot(stack(ds[p]), split(k[p]), 0, 0).astype(BF)
+            dqkv_ref[rows[p], pl.ds(base + D, 128)] = dot(ds[p], qb[p], 1, 0).astype(BF)
+            dqkv_ref[rows[p], pl.ds(base + 2 * D, 128)] = dot(pb[p], gb[p], 1, 0).astype(BF)
         return 0
 
-    lax.fori_loop(0, HEADS // 2, heads, 0)
+    lax.fori_loop(0, HEADS // 2, heads, 0, unroll=True)
     pick = onehot(lax.broadcasted_iota(jnp.int32, (D, D), 0) == feat_ref[...])
     lhs_ref[...] = dot(pick, norm_ref[...], 0, 1).astype(BF)
 
@@ -212,7 +241,7 @@
         send_ref[:, cols] = g[384:]
         return 0
 
-    lax.fori_loop(0, 3, weight_grad, 0)
+    lax.fori_loop(0, 3, weight_grad, 0, unroll=True)
     lhs_ref[...] = dot(pick, attn_ref[...], 0, 1).astype(BF)
     g = dot(lhs_ref[...], gy_ref[...], 1, 0).astype(BF)
     keep_ref[:, 3 * D :] = g[:384]
@@ -220,9 +249,8 @@
 
 
 def token_kernel(recv_ref, gain_ref, dqkv_ref, wqkv_ref, ret_ref):
-    order = onehot(position_order())
     gn = dot(dqkv_ref[...], wqkv_ref[...], 1, 1).astype(BF)
-    gn = dot(order, gn, 0, 0)
+    gn = by_source(gn).astype(F32)
     _, inv_rms, unit = normalise(recv_ref[:, 0].reshape(TOK, D))
     g = jnp.sum(gn * unit, axis=0, keepdims=True)
     dunit = gn * gain_ref[...]
@@ -249,7 +277,7 @@
 def mixed_kernel(recv_ref, attn_ref, wout_ref, grad_ref, ret_hbm, ret_ref, sems):
     store_g = pltpu.make_async_copy(grad_ref, ret_hbm.at[:, 96:], sems.at[0])
     store_g.start()
-    attn = dot(onehot(position_order()), attn_ref[...], 0, 0).astype(BF)
+    attn = by_source(attn_ref[...])
     proj = dot(attn, wout_ref[...], 1, 0).astype(BF)
     mixed = (recv_ref[:, 0].reshape(TOK, D).astype(F32) + proj.astype(F32)).astype(BF)
     for l in range(6):

time: 109 us -> 105 us (0.963)
  Pallas kernels: 31.1 us -> 26.9 us
    pallas_call x1, Pallas kernels: 15.1 us -> 12.2 us  [per_device(): pl.pallas_call(main_kernel, out_shape=(shape(384, 4 * D), shape(384, 4 *...]
  transfers between devices with their start and end apart: 10 -> 10, of which waited for: 4 -> 4; matrix products, arithmetic and copies ran while one was open for 1% -> 1% of each run, Pallas kernels for 10% -> 9%
where the time goes in v5:
time: 105 us; the launch traced here: 104 us
  waiting for transfers between devices  49.8 us (47%)
  Pallas kernels  26.9 us (26%)
  starting transfers between devices  26 us (25%)
    all_to_all x1, waiting for transfers between devices, per_device(): lax.all_to_all(packed, AXES, 0, 0, tiled=True, axis_index_groups=PLANE)  22.4 us
    ppermute x3, waiting for transfers between devices, per_device(): lax.ppermute(q, AXES, y_shift(s))  21.3 us
    pallas_call x1, Pallas kernels, per_device(): pl.pallas_call(main_kernel, out_shape=(shape(384, 4 * D), shape(384, 4 *...  12.2 us
    all_to_all x1, starting transfers between devices, per_device(): lax.all_to_all(packed, AXES, 0, 0, tiled=True, axis_index_groups=PLANE)  8.38 us
    all_to_all x1, waiting for transfers between devices, per_device(): last = lax.all_to_all(mine, AXES, 0, 0, tiled=True, axis_index_groups=CHIPS)  6.08 us
    ppermute x3, starting transfers between devices, per_device(): lax.ppermute(q, AXES, y_shift(s))  5.84 us
    ppermute x3, starting transfers between devices, per_device(): lax.ppermute(gain_part, AXES, y_shift(s))  4 us
    all_to_all x1, starting transfers between devices, per_device(): back = lax.all_to_all(ret, AXES, 0, 0, tiled=True, axis_index_groups=PLANE)  3.98 us
  transfers between devices with their start and end apart: 10, of which 4 were waited for; matrix products, arithmetic and copies ran while one was open for 1% of the time, Pallas kernels for 9%

profile of v5, /device:TPU:0, one launch (start us, length us, event | category | flops | bytes accessed | tf_op | source)
XLA Modules:
  0.0 104.2 jit_solution(9574010472839294659)
XLA Ops:
  0.6 2.9 %pack.1 = bf16[32,2,16,768]{3,2,1,0:T(8,128)(2,1)} custom-call(bf16[4,128,768]{2,1,0:T(8,128)(2,1)} %tok_hbm.1, bf16[4,128,768]{2,1,0:T(8,128)(2,1)} %cot_hbm.1, s32[4,128]{1,0:T(4,128)} %les_hbm.1), custom_call_target="tpu_custom_call" | custom-call | flops 1000000000 | bytes 4000000 | tf_op jit(solution)/shard_map/pack/pallas_call | solution.py:347
  3.5 0.0 copy-start.2
  3.5 0.0 copy-start
  3.5 8.4 %all-to-all-start = ((bf16[32,2,16,768]{3,2,1,0:T(8,128)(2,1)}), bf16[32,2,16,768]{3,2,1,0:T(8,128)(2,1)S(1)}, u32[]{:S(2)}, u32[]{:S(2)}) async-start(bf16[32,2,16,768]{3,2,1,0:T(8,128)(2,1)} %pack.1), calls=%async_computation | async-start | bytes 3145728 | tf_op jit(solution)/shard_map/all_to_all | solution.py:355
  11.9 0.0 copy-done.2
  12.0 0.8 constant_dynamic-slice_fusion.feat_ref
  12.7 22.4 %all-to-all-done.recv_hbm.recv_ref = bf16[32,2,16,768]{3,2,1,0:T(8,128)(2,1)S(1)} async-done(((bf16[32,2,16,768]{3,2,1,0:T(8,128)(2,1)}), bf16[32,2,16,768]{3,2,1,0:T(8,128)(2,1)S(1)}, u32[]{:S(2)}, u32[]{:S(2)}) %all-to-all-start) | async-done | bytes 1572896 | tf_op jit(solution)/shard_map/all_to_all | solution.py:355
  35.1 0.0 copy-done
  35.1 0.0 copy-start.1
  35.1 12.2 %main.1 = (bf16[384,3072]{1,0:T(8,128)(2,1)S(1)}, bf16[384,3072]{1,0:T(8,128)(2,1)S(1)}, bf16[512,768]{1,0:T(8,128)(2,1)S(1)}, bf16[512,2304]{1,0:T(8,128)(2,1)S(1)}) custom-call(bf16[32,2,16,768]{3,2,1,0:T(8,128)(2,1)S(1)} %all-to-all-done.recv_hbm.recv_ref, f32[1,768]{1,0:T(1,128)S(1)} %reshape.19.gain_ref, ...), custom_call_target="tpu_custom_call" | custom-call | flops 10000000000 | bytes 15000000 | tf_op jit(solution)/shard_map/main/pallas_call | solution.py:356
  47.3 0.3 collective-permute-start
  47.6 0.0 copy-done.1
  47.6 3.1 %token_grads.1.grad_ref = bf16[32,104,128]{2,1,0:T(8,128)(2,1)S(1)} custom-call(bf16[32,2,16,768]{3,2,1,0:T(8,128)(2,1)S(1)} %all-to-all-done.recv_hbm.recv_ref, f32[1,768]{1,0:T(1,128)S(1)} %reshape.19.gain_ref, bf16[512,2304]{1,0:T(8,128)(2,1)S(1)} %get-tuple-element.31.dqkv_ref, bf16[768,2304]{1,0:T(8,128)(2,1)S(1)} %copy-done.1), custom_call_target="tpu_custom_call" | custom-call | flops 2800000000 | bytes 9000000 | tf_op jit(solution)/shard_map/token_grads/pallas_call | solution.py:368
  50.7 2.0 %mixed.1 = bf16[32,200,128]{2,1,0:T(8,128)(2,1)} custom-call(bf16[32,2,16,768]{3,2,1,0:T(8,128)(2,1)S(1)} %all-to-all-done.recv_hbm.recv_ref, bf16[512,768]{1,0:T(8,128)(2,1)S(1)} %get-tuple-element.30.attn_ref, bf16[768,768]{1,0:T(8,128)(2,1)S(1)} %copy-done, bf16[32,104,128]{2,1,0:T(8,128)(2,1)S(1)} %token_grads.1.grad_ref), custom_call_target="tpu_custom_call" | custom-call | flops 1000000000 | bytes 5000000 | tf_op jit(solution)/shard_map/mixed/pallas_call | solution.py:372
  52.7 0.0 collective-permute-done.b_ref
  52.7 1.5 %pair_sum.1 = (bf16[96,3072]{1,0:T(8,128)(2,1)S(1)}, bf16[96,3072]{1,0:T(8,128)(2,1)}, bf16[96,3072]{1,0:T(8,128)(2,1)}, bf16[96,3072]{1,0:T(8,128)(2,1)S(1)}) custom-call(bf16[384,3072]{1,0:T(8,128)(2,1)S(1)} %get-tuple-element.24.a_ref, bf16[384,3072]{1,0:T(8,128)(2,1)S(1)} %collective-permute-done.b_ref), custom_call_target="tpu_custom_call" | custom-call | flops 1000000 | bytes 7000000 | tf_op jit(solution)/shard_map/pair_sum/pallas_call | solution.py:377
  54.2 1.6 %collective-permute-start.1 = (bf16[96,3072]{1,0:T(8,128)(2,1)}, bf16[96,3072]{1,0:T(8,128)(2,1)S(1)}, u32[]{:S(2)}, u32[]{:S(2)}) collective-permute-start(bf16[96,3072]{1,0:T(8,128)(2,1)} %get-tuple-element.36), channel_id=1, source_target_pairs={{0,1},{1,2},{2,3},{3,0},{4,5},{5,6},{6,7},{7,4},{8,9},{9,10},{10,1... | collective-permute-start | bytes 1769480 | tf_op jit(solution)/shard_map/ppermute | solution.py:382
  55.8 2.9 %collective-permute-start.2 = (bf16[96,3072]{1,0:T(8,128)(2,1)}, bf16[96,3072]{1,0:T(8,128)(2,1)}, u32[]{:S(2)}, u32[]{:S(2)}) collective-permute-start(bf16[96,3072]{1,0:T(8,128)(2,1)} %get-tuple-element.37), channel_id=1, source_target_pairs={{0,2},{1,3},{2,0},{3,1},{4,6},{5,7},{6,4},{7,5},{8,10},{9,11},{10,... | collective-permute-start | bytes 1769480 | tf_op jit(solution)/shard_map/ppermute | solution.py:382
  58.7 1.3 %collective-permute-start.3 = (bf16[96,3072]{1,0:T(8,128)(2,1)S(1)}, bf16[96,3072]{1,0:T(8,128)(2,1)}, u32[]{:S(2)}, u32[]{:S(2)}) collective-permute-start(bf16[96,3072]{1,0:T(8,128)(2,1)S(1)} %get-tuple-element.38), channel_id=1, source_target_pairs={{0,3},{1,0},{2,1},{3,2},{4,7},{5,4},{6,5},{7,6},{8,11},{9,8},{10,9... | collective-permute-start | bytes 1769480 | tf_op jit(solution)/shard_map/ppermute | solution.py:382
  60.0 4.0 %all-to-all-start.1 = ((bf16[32,200,128]{2,1,0:T(8,128)(2,1)}), bf16[32,200,128]{2,1,0:T(8,128)(2,1)S(1)}, u32[]{:S(2)}, u32[]{:S(2)}) async-start(bf16[32,200,128]{2,1,0:T(8,128)(2,1)} %mixed.1), calls=%async_computation.1 | async-start | bytes 3276800 | tf_op jit(solution)/shard_map/all_to_all | solution.py:383
  64.0 7.4 %collective-permute-done.1.b = bf16[96,3072]{1,0:T(8,128)(2,1)S(1)} collective-permute-done((bf16[96,3072]{1,0:T(8,128)(2,1)}, bf16[96,3072]{1,0:T(8,128)(2,1)S(1)}, u32[]{:S(2)}, u32[]{:S(2)}) %collective-permute-start.1) | collective-permute-done | bytes 589856 | tf_op jit(solution)/shard_map/ppermute | solution.py:382
  71.4 13.9 %collective-permute-done.2.c = bf16[96,3072]{1,0:T(8,128)(2,1)} collective-permute-done((bf16[96,3072]{1,0:T(8,128)(2,1)}, bf16[96,3072]{1,0:T(8,128)(2,1)}, u32[]{:S(2)}, u32[]{:S(2)}) %collective-permute-start.2) | collective-permute-done | bytes 589856 | tf_op jit(solution)/shard_map/ppermute | solution.py:382
  85.3 0.0 collective-permute-done.3.d
  85.3 2.8 %ring_sum.1 = bf16[16,144,128]{2,1,0:T(8,128)(2,1)} custom-call(bf16[96,3072]{1,0:T(8,128)(2,1)S(1)} %get-tuple-element.35.a, bf16[96,3072]{1,0:T(8,128)(2,1)S(1)} %collective-permute-done.1.b, bf16[96,3072]{1,0:T(8,128)(2,1)} %collective-permute-done.2.c, bf16[96,3072]{1,0:T(8,128)(2,1)} %collective-permute-done.3.d), custom_call_target="tpu_custom_call" | custom-call | flops 20000000000 | bytes 3000000 | tf_op jit(solution)/shard_map/ring_sum/pallas_call | solution.py:384
  88.2 0.0 all-to-all-done.1.in_ref
  88.2 3.6 %all-to-all-start.2 = ((bf16[16,144,128]{2,1,0:T(8,128)(2,1)}), bf16[16,144,128]{2,1,0:T(8,128)(2,1)S(1)}, u32[]{:S(2)}, u32[]{:S(2)}) async-start(bf16[16,144,128]{2,1,0:T(8,128)(2,1)} %ring_sum.1), calls=%async_computation.2 | async-start | bytes 1179648 | tf_op jit(solution)/shard_map/all_to_all | solution.py:394
  91.8 1.7 %unpack.1 = (bf16[4,128,768]{2,1,0:T(8,128)(2,1)}, bf16[4,128,768]{2,1,0:T(8,128)(2,1)}, f32[8,128]{1,0:T(8,128)S(1)}) custom-call(bf16[32,200,128]{2,1,0:T(8,128)(2,1)S(1)} %all-to-all-done.1.in_ref), custom_call_target="tpu_custom_call" | custom-call | flops 1000000000 | bytes 4000000 | tf_op jit(solution)/shard_map/unpack/pallas_call | solution.py:389
  93.4 2.1 %collective-permute-start.6 = (f32[8,128]{1,0:T(8,128)S(1)}, f32[8,128]{1,0:T(8,128)S(1)}, u32[]{:S(2)}, u32[]{:S(2)}) collective-permute-start(f32[8,128]{1,0:T(8,128)S(1)} %get-tuple-element.39.g0), channel_id=1, source_target_pairs={{0,3},{1,0},{2,1},{3,2},{4,7},{5,4},{6,5},{7,6},{8,11},{9,8},{10,9... | collective-permute-start | bytes 12296 | tf_op jit(solution)/shard_map/ppermute | solution.py:395
  95.5 0.9 collective-permute-start.5
  96.4 1.0 collective-permute-start.4
  97.4 6.1 %all-to-all-done.2.in_ref = bf16[16,144,128]{2,1,0:T(8,128)(2,1)S(1)} async-done(((bf16[16,144,128]{2,1,0:T(8,128)(2,1)}), bf16[16,144,128]{2,1,0:T(8,128)(2,1)S(1)}, u32[]{:S(2)}, u32[]{:S(2)}) %all-to-all-start.2) | async-done | bytes 589856 | tf_op jit(solution)/shard_map/all_to_all | solution.py:394
  103.5 0.0 collective-permute-done.6.g3
  103.5 0.0 collective-permute-done.5.g2
  103.5 0.0 collective-permute-done.4.g1
  103.5 0.7 final.1
  (1 shorter events, 0.0 us)
Async XLA Ops:
  3.5 8.4 %copy-start.2 = (f32[768]{0:T(1024)S(1)}, f32[768]{0:T(1024)}, u32[]{:S(2)}) copy-start(f32[768]{0:T(1024)} %param.12) | copy-start | bytes 9220
  3.5 31.5 %copy-start = (bf16[768,768]{1,0:T(8,128)(2,1)S(1)}, bf16[768,768]{1,0:T(8,128)(2,1)}, u32[]{:S(2)}) copy-start(bf16[768,768]{1,0:T(8,128)(2,1)} %wout_ref.1) | copy-start | bytes 3538948
  3.5 31.5 %all-to-all-start = ((bf16[32,2,16,768]{3,2,1,0:T(8,128)(2,1)}), bf16[32,2,16,768]{3,2,1,0:T(8,128)(2,1)S(1)}, u32[]{:S(2)}, u32[]{:S(2)}) async-start(bf16[32,2,16,768]{3,2,1,0:T(8,128)(2,1)} %pack.1), calls=%async_computation | async-start | bytes 3145728 | tf_op jit(solution)/shard_map/all_to_all | solution.py:355
  35.1 12.5 %copy-start.1 = (bf16[768,2304]{1,0:T(8,128)(2,1)S(1)}, bf16[768,2304]{1,0:T(8,128)(2,1)}, u32[]{:S(2)}) copy-start(bf16[768,2304]{1,0:T(8,128)(2,1)} %wqkv_ref.1) | copy-start | bytes 10616836
  47.3 5.4 %collective-permute-start = (bf16[384,3072]{1,0:T(8,128)(2,1)S(1)}, bf16[384,3072]{1,0:T(8,128)(2,1)S(1)}, u32[]{:S(2)}, u32[]{:S(2)}) collective-permute-start(bf16[384,3072]{1,0:T(8,128)(2,1)S(1)} %get-tuple-element.25), channel_id=1, source_target_pairs={{0,8},{1,9},{2,10},{3,11},{4,12},{5,13},{6,14},{7,15},{8,0},{9,1},... | collective-permute-start | bytes 7077896 | tf_op jit(solution)/shard_map/ppermute | solution.py:367
  54.2 17.2 %collective-permute-start.1 = (bf16[96,3072]{1,0:T(8,128)(2,1)}, bf16[96,3072]{1,0:T(8,128)(2,1)S(1)}, u32[]{:S(2)}, u32[]{:S(2)}) collective-permute-start(bf16[96,3072]{1,0:T(8,128)(2,1)} %get-tuple-element.36), channel_id=1, source_target_pairs={{0,1},{1,2},{2,3},{3,0},{4,5},{5,6},{6,7},{7,4},{8,9},{9,10},{10,1... | collective-permute-start | bytes 1769480 | tf_op jit(solution)/shard_map/ppermute | solution.py:382
  55.8 29.5 %collective-permute-start.2 = (bf16[96,3072]{1,0:T(8,128)(2,1)}, bf16[96,3072]{1,0:T(8,128)(2,1)}, u32[]{:S(2)}, u32[]{:S(2)}) collective-permute-start(bf16[96,3072]{1,0:T(8,128)(2,1)} %get-tuple-element.37), channel_id=1, source_target_pairs={{0,2},{1,3},{2,0},{3,1},{4,6},{5,7},{6,4},{7,5},{8,10},{9,11},{10,... | collective-permute-start | bytes 1769480 | tf_op jit(solution)/shard_map/ppermute | solution.py:382
  58.7 26.6 %collective-permute-start.3 = (bf16[96,3072]{1,0:T(8,128)(2,1)S(1)}, bf16[96,3072]{1,0:T(8,128)(2,1)}, u32[]{:S(2)}, u32[]{:S(2)}) collective-permute-start(bf16[96,3072]{1,0:T(8,128)(2,1)S(1)} %get-tuple-element.38), channel_id=1, source_target_pairs={{0,3},{1,0},{2,1},{3,2},{4,7},{5,4},{6,5},{7,6},{8,11},{9,8},{10,9... | collective-permute-start | bytes 1769480 | tf_op jit(solution)/shard_map/ppermute | solution.py:382
  60.0 28.1 %all-to-all-start.1 = ((bf16[32,200,128]{2,1,0:T(8,128)(2,1)}), bf16[32,200,128]{2,1,0:T(8,128)(2,1)S(1)}, u32[]{:S(2)}, u32[]{:S(2)}) async-start(bf16[32,200,128]{2,1,0:T(8,128)(2,1)} %mixed.1), calls=%async_computation.1 | async-start | bytes 3276800 | tf_op jit(solution)/shard_map/all_to_all | solution.py:383
  88.2 15.3 %all-to-all-start.2 = ((bf16[16,144,128]{2,1,0:T(8,128)(2,1)}), bf16[16,144,128]{2,1,0:T(8,128)(2,1)S(1)}, u32[]{:S(2)}, u32[]{:S(2)}) async-start(bf16[16,144,128]{2,1,0:T(8,128)(2,1)} %ring_sum.1), calls=%async_computation.2 | async-start | bytes 1179648 | tf_op jit(solution)/shard_map/all_to_all | solution.py:394
  93.4 10.1 %collective-permute-start.6 = (f32[8,128]{1,0:T(8,128)S(1)}, f32[8,128]{1,0:T(8,128)S(1)}, u32[]{:S(2)}, u32[]{:S(2)}) collective-permute-start(f32[8,128]{1,0:T(8,128)S(1)} %get-tuple-element.39.g0), channel_id=1, source_target_pairs={{0,3},{1,0},{2,1},{3,2},{4,7},{5,4},{6,5},{7,6},{8,11},{9,8},{10,9... | collective-permute-start | bytes 12296 | tf_op jit(solution)/shard_map/ppermute | solution.py:395
  95.5 8.0 %collective-permute-start.5 = (f32[8,128]{1,0:T(8,128)S(1)}, f32[8,128]{1,0:T(8,128)S(1)}, u32[]{:S(2)}, u32[]{:S(2)}) collective-permute-start(f32[8,128]{1,0:T(8,128)S(1)} %get-tuple-element.39.g0), channel_id=1, source_target_pairs={{0,2},{1,3},{2,0},{3,1},{4,6},{5,7},{6,4},{7,5},{8,10},{9,11},{10,... | collective-permute-start | bytes 12296 | tf_op jit(solution)/shard_map/ppermute | solution.py:395
  96.4 7.1 %collective-permute-start.4 = (f32[8,128]{1,0:T(8,128)S(1)}, f32[8,128]{1,0:T(8,128)S(1)}, u32[]{:S(2)}, u32[]{:S(2)}) collective-permute-start(f32[8,128]{1,0:T(8,128)S(1)} %get-tuple-element.39.g0), channel_id=1, source_target_pairs={{0,1},{1,2},{2,3},{3,0},{4,5},{5,6},{6,7},{7,4},{8,9},{9,10},{10,1... | collective-permute-start | bytes 12296 | tf_op jit(solution)/shard_map/ppermute | solution.py:395

commit v6 on v5

--- a/solution.py
+++ b/solution.py
@@ -16,9 +16,10 @@
 BF = jnp.bfloat16
 F32 = jnp.float32
 MB = 1024 * 1024
-RING = 2e10
+PASS = 1e6
+RING = 1e10
 MAIN_MB = 42
-TOKEN_MB = 20
+TOKEN_MB = 14
 
 
 def place(xlo, z, c, xhi, y):
@@ -288,20 +289,42 @@
     store_m.wait()
 
 
-def pair_sum_kernel(a_ref, b_ref, o0, o1, o2, o3):
-    for n, o in enumerate((o0, o1, o2, o3)):
+HALF = 2 * D
+
+
+def pair_sum_kernel(a_ref, b_ref, own, up, down, hold):
+    def block(n, cols):
         rows = slice(n * 96, n * 96 + 96)
-        o[...] = (a_ref[rows].astype(F32) + b_ref[rows].astype(F32)).astype(BF)
-
-
-def ring_sum_kernel(a, b, c, d, o, sum_ref, out_ref):
-    sum_ref[...] = (a[...].astype(F32) + b[...].astype(F32)) + (
-        c[...].astype(F32) + d[...].astype(F32)
-    )
-    for k in range(16):
-        for l in range(24):
-            out_ref[k, l * 6 : l * 6 + 6] = sum_ref[k * 6 : k * 6 + 6, l * 128 : l * 128 + 128]
-    o[...] = out_ref[...].astype(BF)
+        return (a_ref[rows, cols].astype(F32) + b_ref[rows, cols].astype(F32)).astype(BF)
+
+    left, right = slice(0, HALF), slice(HALF, 2 * HALF)
+    up[:, left] = block(2, left)
+    up[:, right] = block(1, right)
+    down[:, left] = block(3, left)
+    down[:, right] = block(2, right)
+    own[:, left] = block(0, left)
+    own[:, right] = block(0, right)
+    hold[:, left] = block(1, left)
+    hold[:, right] = block(3, right)
+
+
+def pass_on_kernel(hold, up, down, up_out, down_out):
+    left, right = slice(0, HALF), slice(HALF, 2 * HALF)
+    up_out[...] = (hold[:, left].astype(F32) + up[:, left].astype(F32)).astype(BF)
+    down_out[...] = (hold[:, right].astype(F32) + down[:, right].astype(F32)).astype(BF)
+
+
+def ring_sum_kernel(own, up, down, up_far, down_far, o):
+    left, right = slice(0, HALF), slice(HALF, 2 * HALF)
+    for q in range(4):
+        r = slice(q * 24, q * 24 + 24)
+        x = own[r, left].astype(F32) + down[r, left].astype(F32) + up_far[r].astype(F32)
+        y = own[r, right].astype(F32) + up[r, right].astype(F32) + down_far[r].astype(F32)
+        for k in range(4):
+            pieces = [
+                v[k * 6 : k * 6 + 6, l * 128 : l * 128 + 128] for v in (x, y) for l in range(12)
+            ]
+            o[q * 4 + k] = jnp.concatenate(pieces, axis=0).astype(BF)
 
 
 def final_kernel(first_ref, in_ref, g0, g1, g2, g3, qkv_ref, out_ref, gain_ref, sum_ref):
@@ -372,24 +395,30 @@
     ret = pl.pallas_call(
         mixed_kernel, out_shape=shape(32, 200, 128), out_specs=HBM,
         scratch_shapes=[pltpu.VMEM((32, 96, 128), BF), DMA((2,))],
-        compiler_params=params(16), cost_estimate=cost(1e9, 5e6), name="mixed",
+        compiler_params=params(14), cost_estimate=cost(1e9, 5e6), name="mixed",
     )(recv, attn, w_out, grads)
     quarters = pl.pallas_call(
         pair_sum_kernel, out_shape=tuple(shape(96, 4 * D) for _ in range(4)),
-        compiler_params=params(16), cost_estimate=cost(1e6, 7e6), name="pair_sum",
+        compiler_params=params(6), cost_estimate=cost(1e6, 7e6), name="pair_sum",
     )(keep, got)
-    q0, q1, q2, q3, ret = lax.optimization_barrier((*quarters, ret))
-    moved = [lax.ppermute(q, AXES, y_shift(s)) for s, q in ((1, q1), (2, q2), (3, q3))]
+    own, up, down, hold, ret = lax.optimization_barrier((*quarters, ret))
+    up = lax.ppermute(up, AXES, y_shift(1))
+    down = lax.ppermute(down, AXES, y_shift(3))
+    up_far, down_far = pl.pallas_call(
+        pass_on_kernel, out_shape=(shape(96, HALF), shape(96, HALF)),
+        compiler_params=params(6), cost_estimate=cost(PASS, 3e6), name="pass_on",
+    )(hold, up, down)
+    up_far = lax.ppermute(up_far, AXES, y_shift(1))
+    down_far = lax.ppermute(down_far, AXES, y_shift(3))
     back = lax.all_to_all(ret, AXES, 0, 0, tiled=True, axis_index_groups=PLANE)
     mine = pl.pallas_call(
         ring_sum_kernel, out_shape=shape(16, 144, 128),
-        scratch_shapes=[pltpu.VMEM((96, 4 * D), F32), pltpu.VMEM((16, 144, 128), F32)],
-        compiler_params=params(16), cost_estimate=cost(RING, 3e6), name="ring_sum",
-    )(q0, *moved)
+        compiler_params=params(6), cost_estimate=cost(RING, 3e6), name="ring_sum",
+    )(own, up, down, up_far, down_far)
     mixed, grad_tokens, gain_part = pl.pallas_call(
         unpack_kernel,
         out_shape=(shape(4, 128, D), shape(4, 128, D), shape(8, 128, dtype=F32)),
-        compiler_params=params(20), cost_estimate=cost(1e9, 4e6), name="unpack",
+        compiler_params=params(14), cost_estimate=cost(1e9, 4e6), name="unpack",
     )(back)
     last = lax.all_to_all(mine, AXES, 0, 0, tiled=True, axis_index_groups=CHIPS)
     gains = [gain_part] + [lax.ppermute(gain_part, AXES, y_shift(s)) for s in range(1, 4)]
@@ -398,7 +427,7 @@
         out_shape=(shape(6, 3 * D, dtype=F32), shape(6, D, dtype=F32), shape(1, 6, dtype=F32)),
         in_specs=[pl.BlockSpec(memory_space=pltpu.SMEM)] + [VM] * 5,
         scratch_shapes=[pltpu.VMEM((144, 128), F32)],
-        compiler_params=params(16), cost_estimate=cost(1e6, 1e6), name="final",
+        compiler_params=params(6), cost_estimate=cost(1e6, 1e6), name="final",
     )(first, last, *gains)
     return mixed, grad_tokens, grad_qkv, grad_out, grad_gain.reshape(6)
 

time: 105 us -> 103 us (0.981)
  waiting for transfers between devices: 49.8 us -> 47.3 us
  local copies, waits for them, and re-layouts: 0.77 us -> 2.66 us
  Pallas kernels: 26.9 us -> 25.4 us
    ppermute x3 -> x4, waiting for transfers between devices: 21.3 us -> 16.6 us  [the longest x1 9.98 us: per_device(): up = lax.ppermute(up, AXES, y_shift(1))]
    unnamed x6 -> x10, local copies, waits for them, and re-layouts: 0.02 us -> 1.91 us
    pallas_call x1 -> x2, Pallas kernels: 2.84 us -> 1.29 us  [the longest x1 1.15 us: per_device(): pl.pallas_call(ring_sum_kernel, out_shape=shape(16, 144, 128), compiler_p...]
    all_to_all x1, waiting for transfers between devices: 0.01 us -> 1.53 us  [per_device(): back = lax.all_to_all(ret, AXES, 0, 0, tiled=True, axis_index_groups=PLANE)]
    ppermute x3 -> x4, starting transfers between devices: 5.84 us -> 6.54 us  [the longest x1 1.66 us: per_device(): down = lax.ppermute(down, AXES, y_shift(3))]
  transfers between devices with their start and end apart: 10 -> 11, of which waited for: 4 -> 5; matrix products, arithmetic and copies ran while one was open for 1% -> 1% of each run, Pallas kernels for 9% -> 8%
where the time goes in v6:
time: 103 us; the launch traced here: 102 us
  waiting for transfers between devices  47.3 us (46%)
  starting transfers between devices  26.2 us (25%)
  Pallas kernels  25.4 us (25%)
  local copies, waits for them, and re-layouts  2.66 us (3%)
    all_to_all x1, waiting for transfers between devices, per_device(): lax.all_to_all(packed, AXES, 0, 0, tiled=True, axis_index_groups=PLANE)  22.4 us
    pallas_call x1, Pallas kernels, per_device(): pl.pallas_call(main_kernel, out_shape=(shape(384, 4 * D), shape(384, 4 *...  12.2 us
    ppermute x1, waiting for transfers between devices, per_device(): up = lax.ppermute(up, AXES, y_shift(1))  9.98 us
    all_to_all x1, starting transfers between devices, per_device(): lax.all_to_all(packed, AXES, 0, 0, tiled=True, axis_index_groups=PLANE)  8.38 us
    all_to_all x1, waiting for transfers between devices, per_device(): last = lax.all_to_all(mine, AXES, 0, 0, tiled=True, axis_index_groups=CHIPS)  6.76 us
    ppermute x1, waiting for transfers between devices, per_device(): up_far = lax.ppermute(up_far, AXES, y_shift(1))  6.64 us
    all_to_all x1, starting transfers between devices, per_device(): back = lax.all_to_all(ret, AXES, 0, 0, tiled=True, axis_index_groups=PLANE)  3.97 us
    all_to_all x1, starting transfers between devices, per_device(): last = lax.all_to_all(mine, AXES, 0, 0, tiled=True, axis_index_groups=CHIPS)  3.63 us
  transfers between devices with their start and end apart: 11, of which 5 were waited for; matrix products, arithmetic and copies ran while one was open for 1% of the time, Pallas kernels for 8%

profile of v6, /device:TPU:0, one launch (start us, length us, event | category | flops | bytes accessed | tf_op | source)
XLA Modules:
  0.0 102.3 jit_solution(20693523501266958)
XLA Ops:
  0.6 2.9 %pack.1 = bf16[32,2,16,768]{3,2,1,0:T(8,128)(2,1)} custom-call(bf16[4,128,768]{2,1,0:T(8,128)(2,1)} %tok_hbm.1, bf16[4,128,768]{2,1,0:T(8,128)(2,1)} %cot_hbm.1, s32[4,128]{1,0:T(4,128)} %les_hbm.1), custom_call_target="tpu_custom_call" | custom-call | flops 1000000000 | bytes 4000000 | tf_op jit(solution)/shard_map/pack/pallas_call | solution.py:370
  3.5 0.0 copy-start.4
  3.6 0.0 copy-start
  3.6 8.4 %all-to-all-start = ((bf16[32,2,16,768]{3,2,1,0:T(8,128)(2,1)}), bf16[32,2,16,768]{3,2,1,0:T(8,128)(2,1)S(1)}, u32[]{:S(2)}, u32[]{:S(2)}) async-start(bf16[32,2,16,768]{3,2,1,0:T(8,128)(2,1)} %pack.1), calls=%async_computation | async-start | bytes 3145728 | tf_op jit(solution)/shard_map/all_to_all | solution.py:378
  12.0 0.0 copy-done.4
  12.0 0.8 constant_dynamic-slice_fusion.feat_ref
  12.7 22.4 %all-to-all-done.recv_hbm.recv_ref = bf16[32,2,16,768]{3,2,1,0:T(8,128)(2,1)S(1)} async-done(((bf16[32,2,16,768]{3,2,1,0:T(8,128)(2,1)}), bf16[32,2,16,768]{3,2,1,0:T(8,128)(2,1)S(1)}, u32[]{:S(2)}, u32[]{:S(2)}) %all-to-all-start) | async-done | bytes 1572896 | tf_op jit(solution)/shard_map/all_to_all | solution.py:378
  35.1 0.0 copy-done
  35.1 0.0 copy-start.1
  35.1 12.2 %main.1 = (bf16[384,3072]{1,0:T(8,128)(2,1)S(1)}, bf16[384,3072]{1,0:T(8,128)(2,1)S(1)}, bf16[512,768]{1,0:T(8,128)(2,1)S(1)}, bf16[512,2304]{1,0:T(8,128)(2,1)S(1)}) custom-call(bf16[32,2,16,768]{3,2,1,0:T(8,128)(2,1)S(1)} %all-to-all-done.recv_hbm.recv_ref, f32[1,768]{1,0:T(1,128)S(1)} %reshape.19.gain_ref, ...), custom_call_target="tpu_custom_call" | custom-call | flops 10000000000 | bytes 15000000 | tf_op jit(solution)/shard_map/main/pallas_call | solution.py:379
  47.3 0.3 collective-permute-start
  47.6 0.0 copy-done.1
  47.6 3.1 %token_grads.1.grad_ref = bf16[32,104,128]{2,1,0:T(8,128)(2,1)S(1)} custom-call(bf16[32,2,16,768]{3,2,1,0:T(8,128)(2,1)S(1)} %all-to-all-done.recv_hbm.recv_ref, f32[1,768]{1,0:T(1,128)S(1)} %reshape.19.gain_ref, bf16[512,2304]{1,0:T(8,128)(2,1)S(1)} %get-tuple-element.33.dqkv_ref, bf16[768,2304]{1,0:T(8,128)(2,1)S(1)} %copy-done.1), custom_call_target="tpu_custom_call" | custom-call | flops 2800000000 | bytes 9000000 | tf_op jit(solution)/shard_map/token_grads/pallas_call | solution.py:391
  50.8 2.0 %mixed.1 = bf16[32,200,128]{2,1,0:T(8,128)(2,1)} custom-call(bf16[32,2,16,768]{3,2,1,0:T(8,128)(2,1)S(1)} %all-to-all-done.recv_hbm.recv_ref, bf16[512,768]{1,0:T(8,128)(2,1)S(1)} %get-tuple-element.32.attn_ref, bf16[768,768]{1,0:T(8,128)(2,1)S(1)} %copy-done, bf16[32,104,128]{2,1,0:T(8,128)(2,1)S(1)} %token_grads.1.grad_ref), custom_call_target="tpu_custom_call" | custom-call | flops 1000000000 | bytes 5000000 | tf_op jit(solution)/shard_map/mixed/pallas_call | solution.py:395
  52.7 0.0 collective-permute-done.b_ref
  52.7 1.5 %pair_sum.1 = (bf16[96,3072]{1,0:T(8,128)(2,1)S(1)}, bf16[96,3072]{1,0:T(8,128)(2,1)}, bf16[96,3072]{1,0:T(8,128)(2,1)}, bf16[96,3072]{1,0:T(8,128)(2,1)S(1)}) custom-call(bf16[384,3072]{1,0:T(8,128)(2,1)S(1)} %get-tuple-element.26.a_ref, bf16[384,3072]{1,0:T(8,128)(2,1)S(1)} %collective-permute-done.b_ref), custom_call_target="tpu_custom_call" | custom-call | flops 1000000 | bytes 7000000 | tf_op jit(solution)/shard_map/pair_sum/pallas_call | solution.py:400
  54.2 0.0 copy-start.2
  54.2 0.8 copy-done.2
  55.0 1.6 %collective-permute-start.1 = (bf16[96,3072]{1,0:T(8,128)(2,1)}, bf16[96,3072]{1,0:T(8,128)(2,1)S(1)}, u32[]{:S(2)}, u32[]{:S(2)}) collective-permute-start(bf16[96,3072]{1,0:T(8,128)(2,1)} %get-tuple-element.38), channel_id=1, source_target_pairs={{0,1},{1,2},{2,3},{3,0},{4,5},{5,6},{6,7},{7,4},{8,9},{9,10},{10,1... | collective-permute-start | bytes 1769480 | tf_op jit(solution)/shard_map/ppermute | solution.py:405
  56.6 1.7 %collective-permute-start.2 = (bf16[96,3072]{1,0:T(8,128)(2,1)}, bf16[96,3072]{1,0:T(8,128)(2,1)S(1)}, u32[]{:S(2)}, u32[]{:S(2)}) collective-permute-start(bf16[96,3072]{1,0:T(8,128)(2,1)} %get-tuple-element.39), channel_id=1, source_target_pairs={{0,3},{1,0},{2,1},{3,2},{4,7},{5,4},{6,5},{7,6},{8,11},{9,8},{10,9... | collective-permute-start | bytes 1769480 | tf_op jit(solution)/shard_map/ppermute | solution.py:406
  58.3 4.0 %all-to-all-start.1 = ((bf16[32,200,128]{2,1,0:T(8,128)(2,1)}), bf16[32,200,128]{2,1,0:T(8,128)(2,1)S(1)}, u32[]{:S(2)}, u32[]{:S(2)}) async-start(bf16[32,200,128]{2,1,0:T(8,128)(2,1)} %mixed.1), calls=%async_computation.1 | async-start | bytes 3276800 | tf_op jit(solution)/shard_map/all_to_all | solution.py:413
  62.3 10.0 %collective-permute-done.1.up = bf16[96,3072]{1,0:T(8,128)(2,1)S(1)} collective-permute-done((bf16[96,3072]{1,0:T(8,128)(2,1)}, bf16[96,3072]{1,0:T(8,128)(2,1)S(1)}, u32[]{:S(2)}, u32[]{:S(2)}) %collective-permute-start.1) | collective-permute-done | bytes 589856 | tf_op jit(solution)/shard_map/ppermute | solution.py:405
  72.2 0.0 collective-permute-done.2.down
  72.3 0.1 pass_on.1
  72.4 1.6 %collective-permute-start.3 = (bf16[96,1536]{1,0:T(8,128)(2,1)S(1)}, bf16[96,1536]{1,0:T(8,128)(2,1)S(1)}, u32[]{:S(2)}, u32[]{:S(2)}) collective-permute-start(bf16[96,1536]{1,0:T(8,128)(2,1)S(1)} %get-tuple-element.41), channel_id=1, source_target_pairs={{0,1},{1,2},{2,3},{3,0},{4,5},{5,6},{6,7},{7,4},{8,9},{9,10},{10,1... | collective-permute-start | bytes 884744 | tf_op jit(solution)/shard_map/ppermute | solution.py:411
  74.0 1.7 %collective-permute-start.4 = (bf16[96,1536]{1,0:T(8,128)(2,1)S(1)}, bf16[96,1536]{1,0:T(8,128)(2,1)S(1)}, u32[]{:S(2)}, u32[]{:S(2)}) collective-permute-start(bf16[96,1536]{1,0:T(8,128)(2,1)S(1)} %get-tuple-element.42), channel_id=1, source_target_pairs={{0,3},{1,0},{2,1},{3,2},{4,7},{5,4},{6,5},{7,6},{8,11},{9,8},{10,9... | collective-permute-start | bytes 884744 | tf_op jit(solution)/shard_map/ppermute | solution.py:412
  75.7 6.6 %collective-permute-done.3.up_far = bf16[96,1536]{1,0:T(8,128)(2,1)S(1)} collective-permute-done((bf16[96,1536]{1,0:T(8,128)(2,1)S(1)}, bf16[96,1536]{1,0:T(8,128)(2,1)S(1)}, u32[]{:S(2)}, u32[]{:S(2)}) %collective-permute-start.3) | collective-permute-done | bytes 294944 | tf_op jit(solution)/shard_map/ppermute | solution.py:411
  82.3 0.0 collective-permute-done.4.down_far
  82.3 0.0 copy-start.3
  82.3 1.1 %copy-done.3 = bf16[96,3072]{1,0:T(8,128)(2,1)S(1)} copy-done((bf16[96,3072]{1,0:T(8,128)(2,1)S(1)}, bf16[96,3072]{1,0:T(8,128)(2,1)}, u32[]{:S(2)}) %copy-start.3) | copy-done | bytes 589848
  83.4 1.1 %ring_sum.1 = bf16[16,144,128]{2,1,0:T(8,128)(2,1)} custom-call(bf16[96,3072]{1,0:T(8,128)(2,1)S(1)} %copy-done.3, bf16[96,3072]{1,0:T(8,128)(2,1)S(1)} %collective-permute-done.1.up, bf16[96,3072]{1,0:T(8,128)(2,1)S(1)} %collective-permute-done.2.down, bf16[96,1536]{1,0:T(8,128)(2,1)S(1)} %collective-permute-done.3.up_far, ...), custom_call_target="tpu_custom_call" | custom-call | flops 10000000000 | bytes 3000000 | tf_op jit(solution)/shard_map/ring_sum/pallas_call | solution.py:414
  84.6 1.5 %all-to-all-done.1.in_ref = bf16[32,200,128]{2,1,0:T(8,128)(2,1)S(1)} async-done(((bf16[32,200,128]{2,1,0:T(8,128)(2,1)}), bf16[32,200,128]{2,1,0:T(8,128)(2,1)S(1)}, u32[]{:S(2)}, u32[]{:S(2)}) %all-to-all-start.1) | async-done | bytes 1638432 | tf_op jit(solution)/shard_map/all_to_all | solution.py:413
  86.1 3.6 %all-to-all-start.2 = ((bf16[16,144,128]{2,1,0:T(8,128)(2,1)}), bf16[16,144,128]{2,1,0:T(8,128)(2,1)S(1)}, u32[]{:S(2)}, u32[]{:S(2)}) async-start(bf16[16,144,128]{2,1,0:T(8,128)(2,1)} %ring_sum.1), calls=%async_computation.2 | async-start | bytes 1179648 | tf_op jit(solution)/shard_map/all_to_all | solution.py:423
  89.7 1.7 %unpack.1 = (bf16[4,128,768]{2,1,0:T(8,128)(2,1)}, bf16[4,128,768]{2,1,0:T(8,128)(2,1)}, f32[8,128]{1,0:T(8,128)S(1)}) custom-call(bf16[32,200,128]{2,1,0:T(8,128)(2,1)S(1)} %all-to-all-done.1.in_ref), custom_call_target="tpu_custom_call" | custom-call | flops 1000000000 | bytes 4000000 | tf_op jit(solution)/shard_map/unpack/pallas_call | solution.py:418
  91.4 1.8 %collective-permute-start.7 = (f32[8,128]{1,0:T(8,128)S(1)}, f32[8,128]{1,0:T(8,128)S(1)}, u32[]{:S(2)}, u32[]{:S(2)}) collective-permute-start(f32[8,128]{1,0:T(8,128)S(1)} %get-tuple-element.43.g0), channel_id=1, source_target_pairs={{0,3},{1,0},{2,1},{3,2},{4,7},{5,4},{6,5},{7,6},{8,11},{9,8},{10,9... | collective-permute-start | bytes 12296 | tf_op jit(solution)/shard_map/ppermute | solution.py:424
  93.2 0.6 collective-permute-start.6
  93.8 1.0 collective-permute-start.5
  94.8 6.8 %all-to-all-done.2.in_ref = bf16[16,144,128]{2,1,0:T(8,128)(2,1)S(1)} async-done(((bf16[16,144,128]{2,1,0:T(8,128)(2,1)}), bf16[16,144,128]{2,1,0:T(8,128)(2,1)S(1)}, u32[]{:S(2)}, u32[]{:S(2)}) %all-to-all-start.2) | async-done | bytes 589856 | tf_op jit(solution)/shard_map/all_to_all | solution.py:423
  101.6 0.0 collective-permute-done.7.g3
  101.6 0.0 collective-permute-done.6.g2
  101.6 0.0 collective-permute-done.5.g1
  101.6 0.7 final.1
  (1 shorter events, 0.0 us)
Async XLA Ops:
  3.5 8.4 %copy-start.4 = (f32[768]{0:T(1024)S(1)}, f32[768]{0:T(1024)}, u32[]{:S(2)}) copy-start(f32[768]{0:T(1024)} %param.12) | copy-start | bytes 9220
  3.6 31.5 %copy-start = (bf16[768,768]{1,0:T(8,128)(2,1)S(1)}, bf16[768,768]{1,0:T(8,128)(2,1)}, u32[]{:S(2)}) copy-start(bf16[768,768]{1,0:T(8,128)(2,1)} %wout_ref.1) | copy-start | bytes 3538948
  3.6 31.5 %all-to-all-start = ((bf16[32,2,16,768]{3,2,1,0:T(8,128)(2,1)}), bf16[32,2,16,768]{3,2,1,0:T(8,128)(2,1)S(1)}, u32[]{:S(2)}, u32[]{:S(2)}) async-start(bf16[32,2,16,768]{3,2,1,0:T(8,128)(2,1)} %pack.1), calls=%async_computation | async-start | bytes 3145728 | tf_op jit(solution)/shard_map/all_to_all | solution.py:378
  35.1 12.5 %copy-start.1 = (bf16[768,2304]{1,0:T(8,128)(2,1)S(1)}, bf16[768,2304]{1,0:T(8,128)(2,1)}, u32[]{:S(2)}) copy-start(bf16[768,2304]{1,0:T(8,128)(2,1)} %wqkv_ref.1) | copy-start | bytes 10616836
  47.3 5.4 %collective-permute-start = (bf16[384,3072]{1,0:T(8,128)(2,1)S(1)}, bf16[384,3072]{1,0:T(8,128)(2,1)S(1)}, u32[]{:S(2)}, u32[]{:S(2)}) collective-permute-start(bf16[384,3072]{1,0:T(8,128)(2,1)S(1)} %get-tuple-element.27), channel_id=1, source_target_pairs={{0,8},{1,9},{2,10},{3,11},{4,12},{5,13},{6,14},{7,15},{8,0},{9,1},... | collective-permute-start | bytes 7077896 | tf_op jit(solution)/shard_map/ppermute | solution.py:390
  54.2 0.8 copy-start.2
  55.0 17.2 %collective-permute-start.1 = (bf16[96,3072]{1,0:T(8,128)(2,1)}, bf16[96,3072]{1,0:T(8,128)(2,1)S(1)}, u32[]{:S(2)}, u32[]{:S(2)}) collective-permute-start(bf16[96,3072]{1,0:T(8,128)(2,1)} %get-tuple-element.38), channel_id=1, source_target_pairs={{0,1},{1,2},{2,3},{3,0},{4,5},{5,6},{6,7},{7,4},{8,9},{9,10},{10,1... | collective-permute-start | bytes 1769480 | tf_op jit(solution)/shard_map/ppermute | solution.py:405
  56.6 15.6 %collective-permute-start.2 = (bf16[96,3072]{1,0:T(8,128)(2,1)}, bf16[96,3072]{1,0:T(8,128)(2,1)S(1)}, u32[]{:S(2)}, u32[]{:S(2)}) collective-permute-start(bf16[96,3072]{1,0:T(8,128)(2,1)} %get-tuple-element.39), channel_id=1, source_target_pairs={{0,3},{1,0},{2,1},{3,2},{4,7},{5,4},{6,5},{7,6},{8,11},{9,8},{10,9... | collective-permute-start | bytes 1769480 | tf_op jit(solution)/shard_map/ppermute | solution.py:406
  58.3 27.8 %all-to-all-start.1 = ((bf16[32,200,128]{2,1,0:T(8,128)(2,1)}), bf16[32,200,128]{2,1,0:T(8,128)(2,1)S(1)}, u32[]{:S(2)}, u32[]{:S(2)}) async-start(bf16[32,200,128]{2,1,0:T(8,128)(2,1)} %mixed.1), calls=%async_computation.1 | async-start | bytes 3276800 | tf_op jit(solution)/shard_map/all_to_all | solution.py:413
  72.4 9.9 %collective-permute-start.3 = (bf16[96,1536]{1,0:T(8,128)(2,1)S(1)}, bf16[96,1536]{1,0:T(8,128)(2,1)S(1)}, u32[]{:S(2)}, u32[]{:S(2)}) collective-permute-start(bf16[96,1536]{1,0:T(8,128)(2,1)S(1)} %get-tuple-element.41), channel_id=1, source_target_pairs={{0,1},{1,2},{2,3},{3,0},{4,5},{5,6},{6,7},{7,4},{8,9},{9,10},{10,1... | collective-permute-start | bytes 884744 | tf_op jit(solution)/shard_map/ppermute | solution.py:411
  74.0 8.3 %collective-permute-start.4 = (bf16[96,1536]{1,0:T(8,128)(2,1)S(1)}, bf16[96,1536]{1,0:T(8,128)(2,1)S(1)}, u32[]{:S(2)}, u32[]{:S(2)}) collective-permute-start(bf16[96,1536]{1,0:T(8,128)(2,1)S(1)} %get-tuple-element.42), channel_id=1, source_target_pairs={{0,3},{1,0},{2,1},{3,2},{4,7},{5,4},{6,5},{7,6},{8,11},{9,8},{10,9... | collective-permute-start | bytes 884744 | tf_op jit(solution)/shard_map/ppermute | solution.py:412
  82.3 1.1 %copy-start.3 = (bf16[96,3072]{1,0:T(8,128)(2,1)S(1)}, bf16[96,3072]{1,0:T(8,128)(2,1)}, u32[]{:S(2)}) copy-start(bf16[96,3072]{1,0:T(8,128)(2,1)} %copy-done.2) | copy-start | bytes 1769476
  86.1 15.5 %all-to-all-start.2 = ((bf16[16,144,128]{2,1,0:T(8,128)(2,1)}), bf16[16,144,128]{2,1,0:T(8,128)(2,1)S(1)}, u32[]{:S(2)}, u32[]{:S(2)}) async-start(bf16[16,144,128]{2,1,0:T(8,128)(2,1)} %ring_sum.1), calls=%async_computation.2 | async-start | bytes 1179648 | tf_op jit(solution)/shard_map/all_to_all | solution.py:423
  91.4 10.2 %collective-permute-start.7 = (f32[8,128]{1,0:T(8,128)S(1)}, f32[8,128]{1,0:T(8,128)S(1)}, u32[]{:S(2)}, u32[]{:S(2)}) collective-permute-start(f32[8,128]{1,0:T(8,128)S(1)} %get-tuple-element.43.g0), channel_id=1, source_target_pairs={{0,3},{1,0},{2,1},{3,2},{4,7},{5,4},{6,5},{7,6},{8,11},{9,8},{10,9... | collective-permute-start | bytes 12296 | tf_op jit(solution)/shard_map/ppermute | solution.py:424
  93.2 8.4 %collective-permute-start.6 = (f32[8,128]{1,0:T(8,128)S(1)}, f32[8,128]{1,0:T(8,128)S(1)}, u32[]{:S(2)}, u32[]{:S(2)}) collective-permute-start(f32[8,128]{1,0:T(8,128)S(1)} %get-tuple-element.43.g0), channel_id=1, source_target_pairs={{0,2},{1,3},{2,0},{3,1},{4,6},{5,7},{6,4},{7,5},{8,10},{9,11},{10,... | collective-permute-start | bytes 12296 | tf_op jit(solution)/shard_map/ppermute | solution.py:424
  93.8 7.7 %collective-permute-start.5 = (f32[8,128]{1,0:T(8,128)S(1)}, f32[8,128]{1,0:T(8,128)S(1)}, u32[]{:S(2)}, u32[]{:S(2)}) collective-permute-start(f32[8,128]{1,0:T(8,128)S(1)} %get-tuple-element.43.g0), channel_id=1, source_target_pairs={{0,1},{1,2},{2,3},{3,0},{4,5},{5,6},{6,7},{7,4},{8,9},{9,10},{10,1... | collective-permute-start | bytes 12296 | tf_op jit(solution)/shard_map/ppermute | solution.py:424

commit v7 on v6

--- a/solution.py
+++ b/solution.py
@@ -19,7 +19,7 @@
 PASS = 1e6
 RING = 1e10
 MAIN_MB = 42
-TOKEN_MB = 14
+TOKEN_MB = 20
 
 
 def place(xlo, z, c, xhi, y):
@@ -169,27 +169,26 @@
 
 
 def main_kernel(
-    recv_hbm, gain_ref, feat_ref, wqkv_hbm, wout_hbm,
+    recv_ref, gain_ref, feat_ref, wqkv_hbm, wout_hbm,
     keep_ref, send_ref, attn_ref, dqkv_ref,
-    recv_ref, wqkv_ref, wout_ref, qkv_ref, ga_ref, norm_ref, gy_ref, lhs_ref, sems,
+    wqkv_ref, wout_ref, qkv_ref, ga_ref, norm_ref, gy_ref, lhs_ref, sems,
 ):
     scale = float(HEAD_DIM) ** (-0.5)
     loads = [
         pltpu.make_async_copy(src, dst, sems.at[n])
         for n, (src, dst) in enumerate(
-            ((recv_hbm, recv_ref), (wout_hbm, wout_ref), (wqkv_hbm, wqkv_ref))
+            ((wout_hbm, wout_ref), (wqkv_hbm, wqkv_ref))
         )
     ]
     for c in loads:
         c.start()
-    loads[0].wait()
     _, _, unit = normalise(recv_ref[:, 0].reshape(TOK, D))
     normed = (unit * gain_ref[...]).astype(BF)
     norm_ref[...] = by_position(normed)
     gy_ref[...] = by_position(recv_ref[:, 1].reshape(TOK, D))
+    loads[0].wait()
+    ga_ref[...] = dot(gy_ref[...], wout_ref[...], 1, 1).astype(BF)
     loads[1].wait()
-    ga_ref[...] = dot(gy_ref[...], wout_ref[...], 1, 1).astype(BF)
-    loads[2].wait()
 
     def project(n, _):
         cols = pl.ds(pl.multiple_of(n * 768, 768), 768)
@@ -249,17 +248,19 @@
     send_ref[:, 3 * D :] = g[384:]
 
 
-def token_kernel(recv_ref, gain_ref, dqkv_ref, wqkv_ref, ret_ref):
+def token_kernel(
+    recv_ref, gain_ref, attn_ref, dqkv_ref, wqkv_ref, wout_ref, ret_hbm, ret_ref, sems
+):
     gn = dot(dqkv_ref[...], wqkv_ref[...], 1, 1).astype(BF)
     gn = by_source(gn).astype(F32)
-    _, inv_rms, unit = normalise(recv_ref[:, 0].reshape(TOK, D))
+    xf, inv_rms, unit = normalise(recv_ref[:, 0].reshape(TOK, D))
     g = jnp.sum(gn * unit, axis=0, keepdims=True)
     dunit = gn * gain_ref[...]
     back = inv_rms * (dunit - unit * jnp.mean(dunit * unit, axis=-1, keepdims=True))
     gy = recv_ref[:, 1].reshape(TOK, D).astype(F32)
     grad = (gy + back).astype(BF)
     for l in range(6):
-        ret_ref[:, l * 16 : l * 16 + 16] = grad[:, l * 128 : l * 128 + 128].reshape(32, 16, 128)
+        ret_ref[:, 96 + l * 16 : 112 + l * 16] = grad[:, l * 128 : l * 128 + 128].reshape(32, 16, 128)
     k = lax.broadcasted_iota(jnp.int32, (32, 8, 128), 0) * 24
     lane = lax.broadcasted_iota(jnp.int32, (32, 8, 128), 2)
     own = jnp.zeros((32, 8, 128), F32)
@@ -272,18 +273,15 @@
     row = lax.broadcasted_iota(jnp.int32, (32, 8, 128), 1)
     low = own - high - mid
     terms = jnp.where(row == 0, high, jnp.where(row == 1, mid, jnp.where(row == 2, low, 0.0)))
-    ret_ref[:, 96:] = terms.astype(BF)
-
-
-def mixed_kernel(recv_ref, attn_ref, wout_ref, grad_ref, ret_hbm, ret_ref, sems):
-    store_g = pltpu.make_async_copy(grad_ref, ret_hbm.at[:, 96:], sems.at[0])
+    ret_ref[:, 192:] = terms.astype(BF)
+    store_g = pltpu.make_async_copy(ret_ref.at[:, 96:], ret_hbm.at[:, 96:], sems.at[0])
     store_g.start()
     attn = by_source(attn_ref[...])
     proj = dot(attn, wout_ref[...], 1, 0).astype(BF)
-    mixed = (recv_ref[:, 0].reshape(TOK, D).astype(F32) + proj.astype(F32)).astype(BF)
+    mixed = (xf + proj.astype(F32)).astype(BF)
     for l in range(6):
         ret_ref[:, l * 16 : l * 16 + 16] = mixed[:, l * 128 : l * 128 + 128].reshape(32, 16, 128)
-    store_m = pltpu.make_async_copy(ret_ref, ret_hbm.at[:, :96], sems.at[1])
+    store_m = pltpu.make_async_copy(ret_ref.at[:, :96], ret_hbm.at[:, :96], sems.at[1])
     store_m.start()
     store_g.wait()
     store_m.wait()
@@ -308,18 +306,19 @@
     hold[:, right] = block(3, right)
 
 
-def pass_on_kernel(hold, up, down, up_out, down_out):
+def pass_on_kernel(hold, up, down, own, up_out, down_out, sum_out):
     left, right = slice(0, HALF), slice(HALF, 2 * HALF)
     up_out[...] = (hold[:, left].astype(F32) + up[:, left].astype(F32)).astype(BF)
     down_out[...] = (hold[:, right].astype(F32) + down[:, right].astype(F32)).astype(BF)
-
-
-def ring_sum_kernel(own, up, down, up_far, down_far, o):
-    left, right = slice(0, HALF), slice(HALF, 2 * HALF)
+    sum_out[:, left] = own[:, left].astype(F32) + down[:, left].astype(F32)
+    sum_out[:, right] = own[:, right].astype(F32) + up[:, right].astype(F32)
+
+
+def ring_sum_kernel(near, up_far, down_far, o):
     for q in range(4):
         r = slice(q * 24, q * 24 + 24)
-        x = own[r, left].astype(F32) + down[r, left].astype(F32) + up_far[r].astype(F32)
-        y = own[r, right].astype(F32) + up[r, right].astype(F32) + down_far[r].astype(F32)
+        x = near[r, :HALF] + up_far[r].astype(F32)
+        y = near[r, HALF:] + down_far[r].astype(F32)
         for k in range(4):
             pieces = [
                 v[k * 6 : k * 6 + 6, l * 128 : l * 128 + 128] for v in (x, y) for l in range(12)
@@ -345,7 +344,7 @@
 
 
 def params(mb):
-    return pltpu.CompilerParams(vmem_limit_bytes=mb * MB)
+    return pltpu.CompilerParams(vmem_limit_bytes=int(mb * MB))
 
 
 def cost(flops, nbytes):
@@ -379,24 +378,20 @@
     keep, send, attn, dqkv = pl.pallas_call(
         main_kernel,
         out_shape=(shape(384, 4 * D), shape(384, 4 * D), shape(TOK, D), shape(TOK, 3 * D)),
-        in_specs=[HBM, VM, VM, HBM, HBM],
+        in_specs=[VM, VM, VM, HBM, HBM],
         scratch_shapes=[
-            pltpu.VMEM((32, 2, 16, D), BF), pltpu.VMEM((D, 3 * D), BF), pltpu.VMEM((D, D), BF),
+            pltpu.VMEM((D, 3 * D), BF), pltpu.VMEM((D, D), BF),
             pltpu.VMEM((TOK, 3 * D), BF), pltpu.VMEM((TOK, D), BF), pltpu.VMEM((TOK, D), BF),
-            pltpu.VMEM((TOK, D), BF), pltpu.VMEM((D, TOK), BF), DMA((3,)),
+            pltpu.VMEM((TOK, D), BF), pltpu.VMEM((D, TOK), BF), DMA((2,)),
         ],
         compiler_params=params(MAIN_MB), cost_estimate=cost(1e10, 1.5e7), name="main",
     )(recv, gain, feat, w_qkv, w_out)
     got = lax.ppermute(send, AXES, CORE_SWAP)
-    grads = pl.pallas_call(
-        token_kernel, out_shape=shape(32, 104, 128),
-        compiler_params=params(TOKEN_MB), cost_estimate=cost(2.8e9, 9e6), name="token_grads",
-    )(recv, gain, dqkv, w_qkv)
     ret = pl.pallas_call(
-        mixed_kernel, out_shape=shape(32, 200, 128), out_specs=HBM,
-        scratch_shapes=[pltpu.VMEM((32, 96, 128), BF), DMA((2,))],
-        compiler_params=params(14), cost_estimate=cost(1e9, 5e6), name="mixed",
-    )(recv, attn, w_out, grads)
+        token_kernel, out_shape=shape(32, 200, 128), out_specs=HBM,
+        scratch_shapes=[pltpu.VMEM((32, 200, 128), BF), DMA((2,))],
+        compiler_params=params(TOKEN_MB), cost_estimate=cost(3.5e9, 1.2e7), name="token_grads",
+    )(recv, gain, attn, dqkv, w_qkv, w_out)
     quarters = pl.pallas_call(
         pair_sum_kernel, out_shape=tuple(shape(96, 4 * D) for _ in range(4)),
         compiler_params=params(6), cost_estimate=cost(1e6, 7e6), name="pair_sum",
@@ -404,17 +399,18 @@
     own, up, down, hold, ret = lax.optimization_barrier((*quarters, ret))
     up = lax.ppermute(up, AXES, y_shift(1))
     down = lax.ppermute(down, AXES, y_shift(3))
-    up_far, down_far = pl.pallas_call(
-        pass_on_kernel, out_shape=(shape(96, HALF), shape(96, HALF)),
+    up_far, down_far, near = pl.pallas_call(
+        pass_on_kernel,
+        out_shape=(shape(96, HALF), shape(96, HALF), shape(96, 4 * D, dtype=F32)),
         compiler_params=params(6), cost_estimate=cost(PASS, 3e6), name="pass_on",
-    )(hold, up, down)
+    )(hold, up, down, own)
     up_far = lax.ppermute(up_far, AXES, y_shift(1))
     down_far = lax.ppermute(down_far, AXES, y_shift(3))
     back = lax.all_to_all(ret, AXES, 0, 0, tiled=True, axis_index_groups=PLANE)
     mine = pl.pallas_call(
         ring_sum_kernel, out_shape=shape(16, 144, 128),
         compiler_params=params(6), cost_estimate=cost(RING, 3e6), name="ring_sum",
-    )(own, up, down, up_far, down_far)
+    )(near, up_far, down_far)
     mixed, grad_tokens, gain_part = pl.pallas_call(
         unpack_kernel,
         out_shape=(shape(4, 128, D), shape(4, 128, D), shape(8, 128, dtype=F32)),

time: 103 us -> 103 us (level)
  Pallas kernels: 25.4 us -> 27.5 us
  local copies, waits for them, and re-layouts: 2.66 us -> 0.77 us
    unnamed x10 -> x6, local copies, waits for them, and re-layouts: 1.91 us -> 0.02 us
    pallas_call x1, Pallas kernels: 0.14 us -> 1.31 us  [per_device(): pl.pallas_call(pass_on_kernel, out_shape=(shape(96, HALF), shape(96, HALF...]
    pallas_call x2 -> x1, Pallas kernels: 5.1 us -> 5.62 us  [per_device(): pl.pallas_call(token_kernel, out_shape=shape(32, 200, 128), out_specs=HBM...]
  transfers between devices with their start and end apart: 11 -> 11, of which waited for: 5 -> 6; matrix products, arithmetic and copies ran while one was open for 1% -> 1% of each run, Pallas kernels for 8% -> 9%
where the time goes in v7:
time: 103 us
  waiting for transfers between devices  47.3 us (46%)
  Pallas kernels  27.5 us (27%)
  starting transfers between devices  26.2 us (25%)
    all_to_all x1, waiting for transfers between devices, per_device(): lax.all_to_all(packed, AXES, 0, 0, tiled=True, axis_index_groups=PLANE)  22.4 us
    pallas_call x1, Pallas kernels, per_device(): pl.pallas_call(main_kernel, out_shape=(shape(384, 4 * D), shape(384, 4 *...  12.8 us
    ppermute x1, waiting for transfers between devices, per_device(): up = lax.ppermute(up, AXES, y_shift(1))  9.98 us
    all_to_all x1, starting transfers between devices, per_device(): lax.all_to_all(packed, AXES, 0, 0, tiled=True, axis_index_groups=PLANE)  8.38 us
    all_to_all x1, waiting for transfers between devices, per_device(): last = lax.all_to_all(mine, AXES, 0, 0, tiled=True, axis_index_groups=CHIPS)  6.75 us
    ppermute x1, waiting for transfers between devices, per_device(): up_far = lax.ppermute(up_far, AXES, y_shift(1))  6.54 us
    pallas_call x1, Pallas kernels, per_device(): pl.pallas_call(token_kernel, out_shape=shape(32, 200, 128), out_specs=HBM...  5.62 us
    all_to_all x1, starting transfers between devices, per_device(): back = lax.all_to_all(ret, AXES, 0, 0, tiled=True, axis_index_groups=PLANE)  3.98 us
  transfers between devices with their start and end apart: 11, of which 6 were waited for; matrix products, arithmetic and copies ran while one was open for 1% of the time, Pallas kernels for 9%

profile of v7, /device:TPU:0, one launch (start us, length us, event | category | flops | bytes accessed | tf_op | source)
XLA Modules:
  0.0 102.5 jit_solution(5567320439351504136)
XLA Ops:
  0.6 2.9 %pack.1 = bf16[32,2,16,768]{3,2,1,0:T(8,128)(2,1)} custom-call(bf16[4,128,768]{2,1,0:T(8,128)(2,1)} %tok_hbm.1, bf16[4,128,768]{2,1,0:T(8,128)(2,1)} %cot_hbm.1, s32[4,128]{1,0:T(4,128)} %les_hbm.1), custom_call_target="tpu_custom_call" | custom-call | flops 1000000000 | bytes 4000000 | tf_op jit(solution)/shard_map/pack/pallas_call | solution.py:369
  3.5 0.0 copy-start.2
  3.5 0.0 copy-start.1
  3.5 8.4 %all-to-all-start = ((bf16[32,2,16,768]{3,2,1,0:T(8,128)(2,1)}), bf16[32,2,16,768]{3,2,1,0:T(8,128)(2,1)S(1)}, u32[]{:S(2)}, u32[]{:S(2)}) async-start(bf16[32,2,16,768]{3,2,1,0:T(8,128)(2,1)} %pack.1), calls=%async_computation | async-start | bytes 3145728 | tf_op jit(solution)/shard_map/all_to_all | solution.py:377
  11.9 0.0 copy-done.2
  12.0 0.8 constant_dynamic-slice_fusion.feat_ref
  12.7 22.4 %all-to-all-done.recv_ref = bf16[32,2,16,768]{3,2,1,0:T(8,128)(2,1)S(1)} async-done(((bf16[32,2,16,768]{3,2,1,0:T(8,128)(2,1)}), bf16[32,2,16,768]{3,2,1,0:T(8,128)(2,1)S(1)}, u32[]{:S(2)}, u32[]{:S(2)}) %all-to-all-start) | async-done | bytes 1572896 | tf_op jit(solution)/shard_map/all_to_all | solution.py:377
  35.1 0.0 copy-done.1
  35.1 0.0 copy-start
  35.1 12.8 %main.1 = (bf16[384,3072]{1,0:T(8,128)(2,1)S(1)}, bf16[384,3072]{1,0:T(8,128)(2,1)S(1)}, bf16[512,768]{1,0:T(8,128)(2,1)S(1)}, bf16[512,2304]{1,0:T(8,128)(2,1)S(1)}) custom-call(bf16[32,2,16,768]{3,2,1,0:T(8,128)(2,1)S(1)} %all-to-all-done.recv_ref, f32[1,768]{1,0:T(1,128)S(1)} %reshape.19.gain_ref, s32[1,768]{1,0:T(1,128)S(1)} %constant_dynamic-slice_fusion.feat_ref, ...), custom_call_target="tpu_custom_call" | custom-call | flops 10000000000 | bytes 15000000 | tf_op jit(solution)/shard_map/main/pallas_call | solution.py:378
  47.8 0.3 collective-permute-start
  48.1 0.0 copy-done
  48.1 5.6 %token_grads.1 = bf16[32,200,128]{2,1,0:T(8,128)(2,1)} custom-call(bf16[32,2,16,768]{3,2,1,0:T(8,128)(2,1)S(1)} %all-to-all-done.recv_ref, f32[1,768]{1,0:T(1,128)S(1)} %reshape.19.gain_ref, bf16[512,768]{1,0:T(8,128)(2,1)S(1)} %get-tuple-element.33.attn_ref, bf16[512,2304]{1,0:T(8,128)(2,1)S(1)} %get-tuple-element.34.dqkv_ref, ...), custom_call_target="tpu_custom_call" | custom-call | flops 3500000000 | bytes 12000000 | tf_op jit(solution)/shard_map/token_grads/pallas_call | solution.py:390
  53.8 0.0 collective-permute-done.b_ref
  53.8 1.5 %pair_sum.1 = (bf16[96,3072]{1,0:T(8,128)(2,1)S(1)}, bf16[96,3072]{1,0:T(8,128)(2,1)}, bf16[96,3072]{1,0:T(8,128)(2,1)}, bf16[96,3072]{1,0:T(8,128)(2,1)S(1)}) custom-call(bf16[384,3072]{1,0:T(8,128)(2,1)S(1)} %get-tuple-element.27.a_ref, bf16[384,3072]{1,0:T(8,128)(2,1)S(1)} %collective-permute-done.b_ref), custom_call_target="tpu_custom_call" | custom-call | flops 1000000 | bytes 7000000 | tf_op jit(solution)/shard_map/pair_sum/pallas_call | solution.py:395
  55.2 1.6 %collective-permute-start.1 = (bf16[96,3072]{1,0:T(8,128)(2,1)}, bf16[96,3072]{1,0:T(8,128)(2,1)S(1)}, u32[]{:S(2)}, u32[]{:S(2)}) collective-permute-start(bf16[96,3072]{1,0:T(8,128)(2,1)} %get-tuple-element.39), channel_id=1, source_target_pairs={{0,1},{1,2},{2,3},{3,0},{4,5},{5,6},{6,7},{7,4},{8,9},{9,10},{10,1... | collective-permute-start | bytes 1769480 | tf_op jit(solution)/shard_map/ppermute | solution.py:400
  56.8 1.7 %collective-permute-start.2 = (bf16[96,3072]{1,0:T(8,128)(2,1)}, bf16[96,3072]{1,0:T(8,128)(2,1)}, u32[]{:S(2)}, u32[]{:S(2)}) collective-permute-start(bf16[96,3072]{1,0:T(8,128)(2,1)} %get-tuple-element.40), channel_id=1, source_target_pairs={{0,3},{1,0},{2,1},{3,2},{4,7},{5,4},{6,5},{7,6},{8,11},{9,8},{10,9... | collective-permute-start | bytes 1769480 | tf_op jit(solution)/shard_map/ppermute | solution.py:401
  58.5 4.0 %all-to-all-start.1 = ((bf16[32,200,128]{2,1,0:T(8,128)(2,1)}), bf16[32,200,128]{2,1,0:T(8,128)(2,1)S(1)}, u32[]{:S(2)}, u32[]{:S(2)}) async-start(bf16[32,200,128]{2,1,0:T(8,128)(2,1)} %token_grads.1), calls=%async_computation.1 | async-start | bytes 3276800 | tf_op jit(solution)/shard_map/all_to_all | solution.py:409
  62.5 10.0 %collective-permute-done.1.up = bf16[96,3072]{1,0:T(8,128)(2,1)S(1)} collective-permute-done((bf16[96,3072]{1,0:T(8,128)(2,1)}, bf16[96,3072]{1,0:T(8,128)(2,1)S(1)}, u32[]{:S(2)}, u32[]{:S(2)}) %collective-permute-start.1) | collective-permute-done | bytes 589856 | tf_op jit(solution)/shard_map/ppermute | solution.py:400
  72.4 0.1 collective-permute-done.2.down
  72.6 1.3 %pass_on.1 = (bf16[96,1536]{1,0:T(8,128)(2,1)S(1)}, bf16[96,1536]{1,0:T(8,128)(2,1)S(1)}, f32[96,3072]{1,0:T(8,128)S(1)}) custom-call(bf16[96,3072]{1,0:T(8,128)(2,1)S(1)} %get-tuple-element.38.hold, bf16[96,3072]{1,0:T(8,128)(2,1)S(1)} %collective-permute-done.1.up, bf16[96,3072]{1,0:T(8,128)(2,1)} %collective-permute-done.2.down, ...), custom_call_target="tpu_custom_call" | custom-call | flops 1000000 | bytes 3000000 | tf_op jit(solution)/shard_map/pass_on/pallas_call | solution.py:402
  73.9 1.6 %collective-permute-start.3 = (bf16[96,1536]{1,0:T(8,128)(2,1)S(1)}, bf16[96,1536]{1,0:T(8,128)(2,1)S(1)}, u32[]{:S(2)}, u32[]{:S(2)}) collective-permute-start(bf16[96,1536]{1,0:T(8,128)(2,1)S(1)} %get-tuple-element.43), channel_id=1, source_target_pairs={{0,1},{1,2},{2,3},{3,0},{4,5},{5,6},{6,7},{7,4},{8,9},{9,10},{10,1... | collective-permute-start | bytes 884744 | tf_op jit(solution)/shard_map/ppermute | solution.py:407
  75.5 1.7 %collective-permute-start.4 = (bf16[96,1536]{1,0:T(8,128)(2,1)S(1)}, bf16[96,1536]{1,0:T(8,128)(2,1)S(1)}, u32[]{:S(2)}, u32[]{:S(2)}) collective-permute-start(bf16[96,1536]{1,0:T(8,128)(2,1)S(1)} %get-tuple-element.44), channel_id=1, source_target_pairs={{0,3},{1,0},{2,1},{3,2},{4,7},{5,4},{6,5},{7,6},{8,11},{9,8},{10,9... | collective-permute-start | bytes 884744 | tf_op jit(solution)/shard_map/ppermute | solution.py:408
  77.2 6.5 %collective-permute-done.3.up_far = bf16[96,1536]{1,0:T(8,128)(2,1)S(1)} collective-permute-done((bf16[96,1536]{1,0:T(8,128)(2,1)S(1)}, bf16[96,1536]{1,0:T(8,128)(2,1)S(1)}, u32[]{:S(2)}, u32[]{:S(2)}) %collective-permute-start.3) | collective-permute-done | bytes 294944 | tf_op jit(solution)/shard_map/ppermute | solution.py:407
  83.7 0.0 collective-permute-done.4.down_far
  83.7 1.0 %ring_sum.1 = bf16[16,144,128]{2,1,0:T(8,128)(2,1)} custom-call(f32[96,3072]{1,0:T(8,128)S(1)} %get-tuple-element.42.near, bf16[96,1536]{1,0:T(8,128)(2,1)S(1)} %collective-permute-done.3.up_far, bf16[96,1536]{1,0:T(8,128)(2,1)S(1)} %collective-permute-done.4.down_far), custom_call_target="tpu_custom_call" | custom-call | flops 10000000000 | bytes 3000000 | tf_op jit(solution)/shard_map/ring_sum/pallas_call | solution.py:410
  84.8 1.5 %all-to-all-done.1.in_ref = bf16[32,200,128]{2,1,0:T(8,128)(2,1)S(1)} async-done(((bf16[32,200,128]{2,1,0:T(8,128)(2,1)}), bf16[32,200,128]{2,1,0:T(8,128)(2,1)S(1)}, u32[]{:S(2)}, u32[]{:S(2)}) %all-to-all-start.1) | async-done | bytes 1638432 | tf_op jit(solution)/shard_map/all_to_all | solution.py:409
  86.3 3.6 %all-to-all-start.2 = ((bf16[16,144,128]{2,1,0:T(8,128)(2,1)}), bf16[16,144,128]{2,1,0:T(8,128)(2,1)S(1)}, u32[]{:S(2)}, u32[]{:S(2)}) async-start(bf16[16,144,128]{2,1,0:T(8,128)(2,1)} %ring_sum.1), calls=%async_computation.2 | async-start | bytes 1179648 | tf_op jit(solution)/shard_map/all_to_all | solution.py:419
  89.9 1.7 %unpack.1 = (bf16[4,128,768]{2,1,0:T(8,128)(2,1)}, bf16[4,128,768]{2,1,0:T(8,128)(2,1)}, f32[8,128]{1,0:T(8,128)S(1)}) custom-call(bf16[32,200,128]{2,1,0:T(8,128)(2,1)S(1)} %all-to-all-done.1.in_ref), custom_call_target="tpu_custom_call" | custom-call | flops 1000000000 | bytes 4000000 | tf_op jit(solution)/shard_map/unpack/pallas_call | solution.py:414
  91.6 1.8 %collective-permute-start.7 = (f32[8,128]{1,0:T(8,128)S(1)}, f32[8,128]{1,0:T(8,128)S(1)}, u32[]{:S(2)}, u32[]{:S(2)}) collective-permute-start(f32[8,128]{1,0:T(8,128)S(1)} %get-tuple-element.45.g0), channel_id=1, source_target_pairs={{0,3},{1,0},{2,1},{3,2},{4,7},{5,4},{6,5},{7,6},{8,11},{9,8},{10,9... | collective-permute-start | bytes 12296 | tf_op jit(solution)/shard_map/ppermute | solution.py:420
  93.4 0.6 collective-permute-start.6
  94.0 1.0 collective-permute-start.5
  95.0 6.7 %all-to-all-done.2.in_ref = bf16[16,144,128]{2,1,0:T(8,128)(2,1)S(1)} async-done(((bf16[16,144,128]{2,1,0:T(8,128)(2,1)}), bf16[16,144,128]{2,1,0:T(8,128)(2,1)S(1)}, u32[]{:S(2)}, u32[]{:S(2)}) %all-to-all-start.2) | async-done | bytes 589856 | tf_op jit(solution)/shard_map/all_to_all | solution.py:419
  101.8 0.0 collective-permute-done.7.g3
  101.8 0.0 collective-permute-done.6.g2
  101.8 0.0 collective-permute-done.5.g1
  101.8 0.7 final.1
  (1 shorter events, 0.0 us)
Async XLA Ops:
  3.5 8.4 %copy-start.2 = (f32[768]{0:T(1024)S(1)}, f32[768]{0:T(1024)}, u32[]{:S(2)}) copy-start(f32[768]{0:T(1024)} %param.12) | copy-start | bytes 9220
  3.5 31.5 %copy-start.1 = (bf16[768,768]{1,0:T(8,128)(2,1)S(1)}, bf16[768,768]{1,0:T(8,128)(2,1)}, u32[]{:S(2)}) copy-start(bf16[768,768]{1,0:T(8,128)(2,1)} %wout_ref.1) | copy-start | bytes 3538948
  3.5 31.5 %all-to-all-start = ((bf16[32,2,16,768]{3,2,1,0:T(8,128)(2,1)}), bf16[32,2,16,768]{3,2,1,0:T(8,128)(2,1)S(1)}, u32[]{:S(2)}, u32[]{:S(2)}) async-start(bf16[32,2,16,768]{3,2,1,0:T(8,128)(2,1)} %pack.1), calls=%async_computation | async-start | bytes 3145728 | tf_op jit(solution)/shard_map/all_to_all | solution.py:377
  35.1 13.1 %copy-start = (bf16[768,2304]{1,0:T(8,128)(2,1)S(1)}, bf16[768,2304]{1,0:T(8,128)(2,1)}, u32[]{:S(2)}) copy-start(bf16[768,2304]{1,0:T(8,128)(2,1)} %wqkv_ref.1) | copy-start | bytes 10616836
  47.8 5.9 %collective-permute-start = (bf16[384,3072]{1,0:T(8,128)(2,1)S(1)}, bf16[384,3072]{1,0:T(8,128)(2,1)S(1)}, u32[]{:S(2)}, u32[]{:S(2)}) collective-permute-start(bf16[384,3072]{1,0:T(8,128)(2,1)S(1)} %get-tuple-element.28), channel_id=1, source_target_pairs={{0,8},{1,9},{2,10},{3,11},{4,12},{5,13},{6,14},{7,15},{8,0},{9,1},... | collective-permute-start | bytes 7077896 | tf_op jit(solution)/shard_map/ppermute | solution.py:389
  55.2 17.2 %collective-permute-start.1 = (bf16[96,3072]{1,0:T(8,128)(2,1)}, bf16[96,3072]{1,0:T(8,128)(2,1)S(1)}, u32[]{:S(2)}, u32[]{:S(2)}) collective-permute-start(bf16[96,3072]{1,0:T(8,128)(2,1)} %get-tuple-element.39), channel_id=1, source_target_pairs={{0,1},{1,2},{2,3},{3,0},{4,5},{5,6},{6,7},{7,4},{8,9},{9,10},{10,1... | collective-permute-start | bytes 1769480 | tf_op jit(solution)/shard_map/ppermute | solution.py:400
  56.8 15.8 %collective-permute-start.2 = (bf16[96,3072]{1,0:T(8,128)(2,1)}, bf16[96,3072]{1,0:T(8,128)(2,1)}, u32[]{:S(2)}, u32[]{:S(2)}) collective-permute-start(bf16[96,3072]{1,0:T(8,128)(2,1)} %get-tuple-element.40), channel_id=1, source_target_pairs={{0,3},{1,0},{2,1},{3,2},{4,7},{5,4},{6,5},{7,6},{8,11},{9,8},{10,9... | collective-permute-start | bytes 1769480 | tf_op jit(solution)/shard_map/ppermute | solution.py:401
  58.5 27.8 %all-to-all-start.1 = ((bf16[32,200,128]{2,1,0:T(8,128)(2,1)}), bf16[32,200,128]{2,1,0:T(8,128)(2,1)S(1)}, u32[]{:S(2)}, u32[]{:S(2)}) async-start(bf16[32,200,128]{2,1,0:T(8,128)(2,1)} %token_grads.1), calls=%async_computation.1 | async-start | bytes 3276800 | tf_op jit(solution)/shard_map/all_to_all | solution.py:409
  73.9 9.8 %collective-permute-start.3 = (bf16[96,1536]{1,0:T(8,128)(2,1)S(1)}, bf16[96,1536]{1,0:T(8,128)(2,1)S(1)}, u32[]{:S(2)}, u32[]{:S(2)}) collective-permute-start(bf16[96,1536]{1,0:T(8,128)(2,1)S(1)} %get-tuple-element.43), channel_id=1, source_target_pairs={{0,1},{1,2},{2,3},{3,0},{4,5},{5,6},{6,7},{7,4},{8,9},{9,10},{10,1... | collective-permute-start | bytes 884744 | tf_op jit(solution)/shard_map/ppermute | solution.py:407
  75.5 8.2 %collective-permute-start.4 = (bf16[96,1536]{1,0:T(8,128)(2,1)S(1)}, bf16[96,1536]{1,0:T(8,128)(2,1)S(1)}, u32[]{:S(2)}, u32[]{:S(2)}) collective-permute-start(bf16[96,1536]{1,0:T(8,128)(2,1)S(1)} %get-tuple-element.44), channel_id=1, source_target_pairs={{0,3},{1,0},{2,1},{3,2},{4,7},{5,4},{6,5},{7,6},{8,11},{9,8},{10,9... | collective-permute-start | bytes 884744 | tf_op jit(solution)/shard_map/ppermute | solution.py:408
  86.3 15.5 %all-to-all-start.2 = ((bf16[16,144,128]{2,1,0:T(8,128)(2,1)}), bf16[16,144,128]{2,1,0:T(8,128)(2,1)S(1)}, u32[]{:S(2)}, u32[]{:S(2)}) async-start(bf16[16,144,128]{2,1,0:T(8,128)(2,1)} %ring_sum.1), calls=%async_computation.2 | async-start | bytes 1179648 | tf_op jit(solution)/shard_map/all_to_all | solution.py:419
  91.6 10.2 %collective-permute-start.7 = (f32[8,128]{1,0:T(8,128)S(1)}, f32[8,128]{1,0:T(8,128)S(1)}, u32[]{:S(2)}, u32[]{:S(2)}) collective-permute-start(f32[8,128]{1,0:T(8,128)S(1)} %get-tuple-element.45.g0), channel_id=1, source_target_pairs={{0,3},{1,0},{2,1},{3,2},{4,7},{5,4},{6,5},{7,6},{8,11},{9,8},{10,9... | collective-permute-start | bytes 12296 | tf_op jit(solution)/shard_map/ppermute | solution.py:420
  93.4 8.4 %collective-permute-start.6 = (f32[8,128]{1,0:T(8,128)S(1)}, f32[8,128]{1,0:T(8,128)S(1)}, u32[]{:S(2)}, u32[]{:S(2)}) collective-permute-start(f32[8,128]{1,0:T(8,128)S(1)} %get-tuple-element.45.g0), channel_id=1, source_target_pairs={{0,2},{1,3},{2,0},{3,1},{4,6},{5,7},{6,4},{7,5},{8,10},{9,11},{10,... | collective-permute-start | bytes 12296 | tf_op jit(solution)/shard_map/ppermute | solution.py:420
  94.0 7.7 %collective-permute-start.5 = (f32[8,128]{1,0:T(8,128)S(1)}, f32[8,128]{1,0:T(8,128)S(1)}, u32[]{:S(2)}, u32[]{:S(2)}) collective-permute-start(f32[8,128]{1,0:T(8,128)S(1)} %get-tuple-element.45.g0), channel_id=1, source_target_pairs={{0,1},{1,2},{2,3},{3,0},{4,5},{5,6},{6,7},{7,4},{8,9},{9,10},{10,1... | collective-permute-start | bytes 12296 | tf_op jit(solution)/shard_map/ppermute | solution.py:420

commit v8 on v7

--- a/solution.py
+++ b/solution.py
@@ -19,7 +19,7 @@
 PASS = 1e6
 RING = 1e10
 MAIN_MB = 42
-TOKEN_MB = 20
+TOKEN_MB = 14
 
 
 def place(xlo, z, c, xhi, y):
@@ -169,26 +169,27 @@
 
 
 def main_kernel(
-    recv_ref, gain_ref, feat_ref, wqkv_hbm, wout_hbm,
-    keep_ref, send_ref, attn_ref, dqkv_ref,
-    wqkv_ref, wout_ref, qkv_ref, ga_ref, norm_ref, gy_ref, lhs_ref, sems,
+    recv_hbm, gain_ref, feat_ref, wqkv_hbm, wout_hbm,
+    keep1_ref, keep2_ref, send1_ref, send2_ref, dqkv_ref, mixed_ref,
+    attn_ref, recv_ref, wqkv_ref, wout_ref, qkv_ref, ga_ref, norm_ref, gy_ref, lhs_ref, sems,
 ):
     scale = float(HEAD_DIM) ** (-0.5)
     loads = [
         pltpu.make_async_copy(src, dst, sems.at[n])
         for n, (src, dst) in enumerate(
-            ((wout_hbm, wout_ref), (wqkv_hbm, wqkv_ref))
+            ((recv_hbm, recv_ref), (wout_hbm, wout_ref), (wqkv_hbm, wqkv_ref))
         )
     ]
     for c in loads:
         c.start()
+    loads[0].wait()
     _, _, unit = normalise(recv_ref[:, 0].reshape(TOK, D))
     normed = (unit * gain_ref[...]).astype(BF)
     norm_ref[...] = by_position(normed)
     gy_ref[...] = by_position(recv_ref[:, 1].reshape(TOK, D))
-    loads[0].wait()
+    loads[1].wait()
     ga_ref[...] = dot(gy_ref[...], wout_ref[...], 1, 1).astype(BF)
-    loads[1].wait()
+    loads[2].wait()
 
     def project(n, _):
         cols = pl.ds(pl.multiple_of(n * 768, 768), 768)
@@ -234,33 +235,41 @@
     pick = onehot(lax.broadcasted_iota(jnp.int32, (D, D), 0) == feat_ref[...])
     lhs_ref[...] = dot(pick, norm_ref[...], 0, 1).astype(BF)
 
-    def weight_grad(n, _):
-        cols = pl.ds(pl.multiple_of(n * 768, 768), 768)
-        g = dot(lhs_ref[...], dqkv_ref[:, cols], 1, 0).astype(BF)
-        keep_ref[:, cols] = g[:384]
-        send_ref[:, cols] = g[384:]
-        return 0
-
-    lax.fori_loop(0, 3, weight_grad, 0, unroll=True)
+    def place_rows(g, n):
+        cols = slice(n * D, n * D + D)
+        for r, (first, second) in ((0, (keep1_ref, keep2_ref)), (384, (send1_ref, send2_ref))):
+            own, one, two, three = (g[r + k * 96 : r + k * 96 + 96] for k in range(4))
+            up, down, hold = (two, three, one) if n < 2 else (one, two, three)
+            first[:96, cols] = up
+            first[96:, cols] = down
+            second[:96, cols] = own
+            second[96:, cols] = hold
+
+    for n in range(3):
+        place_rows(dot(lhs_ref[...], dqkv_ref[:, n * D : n * D + D], 1, 0).astype(BF), n)
     lhs_ref[...] = dot(pick, attn_ref[...], 0, 1).astype(BF)
-    g = dot(lhs_ref[...], gy_ref[...], 1, 0).astype(BF)
-    keep_ref[:, 3 * D :] = g[:384]
-    send_ref[:, 3 * D :] = g[384:]
+    place_rows(dot(lhs_ref[...], gy_ref[...], 1, 0).astype(BF), 3)
+    proj = dot(by_source(attn_ref[...]), wout_ref[...], 1, 0).astype(BF)
+    mixed = (recv_ref[:, 0].reshape(TOK, D).astype(F32) + proj.astype(F32)).astype(BF)
+    for l in range(6):
+        mixed_ref[:, l * 16 : l * 16 + 16] = mixed[:, l * 128 : l * 128 + 128].reshape(32, 16, 128)
 
 
 def token_kernel(
-    recv_ref, gain_ref, attn_ref, dqkv_ref, wqkv_ref, wout_ref, ret_hbm, ret_ref, sems
+    recv_ref, gain_ref, dqkv_ref, wqkv_ref, mixed_ref, ret_hbm, ret_ref, sems
 ):
+    store_m = pltpu.make_async_copy(mixed_ref, ret_hbm.at[:, :96], sems.at[1])
+    store_m.start()
     gn = dot(dqkv_ref[...], wqkv_ref[...], 1, 1).astype(BF)
     gn = by_source(gn).astype(F32)
-    xf, inv_rms, unit = normalise(recv_ref[:, 0].reshape(TOK, D))
+    _, inv_rms, unit = normalise(recv_ref[:, 0].reshape(TOK, D))
     g = jnp.sum(gn * unit, axis=0, keepdims=True)
     dunit = gn * gain_ref[...]
     back = inv_rms * (dunit - unit * jnp.mean(dunit * unit, axis=-1, keepdims=True))
     gy = recv_ref[:, 1].reshape(TOK, D).astype(F32)
     grad = (gy + back).astype(BF)
     for l in range(6):
-        ret_ref[:, 96 + l * 16 : 112 + l * 16] = grad[:, l * 128 : l * 128 + 128].reshape(32, 16, 128)
+        ret_ref[:, l * 16 : l * 16 + 16] = grad[:, l * 128 : l * 128 + 128].reshape(32, 16, 128)
     k = lax.broadcasted_iota(jnp.int32, (32, 8, 128), 0) * 24
     lane = lax.broadcasted_iota(jnp.int32, (32, 8, 128), 2)
     own = jnp.zeros((32, 8, 128), F32)
@@ -273,45 +282,32 @@
     row = lax.broadcasted_iota(jnp.int32, (32, 8, 128), 1)
     low = own - high - mid
     terms = jnp.where(row == 0, high, jnp.where(row == 1, mid, jnp.where(row == 2, low, 0.0)))
-    ret_ref[:, 192:] = terms.astype(BF)
-    store_g = pltpu.make_async_copy(ret_ref.at[:, 96:], ret_hbm.at[:, 96:], sems.at[0])
+    ret_ref[:, 96:] = terms.astype(BF)
+    store_g = pltpu.make_async_copy(ret_ref, ret_hbm.at[:, 96:], sems.at[0])
     store_g.start()
-    attn = by_source(attn_ref[...])
-    proj = dot(attn, wout_ref[...], 1, 0).astype(BF)
-    mixed = (xf + proj.astype(F32)).astype(BF)
-    for l in range(6):
-        ret_ref[:, l * 16 : l * 16 + 16] = mixed[:, l * 128 : l * 128 + 128].reshape(32, 16, 128)
-    store_m = pltpu.make_async_copy(ret_ref.at[:, :96], ret_hbm.at[:, :96], sems.at[1])
-    store_m.start()
+    store_m.wait()
     store_g.wait()
-    store_m.wait()
 
 
 HALF = 2 * D
 
 
-def pair_sum_kernel(a_ref, b_ref, own, up, down, hold):
-    def block(n, cols):
-        rows = slice(n * 96, n * 96 + 96)
-        return (a_ref[rows, cols].astype(F32) + b_ref[rows, cols].astype(F32)).astype(BF)
-
+def pair_sum_kernel(a_ref, b_ref, up, down):
+    up[...] = (a_ref[:96].astype(F32) + b_ref[:96].astype(F32)).astype(BF)
+    down[...] = (a_ref[96:].astype(F32) + b_ref[96:].astype(F32)).astype(BF)
+
+
+def pass_on_kernel(a_ref, b_ref, up, down, up_out, down_out, sum_out):
     left, right = slice(0, HALF), slice(HALF, 2 * HALF)
-    up[:, left] = block(2, left)
-    up[:, right] = block(1, right)
-    down[:, left] = block(3, left)
-    down[:, right] = block(2, right)
-    own[:, left] = block(0, left)
-    own[:, right] = block(0, right)
-    hold[:, left] = block(1, left)
-    hold[:, right] = block(3, right)
-
-
-def pass_on_kernel(hold, up, down, own, up_out, down_out, sum_out):
-    left, right = slice(0, HALF), slice(HALF, 2 * HALF)
-    up_out[...] = (hold[:, left].astype(F32) + up[:, left].astype(F32)).astype(BF)
-    down_out[...] = (hold[:, right].astype(F32) + down[:, right].astype(F32)).astype(BF)
-    sum_out[:, left] = own[:, left].astype(F32) + down[:, left].astype(F32)
-    sum_out[:, right] = own[:, right].astype(F32) + up[:, right].astype(F32)
+
+    def pair(rows, cols):
+        return a_ref[rows, cols].astype(F32) + b_ref[rows, cols].astype(F32)
+
+    own, hold = slice(0, 96), slice(96, 192)
+    up_out[...] = (pair(hold, left) + up[:, left].astype(F32)).astype(BF)
+    down_out[...] = (pair(hold, right) + down[:, right].astype(F32)).astype(BF)
+    sum_out[:, left] = pair(own, left) + down[:, left].astype(F32)
+    sum_out[:, right] = pair(own, right) + up[:, right].astype(F32)
 
 
 def ring_sum_kernel(near, up_far, down_far, o):
@@ -375,35 +371,36 @@
         compiler_params=params(60), cost_estimate=cost(1e9, 4e6), name="pack",
     )(tokens, cotangent, lesion)
     recv = lax.all_to_all(packed, AXES, 0, 0, tiled=True, axis_index_groups=PLANE)
-    keep, send, attn, dqkv = pl.pallas_call(
+    keep1, keep2, send1, send2, dqkv, mixed_rows = pl.pallas_call(
         main_kernel,
-        out_shape=(shape(384, 4 * D), shape(384, 4 * D), shape(TOK, D), shape(TOK, 3 * D)),
-        in_specs=[VM, VM, VM, HBM, HBM],
+        out_shape=(*(shape(192, 4 * D) for _ in range(4)), shape(TOK, 3 * D), shape(32, 96, 128)),
+        in_specs=[HBM, VM, VM, HBM, HBM],
         scratch_shapes=[
-            pltpu.VMEM((D, 3 * D), BF), pltpu.VMEM((D, D), BF),
+            pltpu.VMEM((TOK, D), BF), pltpu.VMEM((32, 2, 16, D), BF), pltpu.VMEM((D, 3 * D), BF), pltpu.VMEM((D, D), BF),
             pltpu.VMEM((TOK, 3 * D), BF), pltpu.VMEM((TOK, D), BF), pltpu.VMEM((TOK, D), BF),
-            pltpu.VMEM((TOK, D), BF), pltpu.VMEM((D, TOK), BF), DMA((2,)),
+            pltpu.VMEM((TOK, D), BF), pltpu.VMEM((D, TOK), BF), DMA((3,)),
         ],
         compiler_params=params(MAIN_MB), cost_estimate=cost(1e10, 1.5e7), name="main",
     )(recv, gain, feat, w_qkv, w_out)
-    got = lax.ppermute(send, AXES, CORE_SWAP)
+    got1 = lax.ppermute(send1, AXES, CORE_SWAP)
+    got2 = lax.ppermute(send2, AXES, CORE_SWAP)
     ret = pl.pallas_call(
         token_kernel, out_shape=shape(32, 200, 128), out_specs=HBM,
-        scratch_shapes=[pltpu.VMEM((32, 200, 128), BF), DMA((2,))],
-        compiler_params=params(TOKEN_MB), cost_estimate=cost(3.5e9, 1.2e7), name="token_grads",
-    )(recv, gain, attn, dqkv, w_qkv, w_out)
-    quarters = pl.pallas_call(
-        pair_sum_kernel, out_shape=tuple(shape(96, 4 * D) for _ in range(4)),
-        compiler_params=params(6), cost_estimate=cost(1e6, 7e6), name="pair_sum",
-    )(keep, got)
-    own, up, down, hold, ret = lax.optimization_barrier((*quarters, ret))
+        scratch_shapes=[pltpu.VMEM((32, 104, 128), BF), DMA((2,))],
+        compiler_params=params(TOKEN_MB), cost_estimate=cost(2.8e9, 1e7), name="token_grads",
+    )(recv, gain, dqkv, w_qkv, mixed_rows)
+    up, down = pl.pallas_call(
+        pair_sum_kernel, out_shape=(shape(96, 4 * D), shape(96, 4 * D)),
+        compiler_params=params(6), cost_estimate=cost(1e6, 3e6), name="pair_sum",
+    )(keep1, got1)
+    up, down, ret = lax.optimization_barrier((up, down, ret))
     up = lax.ppermute(up, AXES, y_shift(1))
     down = lax.ppermute(down, AXES, y_shift(3))
     up_far, down_far, near = pl.pallas_call(
         pass_on_kernel,
         out_shape=(shape(96, HALF), shape(96, HALF), shape(96, 4 * D, dtype=F32)),
         compiler_params=params(6), cost_estimate=cost(PASS, 3e6), name="pass_on",
-    )(hold, up, down, own)
+    )(keep2, got2, up, down)
     up_far = lax.ppermute(up_far, AXES, y_shift(1))
     down_far = lax.ppermute(down_far, AXES, y_shift(3))
     back = lax.all_to_all(ret, AXES, 0, 0, tiled=True, axis_index_groups=PLANE)

time: 103 us -> 103 us (level)
  waiting for transfers between devices: 47.3 us -> 45.6 us
  starting transfers between devices: 26.2 us -> 27.6 us
  local copies, waits for them, and re-layouts: 0.77 us -> 2.04 us
    pallas_call x1, Pallas kernels: 5.62 us -> 4.19 us  [per_device(): pl.pallas_call(token_kernel, out_shape=shape(32, 200, 128), out_specs=HBM...]
    unnamed x6, local copies, waits for them, and re-layouts: 0.02 us -> 1.28 us
    ppermute x3, starting transfers between devices: 3.42 us -> 4.62 us  [per_device(): lax.ppermute(gain_part, AXES, y_shift(s))]
    all_to_all x1, waiting for transfers between devices: 6.75 us -> 5.55 us  [per_device(): last = lax.all_to_all(mine, AXES, 0, 0, tiled=True, axis_index_groups=CHIPS)]
  transfers between devices with their start and end apart: 11 -> 12, of which waited for: 6 -> 6; matrix products, arithmetic and copies ran while one was open for 1% -> 1% of each run, Pallas kernels for 9% -> 10%
where the time goes in v8:
time: 103 us
  waiting for transfers between devices  45.6 us (44%)
  starting transfers between devices  27.6 us (27%)
  Pallas kernels  26.9 us (26%)
  local copies, waits for them, and re-layouts  2.04 us (2%)
    all_to_all x1, waiting for transfers between devices, per_device(): lax.all_to_all(packed, AXES, 0, 0, tiled=True, axis_index_groups=PLANE)  22.3 us
    pallas_call x1, Pallas kernels, per_device(): pl.pallas_call(main_kernel, out_shape=(*(shape(192, 4 * D) for _ in range...  13.4 us
    ppermute x1, waiting for transfers between devices, per_device(): up = lax.ppermute(up, AXES, y_shift(1))  9.76 us
    all_to_all x1, starting transfers between devices, per_device(): lax.all_to_all(packed, AXES, 0, 0, tiled=True, axis_index_groups=PLANE)  8.25 us
    ppermute x1, waiting for transfers between devices, per_device(): up_far = lax.ppermute(up_far, AXES, y_shift(1))  6.29 us
    all_to_all x1, waiting for transfers between devices, per_device(): last = lax.all_to_all(mine, AXES, 0, 0, tiled=True, axis_index_groups=CHIPS)  5.55 us
    ppermute x3, starting transfers between devices, per_device(): lax.ppermute(gain_part, AXES, y_shift(s))  4.62 us
    pallas_call x1, Pallas kernels, per_device(): pl.pallas_call(token_kernel, out_shape=shape(32, 200, 128), out_specs=HBM...  4.19 us
  transfers between devices with their start and end apart: 12, of which 6 were waited for; matrix products, arithmetic and copies ran while one was open for 1% of the time, Pallas kernels for 10%

profile of v8, /device:TPU:0, one launch (start us, length us, event | category | flops | bytes accessed | tf_op | source)
XLA Modules:
  0.0 102.9 jit_solution(6284123448373889642)
XLA Ops:
  0.6 2.9 %pack.1 = bf16[32,2,16,768]{3,2,1,0:T(8,128)(2,1)} custom-call(bf16[4,128,768]{2,1,0:T(8,128)(2,1)} %tok_hbm.1, bf16[4,128,768]{2,1,0:T(8,128)(2,1)} %cot_hbm.1, s32[4,128]{1,0:T(4,128)} %les_hbm.1), custom_call_target="tpu_custom_call" | custom-call | flops 1000000000 | bytes 4000000 | tf_op jit(solution)/shard_map/pack/pallas_call | solution.py:365
  3.5 0.0 copy-start.2
  3.5 8.3 %all-to-all-start = ((bf16[32,2,16,768]{3,2,1,0:T(8,128)(2,1)}), bf16[32,2,16,768]{3,2,1,0:T(8,128)(2,1)S(1)}, u32[]{:S(2)}, u32[]{:S(2)}) async-start(bf16[32,2,16,768]{3,2,1,0:T(8,128)(2,1)} %pack.1), calls=%async_computation | async-start | bytes 3145728 | tf_op jit(solution)/shard_map/all_to_all | solution.py:373
  11.8 0.0 copy-done.2
  11.8 0.8 constant_dynamic-slice_fusion.feat_ref
  12.6 22.3 %all-to-all-done.recv_hbm.recv_ref = bf16[32,2,16,768]{3,2,1,0:T(8,128)(2,1)S(1)} async-done(((bf16[32,2,16,768]{3,2,1,0:T(8,128)(2,1)}), bf16[32,2,16,768]{3,2,1,0:T(8,128)(2,1)S(1)}, u32[]{:S(2)}, u32[]{:S(2)}) %all-to-all-start) | async-done | bytes 1572896 | tf_op jit(solution)/shard_map/all_to_all | solution.py:373
  34.9 0.0 copy-start.1
  34.9 1.3 %copy-done.1 = bf16[768,768]{1,0:T(8,128)(2,1)S(1)} copy-done((bf16[768,768]{1,0:T(8,128)(2,1)S(1)}, bf16[768,768]{1,0:T(8,128)(2,1)}, u32[]{:S(2)}) %copy-start.1) | copy-done | bytes 1179672
  36.2 0.0 copy-start
  36.2 13.4 %main.1 = (bf16[192,3072]{1,0:T(8,128)(2,1)S(1)}, bf16[192,3072]{1,0:T(8,128)(2,1)S(1)}, bf16[192,3072]{1,0:T(8,128)(2,1)S(1)}, bf16[192,3072]{1,0:T(8,128)(2,1)...) custom-call(bf16[32,2,16,768]{3,2,1,0:T(8,128)(2,1)S(1)} %all-to-all-done.recv_hbm.recv_ref, ...), custom_call_target="tpu_custom_call" | custom-call | flops 10000000000 | bytes 15000000 | tf_op jit(solution)/shard_map/main/pallas_call | solution.py:374
  49.6 0.1 collective-permute-start
  49.7 0.5 collective-permute-start.1
  50.2 0.0 copy-done
  50.2 4.2 %token_grads.1 = bf16[32,200,128]{2,1,0:T(8,128)(2,1)} custom-call(bf16[32,2,16,768]{3,2,1,0:T(8,128)(2,1)S(1)} %all-to-all-done.recv_hbm.recv_ref, f32[1,768]{1,0:T(1,128)S(1)} %reshape.19.gain_ref, bf16[512,2304]{1,0:T(8,128)(2,1)S(1)} %get-tuple-element.29.dqkv_ref, bf16[768,2304]{1,0:T(8,128)(2,1)S(1)} %copy-done, ...), custom_call_target="tpu_custom_call" | custom-call | flops 2800000000 | bytes 10000000 | tf_op jit(solution)/shard_map/token_grads/pallas_call | solution.py:387
  54.4 0.0 collective-permute-done.b_ref
  54.4 1.2 %pair_sum.1 = (bf16[96,3072]{1,0:T(8,128)(2,1)}, bf16[96,3072]{1,0:T(8,128)(2,1)}) custom-call(bf16[192,3072]{1,0:T(8,128)(2,1)S(1)} %get-tuple-element.25.a_ref, bf16[192,3072]{1,0:T(8,128)(2,1)S(1)} %collective-permute-done.b_ref), custom_call_target="tpu_custom_call" | custom-call | flops 1000000 | bytes 3000000 | tf_op jit(solution)/shard_map/pair_sum/pallas_call | solution.py:392
  55.6 1.6 %collective-permute-start.2 = (bf16[96,3072]{1,0:T(8,128)(2,1)}, bf16[96,3072]{1,0:T(8,128)(2,1)S(1)}, u32[]{:S(2)}, u32[]{:S(2)}) collective-permute-start(bf16[96,3072]{1,0:T(8,128)(2,1)} %get-tuple-element.36), channel_id=1, source_target_pairs={{0,1},{1,2},{2,3},{3,0},{4,5},{5,6},{6,7},{7,4},{8,9},{9,10},{10,1... | collective-permute-start | bytes 1769480 | tf_op jit(solution)/shard_map/ppermute | solution.py:397
  57.2 1.7 %collective-permute-start.3 = (bf16[96,3072]{1,0:T(8,128)(2,1)}, bf16[96,3072]{1,0:T(8,128)(2,1)}, u32[]{:S(2)}, u32[]{:S(2)}) collective-permute-start(bf16[96,3072]{1,0:T(8,128)(2,1)} %get-tuple-element.37), channel_id=1, source_target_pairs={{0,3},{1,0},{2,1},{3,2},{4,7},{5,4},{6,5},{7,6},{8,11},{9,8},{10,9... | collective-permute-start | bytes 1769480 | tf_op jit(solution)/shard_map/ppermute | solution.py:398
  58.9 4.0 %all-to-all-start.1 = ((bf16[32,200,128]{2,1,0:T(8,128)(2,1)}), bf16[32,200,128]{2,1,0:T(8,128)(2,1)S(1)}, u32[]{:S(2)}, u32[]{:S(2)}) async-start(bf16[32,200,128]{2,1,0:T(8,128)(2,1)} %token_grads.1), calls=%async_computation.1 | async-start | bytes 3276800 | tf_op jit(solution)/shard_map/all_to_all | solution.py:406
  62.9 0.0 collective-permute-done.1.b_ref
  62.9 9.8 %collective-permute-done.2.up = bf16[96,3072]{1,0:T(8,128)(2,1)S(1)} collective-permute-done((bf16[96,3072]{1,0:T(8,128)(2,1)}, bf16[96,3072]{1,0:T(8,128)(2,1)S(1)}, u32[]{:S(2)}, u32[]{:S(2)}) %collective-permute-start.2) | collective-permute-done | bytes 589856 | tf_op jit(solution)/shard_map/ppermute | solution.py:397
  72.6 0.1 collective-permute-done.3.down
  72.8 1.8 %pass_on.1 = (bf16[96,1536]{1,0:T(8,128)(2,1)S(1)}, bf16[96,1536]{1,0:T(8,128)(2,1)S(1)}, f32[96,3072]{1,0:T(8,128)S(1)}) custom-call(bf16[192,3072]{1,0:T(8,128)(2,1)S(1)} %get-tuple-element.34.a_ref, bf16[192,3072]{1,0:T(8,128)(2,1)} %collective-permute-done.1.b_ref, bf16[96,3072]{1,0:T(8,128)(2,1)S(1)} %collective-permute-done.2.up, ...), custom_call_target="tpu_custom_call" | custom-call | flops 1000000 | bytes 3000000 | tf_op jit(solution)/shard_map/pass_on/pallas_call | solution.py:399
  74.6 1.6 %collective-permute-start.4 = (bf16[96,1536]{1,0:T(8,128)(2,1)S(1)}, bf16[96,1536]{1,0:T(8,128)(2,1)S(1)}, u32[]{:S(2)}, u32[]{:S(2)}) collective-permute-start(bf16[96,1536]{1,0:T(8,128)(2,1)S(1)} %get-tuple-element.39), channel_id=1, source_target_pairs={{0,1},{1,2},{2,3},{3,0},{4,5},{5,6},{6,7},{7,4},{8,9},{9,10},{10,1... | collective-permute-start | bytes 884744 | tf_op jit(solution)/shard_map/ppermute | solution.py:404
  76.2 1.7 %collective-permute-start.5 = (bf16[96,1536]{1,0:T(8,128)(2,1)S(1)}, bf16[96,1536]{1,0:T(8,128)(2,1)S(1)}, u32[]{:S(2)}, u32[]{:S(2)}) collective-permute-start(bf16[96,1536]{1,0:T(8,128)(2,1)S(1)} %get-tuple-element.40), channel_id=1, source_target_pairs={{0,3},{1,0},{2,1},{3,2},{4,7},{5,4},{6,5},{7,6},{8,11},{9,8},{10,9... | collective-permute-start | bytes 884744 | tf_op jit(solution)/shard_map/ppermute | solution.py:405
  77.9 6.3 %collective-permute-done.4.up_far = bf16[96,1536]{1,0:T(8,128)(2,1)S(1)} collective-permute-done((bf16[96,1536]{1,0:T(8,128)(2,1)S(1)}, bf16[96,1536]{1,0:T(8,128)(2,1)S(1)}, u32[]{:S(2)}, u32[]{:S(2)}) %collective-permute-start.4) | collective-permute-done | bytes 294944 | tf_op jit(solution)/shard_map/ppermute | solution.py:404
  84.2 0.0 collective-permute-done.5.down_far
  84.2 1.0 ring_sum.1
  85.2 1.5 %all-to-all-done.1.in_ref = bf16[32,200,128]{2,1,0:T(8,128)(2,1)S(1)} async-done(((bf16[32,200,128]{2,1,0:T(8,128)(2,1)}), bf16[32,200,128]{2,1,0:T(8,128)(2,1)S(1)}, u32[]{:S(2)}, u32[]{:S(2)}) %all-to-all-start.1) | async-done | bytes 1638432 | tf_op jit(solution)/shard_map/all_to_all | solution.py:406
  86.7 3.6 %all-to-all-start.2 = ((bf16[16,144,128]{2,1,0:T(8,128)(2,1)}), bf16[16,144,128]{2,1,0:T(8,128)(2,1)S(1)}, u32[]{:S(2)}, u32[]{:S(2)}) async-start(bf16[16,144,128]{2,1,0:T(8,128)(2,1)} %ring_sum.1), calls=%async_computation.2 | async-start | bytes 1179648 | tf_op jit(solution)/shard_map/all_to_all | solution.py:416
  90.3 1.7 %unpack.1 = (bf16[4,128,768]{2,1,0:T(8,128)(2,1)}, bf16[4,128,768]{2,1,0:T(8,128)(2,1)}, f32[8,128]{1,0:T(8,128)S(1)}) custom-call(bf16[32,200,128]{2,1,0:T(8,128)(2,1)S(1)} %all-to-all-done.1.in_ref), custom_call_target="tpu_custom_call" | custom-call | flops 1000000000 | bytes 4000000 | tf_op jit(solution)/shard_map/unpack/pallas_call | solution.py:411
  92.0 0.4 collective-permute-start.6
  92.4 2.9 %collective-permute-start.7 = (f32[8,128]{1,0:T(8,128)S(1)}, f32[8,128]{1,0:T(8,128)S(1)}, u32[]{:S(2)}, u32[]{:S(2)}) collective-permute-start(f32[8,128]{1,0:T(8,128)S(1)} %get-tuple-element.41.g0), channel_id=1, source_target_pairs={{0,2},{1,3},{2,0},{3,1},{4,6},{5,7},{6,4},{7,5},{8,10},{9,11},{10,... | collective-permute-start | bytes 12296 | tf_op jit(solution)/shard_map/ppermute | solution.py:417
  95.3 1.3 %collective-permute-start.8 = (f32[8,128]{1,0:T(8,128)S(1)}, f32[8,128]{1,0:T(8,128)S(1)}, u32[]{:S(2)}, u32[]{:S(2)}) collective-permute-start(f32[8,128]{1,0:T(8,128)S(1)} %get-tuple-element.41.g0), channel_id=1, source_target_pairs={{0,3},{1,0},{2,1},{3,2},{4,7},{5,4},{6,5},{7,6},{8,11},{9,8},{10,9... | collective-permute-start | bytes 12296 | tf_op jit(solution)/shard_map/ppermute | solution.py:417
  96.6 5.5 %all-to-all-done.2.in_ref = bf16[16,144,128]{2,1,0:T(8,128)(2,1)S(1)} async-done(((bf16[16,144,128]{2,1,0:T(8,128)(2,1)}), bf16[16,144,128]{2,1,0:T(8,128)(2,1)S(1)}, u32[]{:S(2)}, u32[]{:S(2)}) %all-to-all-start.2) | async-done | bytes 589856 | tf_op jit(solution)/shard_map/all_to_all | solution.py:416
  102.2 0.0 collective-permute-done.6.g1
  102.2 0.0 collective-permute-done.7.g2
  102.2 0.0 collective-permute-done.8.g3
  102.2 0.7 final.1
  (1 shorter events, 0.0 us)
Async XLA Ops:
  3.5 8.3 %copy-start.2 = (f32[768]{0:T(1024)S(1)}, f32[768]{0:T(1024)}, u32[]{:S(2)}) copy-start(f32[768]{0:T(1024)} %param.12) | copy-start | bytes 9220
  3.5 31.4 %all-to-all-start = ((bf16[32,2,16,768]{3,2,1,0:T(8,128)(2,1)}), bf16[32,2,16,768]{3,2,1,0:T(8,128)(2,1)S(1)}, u32[]{:S(2)}, u32[]{:S(2)}) async-start(bf16[32,2,16,768]{3,2,1,0:T(8,128)(2,1)} %pack.1), calls=%async_computation | async-start | bytes 3145728 | tf_op jit(solution)/shard_map/all_to_all | solution.py:373
  34.9 1.3 %copy-start.1 = (bf16[768,768]{1,0:T(8,128)(2,1)S(1)}, bf16[768,768]{1,0:T(8,128)(2,1)}, u32[]{:S(2)}) copy-start(bf16[768,768]{1,0:T(8,128)(2,1)} %wout_hbm.1) | copy-start | bytes 3538948
  36.2 14.0 %copy-start = (bf16[768,2304]{1,0:T(8,128)(2,1)S(1)}, bf16[768,2304]{1,0:T(8,128)(2,1)}, u32[]{:S(2)}) copy-start(bf16[768,2304]{1,0:T(8,128)(2,1)} %wqkv_ref.1) | copy-start | bytes 10616836
  49.6 4.8 %collective-permute-start = (bf16[192,3072]{1,0:T(8,128)(2,1)S(1)}, bf16[192,3072]{1,0:T(8,128)(2,1)S(1)}, u32[]{:S(2)}, u32[]{:S(2)}) collective-permute-start(bf16[192,3072]{1,0:T(8,128)(2,1)S(1)} %get-tuple-element.26), channel_id=1, source_target_pairs={{0,8},{1,9},{2,10},{3,11},{4,12},{5,13},{6,14},{7,15},{8,0},{9,1},... | collective-permute-start | bytes 3538952 | tf_op jit(solution)/shard_map/ppermute | solution.py:385
  49.7 13.1 %collective-permute-start.1 = (bf16[192,3072]{1,0:T(8,128)(2,1)}, bf16[192,3072]{1,0:T(8,128)(2,1)}, u32[]{:S(2)}, u32[]{:S(2)}) collective-permute-start(bf16[192,3072]{1,0:T(8,128)(2,1)} %get-tuple-element.35), channel_id=1, source_target_pairs={{0,8},{1,9},{2,10},{3,11},{4,12},{5,13},{6,14},{7,15},{8,0},{9,1},... | collective-permute-start | bytes 3538952 | tf_op jit(solution)/shard_map/ppermute | solution.py:386
  55.6 17.0 %collective-permute-start.2 = (bf16[96,3072]{1,0:T(8,128)(2,1)}, bf16[96,3072]{1,0:T(8,128)(2,1)S(1)}, u32[]{:S(2)}, u32[]{:S(2)}) collective-permute-start(bf16[96,3072]{1,0:T(8,128)(2,1)} %get-tuple-element.36), channel_id=1, source_target_pairs={{0,1},{1,2},{2,3},{3,0},{4,5},{5,6},{6,7},{7,4},{8,9},{9,10},{10,1... | collective-permute-start | bytes 1769480 | tf_op jit(solution)/shard_map/ppermute | solution.py:397
  57.2 15.5 %collective-permute-start.3 = (bf16[96,3072]{1,0:T(8,128)(2,1)}, bf16[96,3072]{1,0:T(8,128)(2,1)}, u32[]{:S(2)}, u32[]{:S(2)}) collective-permute-start(bf16[96,3072]{1,0:T(8,128)(2,1)} %get-tuple-element.37), channel_id=1, source_target_pairs={{0,3},{1,0},{2,1},{3,2},{4,7},{5,4},{6,5},{7,6},{8,11},{9,8},{10,9... | collective-permute-start | bytes 1769480 | tf_op jit(solution)/shard_map/ppermute | solution.py:398
  58.9 27.8 %all-to-all-start.1 = ((bf16[32,200,128]{2,1,0:T(8,128)(2,1)}), bf16[32,200,128]{2,1,0:T(8,128)(2,1)S(1)}, u32[]{:S(2)}, u32[]{:S(2)}) async-start(bf16[32,200,128]{2,1,0:T(8,128)(2,1)} %token_grads.1), calls=%async_computation.1 | async-start | bytes 3276800 | tf_op jit(solution)/shard_map/all_to_all | solution.py:406
  74.6 9.6 %collective-permute-start.4 = (bf16[96,1536]{1,0:T(8,128)(2,1)S(1)}, bf16[96,1536]{1,0:T(8,128)(2,1)S(1)}, u32[]{:S(2)}, u32[]{:S(2)}) collective-permute-start(bf16[96,1536]{1,0:T(8,128)(2,1)S(1)} %get-tuple-element.39), channel_id=1, source_target_pairs={{0,1},{1,2},{2,3},{3,0},{4,5},{5,6},{6,7},{7,4},{8,9},{9,10},{10,1... | collective-permute-start | bytes 884744 | tf_op jit(solution)/shard_map/ppermute | solution.py:404
  76.2 8.0 %collective-permute-start.5 = (bf16[96,1536]{1,0:T(8,128)(2,1)S(1)}, bf16[96,1536]{1,0:T(8,128)(2,1)S(1)}, u32[]{:S(2)}, u32[]{:S(2)}) collective-permute-start(bf16[96,1536]{1,0:T(8,128)(2,1)S(1)} %get-tuple-element.40), channel_id=1, source_target_pairs={{0,3},{1,0},{2,1},{3,2},{4,7},{5,4},{6,5},{7,6},{8,11},{9,8},{10,9... | collective-permute-start | bytes 884744 | tf_op jit(solution)/shard_map/ppermute | solution.py:405
  86.7 15.5 %all-to-all-start.2 = ((bf16[16,144,128]{2,1,0:T(8,128)(2,1)}), bf16[16,144,128]{2,1,0:T(8,128)(2,1)S(1)}, u32[]{:S(2)}, u32[]{:S(2)}) async-start(bf16[16,144,128]{2,1,0:T(8,128)(2,1)} %ring_sum.1), calls=%async_computation.2 | async-start | bytes 1179648 | tf_op jit(solution)/shard_map/all_to_all | solution.py:416
  92.0 10.2 %collective-permute-start.6 = (f32[8,128]{1,0:T(8,128)S(1)}, f32[8,128]{1,0:T(8,128)S(1)}, u32[]{:S(2)}, u32[]{:S(2)}) collective-permute-start(f32[8,128]{1,0:T(8,128)S(1)} %get-tuple-element.41.g0), channel_id=1, source_target_pairs={{0,1},{1,2},{2,3},{3,0},{4,5},{5,6},{6,7},{7,4},{8,9},{9,10},{10,1... | collective-permute-start | bytes 12296 | tf_op jit(solution)/shard_map/ppermute | solution.py:417
  92.4 9.8 %collective-permute-start.7 = (f32[8,128]{1,0:T(8,128)S(1)}, f32[8,128]{1,0:T(8,128)S(1)}, u32[]{:S(2)}, u32[]{:S(2)}) collective-permute-start(f32[8,128]{1,0:T(8,128)S(1)} %get-tuple-element.41.g0), channel_id=1, source_target_pairs={{0,2},{1,3},{2,0},{3,1},{4,6},{5,7},{6,4},{7,5},{8,10},{9,11},{10,... | collective-permute-start | bytes 12296 | tf_op jit(solution)/shard_map/ppermute | solution.py:417
  95.3 6.9 %collective-permute-start.8 = (f32[8,128]{1,0:T(8,128)S(1)}, f32[8,128]{1,0:T(8,128)S(1)}, u32[]{:S(2)}, u32[]{:S(2)}) collective-permute-start(f32[8,128]{1,0:T(8,128)S(1)} %get-tuple-element.41.g0), channel_id=1, source_target_pairs={{0,3},{1,0},{2,1},{3,2},{4,7},{5,4},{6,5},{7,6},{8,11},{9,8},{10,9... | collective-permute-start | bytes 12296 | tf_op jit(solution)/shard_map/ppermute | solution.py:417

commit v9 on v8

--- a/solution.py
+++ b/solution.py
@@ -126,12 +126,22 @@
     def block(ref, n):
         return jnp.concatenate([ref[d, n * 32 : n * 32 + 32] for d in range(4)], axis=0)
 
+    stores = []
+
+    def put(which, n, x):
+        out_ref[which, n * 8 : n * 8 + 8] = x.reshape(8, 16, D)
+        store = pltpu.make_async_copy(
+            out_ref.at[which, pl.ds(n * 8, 8)],
+            out_hbm.at[pl.ds(n * 8, 8), which],
+            sems.at[3 + which * 4 + n],
+        )
+        store.start()
+        stores.append(store)
+
     loads[1].wait()
     for n in range(4):
         t = dot(plain, block(tok_ref, n), 1, 0).astype(BF)
-        out_ref[0, n * 8 : n * 8 + 8] = t.reshape(8, 16, D)
-    store_t = pltpu.make_async_copy(out_ref.at[0], out_hbm.at[:, 0], sems.at[3])
-    store_t.start()
+        put(0, n, t)
     loads[0].wait()
     weight = 1.0 + LESION_GAIN * les_ref[...].astype(F32)
     loads[2].wait()
@@ -139,11 +149,9 @@
         row = jnp.concatenate([weight[d : d + 1, n * 32 : n * 32 + 32] for d in range(4)], axis=1)
         scaled = jnp.where(mask, row, 0.0).astype(BF)
         g = dot(scaled, block(cot_ref, n), 1, 0).astype(BF)
-        out_ref[1, n * 8 : n * 8 + 8] = g.reshape(8, 16, D)
-    store_g = pltpu.make_async_copy(out_ref.at[1], out_hbm.at[:, 1], sems.at[4])
-    store_g.start()
-    store_t.wait()
-    store_g.wait()
+        put(1, n, g)
+    for c in stores:
+        c.wait()
 
 
 def unpack_kernel(in_ref, mixed_ref, grad_ref, gain_ref):
@@ -168,10 +176,14 @@
     return xf, inv_rms, xf * inv_rms
 
 
+def order_kernel(feat_ref, wout_ref, out_ref):
+    out_ref[...] = feat_ref[...]
+
+
 def main_kernel(
     recv_hbm, gain_ref, feat_ref, wqkv_hbm, wout_hbm,
-    keep1_ref, keep2_ref, send1_ref, send2_ref, dqkv_ref, mixed_ref,
-    attn_ref, recv_ref, wqkv_ref, wout_ref, qkv_ref, ga_ref, norm_ref, gy_ref, lhs_ref, sems,
+    keep1_ref, keep2_ref, send1_ref, send2_ref, attn_ref, dqkv_ref,
+    recv_ref, wqkv_ref, wout_ref, qkv_ref, ga_ref, norm_ref, gy_ref, lhs_ref, sems,
 ):
     scale = float(HEAD_DIM) ** (-0.5)
     loads = [
@@ -249,17 +261,9 @@
         place_rows(dot(lhs_ref[...], dqkv_ref[:, n * D : n * D + D], 1, 0).astype(BF), n)
     lhs_ref[...] = dot(pick, attn_ref[...], 0, 1).astype(BF)
     place_rows(dot(lhs_ref[...], gy_ref[...], 1, 0).astype(BF), 3)
-    proj = dot(by_source(attn_ref[...]), wout_ref[...], 1, 0).astype(BF)
-    mixed = (recv_ref[:, 0].reshape(TOK, D).astype(F32) + proj.astype(F32)).astype(BF)
-    for l in range(6):
-        mixed_ref[:, l * 16 : l * 16 + 16] = mixed[:, l * 128 : l * 128 + 128].reshape(32, 16, 128)
-
-
-def token_kernel(
-    recv_ref, gain_ref, dqkv_ref, wqkv_ref, mixed_ref, ret_hbm, ret_ref, sems
-):
-    store_m = pltpu.make_async_copy(mixed_ref, ret_hbm.at[:, :96], sems.at[1])
-    store_m.start()
+
+
+def token_kernel(recv_ref, gain_ref, dqkv_ref, wqkv_ref, ret_ref):
     gn = dot(dqkv_ref[...], wqkv_ref[...], 1, 1).astype(BF)
     gn = by_source(gn).astype(F32)
     _, inv_rms, unit = normalise(recv_ref[:, 0].reshape(TOK, D))
@@ -283,10 +287,20 @@
     low = own - high - mid
     terms = jnp.where(row == 0, high, jnp.where(row == 1, mid, jnp.where(row == 2, low, 0.0)))
     ret_ref[:, 96:] = terms.astype(BF)
-    store_g = pltpu.make_async_copy(ret_ref, ret_hbm.at[:, 96:], sems.at[0])
+
+
+def mixed_kernel(recv_ref, attn_ref, wout_ref, grad_ref, ret_hbm, ret_ref, sems):
+    store_g = pltpu.make_async_copy(grad_ref, ret_hbm.at[:, 96:], sems.at[0])
     store_g.start()
+    attn = by_source(attn_ref[...])
+    proj = dot(attn, wout_ref[...], 1, 0).astype(BF)
+    mixed = (recv_ref[:, 0].reshape(TOK, D).astype(F32) + proj.astype(F32)).astype(BF)
+    for l in range(6):
+        ret_ref[:, l * 16 : l * 16 + 16] = mixed[:, l * 128 : l * 128 + 128].reshape(32, 16, 128)
+    store_m = pltpu.make_async_copy(ret_ref, ret_hbm.at[:, :96], sems.at[1])
+    store_m.start()
+    store_g.wait()
     store_m.wait()
-    store_g.wait()
 
 
 HALF = 2 * D
@@ -366,17 +380,21 @@
         pack_kernel, out_shape=shape(32, 2, 16, D), in_specs=[HBM] * 3, out_specs=HBM,
         scratch_shapes=[
             pltpu.VMEM((4, 128, D), BF), pltpu.VMEM((4, 128, D), BF), pltpu.VMEM((4, 128), jnp.int32),
-            pltpu.VMEM((2, 32, 16, D), BF), DMA((5,)),
+            pltpu.VMEM((2, 32, 16, D), BF), DMA((11,)),
         ],
         compiler_params=params(60), cost_estimate=cost(1e9, 4e6), name="pack",
     )(tokens, cotangent, lesion)
+    feat = pl.pallas_call(
+        order_kernel, out_shape=shape(1, D, dtype=jnp.int32), compiler_params=params(2),
+        cost_estimate=cost(1e6, 1e6), name="order",
+    )(feat, w_out)
     recv = lax.all_to_all(packed, AXES, 0, 0, tiled=True, axis_index_groups=PLANE)
-    keep1, keep2, send1, send2, dqkv, mixed_rows = pl.pallas_call(
+    keep1, keep2, send1, send2, attn, dqkv = pl.pallas_call(
         main_kernel,
-        out_shape=(*(shape(192, 4 * D) for _ in range(4)), shape(TOK, 3 * D), shape(32, 96, 128)),
+        out_shape=(*(shape(192, 4 * D) for _ in range(4)), shape(TOK, D), shape(TOK, 3 * D)),
         in_specs=[HBM, VM, VM, HBM, HBM],
         scratch_shapes=[
-            pltpu.VMEM((TOK, D), BF), pltpu.VMEM((32, 2, 16, D), BF), pltpu.VMEM((D, 3 * D), BF), pltpu.VMEM((D, D), BF),
+            pltpu.VMEM((32, 2, 16, D), BF), pltpu.VMEM((D, 3 * D), BF), pltpu.VMEM((D, D), BF),
             pltpu.VMEM((TOK, 3 * D), BF), pltpu.VMEM((TOK, D), BF), pltpu.VMEM((TOK, D), BF),
             pltpu.VMEM((TOK, D), BF), pltpu.VMEM((D, TOK), BF), DMA((3,)),
         ],
@@ -384,16 +402,20 @@
     )(recv, gain, feat, w_qkv, w_out)
     got1 = lax.ppermute(send1, AXES, CORE_SWAP)
     got2 = lax.ppermute(send2, AXES, CORE_SWAP)
-    ret = pl.pallas_call(
-        token_kernel, out_shape=shape(32, 200, 128), out_specs=HBM,
-        scratch_shapes=[pltpu.VMEM((32, 104, 128), BF), DMA((2,))],
-        compiler_params=params(TOKEN_MB), cost_estimate=cost(2.8e9, 1e7), name="token_grads",
-    )(recv, gain, dqkv, w_qkv, mixed_rows)
+    grads = pl.pallas_call(
+        token_kernel, out_shape=shape(32, 104, 128),
+        compiler_params=params(TOKEN_MB), cost_estimate=cost(2.8e9, 9e6), name="token_grads",
+    )(recv, gain, dqkv, w_qkv)
     up, down = pl.pallas_call(
         pair_sum_kernel, out_shape=(shape(96, 4 * D), shape(96, 4 * D)),
         compiler_params=params(6), cost_estimate=cost(1e6, 3e6), name="pair_sum",
     )(keep1, got1)
-    up, down, ret = lax.optimization_barrier((up, down, ret))
+    up, down, attn, grads = lax.optimization_barrier((up, down, attn, grads))
+    ret = pl.pallas_call(
+        mixed_kernel, out_shape=shape(32, 200, 128), out_specs=HBM,
+        scratch_shapes=[pltpu.VMEM((32, 96, 128), BF), DMA((2,))],
+        compiler_params=params(14), cost_estimate=cost(1e9, 5e6), name="mixed",
+    )(recv, attn, w_out, grads)
     up = lax.ppermute(up, AXES, y_shift(1))
     down = lax.ppermute(down, AXES, y_shift(3))
     up_far, down_far, near = pl.pallas_call(

time: 103 us -> 103 us (level)
  local copies, waits for them, and re-layouts: 2.04 us -> 0.78 us
    ppermute x1, waiting for transfers between devices: 9.76 us -> 7.72 us  [per_device(): up = lax.ppermute(up, AXES, y_shift(1))]
    all_to_all x1, waiting for transfers between devices: 1.48 us -> 3.33 us  [per_device(): back = lax.all_to_all(ret, AXES, 0, 0, tiled=True, axis_index_groups=PLANE)]
    unnamed x6 -> x10, local copies, waits for them, and re-layouts: 1.28 us -> 0.02 us
    ppermute x3, starting transfers between devices: 4.62 us -> 3.4 us  [per_device(): lax.ppermute(gain_part, AXES, y_shift(s))]
    all_to_all x1, waiting for transfers between devices: 5.55 us -> 6.76 us  [per_device(): last = lax.all_to_all(mine, AXES, 0, 0, tiled=True, axis_index_groups=CHIPS)]
    pallas_call x1 -> x3, Pallas kernels: 4.19 us -> 5.13 us  [the longest x1 3.14 us: per_device(): pl.pallas_call(token_kernel, out_shape=shape(32, 104, 128), compiler_para...]
  transfers between devices with their start and end apart: 12 -> 12, of which waited for: 6 -> 5; matrix products, arithmetic and copies ran while one was open for 1% -> 1% of each run, Pallas kernels for 10% -> 11%
where the time goes in v9:
time: 103 us
  waiting for transfers between devices  46.6 us (45%)
  Pallas kernels  27.8 us (27%)
  starting transfers between devices  26.7 us (26%)
    all_to_all x1, waiting for transfers between devices, per_device(): lax.all_to_all(packed, AXES, 0, 0, tiled=True, axis_index_groups=PLANE)  22.3 us
    pallas_call x1, Pallas kernels, per_device(): pl.pallas_call(main_kernel, out_shape=(*(shape(192, 4 * D) for _ in range...  13.3 us
    all_to_all x1, starting transfers between devices, per_device(): lax.all_to_all(packed, AXES, 0, 0, tiled=True, axis_index_groups=PLANE)  8.38 us
    ppermute x1, waiting for transfers between devices, per_device(): up = lax.ppermute(up, AXES, y_shift(1))  7.72 us
    all_to_all x1, waiting for transfers between devices, per_device(): last = lax.all_to_all(mine, AXES, 0, 0, tiled=True, axis_index_groups=CHIPS)  6.76 us
    ppermute x1, waiting for transfers between devices, per_device(): up_far = lax.ppermute(up_far, AXES, y_shift(1))  6.41 us
    all_to_all x1, starting transfers between devices, per_device(): back = lax.all_to_all(ret, AXES, 0, 0, tiled=True, axis_index_groups=PLANE)  4.12 us
    all_to_all x1, starting transfers between devices, per_device(): last = lax.all_to_all(mine, AXES, 0, 0, tiled=True, axis_index_groups=CHIPS)  3.63 us
  transfers between devices with their start and end apart: 12, of which 5 were waited for; matrix products, arithmetic and copies ran while one was open for 1% of the time, Pallas kernels for 11%

profile of v9, /device:TPU:0, one launch (start us, length us, event | category | flops | bytes accessed | tf_op | source)
XLA Modules:
  0.0 102.6 jit_solution(15379933260105185546)
XLA Ops:
  0.6 2.8 %pack.1 = bf16[32,2,16,768]{3,2,1,0:T(8,128)(2,1)} custom-call(bf16[4,128,768]{2,1,0:T(8,128)(2,1)} %tok_hbm.1, bf16[4,128,768]{2,1,0:T(8,128)(2,1)} %cot_hbm.1, s32[4,128]{1,0:T(4,128)} %les_hbm.1), custom_call_target="tpu_custom_call" | custom-call | flops 1000000000 | bytes 4000000 | tf_op jit(solution)/shard_map/pack/pallas_call | solution.py:379
  3.4 0.0 copy-start.4
  3.4 0.0 copy-start
  3.4 8.4 %all-to-all-start = ((bf16[32,2,16,768]{3,2,1,0:T(8,128)(2,1)}), bf16[32,2,16,768]{3,2,1,0:T(8,128)(2,1)S(1)}, u32[]{:S(2)}, u32[]{:S(2)}) async-start(bf16[32,2,16,768]{3,2,1,0:T(8,128)(2,1)} %pack.1), calls=%async_computation | async-start | bytes 3145728 | tf_op jit(solution)/shard_map/all_to_all | solution.py:391
  11.8 0.0 copy-done.4
  11.9 0.8 constant_dynamic-slice_fusion.feat_ref
  12.6 0.0 copy-done
  12.6 22.3 %all-to-all-done.recv_hbm.recv_ref = bf16[32,2,16,768]{3,2,1,0:T(8,128)(2,1)S(1)} async-done(((bf16[32,2,16,768]{3,2,1,0:T(8,128)(2,1)}), bf16[32,2,16,768]{3,2,1,0:T(8,128)(2,1)S(1)}, u32[]{:S(2)}, u32[]{:S(2)}) %all-to-all-start) | async-done | bytes 1572896 | tf_op jit(solution)/shard_map/all_to_all | solution.py:391
  35.0 0.0 copy-start.3
  35.0 13.3 %main.1 = (bf16[192,3072]{1,0:T(8,128)(2,1)S(1)}, bf16[192,3072]{1,0:T(8,128)(2,1)S(1)}, bf16[192,3072]{1,0:T(8,128)(2,1)S(1)}, bf16[192,3072]{1,0:T(8,128)(2,1)...) custom-call(bf16[32,2,16,768]{3,2,1,0:T(8,128)(2,1)S(1)} %all-to-all-done.recv_hbm.recv_ref, ...), custom_call_target="tpu_custom_call" | custom-call | flops 10000000000 | bytes 15000000 | tf_op jit(solution)/shard_map/main/pallas_call | solution.py:392
  48.2 0.0 copy-start.1
  48.3 0.1 collective-permute-start
  48.3 0.5 collective-permute-start.1
  48.8 0.0 copy-done.3
  48.8 3.1 %token_grads.1.grad_ref = bf16[32,104,128]{2,1,0:T(8,128)(2,1)S(1)} custom-call(bf16[32,2,16,768]{3,2,1,0:T(8,128)(2,1)S(1)} %all-to-all-done.recv_hbm.recv_ref, f32[1,768]{1,0:T(1,128)S(1)} %reshape.19.gain_ref, bf16[512,2304]{1,0:T(8,128)(2,1)S(1)} %get-tuple-element.31.dqkv_ref, bf16[768,2304]{1,0:T(8,128)(2,1)S(1)} %copy-done.3), custom_call_target="tpu_custom_call" | custom-call | flops 2800000000 | bytes 9000000 | tf_op jit(solution)/shard_map/token_grads/pallas_call | solution.py:405
  52.0 0.0 copy-done.1
  52.0 0.0 collective-permute-done.b_ref
  52.0 1.2 %pair_sum.1 = (bf16[96,3072]{1,0:T(8,128)(2,1)}, bf16[96,3072]{1,0:T(8,128)(2,1)}) custom-call(bf16[192,3072]{1,0:T(8,128)(2,1)S(1)} %get-tuple-element.26.a_ref, bf16[192,3072]{1,0:T(8,128)(2,1)S(1)} %collective-permute-done.b_ref), custom_call_target="tpu_custom_call" | custom-call | flops 1000000 | bytes 3000000 | tf_op jit(solution)/shard_map/pair_sum/pallas_call | solution.py:409
  53.2 1.6 %collective-permute-start.2 = (bf16[96,3072]{1,0:T(8,128)(2,1)}, bf16[96,3072]{1,0:T(8,128)(2,1)}, u32[]{:S(2)}, u32[]{:S(2)}) collective-permute-start(bf16[96,3072]{1,0:T(8,128)(2,1)} %get-tuple-element.38), channel_id=1, source_target_pairs={{0,1},{1,2},{2,3},{3,0},{4,5},{5,6},{6,7},{7,4},{8,9},{9,10},{10,1... | collective-permute-start | bytes 1769480 | tf_op jit(solution)/shard_map/ppermute | solution.py:419
  54.8 1.7 %collective-permute-start.3 = (bf16[96,3072]{1,0:T(8,128)(2,1)}, bf16[96,3072]{1,0:T(8,128)(2,1)}, u32[]{:S(2)}, u32[]{:S(2)}) collective-permute-start(bf16[96,3072]{1,0:T(8,128)(2,1)} %get-tuple-element.39), channel_id=1, source_target_pairs={{0,3},{1,0},{2,1},{3,2},{4,7},{5,4},{6,5},{7,6},{8,11},{9,8},{10,9... | collective-permute-start | bytes 1769480 | tf_op jit(solution)/shard_map/ppermute | solution.py:420
  56.5 2.0 %mixed.1 = bf16[32,200,128]{2,1,0:T(8,128)(2,1)} custom-call(bf16[32,2,16,768]{3,2,1,0:T(8,128)(2,1)S(1)} %all-to-all-done.recv_hbm.recv_ref, bf16[512,768]{1,0:T(8,128)(2,1)S(1)} %get-tuple-element.32.attn_ref, bf16[768,768]{1,0:T(8,128)(2,1)S(1)} %copy-done, bf16[32,104,128]{2,1,0:T(8,128)(2,1)S(1)} %token_grads.1.grad_ref), custom_call_target="tpu_custom_call" | custom-call | flops 1000000000 | bytes 5000000 | tf_op jit(solution)/shard_map/mixed/pallas_call | solution.py:414
  58.5 0.0 copy-start.2
  58.5 4.1 %all-to-all-start.1 = ((bf16[32,200,128]{2,1,0:T(8,128)(2,1)}), bf16[32,200,128]{2,1,0:T(8,128)(2,1)S(1)}, u32[]{:S(2)}, u32[]{:S(2)}) async-start(bf16[32,200,128]{2,1,0:T(8,128)(2,1)} %mixed.1), calls=%async_computation.1 | async-start | bytes 3276800 | tf_op jit(solution)/shard_map/all_to_all | solution.py:428
  62.6 0.0 collective-permute-done.1.b_ref
  62.6 7.7 %collective-permute-done.2.up = bf16[96,3072]{1,0:T(8,128)(2,1)} collective-permute-done((bf16[96,3072]{1,0:T(8,128)(2,1)}, bf16[96,3072]{1,0:T(8,128)(2,1)}, u32[]{:S(2)}, u32[]{:S(2)}) %collective-permute-start.2) | collective-permute-done | bytes 589856 | tf_op jit(solution)/shard_map/ppermute | solution.py:419
  70.3 0.0 collective-permute-done.3.down
  70.3 0.0 copy-done.2
  70.3 2.0 %pass_on.1 = (bf16[96,1536]{1,0:T(8,128)(2,1)S(1)}, bf16[96,1536]{1,0:T(8,128)(2,1)S(1)}, f32[96,3072]{1,0:T(8,128)S(1)}) custom-call(bf16[192,3072]{1,0:T(8,128)(2,1)S(1)} %copy-done.2, bf16[192,3072]{1,0:T(8,128)(2,1)} %collective-permute-done.1.b_ref, bf16[96,3072]{1,0:T(8,128)(2,1)} %collective-permute-done.2.up, ...), custom_call_target="tpu_custom_call" | custom-call | flops 1000000 | bytes 3000000 | tf_op jit(solution)/shard_map/pass_on/pallas_call | solution.py:421
  72.3 1.6 %collective-permute-start.4 = (bf16[96,1536]{1,0:T(8,128)(2,1)S(1)}, bf16[96,1536]{1,0:T(8,128)(2,1)S(1)}, u32[]{:S(2)}, u32[]{:S(2)}) collective-permute-start(bf16[96,1536]{1,0:T(8,128)(2,1)S(1)} %get-tuple-element.41), channel_id=1, source_target_pairs={{0,1},{1,2},{2,3},{3,0},{4,5},{5,6},{6,7},{7,4},{8,9},{9,10},{10,1... | collective-permute-start | bytes 884744 | tf_op jit(solution)/shard_map/ppermute | solution.py:426
  74.0 1.7 %collective-permute-start.5 = (bf16[96,1536]{1,0:T(8,128)(2,1)S(1)}, bf16[96,1536]{1,0:T(8,128)(2,1)S(1)}, u32[]{:S(2)}, u32[]{:S(2)}) collective-permute-start(bf16[96,1536]{1,0:T(8,128)(2,1)S(1)} %get-tuple-element.42), channel_id=1, source_target_pairs={{0,3},{1,0},{2,1},{3,2},{4,7},{5,4},{6,5},{7,6},{8,11},{9,8},{10,9... | collective-permute-start | bytes 884744 | tf_op jit(solution)/shard_map/ppermute | solution.py:427
  75.7 6.4 %collective-permute-done.4.up_far = bf16[96,1536]{1,0:T(8,128)(2,1)S(1)} collective-permute-done((bf16[96,1536]{1,0:T(8,128)(2,1)S(1)}, bf16[96,1536]{1,0:T(8,128)(2,1)S(1)}, u32[]{:S(2)}, u32[]{:S(2)}) %collective-permute-start.4) | collective-permute-done | bytes 294944 | tf_op jit(solution)/shard_map/ppermute | solution.py:426
  82.1 0.0 collective-permute-done.5.down_far
  82.1 1.0 %ring_sum.1 = bf16[16,144,128]{2,1,0:T(8,128)(2,1)} custom-call(f32[96,3072]{1,0:T(8,128)S(1)} %get-tuple-element.40.near, bf16[96,1536]{1,0:T(8,128)(2,1)S(1)} %collective-permute-done.4.up_far, bf16[96,1536]{1,0:T(8,128)(2,1)S(1)} %collective-permute-done.5.down_far), custom_call_target="tpu_custom_call" | custom-call | flops 10000000000 | bytes 3000000 | tf_op jit(solution)/shard_map/ring_sum/pallas_call | solution.py:429
  83.1 3.3 %all-to-all-done.1.in_ref = bf16[32,200,128]{2,1,0:T(8,128)(2,1)S(1)} async-done(((bf16[32,200,128]{2,1,0:T(8,128)(2,1)}), bf16[32,200,128]{2,1,0:T(8,128)(2,1)S(1)}, u32[]{:S(2)}, u32[]{:S(2)}) %all-to-all-start.1) | async-done | bytes 1638432 | tf_op jit(solution)/shard_map/all_to_all | solution.py:428
  86.4 3.6 %all-to-all-start.2 = ((bf16[16,144,128]{2,1,0:T(8,128)(2,1)}), bf16[16,144,128]{2,1,0:T(8,128)(2,1)S(1)}, u32[]{:S(2)}, u32[]{:S(2)}) async-start(bf16[16,144,128]{2,1,0:T(8,128)(2,1)} %ring_sum.1), calls=%async_computation.2 | async-start | bytes 1179648 | tf_op jit(solution)/shard_map/all_to_all | solution.py:438
  90.1 1.7 %unpack.1 = (bf16[4,128,768]{2,1,0:T(8,128)(2,1)}, bf16[4,128,768]{2,1,0:T(8,128)(2,1)}, f32[8,128]{1,0:T(8,128)S(1)}) custom-call(bf16[32,200,128]{2,1,0:T(8,128)(2,1)S(1)} %all-to-all-done.1.in_ref), custom_call_target="tpu_custom_call" | custom-call | flops 1000000000 | bytes 4000000 | tf_op jit(solution)/shard_map/unpack/pallas_call | solution.py:433
  91.7 1.8 %collective-permute-start.8 = (f32[8,128]{1,0:T(8,128)S(1)}, f32[8,128]{1,0:T(8,128)S(1)}, u32[]{:S(2)}, u32[]{:S(2)}) collective-permute-start(f32[8,128]{1,0:T(8,128)S(1)} %get-tuple-element.43.g0), channel_id=1, source_target_pairs={{0,3},{1,0},{2,1},{3,2},{4,7},{5,4},{6,5},{7,6},{8,11},{9,8},{10,9... | collective-permute-start | bytes 12296 | tf_op jit(solution)/shard_map/ppermute | solution.py:439
  93.5 0.6 collective-permute-start.7
  94.2 1.0 collective-permute-start.6
  95.1 6.8 %all-to-all-done.2.in_ref = bf16[16,144,128]{2,1,0:T(8,128)(2,1)S(1)} async-done(((bf16[16,144,128]{2,1,0:T(8,128)(2,1)}), bf16[16,144,128]{2,1,0:T(8,128)(2,1)S(1)}, u32[]{:S(2)}, u32[]{:S(2)}) %all-to-all-start.2) | async-done | bytes 589856 | tf_op jit(solution)/shard_map/all_to_all | solution.py:438
  101.9 0.0 collective-permute-done.8.g3
  101.9 0.0 collective-permute-done.7.g2
  101.9 0.0 collective-permute-done.6.g1
  101.9 0.7 final.1
  (2 shorter events, 0.0 us)
Async XLA Ops:
  3.4 8.4 %copy-start.4 = (f32[768]{0:T(1024)S(1)}, f32[768]{0:T(1024)}, u32[]{:S(2)}) copy-start(f32[768]{0:T(1024)} %param.12) | copy-start | bytes 9220
  3.4 9.2 %copy-start = (bf16[768,768]{1,0:T(8,128)(2,1)S(1)}, bf16[768,768]{1,0:T(8,128)(2,1)}, u32[]{:S(2)}) copy-start(bf16[768,768]{1,0:T(8,128)(2,1)} %wout_ref.3) | copy-start | bytes 3538948
  3.4 31.5 %all-to-all-start = ((bf16[32,2,16,768]{3,2,1,0:T(8,128)(2,1)}), bf16[32,2,16,768]{3,2,1,0:T(8,128)(2,1)S(1)}, u32[]{:S(2)}, u32[]{:S(2)}) async-start(bf16[32,2,16,768]{3,2,1,0:T(8,128)(2,1)} %pack.1), calls=%async_computation | async-start | bytes 3145728 | tf_op jit(solution)/shard_map/all_to_all | solution.py:391
  35.0 13.9 %copy-start.3 = (bf16[768,2304]{1,0:T(8,128)(2,1)S(1)}, bf16[768,2304]{1,0:T(8,128)(2,1)}, u32[]{:S(2)}) copy-start(bf16[768,2304]{1,0:T(8,128)(2,1)} %wqkv_ref.1) | copy-start | bytes 10616836
  48.2 3.8 %copy-start.1 = (bf16[192,3072]{1,0:T(8,128)(2,1)}, bf16[192,3072]{1,0:T(8,128)(2,1)S(1)}, u32[]{:S(2)}) copy-start(bf16[192,3072]{1,0:T(8,128)(2,1)S(1)} %get-tuple-element.36.a_ref) | copy-start | bytes 3538948
  48.3 3.8 %collective-permute-start = (bf16[192,3072]{1,0:T(8,128)(2,1)S(1)}, bf16[192,3072]{1,0:T(8,128)(2,1)S(1)}, u32[]{:S(2)}, u32[]{:S(2)}) collective-permute-start(bf16[192,3072]{1,0:T(8,128)(2,1)S(1)} %get-tuple-element.27), channel_id=1, source_target_pairs={{0,8},{1,9},{2,10},{3,11},{4,12},{5,13},{6,14},{7,15},{8,0},{9,1},... | collective-permute-start | bytes 3538952 | tf_op jit(solution)/shard_map/ppermute | solution.py:403
  48.3 14.3 %collective-permute-start.1 = (bf16[192,3072]{1,0:T(8,128)(2,1)}, bf16[192,3072]{1,0:T(8,128)(2,1)}, u32[]{:S(2)}, u32[]{:S(2)}) collective-permute-start(bf16[192,3072]{1,0:T(8,128)(2,1)} %get-tuple-element.37), channel_id=1, source_target_pairs={{0,8},{1,9},{2,10},{3,11},{4,12},{5,13},{6,14},{7,15},{8,0},{9,1},... | collective-permute-start | bytes 3538952 | tf_op jit(solution)/shard_map/ppermute | solution.py:404
  53.2 17.1 %collective-permute-start.2 = (bf16[96,3072]{1,0:T(8,128)(2,1)}, bf16[96,3072]{1,0:T(8,128)(2,1)}, u32[]{:S(2)}, u32[]{:S(2)}) collective-permute-start(bf16[96,3072]{1,0:T(8,128)(2,1)} %get-tuple-element.38), channel_id=1, source_target_pairs={{0,1},{1,2},{2,3},{3,0},{4,5},{5,6},{6,7},{7,4},{8,9},{9,10},{10,1... | collective-permute-start | bytes 1769480 | tf_op jit(solution)/shard_map/ppermute | solution.py:419
  54.8 15.5 %collective-permute-start.3 = (bf16[96,3072]{1,0:T(8,128)(2,1)}, bf16[96,3072]{1,0:T(8,128)(2,1)}, u32[]{:S(2)}, u32[]{:S(2)}) collective-permute-start(bf16[96,3072]{1,0:T(8,128)(2,1)} %get-tuple-element.39), channel_id=1, source_target_pairs={{0,3},{1,0},{2,1},{3,2},{4,7},{5,4},{6,5},{7,6},{8,11},{9,8},{10,9... | collective-permute-start | bytes 1769480 | tf_op jit(solution)/shard_map/ppermute | solution.py:420
  58.5 11.9 %copy-start.2 = (bf16[192,3072]{1,0:T(8,128)(2,1)S(1)}, bf16[192,3072]{1,0:T(8,128)(2,1)}, u32[]{:S(2)}) copy-start(bf16[192,3072]{1,0:T(8,128)(2,1)} %copy-done.1) | copy-start | bytes 3538948
  58.5 28.0 %all-to-all-start.1 = ((bf16[32,200,128]{2,1,0:T(8,128)(2,1)}), bf16[32,200,128]{2,1,0:T(8,128)(2,1)S(1)}, u32[]{:S(2)}, u32[]{:S(2)}) async-start(bf16[32,200,128]{2,1,0:T(8,128)(2,1)} %mixed.1), calls=%async_computation.1 | async-start | bytes 3276800 | tf_op jit(solution)/shard_map/all_to_all | solution.py:428
  72.3 9.7 %collective-permute-start.4 = (bf16[96,1536]{1,0:T(8,128)(2,1)S(1)}, bf16[96,1536]{1,0:T(8,128)(2,1)S(1)}, u32[]{:S(2)}, u32[]{:S(2)}) collective-permute-start(bf16[96,1536]{1,0:T(8,128)(2,1)S(1)} %get-tuple-element.41), channel_id=1, source_target_pairs={{0,1},{1,2},{2,3},{3,0},{4,5},{5,6},{6,7},{7,4},{8,9},{9,10},{10,1... | collective-permute-start | bytes 884744 | tf_op jit(solution)/shard_map/ppermute | solution.py:426
  74.0 8.1 %collective-permute-start.5 = (bf16[96,1536]{1,0:T(8,128)(2,1)S(1)}, bf16[96,1536]{1,0:T(8,128)(2,1)S(1)}, u32[]{:S(2)}, u32[]{:S(2)}) collective-permute-start(bf16[96,1536]{1,0:T(8,128)(2,1)S(1)} %get-tuple-element.42), channel_id=1, source_target_pairs={{0,3},{1,0},{2,1},{3,2},{4,7},{5,4},{6,5},{7,6},{8,11},{9,8},{10,9... | collective-permute-start | bytes 884744 | tf_op jit(solution)/shard_map/ppermute | solution.py:427
  86.4 15.5 %all-to-all-start.2 = ((bf16[16,144,128]{2,1,0:T(8,128)(2,1)}), bf16[16,144,128]{2,1,0:T(8,128)(2,1)S(1)}, u32[]{:S(2)}, u32[]{:S(2)}) async-start(bf16[16,144,128]{2,1,0:T(8,128)(2,1)} %ring_sum.1), calls=%async_computation.2 | async-start | bytes 1179648 | tf_op jit(solution)/shard_map/all_to_all | solution.py:438
  91.7 10.2 %collective-permute-start.8 = (f32[8,128]{1,0:T(8,128)S(1)}, f32[8,128]{1,0:T(8,128)S(1)}, u32[]{:S(2)}, u32[]{:S(2)}) collective-permute-start(f32[8,128]{1,0:T(8,128)S(1)} %get-tuple-element.43.g0), channel_id=1, source_target_pairs={{0,3},{1,0},{2,1},{3,2},{4,7},{5,4},{6,5},{7,6},{8,11},{9,8},{10,9... | collective-permute-start | bytes 12296 | tf_op jit(solution)/shard_map/ppermute | solution.py:439
  93.5 8.4 %collective-permute-start.7 = (f32[8,128]{1,0:T(8,128)S(1)}, f32[8,128]{1,0:T(8,128)S(1)}, u32[]{:S(2)}, u32[]{:S(2)}) collective-permute-start(f32[8,128]{1,0:T(8,128)S(1)} %get-tuple-element.43.g0), channel_id=1, source_target_pairs={{0,2},{1,3},{2,0},{3,1},{4,6},{5,7},{6,4},{7,5},{8,10},{9,11},{10,... | collective-permute-start | bytes 12296 | tf_op jit(solution)/shard_map/ppermute | solution.py:439
  94.2 7.7 %collective-permute-start.6 = (f32[8,128]{1,0:T(8,128)S(1)}, f32[8,128]{1,0:T(8,128)S(1)}, u32[]{:S(2)}, u32[]{:S(2)}) collective-permute-start(f32[8,128]{1,0:T(8,128)S(1)} %get-tuple-element.43.g0), channel_id=1, source_target_pairs={{0,1},{1,2},{2,3},{3,0},{4,5},{5,6},{6,7},{7,4},{8,9},{9,10},{10,1... | collective-permute-start | bytes 12296 | tf_op jit(solution)/shard_map/ppermute | solution.py:439

commit v10 on v6

--- a/solution.py
+++ b/solution.py
@@ -126,12 +126,22 @@
     def block(ref, n):
         return jnp.concatenate([ref[d, n * 32 : n * 32 + 32] for d in range(4)], axis=0)
 
+    stores = []
+
+    def put(which, n, x):
+        out_ref[which, n * 8 : n * 8 + 8] = x.reshape(8, 16, D)
+        store = pltpu.make_async_copy(
+            out_ref.at[which, pl.ds(n * 8, 8)],
+            out_hbm.at[pl.ds(n * 8, 8), which],
+            sems.at[3 + which * 4 + n],
+        )
+        store.start()
+        stores.append(store)
+
     loads[1].wait()
     for n in range(4):
         t = dot(plain, block(tok_ref, n), 1, 0).astype(BF)
-        out_ref[0, n * 8 : n * 8 + 8] = t.reshape(8, 16, D)
-    store_t = pltpu.make_async_copy(out_ref.at[0], out_hbm.at[:, 0], sems.at[3])
-    store_t.start()
+        put(0, n, t)
     loads[0].wait()
     weight = 1.0 + LESION_GAIN * les_ref[...].astype(F32)
     loads[2].wait()
@@ -139,11 +149,9 @@
         row = jnp.concatenate([weight[d : d + 1, n * 32 : n * 32 + 32] for d in range(4)], axis=1)
         scaled = jnp.where(mask, row, 0.0).astype(BF)
         g = dot(scaled, block(cot_ref, n), 1, 0).astype(BF)
-        out_ref[1, n * 8 : n * 8 + 8] = g.reshape(8, 16, D)
-    store_g = pltpu.make_async_copy(out_ref.at[1], out_hbm.at[:, 1], sems.at[4])
-    store_g.start()
-    store_t.wait()
-    store_g.wait()
+        put(1, n, g)
+    for c in stores:
+        c.wait()
 
 
 def unpack_kernel(in_ref, mixed_ref, grad_ref, gain_ref):
@@ -279,20 +287,27 @@
     store_g = pltpu.make_async_copy(grad_ref, ret_hbm.at[:, 96:], sems.at[0])
     store_g.start()
     attn = by_source(attn_ref[...])
-    proj = dot(attn, wout_ref[...], 1, 0).astype(BF)
-    mixed = (recv_ref[:, 0].reshape(TOK, D).astype(F32) + proj.astype(F32)).astype(BF)
-    for l in range(6):
-        ret_ref[:, l * 16 : l * 16 + 16] = mixed[:, l * 128 : l * 128 + 128].reshape(32, 16, 128)
-    store_m = pltpu.make_async_copy(ret_ref, ret_hbm.at[:, :96], sems.at[1])
-    store_m.start()
-    store_g.wait()
-    store_m.wait()
+    stores = [store_g]
+    for n in range(2):
+        proj = dot(attn[n * 256 : n * 256 + 256], wout_ref[...], 1, 0).astype(BF)
+        x = recv_ref[n * 16 : n * 16 + 16, 0].reshape(256, D).astype(F32)
+        mixed = (x + proj.astype(F32)).astype(BF)
+        for l in range(6):
+            ret_ref[n * 16 : n * 16 + 16, l * 16 : l * 16 + 16] = mixed[
+                :, l * 128 : l * 128 + 128
+            ].reshape(16, 16, 128)
+        part = pl.ds(n * 16, 16)
+        store = pltpu.make_async_copy(ret_ref.at[part], ret_hbm.at[part, :96], sems.at[1 + n])
+        store.start()
+        stores.append(store)
+    for c in stores:
+        c.wait()
 
 
 HALF = 2 * D
 
 
-def pair_sum_kernel(a_ref, b_ref, own, up, down, hold):
+def pair_sum_kernel(a_ref, b_ref, own, up_hbm, down_hbm, hold, up, down, sems):
     def block(n, cols):
         rows = slice(n * 96, n * 96 + 96)
         return (a_ref[rows, cols].astype(F32) + b_ref[rows, cols].astype(F32)).astype(BF)
@@ -300,26 +315,33 @@
     left, right = slice(0, HALF), slice(HALF, 2 * HALF)
     up[:, left] = block(2, left)
     up[:, right] = block(1, right)
+    store_up = pltpu.make_async_copy(up, up_hbm, sems.at[0])
+    store_up.start()
     down[:, left] = block(3, left)
     down[:, right] = block(2, right)
+    store_down = pltpu.make_async_copy(down, down_hbm, sems.at[1])
+    store_down.start()
     own[:, left] = block(0, left)
     own[:, right] = block(0, right)
     hold[:, left] = block(1, left)
     hold[:, right] = block(3, right)
-
-
-def pass_on_kernel(hold, up, down, up_out, down_out):
+    store_up.wait()
+    store_down.wait()
+
+
+def pass_on_kernel(hold, up, down, own, up_out, down_out, sum_out):
     left, right = slice(0, HALF), slice(HALF, 2 * HALF)
     up_out[...] = (hold[:, left].astype(F32) + up[:, left].astype(F32)).astype(BF)
     down_out[...] = (hold[:, right].astype(F32) + down[:, right].astype(F32)).astype(BF)
-
-
-def ring_sum_kernel(own, up, down, up_far, down_far, o):
-    left, right = slice(0, HALF), slice(HALF, 2 * HALF)
+    sum_out[:, left] = own[:, left].astype(F32) + down[:, left].astype(F32)
+    sum_out[:, right] = own[:, right].astype(F32) + up[:, right].astype(F32)
+
+
+def ring_sum_kernel(near, up_far, down_far, o):
     for q in range(4):
         r = slice(q * 24, q * 24 + 24)
-        x = own[r, left].astype(F32) + down[r, left].astype(F32) + up_far[r].astype(F32)
-        y = own[r, right].astype(F32) + up[r, right].astype(F32) + down_far[r].astype(F32)
+        x = near[r, :HALF] + up_far[r].astype(F32)
+        y = near[r, HALF:] + down_far[r].astype(F32)
         for k in range(4):
             pieces = [
                 v[k * 6 : k * 6 + 6, l * 128 : l * 128 + 128] for v in (x, y) for l in range(12)
@@ -345,7 +367,7 @@
 
 
 def params(mb):
-    return pltpu.CompilerParams(vmem_limit_bytes=mb * MB)
+    return pltpu.CompilerParams(vmem_limit_bytes=int(mb * MB))
 
 
 def cost(flops, nbytes):
@@ -371,7 +393,7 @@
         pack_kernel, out_shape=shape(32, 2, 16, D), in_specs=[HBM] * 3, out_specs=HBM,
         scratch_shapes=[
             pltpu.VMEM((4, 128, D), BF), pltpu.VMEM((4, 128, D), BF), pltpu.VMEM((4, 128), jnp.int32),
-            pltpu.VMEM((2, 32, 16, D), BF), DMA((5,)),
+            pltpu.VMEM((2, 32, 16, D), BF), DMA((11,)),
         ],
         compiler_params=params(60), cost_estimate=cost(1e9, 4e6), name="pack",
     )(tokens, cotangent, lesion)
@@ -394,27 +416,30 @@
     )(recv, gain, dqkv, w_qkv)
     ret = pl.pallas_call(
         mixed_kernel, out_shape=shape(32, 200, 128), out_specs=HBM,
-        scratch_shapes=[pltpu.VMEM((32, 96, 128), BF), DMA((2,))],
+        scratch_shapes=[pltpu.VMEM((32, 96, 128), BF), DMA((3,))],
         compiler_params=params(14), cost_estimate=cost(1e9, 5e6), name="mixed",
     )(recv, attn, w_out, grads)
     quarters = pl.pallas_call(
         pair_sum_kernel, out_shape=tuple(shape(96, 4 * D) for _ in range(4)),
+        out_specs=(VM, HBM, HBM, VM),
+        scratch_shapes=[pltpu.VMEM((96, 4 * D), BF), pltpu.VMEM((96, 4 * D), BF), DMA((2,))],
         compiler_params=params(6), cost_estimate=cost(1e6, 7e6), name="pair_sum",
     )(keep, got)
     own, up, down, hold, ret = lax.optimization_barrier((*quarters, ret))
     up = lax.ppermute(up, AXES, y_shift(1))
     down = lax.ppermute(down, AXES, y_shift(3))
-    up_far, down_far = pl.pallas_call(
-        pass_on_kernel, out_shape=(shape(96, HALF), shape(96, HALF)),
+    up_far, down_far, near = pl.pallas_call(
+        pass_on_kernel,
+        out_shape=(shape(96, HALF), shape(96, HALF), shape(96, 4 * D, dtype=F32)),
         compiler_params=params(6), cost_estimate=cost(PASS, 3e6), name="pass_on",
-    )(hold, up, down)
+    )(hold, up, down, own)
     up_far = lax.ppermute(up_far, AXES, y_shift(1))
     down_far = lax.ppermute(down_far, AXES, y_shift(3))
     back = lax.all_to_all(ret, AXES, 0, 0, tiled=True, axis_index_groups=PLANE)
     mine = pl.pallas_call(
         ring_sum_kernel, out_shape=shape(16, 144, 128),
         compiler_params=params(6), cost_estimate=cost(RING, 3e6), name="ring_sum",
-    )(own, up, down, up_far, down_far)
+    )(near, up_far, down_far)
     mixed, grad_tokens, gain_part = pl.pallas_call(
         unpack_kernel,
         out_shape=(shape(4, 128, D), shape(4, 128, D), shape(8, 128, dtype=F32)),

time: 103 us -> 102 us (level)
  local copies, waits for them, and re-layouts: 2.66 us -> 0.77 us
    unnamed x10 -> x6, local copies, waits for them, and re-layouts: 1.91 us -> 0.02 us
    pallas_call x1, Pallas kernels: 0.14 us -> 1.31 us  [per_device(): pl.pallas_call(pass_on_kernel, out_shape=(shape(96, HALF), shape(96, HALF...]
  transfers between devices with their start and end apart: 11 -> 11, of which waited for: 5 -> 6; matrix products, arithmetic and copies ran while one was open for 1% -> 1% of each run, Pallas kernels for 8% -> 9%
where the time goes in v10:
time: 102 us; the launch traced here: 101 us
  waiting for transfers between devices  47.3 us (46%)
  starting transfers between devices  26.3 us (26%)
  Pallas kernels  25.9 us (25%)
    all_to_all x1, waiting for transfers between devices, per_device(): lax.all_to_all(packed, AXES, 0, 0, tiled=True, axis_index_groups=PLANE)  22.4 us
    pallas_call x1, Pallas kernels, per_device(): pl.pallas_call(main_kernel, out_shape=(shape(384, 4 * D), shape(384, 4 *...  12.2 us
    ppermute x1, waiting for transfers between devices, per_device(): up = lax.ppermute(up, AXES, y_shift(1))  9.99 us
    all_to_all x1, starting transfers between devices, per_device(): lax.all_to_all(packed, AXES, 0, 0, tiled=True, axis_index_groups=PLANE)  8.38 us
    all_to_all x1, waiting for transfers between devices, per_device(): last = lax.all_to_all(mine, AXES, 0, 0, tiled=True, axis_index_groups=CHIPS)  6.75 us
    ppermute x1, waiting for transfers between devices, per_device(): up_far = lax.ppermute(up_far, AXES, y_shift(1))  6.54 us
    all_to_all x1, starting transfers between devices, per_device(): back = lax.all_to_all(ret, AXES, 0, 0, tiled=True, axis_index_groups=PLANE)  3.98 us
    all_to_all x1, starting transfers between devices, per_device(): last = lax.all_to_all(mine, AXES, 0, 0, tiled=True, axis_index_groups=CHIPS)  3.63 us
  transfers between devices with their start and end apart: 11, of which 6 were waited for; matrix products, arithmetic and copies ran while one was open for 1% of the time, Pallas kernels for 9%

profile of v10, /device:TPU:0, one launch (start us, length us, event | category | flops | bytes accessed | tf_op | source)
XLA Modules:
  0.0 101.0 jit_solution(14638339079853221065)
XLA Ops:
  0.6 2.8 %pack.1 = bf16[32,2,16,768]{3,2,1,0:T(8,128)(2,1)} custom-call(bf16[4,128,768]{2,1,0:T(8,128)(2,1)} %tok_hbm.1, bf16[4,128,768]{2,1,0:T(8,128)(2,1)} %cot_hbm.1, s32[4,128]{1,0:T(4,128)} %les_hbm.1), custom_call_target="tpu_custom_call" | custom-call | flops 1000000000 | bytes 4000000 | tf_op jit(solution)/shard_map/pack/pallas_call | solution.py:392
  3.4 0.0 copy-start.2
  3.4 0.0 copy-start
  3.5 8.4 %all-to-all-start = ((bf16[32,2,16,768]{3,2,1,0:T(8,128)(2,1)}), bf16[32,2,16,768]{3,2,1,0:T(8,128)(2,1)S(1)}, u32[]{:S(2)}, u32[]{:S(2)}) async-start(bf16[32,2,16,768]{3,2,1,0:T(8,128)(2,1)} %pack.1), calls=%async_computation | async-start | bytes 3145728 | tf_op jit(solution)/shard_map/all_to_all | solution.py:400
  11.9 0.0 copy-done.2
  11.9 0.8 constant_dynamic-slice_fusion.feat_ref
  12.6 22.4 %all-to-all-done.recv_hbm.recv_ref = bf16[32,2,16,768]{3,2,1,0:T(8,128)(2,1)S(1)} async-done(((bf16[32,2,16,768]{3,2,1,0:T(8,128)(2,1)}), bf16[32,2,16,768]{3,2,1,0:T(8,128)(2,1)S(1)}, u32[]{:S(2)}, u32[]{:S(2)}) %all-to-all-start) | async-done | bytes 1572896 | tf_op jit(solution)/shard_map/all_to_all | solution.py:400
  35.0 0.0 copy-done
  35.0 0.0 copy-start.1
  35.0 12.2 %main.1 = (bf16[384,3072]{1,0:T(8,128)(2,1)S(1)}, bf16[384,3072]{1,0:T(8,128)(2,1)S(1)}, bf16[512,768]{1,0:T(8,128)(2,1)S(1)}, bf16[512,2304]{1,0:T(8,128)(2,1)S(1)}) custom-call(bf16[32,2,16,768]{3,2,1,0:T(8,128)(2,1)S(1)} %all-to-all-done.recv_hbm.recv_ref, f32[1,768]{1,0:T(1,128)S(1)} %reshape.19.gain_ref, ...), custom_call_target="tpu_custom_call" | custom-call | flops 10000000000 | bytes 15000000 | tf_op jit(solution)/shard_map/main/pallas_call | solution.py:401
  47.2 0.3 collective-permute-start
  47.5 0.0 copy-done.1
  47.5 3.1 %token_grads.1.grad_ref = bf16[32,104,128]{2,1,0:T(8,128)(2,1)S(1)} custom-call(bf16[32,2,16,768]{3,2,1,0:T(8,128)(2,1)S(1)} %all-to-all-done.recv_hbm.recv_ref, f32[1,768]{1,0:T(1,128)S(1)} %reshape.19.gain_ref, bf16[512,2304]{1,0:T(8,128)(2,1)S(1)} %get-tuple-element.34.dqkv_ref, bf16[768,2304]{1,0:T(8,128)(2,1)S(1)} %copy-done.1), custom_call_target="tpu_custom_call" | custom-call | flops 2800000000 | bytes 9000000 | tf_op jit(solution)/shard_map/token_grads/pallas_call | solution.py:413
  50.6 1.9 %mixed.1 = bf16[32,200,128]{2,1,0:T(8,128)(2,1)} custom-call(bf16[32,2,16,768]{3,2,1,0:T(8,128)(2,1)S(1)} %all-to-all-done.recv_hbm.recv_ref, bf16[512,768]{1,0:T(8,128)(2,1)S(1)} %get-tuple-element.33.attn_ref, bf16[768,768]{1,0:T(8,128)(2,1)S(1)} %copy-done, bf16[32,104,128]{2,1,0:T(8,128)(2,1)S(1)} %token_grads.1.grad_ref), custom_call_target="tpu_custom_call" | custom-call | flops 1000000000 | bytes 5000000 | tf_op jit(solution)/shard_map/mixed/pallas_call | solution.py:417
  52.5 0.0 collective-permute-done.b_ref
  52.5 1.2 %pair_sum.1 = (bf16[96,3072]{1,0:T(8,128)(2,1)S(1)}, bf16[96,3072]{1,0:T(8,128)(2,1)}, bf16[96,3072]{1,0:T(8,128)(2,1)}, bf16[96,3072]{1,0:T(8,128)(2,1)S(1)}) custom-call(bf16[384,3072]{1,0:T(8,128)(2,1)S(1)} %get-tuple-element.27.a_ref, bf16[384,3072]{1,0:T(8,128)(2,1)S(1)} %collective-permute-done.b_ref), custom_call_target="tpu_custom_call" | custom-call | flops 1000000 | bytes 7000000 | tf_op jit(solution)/shard_map/pair_sum/pallas_call | solution.py:422
  53.7 1.7 %collective-permute-start.1 = (bf16[96,3072]{1,0:T(8,128)(2,1)}, bf16[96,3072]{1,0:T(8,128)(2,1)S(1)}, u32[]{:S(2)}, u32[]{:S(2)}) collective-permute-start(bf16[96,3072]{1,0:T(8,128)(2,1)} %get-tuple-element.39), channel_id=1, source_target_pairs={{0,1},{1,2},{2,3},{3,0},{4,5},{5,6},{6,7},{7,4},{8,9},{9,10},{10,1... | collective-permute-start | bytes 1769480 | tf_op jit(solution)/shard_map/ppermute | solution.py:429
  55.4 1.7 %collective-permute-start.2 = (bf16[96,3072]{1,0:T(8,128)(2,1)}, bf16[96,3072]{1,0:T(8,128)(2,1)}, u32[]{:S(2)}, u32[]{:S(2)}) collective-permute-start(bf16[96,3072]{1,0:T(8,128)(2,1)} %get-tuple-element.40), channel_id=1, source_target_pairs={{0,3},{1,0},{2,1},{3,2},{4,7},{5,4},{6,5},{7,6},{8,11},{9,8},{10,9... | collective-permute-start | bytes 1769480 | tf_op jit(solution)/shard_map/ppermute | solution.py:430
  57.0 4.0 %all-to-all-start.1 = ((bf16[32,200,128]{2,1,0:T(8,128)(2,1)}), bf16[32,200,128]{2,1,0:T(8,128)(2,1)S(1)}, u32[]{:S(2)}, u32[]{:S(2)}) async-start(bf16[32,200,128]{2,1,0:T(8,128)(2,1)} %mixed.1), calls=%async_computation.1 | async-start | bytes 3276800 | tf_op jit(solution)/shard_map/all_to_all | solution.py:438
  61.0 10.0 %collective-permute-done.1.up = bf16[96,3072]{1,0:T(8,128)(2,1)S(1)} collective-permute-done((bf16[96,3072]{1,0:T(8,128)(2,1)}, bf16[96,3072]{1,0:T(8,128)(2,1)S(1)}, u32[]{:S(2)}, u32[]{:S(2)}) %collective-permute-start.1) | collective-permute-done | bytes 589856 | tf_op jit(solution)/shard_map/ppermute | solution.py:429
  71.0 0.1 collective-permute-done.2.down
  71.1 1.3 %pass_on.1 = (bf16[96,1536]{1,0:T(8,128)(2,1)S(1)}, bf16[96,1536]{1,0:T(8,128)(2,1)S(1)}, f32[96,3072]{1,0:T(8,128)S(1)}) custom-call(bf16[96,3072]{1,0:T(8,128)(2,1)S(1)} %get-tuple-element.38.hold, bf16[96,3072]{1,0:T(8,128)(2,1)S(1)} %collective-permute-done.1.up, bf16[96,3072]{1,0:T(8,128)(2,1)} %collective-permute-done.2.down, ...), custom_call_target="tpu_custom_call" | custom-call | flops 1000000 | bytes 3000000 | tf_op jit(solution)/shard_map/pass_on/pallas_call | solution.py:431
  72.4 1.6 %collective-permute-start.3 = (bf16[96,1536]{1,0:T(8,128)(2,1)S(1)}, bf16[96,1536]{1,0:T(8,128)(2,1)S(1)}, u32[]{:S(2)}, u32[]{:S(2)}) collective-permute-start(bf16[96,1536]{1,0:T(8,128)(2,1)S(1)} %get-tuple-element.43), channel_id=1, source_target_pairs={{0,1},{1,2},{2,3},{3,0},{4,5},{5,6},{6,7},{7,4},{8,9},{9,10},{10,1... | collective-permute-start | bytes 884744 | tf_op jit(solution)/shard_map/ppermute | solution.py:436
  74.1 1.7 %collective-permute-start.4 = (bf16[96,1536]{1,0:T(8,128)(2,1)S(1)}, bf16[96,1536]{1,0:T(8,128)(2,1)S(1)}, u32[]{:S(2)}, u32[]{:S(2)}) collective-permute-start(bf16[96,1536]{1,0:T(8,128)(2,1)S(1)} %get-tuple-element.44), channel_id=1, source_target_pairs={{0,3},{1,0},{2,1},{3,2},{4,7},{5,4},{6,5},{7,6},{8,11},{9,8},{10,9... | collective-permute-start | bytes 884744 | tf_op jit(solution)/shard_map/ppermute | solution.py:437
  75.7 6.5 %collective-permute-done.3.up_far = bf16[96,1536]{1,0:T(8,128)(2,1)S(1)} collective-permute-done((bf16[96,1536]{1,0:T(8,128)(2,1)S(1)}, bf16[96,1536]{1,0:T(8,128)(2,1)S(1)}, u32[]{:S(2)}, u32[]{:S(2)}) %collective-permute-start.3) | collective-permute-done | bytes 294944 | tf_op jit(solution)/shard_map/ppermute | solution.py:436
  82.3 0.0 collective-permute-done.4.down_far
  82.3 1.0 %ring_sum.1 = bf16[16,144,128]{2,1,0:T(8,128)(2,1)} custom-call(f32[96,3072]{1,0:T(8,128)S(1)} %get-tuple-element.42.near, bf16[96,1536]{1,0:T(8,128)(2,1)S(1)} %collective-permute-done.3.up_far, bf16[96,1536]{1,0:T(8,128)(2,1)S(1)} %collective-permute-done.4.down_far), custom_call_target="tpu_custom_call" | custom-call | flops 10000000000 | bytes 3000000 | tf_op jit(solution)/shard_map/ring_sum/pallas_call | solution.py:439
  83.3 1.5 %all-to-all-done.1.in_ref = bf16[32,200,128]{2,1,0:T(8,128)(2,1)S(1)} async-done(((bf16[32,200,128]{2,1,0:T(8,128)(2,1)}), bf16[32,200,128]{2,1,0:T(8,128)(2,1)S(1)}, u32[]{:S(2)}, u32[]{:S(2)}) %all-to-all-start.1) | async-done | bytes 1638432 | tf_op jit(solution)/shard_map/all_to_all | solution.py:438
  84.8 3.6 %all-to-all-start.2 = ((bf16[16,144,128]{2,1,0:T(8,128)(2,1)}), bf16[16,144,128]{2,1,0:T(8,128)(2,1)S(1)}, u32[]{:S(2)}, u32[]{:S(2)}) async-start(bf16[16,144,128]{2,1,0:T(8,128)(2,1)} %ring_sum.1), calls=%async_computation.2 | async-start | bytes 1179648 | tf_op jit(solution)/shard_map/all_to_all | solution.py:448
  88.5 1.7 %unpack.1 = (bf16[4,128,768]{2,1,0:T(8,128)(2,1)}, bf16[4,128,768]{2,1,0:T(8,128)(2,1)}, f32[8,128]{1,0:T(8,128)S(1)}) custom-call(bf16[32,200,128]{2,1,0:T(8,128)(2,1)S(1)} %all-to-all-done.1.in_ref), custom_call_target="tpu_custom_call" | custom-call | flops 1000000000 | bytes 4000000 | tf_op jit(solution)/shard_map/unpack/pallas_call | solution.py:443
  90.1 1.8 %collective-permute-start.7 = (f32[8,128]{1,0:T(8,128)S(1)}, f32[8,128]{1,0:T(8,128)S(1)}, u32[]{:S(2)}, u32[]{:S(2)}) collective-permute-start(f32[8,128]{1,0:T(8,128)S(1)} %get-tuple-element.45.g0), channel_id=1, source_target_pairs={{0,3},{1,0},{2,1},{3,2},{4,7},{5,4},{6,5},{7,6},{8,11},{9,8},{10,9... | collective-permute-start | bytes 12296 | tf_op jit(solution)/shard_map/ppermute | solution.py:449
  91.9 0.6 collective-permute-start.6
  92.6 1.0 collective-permute-start.5
  93.5 6.8 %all-to-all-done.2.in_ref = bf16[16,144,128]{2,1,0:T(8,128)(2,1)S(1)} async-done(((bf16[16,144,128]{2,1,0:T(8,128)(2,1)}), bf16[16,144,128]{2,1,0:T(8,128)(2,1)S(1)}, u32[]{:S(2)}, u32[]{:S(2)}) %all-to-all-start.2) | async-done | bytes 589856 | tf_op jit(solution)/shard_map/all_to_all | solution.py:448
  100.3 0.0 collective-permute-done.7.g3
  100.3 0.0 collective-permute-done.6.g2
  100.3 0.0 collective-permute-done.5.g1
  100.3 0.7 final.1
  (1 shorter events, 0.0 us)
Async XLA Ops:
  3.4 8.4 %copy-start.2 = (f32[768]{0:T(1024)S(1)}, f32[768]{0:T(1024)}, u32[]{:S(2)}) copy-start(f32[768]{0:T(1024)} %param.12) | copy-start | bytes 9220
  3.4 31.5 %copy-start = (bf16[768,768]{1,0:T(8,128)(2,1)S(1)}, bf16[768,768]{1,0:T(8,128)(2,1)}, u32[]{:S(2)}) copy-start(bf16[768,768]{1,0:T(8,128)(2,1)} %wout_ref.1) | copy-start | bytes 3538948
  3.5 31.5 %all-to-all-start = ((bf16[32,2,16,768]{3,2,1,0:T(8,128)(2,1)}), bf16[32,2,16,768]{3,2,1,0:T(8,128)(2,1)S(1)}, u32[]{:S(2)}, u32[]{:S(2)}) async-start(bf16[32,2,16,768]{3,2,1,0:T(8,128)(2,1)} %pack.1), calls=%async_computation | async-start | bytes 3145728 | tf_op jit(solution)/shard_map/all_to_all | solution.py:400
  35.0 12.5 %copy-start.1 = (bf16[768,2304]{1,0:T(8,128)(2,1)S(1)}, bf16[768,2304]{1,0:T(8,128)(2,1)}, u32[]{:S(2)}) copy-start(bf16[768,2304]{1,0:T(8,128)(2,1)} %wqkv_ref.1) | copy-start | bytes 10616836
  47.2 5.3 %collective-permute-start = (bf16[384,3072]{1,0:T(8,128)(2,1)S(1)}, bf16[384,3072]{1,0:T(8,128)(2,1)S(1)}, u32[]{:S(2)}, u32[]{:S(2)}) collective-permute-start(bf16[384,3072]{1,0:T(8,128)(2,1)S(1)} %get-tuple-element.28), channel_id=1, source_target_pairs={{0,8},{1,9},{2,10},{3,11},{4,12},{5,13},{6,14},{7,15},{8,0},{9,1},... | collective-permute-start | bytes 7077896 | tf_op jit(solution)/shard_map/ppermute | solution.py:412
  53.7 17.3 %collective-permute-start.1 = (bf16[96,3072]{1,0:T(8,128)(2,1)}, bf16[96,3072]{1,0:T(8,128)(2,1)S(1)}, u32[]{:S(2)}, u32[]{:S(2)}) collective-permute-start(bf16[96,3072]{1,0:T(8,128)(2,1)} %get-tuple-element.39), channel_id=1, source_target_pairs={{0,1},{1,2},{2,3},{3,0},{4,5},{5,6},{6,7},{7,4},{8,9},{9,10},{10,1... | collective-permute-start | bytes 1769480 | tf_op jit(solution)/shard_map/ppermute | solution.py:429
  55.4 15.8 %collective-permute-start.2 = (bf16[96,3072]{1,0:T(8,128)(2,1)}, bf16[96,3072]{1,0:T(8,128)(2,1)}, u32[]{:S(2)}, u32[]{:S(2)}) collective-permute-start(bf16[96,3072]{1,0:T(8,128)(2,1)} %get-tuple-element.40), channel_id=1, source_target_pairs={{0,3},{1,0},{2,1},{3,2},{4,7},{5,4},{6,5},{7,6},{8,11},{9,8},{10,9... | collective-permute-start | bytes 1769480 | tf_op jit(solution)/shard_map/ppermute | solution.py:430
  57.0 27.8 %all-to-all-start.1 = ((bf16[32,200,128]{2,1,0:T(8,128)(2,1)}), bf16[32,200,128]{2,1,0:T(8,128)(2,1)S(1)}, u32[]{:S(2)}, u32[]{:S(2)}) async-start(bf16[32,200,128]{2,1,0:T(8,128)(2,1)} %mixed.1), calls=%async_computation.1 | async-start | bytes 3276800 | tf_op jit(solution)/shard_map/all_to_all | solution.py:438
  72.4 9.8 %collective-permute-start.3 = (bf16[96,1536]{1,0:T(8,128)(2,1)S(1)}, bf16[96,1536]{1,0:T(8,128)(2,1)S(1)}, u32[]{:S(2)}, u32[]{:S(2)}) collective-permute-start(bf16[96,1536]{1,0:T(8,128)(2,1)S(1)} %get-tuple-element.43), channel_id=1, source_target_pairs={{0,1},{1,2},{2,3},{3,0},{4,5},{5,6},{6,7},{7,4},{8,9},{9,10},{10,1... | collective-permute-start | bytes 884744 | tf_op jit(solution)/shard_map/ppermute | solution.py:436
  74.1 8.2 %collective-permute-start.4 = (bf16[96,1536]{1,0:T(8,128)(2,1)S(1)}, bf16[96,1536]{1,0:T(8,128)(2,1)S(1)}, u32[]{:S(2)}, u32[]{:S(2)}) collective-permute-start(bf16[96,1536]{1,0:T(8,128)(2,1)S(1)} %get-tuple-element.44), channel_id=1, source_target_pairs={{0,3},{1,0},{2,1},{3,2},{4,7},{5,4},{6,5},{7,6},{8,11},{9,8},{10,9... | collective-permute-start | bytes 884744 | tf_op jit(solution)/shard_map/ppermute | solution.py:437
  84.8 15.5 %all-to-all-start.2 = ((bf16[16,144,128]{2,1,0:T(8,128)(2,1)}), bf16[16,144,128]{2,1,0:T(8,128)(2,1)S(1)}, u32[]{:S(2)}, u32[]{:S(2)}) async-start(bf16[16,144,128]{2,1,0:T(8,128)(2,1)} %ring_sum.1), calls=%async_computation.2 | async-start | bytes 1179648 | tf_op jit(solution)/shard_map/all_to_all | solution.py:448
  90.1 10.2 %collective-permute-start.7 = (f32[8,128]{1,0:T(8,128)S(1)}, f32[8,128]{1,0:T(8,128)S(1)}, u32[]{:S(2)}, u32[]{:S(2)}) collective-permute-start(f32[8,128]{1,0:T(8,128)S(1)} %get-tuple-element.45.g0), channel_id=1, source_target_pairs={{0,3},{1,0},{2,1},{3,2},{4,7},{5,4},{6,5},{7,6},{8,11},{9,8},{10,9... | collective-permute-start | bytes 12296 | tf_op jit(solution)/shard_map/ppermute | solution.py:449
  91.9 8.4 %collective-permute-start.6 = (f32[8,128]{1,0:T(8,128)S(1)}, f32[8,128]{1,0:T(8,128)S(1)}, u32[]{:S(2)}, u32[]{:S(2)}) collective-permute-start(f32[8,128]{1,0:T(8,128)S(1)} %get-tuple-element.45.g0), channel_id=1, source_target_pairs={{0,2},{1,3},{2,0},{3,1},{4,6},{5,7},{6,4},{7,5},{8,10},{9,11},{10,... | collective-permute-start | bytes 12296 | tf_op jit(solution)/shard_map/ppermute | solution.py:449
  92.6 7.7 %collective-permute-start.5 = (f32[8,128]{1,0:T(8,128)S(1)}, f32[8,128]{1,0:T(8,128)S(1)}, u32[]{:S(2)}, u32[]{:S(2)}) collective-permute-start(f32[8,128]{1,0:T(8,128)S(1)} %get-tuple-element.45.g0), channel_id=1, source_target_pairs={{0,1},{1,2},{2,3},{3,0},{4,5},{5,6},{6,7},{7,4},{8,9},{9,10},{10,1... | collective-permute-start | bytes 12296 | tf_op jit(solution)/shard_map/ppermute | solution.py:449

commit v11 on v10

--- a/solution.py
+++ b/solution.py
@@ -51,7 +51,7 @@
     return out
 
 
-def feature_table():
+def place_table():
     table = np.zeros((8, D), np.int32)
     for c in range(2):
         for y in range(4):
@@ -63,12 +63,12 @@
                             for b in range(2):
                                 i = place(a, z, c ^ rc, b, (y + ry) % 4)
                                 for r in range(6):
-                                    table[c * 4 + y, n] = 6 * i + r
+                                    table[c * 4 + y, 6 * i + r] = n
                                     n += 1
     return table
 
 
-FEATURES = feature_table()
+PLACES = place_table()
 
 
 def dot(a, b, ca, cb):
@@ -177,7 +177,7 @@
 
 
 def main_kernel(
-    recv_hbm, gain_ref, feat_ref, wqkv_hbm, wout_hbm,
+    recv_hbm, gain_ref, place_ref, wqkv_hbm, wout_hbm,
     keep_ref, send_ref, attn_ref, dqkv_ref,
     recv_ref, wqkv_ref, wout_ref, qkv_ref, ga_ref, norm_ref, gy_ref, lhs_ref, sems,
 ):
@@ -199,12 +199,35 @@
     ga_ref[...] = dot(gy_ref[...], wout_ref[...], 1, 1).astype(BF)
     loads[2].wait()
 
-    def project(n, _):
-        cols = pl.ds(pl.multiple_of(n * 768, 768), 768)
-        qkv_ref[:, cols] = dot(norm_ref[...], wqkv_ref[:, cols], 1, 0).astype(BF)
-        return 0
-
-    lax.fori_loop(0, 3, project, 0, unroll=True)
+    def span(n, part):
+        return slice(part * D + n * 256, part * D + n * 256 + 256)
+
+    def project(n):
+        for part in range(3):
+            cols = span(n, part)
+            qkv_ref[:, cols] = dot(norm_ref[...], wqkv_ref[:, cols], 1, 0).astype(BF)
+
+    def weight_grad(n, parts):
+        for part in parts:
+            cols = span(n, part)
+            g = dot(lhs_ref[...], dqkv_ref[:, cols], 1, 0).astype(BF)
+            keep_ref[:, cols] = g[:384]
+            send_ref[:, cols] = g[384:]
+
+    pick = onehot(lax.broadcasted_iota(jnp.int32, (D, D), 0) == place_ref[...])
+
+    def turn():
+        lhs_ref[...] = dot(pick, norm_ref[...], 1, 1).astype(BF)
+
+    beside = {
+        0: lambda: project(1),
+        1: lambda: project(2),
+        2: turn,
+        3: lambda: weight_grad(0, (0, 1, 2)),
+        4: lambda: weight_grad(1, (0, 1)),
+        5: lambda: weight_grad(1, (2,)),
+    }
+    project(0)
     first = lax.broadcasted_iota(jnp.int32, (128, 128), 1) < 64
 
     def split(x):
@@ -214,8 +237,8 @@
     def stack(x):
         return jnp.concatenate([x[:, :128], x[:, 128:]], axis=0)
 
-    def heads(hp, _):
-        base = pl.multiple_of(hp * 128, 128)
+    def heads(hp):
+        base = hp * 128
         rows = [slice(p * 128, (p + 1) * 128) for p in range(4)]
         q = [qkv_ref[r, pl.ds(base, 128)] for r in rows]
         k = [qkv_ref[r, pl.ds(base + D, 128)] for r in rows]
@@ -224,6 +247,7 @@
         gb = [split(ga_ref[r, pl.ds(base, 128)]) for r in rows]
         s = [dot(k[p], qb[p], 1, 1) for p in range(4)]
         dp = [dot(v[p], gb[p], 1, 1) for p in range(4)]
+        beside[hp]()
         pb, ds = [], []
         for p in range(4):
             sp = s[p] * scale
@@ -237,21 +261,11 @@
             dqkv_ref[rows[p], pl.ds(base, 128)] = dot(stack(ds[p]), split(k[p]), 0, 0).astype(BF)
             dqkv_ref[rows[p], pl.ds(base + D, 128)] = dot(ds[p], qb[p], 1, 0).astype(BF)
             dqkv_ref[rows[p], pl.ds(base + 2 * D, 128)] = dot(pb[p], gb[p], 1, 0).astype(BF)
-        return 0
-
-    lax.fori_loop(0, HEADS // 2, heads, 0, unroll=True)
-    pick = onehot(lax.broadcasted_iota(jnp.int32, (D, D), 0) == feat_ref[...])
-    lhs_ref[...] = dot(pick, norm_ref[...], 0, 1).astype(BF)
-
-    def weight_grad(n, _):
-        cols = pl.ds(pl.multiple_of(n * 768, 768), 768)
-        g = dot(lhs_ref[...], dqkv_ref[:, cols], 1, 0).astype(BF)
-        keep_ref[:, cols] = g[:384]
-        send_ref[:, cols] = g[384:]
-        return 0
-
-    lax.fori_loop(0, 3, weight_grad, 0, unroll=True)
-    lhs_ref[...] = dot(pick, attn_ref[...], 0, 1).astype(BF)
+
+    for hp in range(HEADS // 2):
+        heads(hp)
+    weight_grad(2, (0, 1, 2))
+    lhs_ref[...] = dot(pick, attn_ref[...], 1, 1).astype(BF)
     g = dot(lhs_ref[...], gy_ref[...], 1, 0).astype(BF)
     keep_ref[:, 3 * D :] = g[:384]
     send_ref[:, 3 * D :] = g[384:]
@@ -387,7 +401,7 @@
     gain = norm_gain.reshape(1, D)
     depth = lax.axis_index("depth")
     mod = lax.axis_index("mod")
-    feat = lax.dynamic_slice(jnp.asarray(FEATURES), ((depth & 1) * 4 + (mod & 3), 0), (1, D))
+    place = lax.dynamic_slice(jnp.asarray(PLACES), ((depth & 1) * 4 + (mod & 3), 0), (1, D))
     first = ((depth * 8 + mod) * 6).astype(jnp.int32).reshape(1)
     packed = pl.pallas_call(
         pack_kernel, out_shape=shape(32, 2, 16, D), in_specs=[HBM] * 3, out_specs=HBM,
@@ -408,7 +422,7 @@
             pltpu.VMEM((TOK, D), BF), pltpu.VMEM((D, TOK), BF), DMA((3,)),
         ],
         compiler_params=params(MAIN_MB), cost_estimate=cost(1e10, 1.5e7), name="main",
-    )(recv, gain, feat, w_qkv, w_out)
+    )(recv, gain, place, w_qkv, w_out)
     got = lax.ppermute(send, AXES, CORE_SWAP)
     grads = pl.pallas_call(
         token_kernel, out_shape=shape(32, 104, 128),

time: 102 us -> 101 us (level)
  no operation moved by 1% of the time
where the time goes in v11:
time: 101 us; the launch traced here: 100 us
  waiting for transfers between devices  47.3 us (47%)
  starting transfers between devices  26.3 us (26%)
  Pallas kernels  25.2 us (25%)
    all_to_all x1, waiting for transfers between devices, per_device(): lax.all_to_all(packed, AXES, 0, 0, tiled=True, axis_index_groups=PLANE)  22.4 us
    pallas_call x1, Pallas kernels, per_device(): pl.pallas_call(main_kernel, out_shape=(shape(384, 4 * D), shape(384, 4 *...  11.5 us
    ppermute x1, waiting for transfers between devices, per_device(): up = lax.ppermute(up, AXES, y_shift(1))  9.99 us
    all_to_all x1, starting transfers between devices, per_device(): lax.all_to_all(packed, AXES, 0, 0, tiled=True, axis_index_groups=PLANE)  8.38 us
    all_to_all x1, waiting for transfers between devices, per_device(): last = lax.all_to_all(mine, AXES, 0, 0, tiled=True, axis_index_groups=CHIPS)  6.75 us
    ppermute x1, waiting for transfers between devices, per_device(): up_far = lax.ppermute(up_far, AXES, y_shift(1))  6.54 us
    all_to_all x1, starting transfers between devices, per_device(): back = lax.all_to_all(ret, AXES, 0, 0, tiled=True, axis_index_groups=PLANE)  3.98 us
    all_to_all x1, starting transfers between devices, per_device(): last = lax.all_to_all(mine, AXES, 0, 0, tiled=True, axis_index_groups=CHIPS)  3.63 us
  transfers between devices with their start and end apart: 11, of which 6 were waited for; matrix products, arithmetic and copies ran while one was open for 1% of the time, Pallas kernels for 9%

profile of v11, /device:TPU:0, one launch (start us, length us, event | category | flops | bytes accessed | tf_op | source)
XLA Modules:
  0.0 100.4 jit_solution(9880330130536197971)
XLA Ops:
  0.6 2.8 %pack.1 = bf16[32,2,16,768]{3,2,1,0:T(8,128)(2,1)} custom-call(bf16[4,128,768]{2,1,0:T(8,128)(2,1)} %tok_hbm.1, bf16[4,128,768]{2,1,0:T(8,128)(2,1)} %cot_hbm.1, s32[4,128]{1,0:T(4,128)} %les_hbm.1), custom_call_target="tpu_custom_call" | custom-call | flops 1000000000 | bytes 4000000 | tf_op jit(solution)/shard_map/pack/pallas_call | solution.py:406
  3.4 0.0 copy-start.2
  3.4 0.0 copy-start
  3.5 8.4 %all-to-all-start = ((bf16[32,2,16,768]{3,2,1,0:T(8,128)(2,1)}), bf16[32,2,16,768]{3,2,1,0:T(8,128)(2,1)S(1)}, u32[]{:S(2)}, u32[]{:S(2)}) async-start(bf16[32,2,16,768]{3,2,1,0:T(8,128)(2,1)} %pack.1), calls=%async_computation | async-start | bytes 3145728 | tf_op jit(solution)/shard_map/all_to_all | solution.py:414
  11.9 0.0 copy-done.2
  11.9 0.8 constant_dynamic-slice_fusion.place_ref
  12.6 22.4 %all-to-all-done.recv_hbm.recv_ref = bf16[32,2,16,768]{3,2,1,0:T(8,128)(2,1)S(1)} async-done(((bf16[32,2,16,768]{3,2,1,0:T(8,128)(2,1)}), bf16[32,2,16,768]{3,2,1,0:T(8,128)(2,1)S(1)}, u32[]{:S(2)}, u32[]{:S(2)}) %all-to-all-start) | async-done | bytes 1572896 | tf_op jit(solution)/shard_map/all_to_all | solution.py:414
  35.0 0.0 copy-done
  35.0 0.0 copy-start.1
  35.0 11.5 %main.1 = (bf16[384,3072]{1,0:T(8,128)(2,1)S(1)}, bf16[384,3072]{1,0:T(8,128)(2,1)S(1)}, bf16[512,768]{1,0:T(8,128)(2,1)S(1)}, bf16[512,2304]{1,0:T(8,128)(2,1)S(1)}) custom-call(bf16[32,2,16,768]{3,2,1,0:T(8,128)(2,1)S(1)} %all-to-all-done.recv_hbm.recv_ref, f32[1,768]{1,0:T(1,128)S(1)} %reshape.19.gain_ref, ...), custom_call_target="tpu_custom_call" | custom-call | flops 10000000000 | bytes 15000000 | tf_op jit(solution)/shard_map/main/pallas_call | solution.py:415
  46.5 0.3 collective-permute-start
  46.8 0.0 copy-done.1
  46.8 3.1 %token_grads.1.grad_ref = bf16[32,104,128]{2,1,0:T(8,128)(2,1)S(1)} custom-call(bf16[32,2,16,768]{3,2,1,0:T(8,128)(2,1)S(1)} %all-to-all-done.recv_hbm.recv_ref, f32[1,768]{1,0:T(1,128)S(1)} %reshape.19.gain_ref, bf16[512,2304]{1,0:T(8,128)(2,1)S(1)} %get-tuple-element.34.dqkv_ref, bf16[768,2304]{1,0:T(8,128)(2,1)S(1)} %copy-done.1), custom_call_target="tpu_custom_call" | custom-call | flops 2800000000 | bytes 9000000 | tf_op jit(solution)/shard_map/token_grads/pallas_call | solution.py:427
  50.0 1.9 %mixed.1 = bf16[32,200,128]{2,1,0:T(8,128)(2,1)} custom-call(bf16[32,2,16,768]{3,2,1,0:T(8,128)(2,1)S(1)} %all-to-all-done.recv_hbm.recv_ref, bf16[512,768]{1,0:T(8,128)(2,1)S(1)} %get-tuple-element.33.attn_ref, bf16[768,768]{1,0:T(8,128)(2,1)S(1)} %copy-done, bf16[32,104,128]{2,1,0:T(8,128)(2,1)S(1)} %token_grads.1.grad_ref), custom_call_target="tpu_custom_call" | custom-call | flops 1000000000 | bytes 5000000 | tf_op jit(solution)/shard_map/mixed/pallas_call | solution.py:431
  51.8 0.0 collective-permute-done.b_ref
  51.9 1.2 %pair_sum.1 = (bf16[96,3072]{1,0:T(8,128)(2,1)S(1)}, bf16[96,3072]{1,0:T(8,128)(2,1)}, bf16[96,3072]{1,0:T(8,128)(2,1)}, bf16[96,3072]{1,0:T(8,128)(2,1)S(1)}) custom-call(bf16[384,3072]{1,0:T(8,128)(2,1)S(1)} %get-tuple-element.27.a_ref, bf16[384,3072]{1,0:T(8,128)(2,1)S(1)} %collective-permute-done.b_ref), custom_call_target="tpu_custom_call" | custom-call | flops 1000000 | bytes 7000000 | tf_op jit(solution)/shard_map/pair_sum/pallas_call | solution.py:436
  53.0 1.7 %collective-permute-start.1 = (bf16[96,3072]{1,0:T(8,128)(2,1)}, bf16[96,3072]{1,0:T(8,128)(2,1)S(1)}, u32[]{:S(2)}, u32[]{:S(2)}) collective-permute-start(bf16[96,3072]{1,0:T(8,128)(2,1)} %get-tuple-element.39), channel_id=1, source_target_pairs={{0,1},{1,2},{2,3},{3,0},{4,5},{5,6},{6,7},{7,4},{8,9},{9,10},{10,1... | collective-permute-start | bytes 1769480 | tf_op jit(solution)/shard_map/ppermute | solution.py:443
  54.7 1.7 %collective-permute-start.2 = (bf16[96,3072]{1,0:T(8,128)(2,1)}, bf16[96,3072]{1,0:T(8,128)(2,1)}, u32[]{:S(2)}, u32[]{:S(2)}) collective-permute-start(bf16[96,3072]{1,0:T(8,128)(2,1)} %get-tuple-element.40), channel_id=1, source_target_pairs={{0,3},{1,0},{2,1},{3,2},{4,7},{5,4},{6,5},{7,6},{8,11},{9,8},{10,9... | collective-permute-start | bytes 1769480 | tf_op jit(solution)/shard_map/ppermute | solution.py:444
  56.3 4.0 %all-to-all-start.1 = ((bf16[32,200,128]{2,1,0:T(8,128)(2,1)}), bf16[32,200,128]{2,1,0:T(8,128)(2,1)S(1)}, u32[]{:S(2)}, u32[]{:S(2)}) async-start(bf16[32,200,128]{2,1,0:T(8,128)(2,1)} %mixed.1), calls=%async_computation.1 | async-start | bytes 3276800 | tf_op jit(solution)/shard_map/all_to_all | solution.py:452
  60.3 10.0 %collective-permute-done.1.up = bf16[96,3072]{1,0:T(8,128)(2,1)S(1)} collective-permute-done((bf16[96,3072]{1,0:T(8,128)(2,1)}, bf16[96,3072]{1,0:T(8,128)(2,1)S(1)}, u32[]{:S(2)}, u32[]{:S(2)}) %collective-permute-start.1) | collective-permute-done | bytes 589856 | tf_op jit(solution)/shard_map/ppermute | solution.py:443
  70.3 0.1 collective-permute-done.2.down
  70.4 1.3 %pass_on.1 = (bf16[96,1536]{1,0:T(8,128)(2,1)S(1)}, bf16[96,1536]{1,0:T(8,128)(2,1)S(1)}, f32[96,3072]{1,0:T(8,128)S(1)}) custom-call(bf16[96,3072]{1,0:T(8,128)(2,1)S(1)} %get-tuple-element.38.hold, bf16[96,3072]{1,0:T(8,128)(2,1)S(1)} %collective-permute-done.1.up, bf16[96,3072]{1,0:T(8,128)(2,1)} %collective-permute-done.2.down, ...), custom_call_target="tpu_custom_call" | custom-call | flops 1000000 | bytes 3000000 | tf_op jit(solution)/shard_map/pass_on/pallas_call | solution.py:445
  71.8 1.6 %collective-permute-start.3 = (bf16[96,1536]{1,0:T(8,128)(2,1)S(1)}, bf16[96,1536]{1,0:T(8,128)(2,1)S(1)}, u32[]{:S(2)}, u32[]{:S(2)}) collective-permute-start(bf16[96,1536]{1,0:T(8,128)(2,1)S(1)} %get-tuple-element.43), channel_id=1, source_target_pairs={{0,1},{1,2},{2,3},{3,0},{4,5},{5,6},{6,7},{7,4},{8,9},{9,10},{10,1... | collective-permute-start | bytes 884744 | tf_op jit(solution)/shard_map/ppermute | solution.py:450
  73.4 1.7 %collective-permute-start.4 = (bf16[96,1536]{1,0:T(8,128)(2,1)S(1)}, bf16[96,1536]{1,0:T(8,128)(2,1)S(1)}, u32[]{:S(2)}, u32[]{:S(2)}) collective-permute-start(bf16[96,1536]{1,0:T(8,128)(2,1)S(1)} %get-tuple-element.44), channel_id=1, source_target_pairs={{0,3},{1,0},{2,1},{3,2},{4,7},{5,4},{6,5},{7,6},{8,11},{9,8},{10,9... | collective-permute-start | bytes 884744 | tf_op jit(solution)/shard_map/ppermute | solution.py:451
  75.1 6.5 %collective-permute-done.3.up_far = bf16[96,1536]{1,0:T(8,128)(2,1)S(1)} collective-permute-done((bf16[96,1536]{1,0:T(8,128)(2,1)S(1)}, bf16[96,1536]{1,0:T(8,128)(2,1)S(1)}, u32[]{:S(2)}, u32[]{:S(2)}) %collective-permute-start.3) | collective-permute-done | bytes 294944 | tf_op jit(solution)/shard_map/ppermute | solution.py:450
  81.6 0.0 collective-permute-done.4.down_far
  81.6 1.0 %ring_sum.1 = bf16[16,144,128]{2,1,0:T(8,128)(2,1)} custom-call(f32[96,3072]{1,0:T(8,128)S(1)} %get-tuple-element.42.near, bf16[96,1536]{1,0:T(8,128)(2,1)S(1)} %collective-permute-done.3.up_far, bf16[96,1536]{1,0:T(8,128)(2,1)S(1)} %collective-permute-done.4.down_far), custom_call_target="tpu_custom_call" | custom-call | flops 10000000000 | bytes 3000000 | tf_op jit(solution)/shard_map/ring_sum/pallas_call | solution.py:453
  82.6 1.5 %all-to-all-done.1.in_ref = bf16[32,200,128]{2,1,0:T(8,128)(2,1)S(1)} async-done(((bf16[32,200,128]{2,1,0:T(8,128)(2,1)}), bf16[32,200,128]{2,1,0:T(8,128)(2,1)S(1)}, u32[]{:S(2)}, u32[]{:S(2)}) %all-to-all-start.1) | async-done | bytes 1638432 | tf_op jit(solution)/shard_map/all_to_all | solution.py:452
  84.2 3.6 %all-to-all-start.2 = ((bf16[16,144,128]{2,1,0:T(8,128)(2,1)}), bf16[16,144,128]{2,1,0:T(8,128)(2,1)S(1)}, u32[]{:S(2)}, u32[]{:S(2)}) async-start(bf16[16,144,128]{2,1,0:T(8,128)(2,1)} %ring_sum.1), calls=%async_computation.2 | async-start | bytes 1179648 | tf_op jit(solution)/shard_map/all_to_all | solution.py:462
  87.8 1.7 %unpack.1 = (bf16[4,128,768]{2,1,0:T(8,128)(2,1)}, bf16[4,128,768]{2,1,0:T(8,128)(2,1)}, f32[8,128]{1,0:T(8,128)S(1)}) custom-call(bf16[32,200,128]{2,1,0:T(8,128)(2,1)S(1)} %all-to-all-done.1.in_ref), custom_call_target="tpu_custom_call" | custom-call | flops 1000000000 | bytes 4000000 | tf_op jit(solution)/shard_map/unpack/pallas_call | solution.py:457
  89.4 1.8 %collective-permute-start.7 = (f32[8,128]{1,0:T(8,128)S(1)}, f32[8,128]{1,0:T(8,128)S(1)}, u32[]{:S(2)}, u32[]{:S(2)}) collective-permute-start(f32[8,128]{1,0:T(8,128)S(1)} %get-tuple-element.45.g0), channel_id=1, source_target_pairs={{0,3},{1,0},{2,1},{3,2},{4,7},{5,4},{6,5},{7,6},{8,11},{9,8},{10,9... | collective-permute-start | bytes 12296 | tf_op jit(solution)/shard_map/ppermute | solution.py:463
  91.3 0.6 collective-permute-start.6
  91.9 1.0 collective-permute-start.5
  92.9 6.8 %all-to-all-done.2.in_ref = bf16[16,144,128]{2,1,0:T(8,128)(2,1)S(1)} async-done(((bf16[16,144,128]{2,1,0:T(8,128)(2,1)}), bf16[16,144,128]{2,1,0:T(8,128)(2,1)S(1)}, u32[]{:S(2)}, u32[]{:S(2)}) %all-to-all-start.2) | async-done | bytes 589856 | tf_op jit(solution)/shard_map/all_to_all | solution.py:462
  99.6 0.0 collective-permute-done.7.g3
  99.6 0.0 collective-permute-done.6.g2
  99.6 0.0 collective-permute-done.5.g1
  99.6 0.7 final.1
  (1 shorter events, 0.0 us)
Async XLA Ops:
  3.4 8.4 %copy-start.2 = (f32[768]{0:T(1024)S(1)}, f32[768]{0:T(1024)}, u32[]{:S(2)}) copy-start(f32[768]{0:T(1024)} %param.12) | copy-start | bytes 9220
  3.4 31.5 %copy-start = (bf16[768,768]{1,0:T(8,128)(2,1)S(1)}, bf16[768,768]{1,0:T(8,128)(2,1)}, u32[]{:S(2)}) copy-start(bf16[768,768]{1,0:T(8,128)(2,1)} %wout_ref.1) | copy-start | bytes 3538948
  3.5 31.5 %all-to-all-start = ((bf16[32,2,16,768]{3,2,1,0:T(8,128)(2,1)}), bf16[32,2,16,768]{3,2,1,0:T(8,128)(2,1)S(1)}, u32[]{:S(2)}, u32[]{:S(2)}) async-start(bf16[32,2,16,768]{3,2,1,0:T(8,128)(2,1)} %pack.1), calls=%async_computation | async-start | bytes 3145728 | tf_op jit(solution)/shard_map/all_to_all | solution.py:414
  35.0 11.8 %copy-start.1 = (bf16[768,2304]{1,0:T(8,128)(2,1)S(1)}, bf16[768,2304]{1,0:T(8,128)(2,1)}, u32[]{:S(2)}) copy-start(bf16[768,2304]{1,0:T(8,128)(2,1)} %wqkv_ref.1) | copy-start | bytes 10616836
  46.5 5.3 %collective-permute-start = (bf16[384,3072]{1,0:T(8,128)(2,1)S(1)}, bf16[384,3072]{1,0:T(8,128)(2,1)S(1)}, u32[]{:S(2)}, u32[]{:S(2)}) collective-permute-start(bf16[384,3072]{1,0:T(8,128)(2,1)S(1)} %get-tuple-element.28), channel_id=1, source_target_pairs={{0,8},{1,9},{2,10},{3,11},{4,12},{5,13},{6,14},{7,15},{8,0},{9,1},... | collective-permute-start | bytes 7077896 | tf_op jit(solution)/shard_map/ppermute | solution.py:426
  53.0 17.3 %collective-permute-start.1 = (bf16[96,3072]{1,0:T(8,128)(2,1)}, bf16[96,3072]{1,0:T(8,128)(2,1)S(1)}, u32[]{:S(2)}, u32[]{:S(2)}) collective-permute-start(bf16[96,3072]{1,0:T(8,128)(2,1)} %get-tuple-element.39), channel_id=1, source_target_pairs={{0,1},{1,2},{2,3},{3,0},{4,5},{5,6},{6,7},{7,4},{8,9},{9,10},{10,1... | collective-permute-start | bytes 1769480 | tf_op jit(solution)/shard_map/ppermute | solution.py:443
  54.7 15.8 %collective-permute-start.2 = (bf16[96,3072]{1,0:T(8,128)(2,1)}, bf16[96,3072]{1,0:T(8,128)(2,1)}, u32[]{:S(2)}, u32[]{:S(2)}) collective-permute-start(bf16[96,3072]{1,0:T(8,128)(2,1)} %get-tuple-element.40), channel_id=1, source_target_pairs={{0,3},{1,0},{2,1},{3,2},{4,7},{5,4},{6,5},{7,6},{8,11},{9,8},{10,9... | collective-permute-start | bytes 1769480 | tf_op jit(solution)/shard_map/ppermute | solution.py:444
  56.3 27.8 %all-to-all-start.1 = ((bf16[32,200,128]{2,1,0:T(8,128)(2,1)}), bf16[32,200,128]{2,1,0:T(8,128)(2,1)S(1)}, u32[]{:S(2)}, u32[]{:S(2)}) async-start(bf16[32,200,128]{2,1,0:T(8,128)(2,1)} %mixed.1), calls=%async_computation.1 | async-start | bytes 3276800 | tf_op jit(solution)/shard_map/all_to_all | solution.py:452
  71.8 9.8 %collective-permute-start.3 = (bf16[96,1536]{1,0:T(8,128)(2,1)S(1)}, bf16[96,1536]{1,0:T(8,128)(2,1)S(1)}, u32[]{:S(2)}, u32[]{:S(2)}) collective-permute-start(bf16[96,1536]{1,0:T(8,128)(2,1)S(1)} %get-tuple-element.43), channel_id=1, source_target_pairs={{0,1},{1,2},{2,3},{3,0},{4,5},{5,6},{6,7},{7,4},{8,9},{9,10},{10,1... | collective-permute-start | bytes 884744 | tf_op jit(solution)/shard_map/ppermute | solution.py:450
  73.4 8.2 %collective-permute-start.4 = (bf16[96,1536]{1,0:T(8,128)(2,1)S(1)}, bf16[96,1536]{1,0:T(8,128)(2,1)S(1)}, u32[]{:S(2)}, u32[]{:S(2)}) collective-permute-start(bf16[96,1536]{1,0:T(8,128)(2,1)S(1)} %get-tuple-element.44), channel_id=1, source_target_pairs={{0,3},{1,0},{2,1},{3,2},{4,7},{5,4},{6,5},{7,6},{8,11},{9,8},{10,9... | collective-permute-start | bytes 884744 | tf_op jit(solution)/shard_map/ppermute | solution.py:451
  84.2 15.5 %all-to-all-start.2 = ((bf16[16,144,128]{2,1,0:T(8,128)(2,1)}), bf16[16,144,128]{2,1,0:T(8,128)(2,1)S(1)}, u32[]{:S(2)}, u32[]{:S(2)}) async-start(bf16[16,144,128]{2,1,0:T(8,128)(2,1)} %ring_sum.1), calls=%async_computation.2 | async-start | bytes 1179648 | tf_op jit(solution)/shard_map/all_to_all | solution.py:462
  89.4 10.2 %collective-permute-start.7 = (f32[8,128]{1,0:T(8,128)S(1)}, f32[8,128]{1,0:T(8,128)S(1)}, u32[]{:S(2)}, u32[]{:S(2)}) collective-permute-start(f32[8,128]{1,0:T(8,128)S(1)} %get-tuple-element.45.g0), channel_id=1, source_target_pairs={{0,3},{1,0},{2,1},{3,2},{4,7},{5,4},{6,5},{7,6},{8,11},{9,8},{10,9... | collective-permute-start | bytes 12296 | tf_op jit(solution)/shard_map/ppermute | solution.py:463
  91.3 8.4 %collective-permute-start.6 = (f32[8,128]{1,0:T(8,128)S(1)}, f32[8,128]{1,0:T(8,128)S(1)}, u32[]{:S(2)}, u32[]{:S(2)}) collective-permute-start(f32[8,128]{1,0:T(8,128)S(1)} %get-tuple-element.45.g0), channel_id=1, source_target_pairs={{0,2},{1,3},{2,0},{3,1},{4,6},{5,7},{6,4},{7,5},{8,10},{9,11},{10,... | collective-permute-start | bytes 12296 | tf_op jit(solution)/shard_map/ppermute | solution.py:463
  91.9 7.7 %collective-permute-start.5 = (f32[8,128]{1,0:T(8,128)S(1)}, f32[8,128]{1,0:T(8,128)S(1)}, u32[]{:S(2)}, u32[]{:S(2)}) collective-permute-start(f32[8,128]{1,0:T(8,128)S(1)} %get-tuple-element.45.g0), channel_id=1, source_target_pairs={{0,1},{1,2},{2,3},{3,0},{4,5},{5,6},{6,7},{7,4},{8,9},{9,10},{10,1... | collective-permute-start | bytes 12296 | tf_op jit(solution)/shard_map/ppermute | solution.py:463

commit v12 on v11

--- a/solution.py
+++ b/solution.py
@@ -343,12 +343,15 @@
     store_down.wait()
 
 
-def pass_on_kernel(hold, up, down, own, up_out, down_out, sum_out):
+def pass_on_kernel(hold, up, down_hbm, own, up_out, down_out, sum_out, down, sem):
+    load = pltpu.make_async_copy(down_hbm, down, sem)
+    load.start()
     left, right = slice(0, HALF), slice(HALF, 2 * HALF)
     up_out[...] = (hold[:, left].astype(F32) + up[:, left].astype(F32)).astype(BF)
+    sum_out[:, right] = own[:, right].astype(F32) + up[:, right].astype(F32)
+    load.wait()
     down_out[...] = (hold[:, right].astype(F32) + down[:, right].astype(F32)).astype(BF)
     sum_out[:, left] = own[:, left].astype(F32) + down[:, left].astype(F32)
-    sum_out[:, right] = own[:, right].astype(F32) + up[:, right].astype(F32)
 
 
 def ring_sum_kernel(near, up_far, down_far, o):
@@ -445,6 +448,8 @@
     up_far, down_far, near = pl.pallas_call(
         pass_on_kernel,
         out_shape=(shape(96, HALF), shape(96, HALF), shape(96, 4 * D, dtype=F32)),
+        in_specs=[VM, VM, HBM, VM],
+        scratch_shapes=[pltpu.VMEM((96, 4 * D), BF), DMA],
         compiler_params=params(6), cost_estimate=cost(PASS, 3e6), name="pass_on",
     )(hold, up, down, own)
     up_far = lax.ppermute(up_far, AXES, y_shift(1))

time: 101 us -> 101 us (level)
  no operation moved by 1% of the time
where the time goes in v12:
time: 101 us; the launch traced here: 100 us
  waiting for transfers between devices  47.4 us (47%)
  starting transfers between devices  26.3 us (26%)
  Pallas kernels  25.1 us (25%)
    all_to_all x1, waiting for transfers between devices, per_device(): lax.all_to_all(packed, AXES, 0, 0, tiled=True, axis_index_groups=PLANE)  22.4 us
    pallas_call x1, Pallas kernels, per_device(): pl.pallas_call(main_kernel, out_shape=(shape(384, 4 * D), shape(384, 4 *...  11.5 us
    ppermute x1, waiting for transfers between devices, per_device(): up = lax.ppermute(up, AXES, y_shift(1))  9.99 us
    all_to_all x1, starting transfers between devices, per_device(): lax.all_to_all(packed, AXES, 0, 0, tiled=True, axis_index_groups=PLANE)  8.38 us
    all_to_all x1, waiting for transfers between devices, per_device(): last = lax.all_to_all(mine, AXES, 0, 0, tiled=True, axis_index_groups=CHIPS)  6.75 us
    ppermute x1, waiting for transfers between devices, per_device(): up_far = lax.ppermute(up_far, AXES, y_shift(1))  6.54 us
    all_to_all x1, starting transfers between devices, per_device(): back = lax.all_to_all(ret, AXES, 0, 0, tiled=True, axis_index_groups=PLANE)  3.98 us
    all_to_all x1, starting transfers between devices, per_device(): last = lax.all_to_all(mine, AXES, 0, 0, tiled=True, axis_index_groups=CHIPS)  3.63 us
  transfers between devices with their start and end apart: 11, of which 6 were waited for; matrix products, arithmetic and copies ran while one was open for 1% of the time, Pallas kernels for 9%

profile of v12, /device:TPU:0, one launch (start us, length us, event | category | flops | bytes accessed | tf_op | source)
XLA Modules:
  0.0 100.4 jit_solution(14984894764871912677)
XLA Ops:
  0.6 2.8 %pack.1 = bf16[32,2,16,768]{3,2,1,0:T(8,128)(2,1)} custom-call(bf16[4,128,768]{2,1,0:T(8,128)(2,1)} %tok_hbm.1, bf16[4,128,768]{2,1,0:T(8,128)(2,1)} %cot_hbm.1, s32[4,128]{1,0:T(4,128)} %les_hbm.1), custom_call_target="tpu_custom_call" | custom-call | flops 1000000000 | bytes 4000000 | tf_op jit(solution)/shard_map/pack/pallas_call | solution.py:409
  3.4 0.0 copy-start.2
  3.4 0.0 copy-start
  3.5 8.4 %all-to-all-start = ((bf16[32,2,16,768]{3,2,1,0:T(8,128)(2,1)}), bf16[32,2,16,768]{3,2,1,0:T(8,128)(2,1)S(1)}, u32[]{:S(2)}, u32[]{:S(2)}) async-start(bf16[32,2,16,768]{3,2,1,0:T(8,128)(2,1)} %pack.1), calls=%async_computation | async-start | bytes 3145728 | tf_op jit(solution)/shard_map/all_to_all | solution.py:417
  11.9 0.0 copy-done.2
  11.9 0.8 constant_dynamic-slice_fusion.place_ref
  12.6 22.4 %all-to-all-done.recv_hbm.recv_ref = bf16[32,2,16,768]{3,2,1,0:T(8,128)(2,1)S(1)} async-done(((bf16[32,2,16,768]{3,2,1,0:T(8,128)(2,1)}), bf16[32,2,16,768]{3,2,1,0:T(8,128)(2,1)S(1)}, u32[]{:S(2)}, u32[]{:S(2)}) %all-to-all-start) | async-done | bytes 1572896 | tf_op jit(solution)/shard_map/all_to_all | solution.py:417
  35.0 0.0 copy-done
  35.0 0.0 copy-start.1
  35.0 11.5 %main.1 = (bf16[384,3072]{1,0:T(8,128)(2,1)S(1)}, bf16[384,3072]{1,0:T(8,128)(2,1)S(1)}, bf16[512,768]{1,0:T(8,128)(2,1)S(1)}, bf16[512,2304]{1,0:T(8,128)(2,1)S(1)}) custom-call(bf16[32,2,16,768]{3,2,1,0:T(8,128)(2,1)S(1)} %all-to-all-done.recv_hbm.recv_ref, f32[1,768]{1,0:T(1,128)S(1)} %reshape.19.gain_ref, ...), custom_call_target="tpu_custom_call" | custom-call | flops 10000000000 | bytes 15000000 | tf_op jit(solution)/shard_map/main/pallas_call | solution.py:418
  46.5 0.3 collective-permute-start
  46.8 0.0 copy-done.1
  46.8 3.1 %token_grads.1.grad_ref = bf16[32,104,128]{2,1,0:T(8,128)(2,1)S(1)} custom-call(bf16[32,2,16,768]{3,2,1,0:T(8,128)(2,1)S(1)} %all-to-all-done.recv_hbm.recv_ref, f32[1,768]{1,0:T(1,128)S(1)} %reshape.19.gain_ref, bf16[512,2304]{1,0:T(8,128)(2,1)S(1)} %get-tuple-element.34.dqkv_ref, bf16[768,2304]{1,0:T(8,128)(2,1)S(1)} %copy-done.1), custom_call_target="tpu_custom_call" | custom-call | flops 2800000000 | bytes 9000000 | tf_op jit(solution)/shard_map/token_grads/pallas_call | solution.py:430
  50.0 1.9 %mixed.1 = bf16[32,200,128]{2,1,0:T(8,128)(2,1)} custom-call(bf16[32,2,16,768]{3,2,1,0:T(8,128)(2,1)S(1)} %all-to-all-done.recv_hbm.recv_ref, bf16[512,768]{1,0:T(8,128)(2,1)S(1)} %get-tuple-element.33.attn_ref, bf16[768,768]{1,0:T(8,128)(2,1)S(1)} %copy-done, bf16[32,104,128]{2,1,0:T(8,128)(2,1)S(1)} %token_grads.1.grad_ref), custom_call_target="tpu_custom_call" | custom-call | flops 1000000000 | bytes 5000000 | tf_op jit(solution)/shard_map/mixed/pallas_call | solution.py:434
  51.8 0.0 collective-permute-done.b_ref
  51.9 1.2 %pair_sum.1 = (bf16[96,3072]{1,0:T(8,128)(2,1)S(1)}, bf16[96,3072]{1,0:T(8,128)(2,1)}, bf16[96,3072]{1,0:T(8,128)(2,1)}, bf16[96,3072]{1,0:T(8,128)(2,1)S(1)}) custom-call(bf16[384,3072]{1,0:T(8,128)(2,1)S(1)} %get-tuple-element.27.a_ref, bf16[384,3072]{1,0:T(8,128)(2,1)S(1)} %collective-permute-done.b_ref), custom_call_target="tpu_custom_call" | custom-call | flops 1000000 | bytes 7000000 | tf_op jit(solution)/shard_map/pair_sum/pallas_call | solution.py:439
  53.0 1.7 %collective-permute-start.1 = (bf16[96,3072]{1,0:T(8,128)(2,1)}, bf16[96,3072]{1,0:T(8,128)(2,1)S(1)}, u32[]{:S(2)}, u32[]{:S(2)}) collective-permute-start(bf16[96,3072]{1,0:T(8,128)(2,1)} %get-tuple-element.39), channel_id=1, source_target_pairs={{0,1},{1,2},{2,3},{3,0},{4,5},{5,6},{6,7},{7,4},{8,9},{9,10},{10,1... | collective-permute-start | bytes 1769480 | tf_op jit(solution)/shard_map/ppermute | solution.py:446
  54.7 1.7 %collective-permute-start.2 = (bf16[96,3072]{1,0:T(8,128)(2,1)}, bf16[96,3072]{1,0:T(8,128)(2,1)}, u32[]{:S(2)}, u32[]{:S(2)}) collective-permute-start(bf16[96,3072]{1,0:T(8,128)(2,1)} %get-tuple-element.40), channel_id=1, source_target_pairs={{0,3},{1,0},{2,1},{3,2},{4,7},{5,4},{6,5},{7,6},{8,11},{9,8},{10,9... | collective-permute-start | bytes 1769480 | tf_op jit(solution)/shard_map/ppermute | solution.py:447
  56.3 4.0 %all-to-all-start.1 = ((bf16[32,200,128]{2,1,0:T(8,128)(2,1)}), bf16[32,200,128]{2,1,0:T(8,128)(2,1)S(1)}, u32[]{:S(2)}, u32[]{:S(2)}) async-start(bf16[32,200,128]{2,1,0:T(8,128)(2,1)} %mixed.1), calls=%async_computation.1 | async-start | bytes 3276800 | tf_op jit(solution)/shard_map/all_to_all | solution.py:457
  60.3 10.0 %collective-permute-done.1.up = bf16[96,3072]{1,0:T(8,128)(2,1)S(1)} collective-permute-done((bf16[96,3072]{1,0:T(8,128)(2,1)}, bf16[96,3072]{1,0:T(8,128)(2,1)S(1)}, u32[]{:S(2)}, u32[]{:S(2)}) %collective-permute-start.1) | collective-permute-done | bytes 589856 | tf_op jit(solution)/shard_map/ppermute | solution.py:446
  70.3 0.1 collective-permute-done.2.down_hbm
  70.4 1.2 %pass_on.1 = (bf16[96,1536]{1,0:T(8,128)(2,1)S(1)}, bf16[96,1536]{1,0:T(8,128)(2,1)S(1)}, f32[96,3072]{1,0:T(8,128)S(1)}) custom-call(bf16[96,3072]{1,0:T(8,128)(2,1)S(1)} %get-tuple-element.38.hold, bf16[96,3072]{1,0:T(8,128)(2,1)S(1)} %collective-permute-done.1.up, bf16[96,3072]{1,0:T(8,128)(2,1)} %collective-permute-done.2.down_hbm, ...), custom_call_target="tpu_custom_call" | custom-call | flops 1000000 | bytes 3000000 | tf_op jit(solution)/shard_map/pass_on/pallas_call | solution.py:448
  71.6 1.6 %collective-permute-start.3 = (bf16[96,1536]{1,0:T(8,128)(2,1)S(1)}, bf16[96,1536]{1,0:T(8,128)(2,1)S(1)}, u32[]{:S(2)}, u32[]{:S(2)}) collective-permute-start(bf16[96,1536]{1,0:T(8,128)(2,1)S(1)} %get-tuple-element.43), channel_id=1, source_target_pairs={{0,1},{1,2},{2,3},{3,0},{4,5},{5,6},{6,7},{7,4},{8,9},{9,10},{10,1... | collective-permute-start | bytes 884744 | tf_op jit(solution)/shard_map/ppermute | solution.py:455
  73.3 1.7 %collective-permute-start.4 = (bf16[96,1536]{1,0:T(8,128)(2,1)S(1)}, bf16[96,1536]{1,0:T(8,128)(2,1)S(1)}, u32[]{:S(2)}, u32[]{:S(2)}) collective-permute-start(bf16[96,1536]{1,0:T(8,128)(2,1)S(1)} %get-tuple-element.44), channel_id=1, source_target_pairs={{0,3},{1,0},{2,1},{3,2},{4,7},{5,4},{6,5},{7,6},{8,11},{9,8},{10,9... | collective-permute-start | bytes 884744 | tf_op jit(solution)/shard_map/ppermute | solution.py:456
  74.9 6.5 %collective-permute-done.3.up_far = bf16[96,1536]{1,0:T(8,128)(2,1)S(1)} collective-permute-done((bf16[96,1536]{1,0:T(8,128)(2,1)S(1)}, bf16[96,1536]{1,0:T(8,128)(2,1)S(1)}, u32[]{:S(2)}, u32[]{:S(2)}) %collective-permute-start.3) | collective-permute-done | bytes 294944 | tf_op jit(solution)/shard_map/ppermute | solution.py:455
  81.5 0.0 collective-permute-done.4.down_far
  81.5 1.0 %ring_sum.1 = bf16[16,144,128]{2,1,0:T(8,128)(2,1)} custom-call(f32[96,3072]{1,0:T(8,128)S(1)} %get-tuple-element.42.near, bf16[96,1536]{1,0:T(8,128)(2,1)S(1)} %collective-permute-done.3.up_far, bf16[96,1536]{1,0:T(8,128)(2,1)S(1)} %collective-permute-done.4.down_far), custom_call_target="tpu_custom_call" | custom-call | flops 10000000000 | bytes 3000000 | tf_op jit(solution)/shard_map/ring_sum/pallas_call | solution.py:458
  82.5 1.6 %all-to-all-done.1.in_ref = bf16[32,200,128]{2,1,0:T(8,128)(2,1)S(1)} async-done(((bf16[32,200,128]{2,1,0:T(8,128)(2,1)}), bf16[32,200,128]{2,1,0:T(8,128)(2,1)S(1)}, u32[]{:S(2)}, u32[]{:S(2)}) %all-to-all-start.1) | async-done | bytes 1638432 | tf_op jit(solution)/shard_map/all_to_all | solution.py:457
  84.2 3.6 %all-to-all-start.2 = ((bf16[16,144,128]{2,1,0:T(8,128)(2,1)}), bf16[16,144,128]{2,1,0:T(8,128)(2,1)S(1)}, u32[]{:S(2)}, u32[]{:S(2)}) async-start(bf16[16,144,128]{2,1,0:T(8,128)(2,1)} %ring_sum.1), calls=%async_computation.2 | async-start | bytes 1179648 | tf_op jit(solution)/shard_map/all_to_all | solution.py:467
  87.8 1.7 %unpack.1 = (bf16[4,128,768]{2,1,0:T(8,128)(2,1)}, bf16[4,128,768]{2,1,0:T(8,128)(2,1)}, f32[8,128]{1,0:T(8,128)S(1)}) custom-call(bf16[32,200,128]{2,1,0:T(8,128)(2,1)S(1)} %all-to-all-done.1.in_ref), custom_call_target="tpu_custom_call" | custom-call | flops 1000000000 | bytes 4000000 | tf_op jit(solution)/shard_map/unpack/pallas_call | solution.py:462
  89.4 1.8 %collective-permute-start.7 = (f32[8,128]{1,0:T(8,128)S(1)}, f32[8,128]{1,0:T(8,128)S(1)}, u32[]{:S(2)}, u32[]{:S(2)}) collective-permute-start(f32[8,128]{1,0:T(8,128)S(1)} %get-tuple-element.45.g0), channel_id=1, source_target_pairs={{0,3},{1,0},{2,1},{3,2},{4,7},{5,4},{6,5},{7,6},{8,11},{9,8},{10,9... | collective-permute-start | bytes 12296 | tf_op jit(solution)/shard_map/ppermute | solution.py:468
  91.3 0.6 collective-permute-start.6
  91.9 1.0 collective-permute-start.5
  92.9 6.8 %all-to-all-done.2.in_ref = bf16[16,144,128]{2,1,0:T(8,128)(2,1)S(1)} async-done(((bf16[16,144,128]{2,1,0:T(8,128)(2,1)}), bf16[16,144,128]{2,1,0:T(8,128)(2,1)S(1)}, u32[]{:S(2)}, u32[]{:S(2)}) %all-to-all-start.2) | async-done | bytes 589856 | tf_op jit(solution)/shard_map/all_to_all | solution.py:467
  99.6 0.0 collective-permute-done.7.g3
  99.6 0.0 collective-permute-done.6.g2
  99.6 0.0 collective-permute-done.5.g1
  99.6 0.7 final.1
  (1 shorter events, 0.0 us)
Async XLA Ops:
  3.4 8.4 %copy-start.2 = (f32[768]{0:T(1024)S(1)}, f32[768]{0:T(1024)}, u32[]{:S(2)}) copy-start(f32[768]{0:T(1024)} %param.12) | copy-start | bytes 9220
  3.4 31.5 %copy-start = (bf16[768,768]{1,0:T(8,128)(2,1)S(1)}, bf16[768,768]{1,0:T(8,128)(2,1)}, u32[]{:S(2)}) copy-start(bf16[768,768]{1,0:T(8,128)(2,1)} %wout_ref.1) | copy-start | bytes 3538948
  3.5 31.5 %all-to-all-start = ((bf16[32,2,16,768]{3,2,1,0:T(8,128)(2,1)}), bf16[32,2,16,768]{3,2,1,0:T(8,128)(2,1)S(1)}, u32[]{:S(2)}, u32[]{:S(2)}) async-start(bf16[32,2,16,768]{3,2,1,0:T(8,128)(2,1)} %pack.1), calls=%async_computation | async-start | bytes 3145728 | tf_op jit(solution)/shard_map/all_to_all | solution.py:417
  35.0 11.8 %copy-start.1 = (bf16[768,2304]{1,0:T(8,128)(2,1)S(1)}, bf16[768,2304]{1,0:T(8,128)(2,1)}, u32[]{:S(2)}) copy-start(bf16[768,2304]{1,0:T(8,128)(2,1)} %wqkv_ref.1) | copy-start | bytes 10616836
  46.5 5.3 %collective-permute-start = (bf16[384,3072]{1,0:T(8,128)(2,1)S(1)}, bf16[384,3072]{1,0:T(8,128)(2,1)S(1)}, u32[]{:S(2)}, u32[]{:S(2)}) collective-permute-start(bf16[384,3072]{1,0:T(8,128)(2,1)S(1)} %get-tuple-element.28), channel_id=1, source_target_pairs={{0,8},{1,9},{2,10},{3,11},{4,12},{5,13},{6,14},{7,15},{8,0},{9,1},... | collective-permute-start | bytes 7077896 | tf_op jit(solution)/shard_map/ppermute | solution.py:429
  53.0 17.3 %collective-permute-start.1 = (bf16[96,3072]{1,0:T(8,128)(2,1)}, bf16[96,3072]{1,0:T(8,128)(2,1)S(1)}, u32[]{:S(2)}, u32[]{:S(2)}) collective-permute-start(bf16[96,3072]{1,0:T(8,128)(2,1)} %get-tuple-element.39), channel_id=1, source_target_pairs={{0,1},{1,2},{2,3},{3,0},{4,5},{5,6},{6,7},{7,4},{8,9},{9,10},{10,1... | collective-permute-start | bytes 1769480 | tf_op jit(solution)/shard_map/ppermute | solution.py:446
  54.7 15.8 %collective-permute-start.2 = (bf16[96,3072]{1,0:T(8,128)(2,1)}, bf16[96,3072]{1,0:T(8,128)(2,1)}, u32[]{:S(2)}, u32[]{:S(2)}) collective-permute-start(bf16[96,3072]{1,0:T(8,128)(2,1)} %get-tuple-element.40), channel_id=1, source_target_pairs={{0,3},{1,0},{2,1},{3,2},{4,7},{5,4},{6,5},{7,6},{8,11},{9,8},{10,9... | collective-permute-start | bytes 1769480 | tf_op jit(solution)/shard_map/ppermute | solution.py:447
  56.3 27.8 %all-to-all-start.1 = ((bf16[32,200,128]{2,1,0:T(8,128)(2,1)}), bf16[32,200,128]{2,1,0:T(8,128)(2,1)S(1)}, u32[]{:S(2)}, u32[]{:S(2)}) async-start(bf16[32,200,128]{2,1,0:T(8,128)(2,1)} %mixed.1), calls=%async_computation.1 | async-start | bytes 3276800 | tf_op jit(solution)/shard_map/all_to_all | solution.py:457
  71.6 9.8 %collective-permute-start.3 = (bf16[96,1536]{1,0:T(8,128)(2,1)S(1)}, bf16[96,1536]{1,0:T(8,128)(2,1)S(1)}, u32[]{:S(2)}, u32[]{:S(2)}) collective-permute-start(bf16[96,1536]{1,0:T(8,128)(2,1)S(1)} %get-tuple-element.43), channel_id=1, source_target_pairs={{0,1},{1,2},{2,3},{3,0},{4,5},{5,6},{6,7},{7,4},{8,9},{9,10},{10,1... | collective-permute-start | bytes 884744 | tf_op jit(solution)/shard_map/ppermute | solution.py:455
  73.3 8.2 %collective-permute-start.4 = (bf16[96,1536]{1,0:T(8,128)(2,1)S(1)}, bf16[96,1536]{1,0:T(8,128)(2,1)S(1)}, u32[]{:S(2)}, u32[]{:S(2)}) collective-permute-start(bf16[96,1536]{1,0:T(8,128)(2,1)S(1)} %get-tuple-element.44), channel_id=1, source_target_pairs={{0,3},{1,0},{2,1},{3,2},{4,7},{5,4},{6,5},{7,6},{8,11},{9,8},{10,9... | collective-permute-start | bytes 884744 | tf_op jit(solution)/shard_map/ppermute | solution.py:456
  84.2 15.5 %all-to-all-start.2 = ((bf16[16,144,128]{2,1,0:T(8,128)(2,1)}), bf16[16,144,128]{2,1,0:T(8,128)(2,1)S(1)}, u32[]{:S(2)}, u32[]{:S(2)}) async-start(bf16[16,144,128]{2,1,0:T(8,128)(2,1)} %ring_sum.1), calls=%async_computation.2 | async-start | bytes 1179648 | tf_op jit(solution)/shard_map/all_to_all | solution.py:467
  89.4 10.2 %collective-permute-start.7 = (f32[8,128]{1,0:T(8,128)S(1)}, f32[8,128]{1,0:T(8,128)S(1)}, u32[]{:S(2)}, u32[]{:S(2)}) collective-permute-start(f32[8,128]{1,0:T(8,128)S(1)} %get-tuple-element.45.g0), channel_id=1, source_target_pairs={{0,3},{1,0},{2,1},{3,2},{4,7},{5,4},{6,5},{7,6},{8,11},{9,8},{10,9... | collective-permute-start | bytes 12296 | tf_op jit(solution)/shard_map/ppermute | solution.py:468
  91.3 8.4 %collective-permute-start.6 = (f32[8,128]{1,0:T(8,128)S(1)}, f32[8,128]{1,0:T(8,128)S(1)}, u32[]{:S(2)}, u32[]{:S(2)}) collective-permute-start(f32[8,128]{1,0:T(8,128)S(1)} %get-tuple-element.45.g0), channel_id=1, source_target_pairs={{0,2},{1,3},{2,0},{3,1},{4,6},{5,7},{6,4},{7,5},{8,10},{9,11},{10,... | collective-permute-start | bytes 12296 | tf_op jit(solution)/shard_map/ppermute | solution.py:468
  91.9 7.7 %collective-permute-start.5 = (f32[8,128]{1,0:T(8,128)S(1)}, f32[8,128]{1,0:T(8,128)S(1)}, u32[]{:S(2)}, u32[]{:S(2)}) collective-permute-start(f32[8,128]{1,0:T(8,128)S(1)} %get-tuple-element.45.g0), channel_id=1, source_target_pairs={{0,1},{1,2},{2,3},{3,0},{4,5},{5,6},{6,7},{7,4},{8,9},{9,10},{10,1... | collective-permute-start | bytes 12296 | tf_op jit(solution)/shard_map/ppermute | solution.py:468

commit v13 on v12

--- a/solution.py
+++ b/solution.py
@@ -282,16 +282,16 @@
     grad = (gy + back).astype(BF)
     for l in range(6):
         ret_ref[:, l * 16 : l * 16 + 16] = grad[:, l * 128 : l * 128 + 128].reshape(32, 16, 128)
-    k = lax.broadcasted_iota(jnp.int32, (32, 8, 128), 0) * 24
-    lane = lax.broadcasted_iota(jnp.int32, (32, 8, 128), 2)
-    own = jnp.zeros((32, 8, 128), F32)
+    k = lax.broadcasted_iota(jnp.int32, (32, 16, 128), 0) * 24
+    lane = lax.broadcasted_iota(jnp.int32, (32, 16, 128), 2)
+    own = jnp.zeros((32, 16, 128), F32)
     for l in range(6):
         f = lane + l * 128
         part = g[:, l * 128 : l * 128 + 128].reshape(1, 1, 128)
         own = own + jnp.where(jnp.logical_and(f >= k, f < k + 24), part, 0.0)
     high = own.astype(BF).astype(F32)
     mid = (own - high).astype(BF).astype(F32)
-    row = lax.broadcasted_iota(jnp.int32, (32, 8, 128), 1)
+    row = lax.broadcasted_iota(jnp.int32, (32, 16, 128), 1)
     low = own - high - mid
     terms = jnp.where(row == 0, high, jnp.where(row == 1, mid, jnp.where(row == 2, low, 0.0)))
     ret_ref[:, 96:] = terms.astype(BF)
@@ -355,15 +355,15 @@
 
 
 def ring_sum_kernel(near, up_far, down_far, o):
-    for q in range(4):
-        r = slice(q * 24, q * 24 + 24)
+    for q in range(2):
+        r = slice(q * 48, q * 48 + 48)
         x = near[r, :HALF] + up_far[r].astype(F32)
         y = near[r, HALF:] + down_far[r].astype(F32)
-        for k in range(4):
+        for k in range(8):
             pieces = [
                 v[k * 6 : k * 6 + 6, l * 128 : l * 128 + 128] for v in (x, y) for l in range(12)
             ]
-            o[q * 4 + k] = jnp.concatenate(pieces, axis=0).astype(BF)
+            o[q * 8 + k] = jnp.concatenate(pieces, axis=0).astype(BF)
 
 
 def final_kernel(first_ref, in_ref, g0, g1, g2, g3, qkv_ref, out_ref, gain_ref, sum_ref):
@@ -428,11 +428,11 @@
     )(recv, gain, place, w_qkv, w_out)
     got = lax.ppermute(send, AXES, CORE_SWAP)
     grads = pl.pallas_call(
-        token_kernel, out_shape=shape(32, 104, 128),
+        token_kernel, out_shape=shape(32, 112, 128),
         compiler_params=params(TOKEN_MB), cost_estimate=cost(2.8e9, 9e6), name="token_grads",
     )(recv, gain, dqkv, w_qkv)
     ret = pl.pallas_call(
-        mixed_kernel, out_shape=shape(32, 200, 128), out_specs=HBM,
+        mixed_kernel, out_shape=shape(32, 208, 128), out_specs=HBM,
         scratch_shapes=[pltpu.VMEM((32, 96, 128), BF), DMA((3,))],
         compiler_params=params(14), cost_estimate=cost(1e9, 5e6), name="mixed",
     )(recv, attn, w_out, grads)

time: 101 us -> 102 us (level)
  no operation moved by 1% of the time
where the time goes in v13:
time: 102 us; the launch traced here: 101 us
  waiting for transfers between devices  48 us (47%)
  starting transfers between devices  26.4 us (26%)
  Pallas kernels  25.1 us (25%)
    all_to_all x1, waiting for transfers between devices, per_device(): lax.all_to_all(packed, AXES, 0, 0, tiled=True, axis_index_groups=PLANE)  22.4 us
    pallas_call x1, Pallas kernels, per_device(): pl.pallas_call(main_kernel, out_shape=(shape(384, 4 * D), shape(384, 4 *...  11.5 us
    ppermute x1, waiting for transfers between devices, per_device(): up = lax.ppermute(up, AXES, y_shift(1))  9.99 us
    all_to_all x1, starting transfers between devices, per_device(): lax.all_to_all(packed, AXES, 0, 0, tiled=True, axis_index_groups=PLANE)  8.38 us
    all_to_all x1, waiting for transfers between devices, per_device(): last = lax.all_to_all(mine, AXES, 0, 0, tiled=True, axis_index_groups=CHIPS)  6.64 us
    ppermute x1, waiting for transfers between devices, per_device(): up_far = lax.ppermute(up_far, AXES, y_shift(1))  6.54 us
    all_to_all x1, starting transfers between devices, per_device(): back = lax.all_to_all(ret, AXES, 0, 0, tiled=True, axis_index_groups=PLANE)  3.98 us
    all_to_all x1, starting transfers between devices, per_device(): last = lax.all_to_all(mine, AXES, 0, 0, tiled=True, axis_index_groups=CHIPS)  3.75 us
  transfers between devices with their start and end apart: 11, of which 6 were waited for; matrix products, arithmetic and copies ran while one was open for 1% of the time, Pallas kernels for 9%

profile of v13, /device:TPU:0, one launch (start us, length us, event | category | flops | bytes accessed | tf_op | source)
XLA Modules:
  0.0 101.0 jit_solution(5304064429567333604)
XLA Ops:
  0.6 2.8 %pack.1 = bf16[32,2,16,768]{3,2,1,0:T(8,128)(2,1)} custom-call(bf16[4,128,768]{2,1,0:T(8,128)(2,1)} %tok_hbm.1, bf16[4,128,768]{2,1,0:T(8,128)(2,1)} %cot_hbm.1, s32[4,128]{1,0:T(4,128)} %les_hbm.1), custom_call_target="tpu_custom_call" | custom-call | flops 1000000000 | bytes 4000000 | tf_op jit(solution)/shard_map/pack/pallas_call | solution.py:409
  3.4 0.0 copy-start.2
  3.4 0.0 copy-start
  3.5 8.4 %all-to-all-start = ((bf16[32,2,16,768]{3,2,1,0:T(8,128)(2,1)}), bf16[32,2,16,768]{3,2,1,0:T(8,128)(2,1)S(1)}, u32[]{:S(2)}, u32[]{:S(2)}) async-start(bf16[32,2,16,768]{3,2,1,0:T(8,128)(2,1)} %pack.1), calls=%async_computation | async-start | bytes 3145728 | tf_op jit(solution)/shard_map/all_to_all | solution.py:417
  11.9 0.0 copy-done.2
  11.9 0.8 constant_dynamic-slice_fusion.place_ref
  12.6 22.4 %all-to-all-done.recv_hbm.recv_ref = bf16[32,2,16,768]{3,2,1,0:T(8,128)(2,1)S(1)} async-done(((bf16[32,2,16,768]{3,2,1,0:T(8,128)(2,1)}), bf16[32,2,16,768]{3,2,1,0:T(8,128)(2,1)S(1)}, u32[]{:S(2)}, u32[]{:S(2)}) %all-to-all-start) | async-done | bytes 1572896 | tf_op jit(solution)/shard_map/all_to_all | solution.py:417
  35.0 0.0 copy-done
  35.0 0.0 copy-start.1
  35.0 11.5 %main.1 = (bf16[384,3072]{1,0:T(8,128)(2,1)S(1)}, bf16[384,3072]{1,0:T(8,128)(2,1)S(1)}, bf16[512,768]{1,0:T(8,128)(2,1)S(1)}, bf16[512,2304]{1,0:T(8,128)(2,1)S(1)}) custom-call(bf16[32,2,16,768]{3,2,1,0:T(8,128)(2,1)S(1)} %all-to-all-done.recv_hbm.recv_ref, f32[1,768]{1,0:T(1,128)S(1)} %reshape.19.gain_ref, ...), custom_call_target="tpu_custom_call" | custom-call | flops 10000000000 | bytes 15000000 | tf_op jit(solution)/shard_map/main/pallas_call | solution.py:418
  46.5 0.3 collective-permute-start
  46.8 0.0 copy-done.1
  46.8 3.1 %token_grads.1.grad_ref = bf16[32,112,128]{2,1,0:T(8,128)(2,1)S(1)} custom-call(bf16[32,2,16,768]{3,2,1,0:T(8,128)(2,1)S(1)} %all-to-all-done.recv_hbm.recv_ref, f32[1,768]{1,0:T(1,128)S(1)} %reshape.19.gain_ref, bf16[512,2304]{1,0:T(8,128)(2,1)S(1)} %get-tuple-element.34.dqkv_ref, bf16[768,2304]{1,0:T(8,128)(2,1)S(1)} %copy-done.1), custom_call_target="tpu_custom_call" | custom-call | flops 2800000000 | bytes 9000000 | tf_op jit(solution)/shard_map/token_grads/pallas_call | solution.py:430
  50.0 1.8 %mixed.1 = bf16[32,208,128]{2,1,0:T(8,128)(2,1)} custom-call(bf16[32,2,16,768]{3,2,1,0:T(8,128)(2,1)S(1)} %all-to-all-done.recv_hbm.recv_ref, bf16[512,768]{1,0:T(8,128)(2,1)S(1)} %get-tuple-element.33.attn_ref, bf16[768,768]{1,0:T(8,128)(2,1)S(1)} %copy-done, bf16[32,112,128]{2,1,0:T(8,128)(2,1)S(1)} %token_grads.1.grad_ref), custom_call_target="tpu_custom_call" | custom-call | flops 1000000000 | bytes 5000000 | tf_op jit(solution)/shard_map/mixed/pallas_call | solution.py:434
  51.8 0.0 collective-permute-done.b_ref
  51.8 1.2 %pair_sum.1 = (bf16[96,3072]{1,0:T(8,128)(2,1)S(1)}, bf16[96,3072]{1,0:T(8,128)(2,1)}, bf16[96,3072]{1,0:T(8,128)(2,1)}, bf16[96,3072]{1,0:T(8,128)(2,1)S(1)}) custom-call(bf16[384,3072]{1,0:T(8,128)(2,1)S(1)} %get-tuple-element.27.a_ref, bf16[384,3072]{1,0:T(8,128)(2,1)S(1)} %collective-permute-done.b_ref), custom_call_target="tpu_custom_call" | custom-call | flops 1000000 | bytes 7000000 | tf_op jit(solution)/shard_map/pair_sum/pallas_call | solution.py:439
  53.0 1.7 %collective-permute-start.1 = (bf16[96,3072]{1,0:T(8,128)(2,1)}, bf16[96,3072]{1,0:T(8,128)(2,1)S(1)}, u32[]{:S(2)}, u32[]{:S(2)}) collective-permute-start(bf16[96,3072]{1,0:T(8,128)(2,1)} %get-tuple-element.39), channel_id=1, source_target_pairs={{0,1},{1,2},{2,3},{3,0},{4,5},{5,6},{6,7},{7,4},{8,9},{9,10},{10,1... | collective-permute-start | bytes 1769480 | tf_op jit(solution)/shard_map/ppermute | solution.py:446
  54.6 1.7 %collective-permute-start.2 = (bf16[96,3072]{1,0:T(8,128)(2,1)}, bf16[96,3072]{1,0:T(8,128)(2,1)}, u32[]{:S(2)}, u32[]{:S(2)}) collective-permute-start(bf16[96,3072]{1,0:T(8,128)(2,1)} %get-tuple-element.40), channel_id=1, source_target_pairs={{0,3},{1,0},{2,1},{3,2},{4,7},{5,4},{6,5},{7,6},{8,11},{9,8},{10,9... | collective-permute-start | bytes 1769480 | tf_op jit(solution)/shard_map/ppermute | solution.py:447
  56.3 4.0 %all-to-all-start.1 = ((bf16[32,208,128]{2,1,0:T(8,128)(2,1)}), bf16[32,208,128]{2,1,0:T(8,128)(2,1)S(1)}, u32[]{:S(2)}, u32[]{:S(2)}) async-start(bf16[32,208,128]{2,1,0:T(8,128)(2,1)} %mixed.1), calls=%async_computation.1 | async-start | bytes 3407872 | tf_op jit(solution)/shard_map/all_to_all | solution.py:457
  60.3 10.0 %collective-permute-done.1.up = bf16[96,3072]{1,0:T(8,128)(2,1)S(1)} collective-permute-done((bf16[96,3072]{1,0:T(8,128)(2,1)}, bf16[96,3072]{1,0:T(8,128)(2,1)S(1)}, u32[]{:S(2)}, u32[]{:S(2)}) %collective-permute-start.1) | collective-permute-done | bytes 589856 | tf_op jit(solution)/shard_map/ppermute | solution.py:446
  70.3 0.1 collective-permute-done.2.down_hbm
  70.4 1.2 %pass_on.1 = (bf16[96,1536]{1,0:T(8,128)(2,1)S(1)}, bf16[96,1536]{1,0:T(8,128)(2,1)S(1)}, f32[96,3072]{1,0:T(8,128)S(1)}) custom-call(bf16[96,3072]{1,0:T(8,128)(2,1)S(1)} %get-tuple-element.38.hold, bf16[96,3072]{1,0:T(8,128)(2,1)S(1)} %collective-permute-done.1.up, bf16[96,3072]{1,0:T(8,128)(2,1)} %collective-permute-done.2.down_hbm, ...), custom_call_target="tpu_custom_call" | custom-call | flops 1000000 | bytes 3000000 | tf_op jit(solution)/shard_map/pass_on/pallas_call | solution.py:448
  71.6 1.6 %collective-permute-start.3 = (bf16[96,1536]{1,0:T(8,128)(2,1)S(1)}, bf16[96,1536]{1,0:T(8,128)(2,1)S(1)}, u32[]{:S(2)}, u32[]{:S(2)}) collective-permute-start(bf16[96,1536]{1,0:T(8,128)(2,1)S(1)} %get-tuple-element.43), channel_id=1, source_target_pairs={{0,1},{1,2},{2,3},{3,0},{4,5},{5,6},{6,7},{7,4},{8,9},{9,10},{10,1... | collective-permute-start | bytes 884744 | tf_op jit(solution)/shard_map/ppermute | solution.py:455
  73.2 1.7 %collective-permute-start.4 = (bf16[96,1536]{1,0:T(8,128)(2,1)S(1)}, bf16[96,1536]{1,0:T(8,128)(2,1)S(1)}, u32[]{:S(2)}, u32[]{:S(2)}) collective-permute-start(bf16[96,1536]{1,0:T(8,128)(2,1)S(1)} %get-tuple-element.44), channel_id=1, source_target_pairs={{0,3},{1,0},{2,1},{3,2},{4,7},{5,4},{6,5},{7,6},{8,11},{9,8},{10,9... | collective-permute-start | bytes 884744 | tf_op jit(solution)/shard_map/ppermute | solution.py:456
  74.9 6.5 %collective-permute-done.3.up_far = bf16[96,1536]{1,0:T(8,128)(2,1)S(1)} collective-permute-done((bf16[96,1536]{1,0:T(8,128)(2,1)S(1)}, bf16[96,1536]{1,0:T(8,128)(2,1)S(1)}, u32[]{:S(2)}, u32[]{:S(2)}) %collective-permute-start.3) | collective-permute-done | bytes 294944 | tf_op jit(solution)/shard_map/ppermute | solution.py:455
  81.4 0.0 collective-permute-done.4.down_far
  81.4 1.0 %ring_sum.1 = bf16[16,144,128]{2,1,0:T(8,128)(2,1)} custom-call(f32[96,3072]{1,0:T(8,128)S(1)} %get-tuple-element.42.near, bf16[96,1536]{1,0:T(8,128)(2,1)S(1)} %collective-permute-done.3.up_far, bf16[96,1536]{1,0:T(8,128)(2,1)S(1)} %collective-permute-done.4.down_far), custom_call_target="tpu_custom_call" | custom-call | flops 10000000000 | bytes 3000000 | tf_op jit(solution)/shard_map/ring_sum/pallas_call | solution.py:458
  82.5 2.3 %all-to-all-done.1.in_ref = bf16[32,208,128]{2,1,0:T(8,128)(2,1)S(1)} async-done(((bf16[32,208,128]{2,1,0:T(8,128)(2,1)}), bf16[32,208,128]{2,1,0:T(8,128)(2,1)S(1)}, u32[]{:S(2)}, u32[]{:S(2)}) %all-to-all-start.1) | async-done | bytes 1703968 | tf_op jit(solution)/shard_map/all_to_all | solution.py:457
  84.8 3.7 %all-to-all-start.2 = ((bf16[16,144,128]{2,1,0:T(8,128)(2,1)}), bf16[16,144,128]{2,1,0:T(8,128)(2,1)S(1)}, u32[]{:S(2)}, u32[]{:S(2)}) async-start(bf16[16,144,128]{2,1,0:T(8,128)(2,1)} %ring_sum.1), calls=%async_computation.2 | async-start | bytes 1179648 | tf_op jit(solution)/shard_map/all_to_all | solution.py:467
  88.6 1.7 %unpack.1 = (bf16[4,128,768]{2,1,0:T(8,128)(2,1)}, bf16[4,128,768]{2,1,0:T(8,128)(2,1)}, f32[8,128]{1,0:T(8,128)S(1)}) custom-call(bf16[32,208,128]{2,1,0:T(8,128)(2,1)S(1)} %all-to-all-done.1.in_ref), custom_call_target="tpu_custom_call" | custom-call | flops 1000000000 | bytes 4000000 | tf_op jit(solution)/shard_map/unpack/pallas_call | solution.py:462
  90.2 1.8 %collective-permute-start.7 = (f32[8,128]{1,0:T(8,128)S(1)}, f32[8,128]{1,0:T(8,128)S(1)}, u32[]{:S(2)}, u32[]{:S(2)}) collective-permute-start(f32[8,128]{1,0:T(8,128)S(1)} %get-tuple-element.45.g0), channel_id=1, source_target_pairs={{0,3},{1,0},{2,1},{3,2},{4,7},{5,4},{6,5},{7,6},{8,11},{9,8},{10,9... | collective-permute-start | bytes 12296 | tf_op jit(solution)/shard_map/ppermute | solution.py:468
  92.0 0.6 collective-permute-start.6
  92.7 1.0 collective-permute-start.5
  93.6 6.6 %all-to-all-done.2.in_ref = bf16[16,144,128]{2,1,0:T(8,128)(2,1)S(1)} async-done(((bf16[16,144,128]{2,1,0:T(8,128)(2,1)}), bf16[16,144,128]{2,1,0:T(8,128)(2,1)S(1)}, u32[]{:S(2)}, u32[]{:S(2)}) %all-to-all-start.2) | async-done | bytes 589856 | tf_op jit(solution)/shard_map/all_to_all | solution.py:467
  100.3 0.0 collective-permute-done.7.g3
  100.3 0.0 collective-permute-done.6.g2
  100.3 0.0 collective-permute-done.5.g1
  100.3 0.7 final.1
  (1 shorter events, 0.0 us)
Async XLA Ops:
  3.4 8.4 %copy-start.2 = (f32[768]{0:T(1024)S(1)}, f32[768]{0:T(1024)}, u32[]{:S(2)}) copy-start(f32[768]{0:T(1024)} %param.12) | copy-start | bytes 9220
  3.4 31.5 %copy-start = (bf16[768,768]{1,0:T(8,128)(2,1)S(1)}, bf16[768,768]{1,0:T(8,128)(2,1)}, u32[]{:S(2)}) copy-start(bf16[768,768]{1,0:T(8,128)(2,1)} %wout_ref.1) | copy-start | bytes 3538948
  3.5 31.5 %all-to-all-start = ((bf16[32,2,16,768]{3,2,1,0:T(8,128)(2,1)}), bf16[32,2,16,768]{3,2,1,0:T(8,128)(2,1)S(1)}, u32[]{:S(2)}, u32[]{:S(2)}) async-start(bf16[32,2,16,768]{3,2,1,0:T(8,128)(2,1)} %pack.1), calls=%async_computation | async-start | bytes 3145728 | tf_op jit(solution)/shard_map/all_to_all | solution.py:417
  35.0 11.8 %copy-start.1 = (bf16[768,2304]{1,0:T(8,128)(2,1)S(1)}, bf16[768,2304]{1,0:T(8,128)(2,1)}, u32[]{:S(2)}) copy-start(bf16[768,2304]{1,0:T(8,128)(2,1)} %wqkv_ref.1) | copy-start | bytes 10616836
  46.5 5.2 %collective-permute-start = (bf16[384,3072]{1,0:T(8,128)(2,1)S(1)}, bf16[384,3072]{1,0:T(8,128)(2,1)S(1)}, u32[]{:S(2)}, u32[]{:S(2)}) collective-permute-start(bf16[384,3072]{1,0:T(8,128)(2,1)S(1)} %get-tuple-element.28), channel_id=1, source_target_pairs={{0,8},{1,9},{2,10},{3,11},{4,12},{5,13},{6,14},{7,15},{8,0},{9,1},... | collective-permute-start | bytes 7077896 | tf_op jit(solution)/shard_map/ppermute | solution.py:429
  53.0 17.3 %collective-permute-start.1 = (bf16[96,3072]{1,0:T(8,128)(2,1)}, bf16[96,3072]{1,0:T(8,128)(2,1)S(1)}, u32[]{:S(2)}, u32[]{:S(2)}) collective-permute-start(bf16[96,3072]{1,0:T(8,128)(2,1)} %get-tuple-element.39), channel_id=1, source_target_pairs={{0,1},{1,2},{2,3},{3,0},{4,5},{5,6},{6,7},{7,4},{8,9},{9,10},{10,1... | collective-permute-start | bytes 1769480 | tf_op jit(solution)/shard_map/ppermute | solution.py:446
  54.6 15.8 %collective-permute-start.2 = (bf16[96,3072]{1,0:T(8,128)(2,1)}, bf16[96,3072]{1,0:T(8,128)(2,1)}, u32[]{:S(2)}, u32[]{:S(2)}) collective-permute-start(bf16[96,3072]{1,0:T(8,128)(2,1)} %get-tuple-element.40), channel_id=1, source_target_pairs={{0,3},{1,0},{2,1},{3,2},{4,7},{5,4},{6,5},{7,6},{8,11},{9,8},{10,9... | collective-permute-start | bytes 1769480 | tf_op jit(solution)/shard_map/ppermute | solution.py:447
  56.3 28.5 %all-to-all-start.1 = ((bf16[32,208,128]{2,1,0:T(8,128)(2,1)}), bf16[32,208,128]{2,1,0:T(8,128)(2,1)S(1)}, u32[]{:S(2)}, u32[]{:S(2)}) async-start(bf16[32,208,128]{2,1,0:T(8,128)(2,1)} %mixed.1), calls=%async_computation.1 | async-start | bytes 3407872 | tf_op jit(solution)/shard_map/all_to_all | solution.py:457
  71.6 9.8 %collective-permute-start.3 = (bf16[96,1536]{1,0:T(8,128)(2,1)S(1)}, bf16[96,1536]{1,0:T(8,128)(2,1)S(1)}, u32[]{:S(2)}, u32[]{:S(2)}) collective-permute-start(bf16[96,1536]{1,0:T(8,128)(2,1)S(1)} %get-tuple-element.43), channel_id=1, source_target_pairs={{0,1},{1,2},{2,3},{3,0},{4,5},{5,6},{6,7},{7,4},{8,9},{9,10},{10,1... | collective-permute-start | bytes 884744 | tf_op jit(solution)/shard_map/ppermute | solution.py:455
  73.2 8.2 %collective-permute-start.4 = (bf16[96,1536]{1,0:T(8,128)(2,1)S(1)}, bf16[96,1536]{1,0:T(8,128)(2,1)S(1)}, u32[]{:S(2)}, u32[]{:S(2)}) collective-permute-start(bf16[96,1536]{1,0:T(8,128)(2,1)S(1)} %get-tuple-element.44), channel_id=1, source_target_pairs={{0,3},{1,0},{2,1},{3,2},{4,7},{5,4},{6,5},{7,6},{8,11},{9,8},{10,9... | collective-permute-start | bytes 884744 | tf_op jit(solution)/shard_map/ppermute | solution.py:456
  84.8 15.5 %all-to-all-start.2 = ((bf16[16,144,128]{2,1,0:T(8,128)(2,1)}), bf16[16,144,128]{2,1,0:T(8,128)(2,1)S(1)}, u32[]{:S(2)}, u32[]{:S(2)}) async-start(bf16[16,144,128]{2,1,0:T(8,128)(2,1)} %ring_sum.1), calls=%async_computation.2 | async-start | bytes 1179648 | tf_op jit(solution)/shard_map/all_to_all | solution.py:467
  90.2 10.1 %collective-permute-start.7 = (f32[8,128]{1,0:T(8,128)S(1)}, f32[8,128]{1,0:T(8,128)S(1)}, u32[]{:S(2)}, u32[]{:S(2)}) collective-permute-start(f32[8,128]{1,0:T(8,128)S(1)} %get-tuple-element.45.g0), channel_id=1, source_target_pairs={{0,3},{1,0},{2,1},{3,2},{4,7},{5,4},{6,5},{7,6},{8,11},{9,8},{10,9... | collective-permute-start | bytes 12296 | tf_op jit(solution)/shard_map/ppermute | solution.py:468
  92.0 8.3 %collective-permute-start.6 = (f32[8,128]{1,0:T(8,128)S(1)}, f32[8,128]{1,0:T(8,128)S(1)}, u32[]{:S(2)}, u32[]{:S(2)}) collective-permute-start(f32[8,128]{1,0:T(8,128)S(1)} %get-tuple-element.45.g0), channel_id=1, source_target_pairs={{0,2},{1,3},{2,0},{3,1},{4,6},{5,7},{6,4},{7,5},{8,10},{9,11},{10,... | collective-permute-start | bytes 12296 | tf_op jit(solution)/shard_map/ppermute | solution.py:468
  92.7 7.6 %collective-permute-start.5 = (f32[8,128]{1,0:T(8,128)S(1)}, f32[8,128]{1,0:T(8,128)S(1)}, u32[]{:S(2)}, u32[]{:S(2)}) collective-permute-start(f32[8,128]{1,0:T(8,128)S(1)} %get-tuple-element.45.g0), channel_id=1, source_target_pairs={{0,1},{1,2},{2,3},{3,0},{4,5},{5,6},{6,7},{7,4},{8,9},{9,10},{10,1... | collective-permute-start | bytes 12296 | tf_op jit(solution)/shard_map/ppermute | solution.py:468
